TPU v7x, 512 devices: a whole 4x4x16 slice. The times are simulated.
512 devices in a mesh: row: 32 (over z_hi, y, core), res: 16 (over x, z_lo).
Axes of the slice: x: 4, y: 4, z: 16 (z_hi: 4, z_lo: 4; z = z_hi * 4 + z_lo), core: 2. Of those that a mesh axis runs over, the one named last changes fastest.
Arguments:
- queries: bfloat16 [128, 1024, 384], P('row', 'res'), may hold values from -64 to 64
- keys: bfloat16 [128, 1024, 384], P('row', 'res'), may hold values from -4 to 4
- values: bfloat16 [128, 1024, 384], P('row', 'res'), may hold values from -36 to 36
- out_weight: bfloat16 [384, 768], replicated, may hold values from -0.3125 to 0.3125
- grad_out: bfloat16 [128, 1024, 768], P('row', 'res'), may hold values from -24 to 24
Outputs:
- mixed_out: bfloat16 [128, 1024, 768], P('row', 'res')
- grad_query: bfloat16 [128, 1024, 384], P('row', 'res')
- grad_key: bfloat16 [128, 1024, 384], P('row', 'res')
- grad_value: bfloat16 [128, 1024, 384], P('row', 'res')
All inputs are finite; a program needn't handle non-finite values.
Results may differ from a plain program's by a relative error of at most 0.013.
Values may be sent and summed in bfloat16 or wider, within the bound.
No kernel may reach another device: no remote copies, remote signals or barrier semaphores. Data moves between devices by JAX's collectives and lax.ppermute only.
A program may use at most 64 MiB of HBM per device.

v0:
```python
import math

import jax
import jax.numpy as jnp
from jax import lax
from jax.sharding import PartitionSpec as P

HEADS = 6


def split_heads(array):
    return array.reshape(array.shape[0], array.shape[1], HEADS, array.shape[2] // HEADS)


def softmax_rows(logits):
    top = jnp.max(logits, axis=-1, keepdims=True)
    expo = jnp.exp(logits - top)
    return expo / jnp.sum(expo, axis=-1, keepdims=True)


def score_grad(weights, grads):
    return weights * (grads - jnp.sum(weights * grads, axis=-1, keepdims=True))


def on_device(queries, keys, values, out_weight, grad_out):
    seq_dev, res_dev, width = queries.shape
    model_dim = out_weight.shape[1]
    head_dim = width // HEADS
    total_res = res_dev * lax.axis_size("res")
    logit_scale = 1.0 / math.sqrt(head_dim * seq_dev * lax.axis_size("row"))
    grad_flat = lax.dot_general(
        grad_out.reshape(seq_dev * res_dev, model_dim),
        out_weight,
        (((1,), (1,)), ((), ())),
        preferred_element_type=jnp.float32,
    )
    grad_attended = grad_flat.astype(jnp.bfloat16).reshape(seq_dev, res_dev, width)
    key_all, value_all = (
        lax.all_gather(keys, "res", axis=1, tiled=True),
        lax.all_gather(values, "res", axis=1, tiled=True),
    )
    key_heads = split_heads(key_all)
    value_heads = split_heads(value_all)
    partial_logits = jnp.einsum(
        "sihd,sjhd->hij", split_heads(queries), key_heads, preferred_element_type=jnp.float32
    )
    partial_logits = partial_logits.reshape(HEADS * res_dev, total_res)
    tied_sum = lax.psum(partial_logits, "row") * logit_scale
    full_weights = softmax_rows(tied_sum)
    weights16 = full_weights.astype(jnp.bfloat16)
    weights_heads = weights16.reshape(HEADS, res_dev, total_res)
    attended = jnp.einsum(
        "hij,sjhd->sihd", weights_heads, value_heads, preferred_element_type=jnp.float32
    )
    attended = attended.astype(jnp.bfloat16).reshape(seq_dev * res_dev, width)
    mixed_out = jnp.dot(attended, out_weight, preferred_element_type=jnp.float32)
    mixed_out = mixed_out.astype(jnp.bfloat16).reshape(seq_dev, res_dev, model_dim)
    grad_partial = jnp.einsum(
        "sihd,sjhd->hij",
        split_heads(grad_attended),
        value_heads,
        preferred_element_type=jnp.float32,
    )
    grad_partial = grad_partial.reshape(HEADS * res_dev, total_res)
    tied_grads = lax.psum(grad_partial, "row")
    scores16 = score_grad(full_weights, tied_grads).astype(jnp.bfloat16)
    score_heads = scores16.reshape(HEADS, res_dev, total_res)
    grad_query = (
        jnp.einsum("hij,sjhd->sihd", score_heads, key_heads, preferred_element_type=jnp.float32)
        * logit_scale
    )
    grad_query = grad_query.astype(jnp.bfloat16).reshape(seq_dev, res_dev, width)
    query_all, grad_all = (
        lax.all_gather(queries, "res", axis=1, tiled=True),
        lax.all_gather(grad_attended, "res", axis=1, tiled=True),
    )
    weights_cols, scores_cols = (
        lax.all_to_all(weights_heads, "res", split_axis=2, concat_axis=1, tiled=True),
        lax.all_to_all(score_heads, "res", split_axis=2, concat_axis=1, tiled=True),
    )
    grad_value = jnp.einsum(
        "hij,sihd->sjhd", weights_cols, split_heads(grad_all), preferred_element_type=jnp.float32
    )
    grad_value = grad_value.astype(jnp.bfloat16).reshape(seq_dev, res_dev, width)
    grad_key = (
        jnp.einsum(
            "hij,sihd->sjhd",
            scores_cols,
            split_heads(query_all),
            preferred_element_type=jnp.float32,
        )
        * logit_scale
    )
    grad_key = grad_key.astype(jnp.bfloat16).reshape(seq_dev, res_dev, width)
    return (mixed_out, grad_query, grad_key, grad_value)


def solution(mesh):
    placed = (
        P("row", "res", None),
        P("row", "res", None),
        P("row", "res", None),
        P(),
        P("row", "res", None),
    )
    return jax.shard_map(
        on_device,
        mesh=mesh,
        in_specs=placed,
        out_specs=(
            P("row", "res", None),
            P("row", "res", None),
            P("row", "res", None),
            P("row", "res", None),
        ),
        check_vma=False,
    )
```

profile of v0, /device:TPU:1, one launch (start us, length us, event | category | flops | bytes accessed | tf_op | source)
XLA Modules:
  0.0 843.7 jit_solution(12867566409044667914)
XLA Ops:
  7.2 0.0 copy-start
  7.2 0.0 copy-start.5
  7.2 0.0 all-gather.5.cloned.1.call-start
  7.2 1.8 copy.59
  9.1 0.0 all-gather.5.cloned.1.call-update
  9.1 0.0 all-gather.7.cloned.1.call-start
  9.1 1.8 copy.63
  10.9 0.0 all-gather.7.cloned.1.call-update
  10.9 0.0 all-reduce.3.cloned.1.call-start
  11.0 1.2 reshape.59
  12.2 0.4 convolution_convert_fusion.1
  12.6 0.3 reshape.81
  12.9 92.6 %all-gather.5.cloned.1.call-done = bf16[4,1024,384]{2,0,1:T(4,128)(2,1)} async-done(((bf16[4,64,384]{2,0,1:T(4,128)(2,1)}), bf16[4,1024,384]{2,0,1:T(4,128)(2,1)}) %all-gather.5.cloned.1.call-update) | async-done | bytes 3145744 | tf_op jit(solution)/shard_map/all_gather | solution.py:39
  105.6 5.9 copy.60
  111.5 3.8 fusion.10
  115.3 88.5 %all-gather.7.cloned.1.call-done = bf16[4,1024,384]{2,0,1:T(4,128)(2,1)} async-done(((bf16[4,64,384]{2,0,1:T(4,128)(2,1)}), bf16[4,1024,384]{2,0,1:T(4,128)(2,1)}) %all-gather.7.cloned.1.call-update) | async-done | bytes 3145744 | tf_op jit(solution)/shard_map/all_gather | solution.py:40
  203.8 6.0 copy.64
  209.8 3.8 fusion.4
  213.5 0.0 all-reduce.3.cloned.1.call-update
  213.6 0.0 all-gather.9.cloned.1.call-start
  213.6 0.9 copy-done.4
  214.5 0.8 copy.74
  215.3 0.0 all-gather.9.cloned.1.call-update
  215.3 0.0 all-gather.11.cloned.1.call-start
  215.4 0.8 copy.78
  216.2 0.0 all-gather.11.cloned.1.call-update
  216.2 371.6 %all-reduce.3.cloned.1.call-done = (f32[384,1024]{1,0:T(8,128)}, f32[384,1024]{1,0:T(8,128)}) async-done(((f32[384,1024]{1,0:T(8,128)}, f32[384,1024]{1,0:T(8,128)}), (f32[384,1024]{1,0:T(8,128)}, f32[384,1024]{1,0:T(8,128)})) %all-reduce.3.cloned.1.call-update) | async-done | bytes 3145744 | tf_op jit(solution)/shard_map/psum | solution.py:48
  587.8 1.8 multiply_reduce_fusion.1
  589.5 0.1 copy-done.1
  589.7 0.4 fusion.19
  590.1 0.1 copy-done.2
  590.1 0.6 multiply_reduce_fusion
  590.7 1.4 multiply_convert_fusion
  592.1 1.7 copy.72
  593.8 2.2 reshape.84
  596.0 4.4 all-to-all-start
  600.4 2.6 copy.80
  603.0 2.2 reshape.86
  605.1 29.5 %all-to-all-done = bf16[16,2,12288]{2,1,0:T(2,128)(2,1)} async-done(((bf16[16,2,12288]{2,1,0:T(2,128)(2,1)}), bf16[16,2,12288]{2,1,0:T(2,128)(2,1)}, u32[]{:S(2)}, u32[]{:S(2)}) %all-to-all-start) | async-done | bytes 786464 | tf_op jit(solution)/shard_map/all_to_all | solution.py:79
  634.7 4.5 all-to-all-start.1
  639.1 64.1 %all-gather.9.cloned.1.call-done = bf16[4,1024,384]{2,0,1:T(4,128)(2,1)} async-done(((bf16[4,64,384]{2,0,1:T(4,128)(2,1)}), bf16[4,1024,384]{2,0,1:T(4,128)(2,1)}) %all-gather.9.cloned.1.call-update) | async-done | bytes 3145744 | tf_op jit(solution)/shard_map/all_gather | solution.py:74
  703.2 6.0 copy.75
  709.2 86.3 %all-gather.11.cloned.1.call-done = bf16[4,1024,384]{2,0,1:T(4,128)(2,1)} async-done(((bf16[4,64,384]{2,0,1:T(4,128)(2,1)}), bf16[4,1024,384]{2,0,1:T(4,128)(2,1)}) %all-gather.11.cloned.1.call-update) | async-done | bytes 3145744 | tf_op jit(solution)/shard_map/all_gather | solution.py:75
  795.5 6.0 copy.79
  801.5 3.5 fusion.32
  805.0 0.3 copy.66
  805.3 0.3 reshape.64
  805.6 3.5 fusion.38
  809.1 0.3 copy.71
  809.3 1.0 reshape.69
  810.4 1.1 convolution_convert_fusion
  811.5 3.5 reshape.85
  815.0 2.2 copy.131
  817.1 2.7 reshape.79
  819.9 3.5 fusion.41
  823.4 0.3 copy.77
  823.6 1.0 reshape.71
  824.7 0.0 all-to-all-done.1
  824.7 3.5 reshape.87
  828.1 2.2 copy.130
  830.3 2.7 reshape.80
  833.0 2.9 fusion.35
  835.9 0.3 copy.83
  836.2 1.0 reshape.74
  (7 shorter events, 0.0 us)
Async XLA Ops:
  7.2 5.1 copy-start
  7.2 5.0 copy-start.5
  7.2 98.4 %all-gather.5.cloned.1.call-start = ((), (), s32[]{:S(2)}) async-start(), calls=%async_computation.2 | async-start | bytes 3342336 | tf_op jit(solution)/shard_map/all_gather | solution.py:39
  9.1 194.7 %all-gather.7.cloned.1.call-start = ((), (), s32[]{:S(2)}) async-start(), calls=%async_computation.3 | async-start | bytes 3342336 | tf_op jit(solution)/shard_map/all_gather | solution.py:40
  10.9 576.9 %all-reduce.3.cloned.1.call-start = ((), (), s32[]{:S(2)}) async-start(), calls=%async_computation.6 | async-start | bytes 6291456 | tf_op jit(solution)/shard_map/psum | solution.py:48
  213.5 0.9 copy-start.4
  213.6 489.7 %all-gather.9.cloned.1.call-start = ((), (), s32[]{:S(2)}) async-start(), calls=%async_computation.4 | async-start | bytes 3342336 | tf_op jit(solution)/shard_map/all_gather | solution.py:74
  215.3 580.2 %all-gather.11.cloned.1.call-start = ((), (), s32[]{:S(2)}) async-start(), calls=%async_computation.5 | async-start | bytes 3342336 | tf_op jit(solution)/shard_map/all_gather | solution.py:75
  587.8 1.9 copy-start.1
  587.8 2.4 copy-start.2
  596.0 38.7 %all-to-all-start = ((bf16[16,2,12288]{2,1,0:T(2,128)(2,1)}), bf16[16,2,12288]{2,1,0:T(2,128)(2,1)}, u32[]{:S(2)}, u32[]{:S(2)}) async-start(bf16[16,2,12288]{2,1,0:T(2,128)(2,1)} %reshape.84), calls=%async_computation | async-start | bytes 1572864 | tf_op jit(solution)/shard_map/all_to_all | solution.py:79
  634.7 190.0 %all-to-all-start.1 = ((bf16[16,2,12288]{2,1,0:T(2,128)(2,1)}), bf16[16,2,12288]{2,1,0:T(2,128)(2,1)}, u32[]{:S(2)}, u32[]{:S(2)}) async-start(bf16[16,2,12288]{2,1,0:T(2,128)(2,1)} %reshape.86), calls=%async_computation.1 | async-start | bytes 1572864 | tf_op jit(solution)/shard_map/all_to_all | solution.py:78
  709.2 92.3 %copy-start.3 = (bf16[384,1024]{1,0:T(8,128)(2,1)S(1)}, bf16[384,1024]{1,0:T(8,128)(2,1)}, u32[]{:S(2)}) copy-start(bf16[384,1024]{1,0:T(8,128)(2,1)} %get-tuple-element.7) | copy-start | bytes 2359300
Sparse Core Ops, SparseCore 0:
  10.7 94.8 all-gather.4
  108.2 95.5 all-gather.6
  213.7 374.0 all-reduce.2
  590.5 112.6 all-gather.8
  705.9 89.5 all-gather.10
where the time goes:
time: 853 us; the launch traced here: 844 us
  waiting for transfers between devices  733 us (86%)
  local copies, waits for them, and re-layouts  61.4 us (7%)
  matrix products  22.4 us (3%)
  between operations  14 us (2%)
  starting transfers between devices  9.07 us (1%)
    psum x1, waiting for transfers between devices, on_device(): tied_sum = lax.psum(partial_logits, 'row') * logit_scale  372 us
    all_gather x1, waiting for transfers between devices, on_device(): lax.all_gather(keys, 'res', axis=1, tiled=True)  92.6 us
    all_gather x1, waiting for transfers between devices, on_device(): lax.all_gather(values, 'res', axis=1, tiled=True)  88.5 us
    all_gather x1, waiting for transfers between devices, on_device(): lax.all_gather(grad_attended, 'res', axis=1, tiled=True)  86.3 us
    all_gather x1, waiting for transfers between devices, on_device(): lax.all_gather(queries, 'res', axis=1, tiled=True)  64.1 us
    all_to_all x1, waiting for transfers between devices, on_device(): lax.all_to_all(score_heads, 'res', split_axis=2, concat_axis=1, tiled=True)  29.5 us
  transfers between devices with their start and end apart: 7, of which 6 were waited for; matrix products, arithmetic and copies ran while one was open for 7% of the time, Pallas kernels for 0%

commit v1 on v0

v1 whole, which is shorter than its diff:
```python
import math

import jax
import jax.numpy as jnp
from jax import lax
from jax.experimental import pallas as pl
from jax.experimental.pallas import tpu as pltpu
from jax.sharding import Mesh, PartitionSpec as P

HEADS = 6
PAIRS = 3
F32 = jnp.float32
BF16 = jnp.bfloat16
VMEM = 40 * 1024 * 1024


def params():
    return pltpu.CompilerParams(vmem_limit_bytes=VMEM)


def exchange(blocks, axis):
    return lax.all_to_all(blocks, axis, 0, 0, tiled=True)


def prep_kernel(q_ref, k_ref, v_ref, w_ref, go_ref, kv_ref, qg_ref):
    seqs, res, width = q_ref.shape
    for s in range(seqs):
        ga = lax.dot_general(
            go_ref[s], w_ref[...], (((1,), (1,)), ((), ())), preferred_element_type=F32
        ).astype(BF16)
        for n in range(kv_ref.shape[0]):
            qg_ref[n, 1, s] = ga
    for n in range(kv_ref.shape[0]):
        kv_ref[n, 0] = k_ref[...]
        kv_ref[n, 1] = v_ref[...]
        qg_ref[n, 0] = q_ref[...]


def columns(ref, which):
    n, _, seqs, res, lanes = ref.shape
    return jnp.concatenate([ref[:, which, s].reshape(n * res, lanes) for s in range(seqs)], axis=1)


def head_mask(shape, head):
    lane = lax.broadcasted_iota(jnp.int32, shape, 1)
    return ((lane // 64) % 2) == head


def product_kernel(kv_ref, qg_ref, out_ref):
    for which in range(2):
        left = columns(qg_ref, which)
        right = columns(kv_ref, which)
        for head in range(2):
            own = jnp.where(head_mask(left.shape, head), left, jnp.zeros_like(left))
            full = lax.dot_general(own, right, (((1,), (1,)), ((), ())), preferred_element_type=F32)
            out_ref[head, :, 0, which] = full.reshape(out_ref.shape[1], out_ref.shape[4], out_ref.shape[5])


def stats_kernel(scale, part_ref, e_ref, g_ref, stat_ref):
    total = part_ref[0] + part_ref[1] + part_ref[2] + part_ref[3]
    logits = total[:, 0] * scale
    grads = total[:, 1]
    top = jnp.max(logits, axis=-1, keepdims=True)
    expo = jnp.exp(logits - top)
    e_ref[...] = expo
    g_ref[...] = grads
    norm = jnp.sum(expo, axis=-1, keepdims=True)
    dot = jnp.sum(expo * grads, axis=-1, keepdims=True)
    lane = lax.broadcasted_iota(jnp.int32, stat_ref.shape[1:], 2)
    stat = jnp.where(lane == 0, top, jnp.where(lane == 1, norm, dot))
    for n in range(stat_ref.shape[0]):
        stat_ref[n] = stat


def weights_kernel(own_ref, stat_ref, e_ref, g_ref, out_ref):
    tops = stat_ref[:, :, :, 0:1]
    top = jnp.max(tops, axis=0)
    parts = jnp.exp(tops - top[None])
    norm = jnp.sum(parts * stat_ref[:, :, :, 1:2], axis=0)
    dot = jnp.sum(parts * stat_ref[:, :, :, 2:3], axis=0) / norm
    weights = e_ref[...] * (jnp.exp(own_ref[0, :, :, 0:1] - top) / norm)
    scores = weights * (g_ref[...] - dot)
    for n in range(out_ref.shape[0]):
        out_ref[n, 0] = weights.astype(BF16)
        out_ref[n, 1] = scores.astype(BF16)


def output_kernel(scale, ws_ref, kv_ref, qg_ref, row_ref, col_ref):
    def heads(which):
        return [ws_ref[c, :, :, which, 0].reshape(256, 256) for c in range(2)]

    def product(mats, side, contract):
        both = [
            lax.dot_general(m, side, (((contract,), (0,)), ((), ())), preferred_element_type=F32)
            for m in mats
        ]
        return jnp.where(head_mask(both[0].shape, 0), both[0], both[1])

    def put(ref, which, value):
        n, _, seqs, res, lanes = ref.shape
        value = value.astype(BF16)
        for s in range(seqs):
            ref[:, which, s] = value[:, s * lanes : (s + 1) * lanes].reshape(n, res, lanes)

    weights, scores = heads(0), heads(1)
    put(row_ref, 0, product(weights, columns(kv_ref, 1), 1))
    put(row_ref, 1, product(scores, columns(kv_ref, 0), 1) * scale)
    put(col_ref, 0, product(weights, columns(qg_ref, 1), 0))
    put(col_ref, 1, product(scores, columns(qg_ref, 0), 0) * scale)


def total_of(ref, which, s):
    parts = [ref[n, which, s].astype(F32) for n in range(ref.shape[0])]
    return ((parts[0] + parts[1]) + (parts[2] + parts[3])).astype(BF16)


def finish_kernel(row_ref, col_ref, w_ref, mixed_ref, gq_ref, gk_ref, gv_ref):
    for s in range(mixed_ref.shape[0]):
        attended = total_of(row_ref, 0, s)
        mixed_ref[s] = jnp.dot(attended, w_ref[...], preferred_element_type=F32).astype(BF16)
        gq_ref[s] = total_of(row_ref, 1, s)
        gv_ref[s] = total_of(col_ref, 0, s)
        gk_ref[s] = total_of(col_ref, 1, s)


def on_device(queries, keys, values, out_weight, grad_out):
    seqs, res, width = queries.shape
    model_dim = out_weight.shape[1]
    scale = 1.0 / math.sqrt(width // HEADS * seqs * 32)
    gathered = jax.ShapeDtypeStruct((4, 2, seqs, res, width), BF16)
    kv_send, qg_send = pl.pallas_call(
        prep_kernel, out_shape=(gathered, gathered), compiler_params=params(), name="prep"
    )(queries, keys, values, out_weight, grad_out)
    kv = exchange(kv_send, "x")
    qg = exchange(qg_send, "zl")

    slab = pl.BlockSpec((4, 2, seqs, res, 128), lambda p: (0, 0, 0, 0, p))
    partial = pl.pallas_call(
        product_kernel,
        grid=(PAIRS,),
        in_specs=[slab, slab],
        out_specs=pl.BlockSpec((2, 4, 1, 2, 64, 256), lambda p: (0, 0, p, 0, 0, 0)),
        out_shape=jax.ShapeDtypeStruct((2, 4, PAIRS, 2, 64, 256), F32),
        compiler_params=params(),
        name="products",
    )(kv, qg)
    partial = exchange(partial, "c")
    partial = partial[0] + partial[1]
    partial = exchange(partial, "y")
    partial = jnp.sum(partial, axis=0).reshape(PAIRS, 2, 4, 16, 256)
    partial = exchange(jnp.transpose(partial, (2, 0, 1, 3, 4)), "zh")

    tile = jax.ShapeDtypeStruct((PAIRS, 16, 256), F32)
    e, g, stat = pl.pallas_call(
        lambda *refs: stats_kernel(scale, *refs),
        out_shape=(tile, tile, jax.ShapeDtypeStruct((4, PAIRS, 16, 128), F32)),
        compiler_params=params(),
        name="stats",
    )(partial)
    stats = exchange(stat, "zl")
    ws = pl.pallas_call(
        weights_kernel,
        out_shape=jax.ShapeDtypeStruct((4, 2, PAIRS, 16, 256), BF16),
        compiler_params=params(),
        name="weights",
    )(stat, stats, e, g)
    ws = exchange(ws, "zh")
    ws = exchange(jnp.broadcast_to(ws[None], (4,) + ws.shape), "y")
    ws = exchange(jnp.broadcast_to(ws[None], (2,) + ws.shape), "c")

    row, col = pl.pallas_call(
        lambda *refs: output_kernel(scale, *refs),
        grid=(PAIRS,),
        in_specs=[pl.BlockSpec((2, 4, 4, 2, 1, 16, 256), lambda p: (0, 0, 0, 0, p, 0, 0)), slab, slab],
        out_specs=[slab, slab],
        out_shape=(gathered, gathered),
        compiler_params=params(),
        name="outputs",
    )(ws, kv, qg)
    row = exchange(row, "zl")
    col = exchange(col, "x")
    grad = jax.ShapeDtypeStruct((seqs, res, width), BF16)
    return pl.pallas_call(
        finish_kernel,
        out_shape=(jax.ShapeDtypeStruct((seqs, res, model_dim), BF16), grad, grad, grad),
        compiler_params=params(),
        name="finish",
    )(row, col, out_weight)


def solution(mesh):
    grid = Mesh(mesh.devices.reshape(4, 4, 2, 4, 4), ("zh", "y", "c", "x", "zl"))
    placed = P(("zh", "y", "c"), ("x", "zl"), None)
    return jax.shard_map(
        on_device,
        mesh=grid,
        in_specs=(placed, placed, placed, P(), placed),
        out_specs=(placed, placed, placed, placed),
        check_vma=False,
    )
```

time: 853 us -> 259 us (0.30); the launches traced: 844 us -> 259 us
  waiting for transfers between devices: 733 us -> 0 us
  blocking collectives: 0 us -> 243 us
  local copies, waits for them, and re-layouts: 61.4 us -> 5.13 us
  matrix products: 22.4 us -> 0 us
  between operations: 14 us -> 0.72 us
  starting transfers between devices: 9.07 us -> 0 us
    psum x1 -> x0, waiting for transfers between devices: 372 us -> none  [on_device(): tied_sum = lax.psum(partial_logits, 'row') * logit_scale]
    all_gather x4 -> x0, waiting for transfers between devices: 332 us -> none  [the longest x1 92.6 us: on_device(): lax.all_gather(keys, 'res', axis=1, tiled=True)]
    all_to_all x0 -> x11, blocking collectives: none -> 243 us  [exchange(): return lax.all_to_all(blocks, axis, 0, 0, tiled=True)]
    all_to_all x2 -> x0, waiting for transfers between devices: 29.5 us -> none  [the longest x1 29.5 us: on_device(): lax.all_to_all(score_heads, 'res', split_axis=2, concat_axis=1, tiled=True)]
    all_gather x4 -> x0, local copies, waits for them, and re-layouts: 23.9 us -> none  [the longest x1 6 us: on_device(): lax.all_gather(values, 'res', axis=1, tiled=True)]
    dot_general x8 -> x0, matrix products: 22.4 us -> none  [the longest x1 3.78 us: on_device(): jnp.einsum('sihd,sjhd->hij', split_heads(queries), key_heads, preferred_e...]
    unnamed x19 -> x12, local copies, waits for them, and re-layouts: 16.7 us -> 4.84 us
    all_to_all x4 -> x0, local copies, waits for them, and re-layouts: 9.79 us -> none  [the longest x2 4.89 us: on_device(): lax.all_to_all(score_heads, 'res', split_axis=2, concat_axis=1, tiled=True)]
  transfers between devices with their start and end apart: 7 -> 0, of which waited for: 6 -> 0; matrix products, arithmetic and copies ran while one was open for 7% -> 0% of each run, Pallas kernels for 0% -> 0%
where the time goes in v1:
time: 259 us
  blocking collectives  243 us (94%)
  Pallas kernels  8.31 us (3%)
  local copies, waits for them, and re-layouts  5.13 us (2%)
    all_to_all x11, blocking collectives, exchange(): return lax.all_to_all(blocks, axis, 0, 0, tiled=True)  243 us

profile of v1, /device:TPU:1, one launch (start us, length us, event | category | flops | bytes accessed | tf_op | source)
XLA Modules:
  0.0 258.6 jit_solution(3438736746778377131)
XLA Ops:
  0.6 0.0 copy-start
  0.6 1.1 copy-done
  1.7 0.0 copy-start.2
  1.7 1.0 copy-done.2
  2.7 0.0 copy-start.3
  2.7 0.9 copy-done.3
  3.6 0.0 copy-start.4
  3.6 0.9 copy-done.4
  4.5 0.0 copy-start.5
  4.6 0.9 copy-done.5
  5.5 0.9 prep.1
  6.4 20.7 %all_to_all.55.kv_ref.refs_1_ = bf16[4,2,4,64,384]{4,3,2,1,0:T(8,128)(2,1)S(1)} all-to-all(bf16[4,2,4,64,384]{4,3,2,1,0:T(8,128)(2,1)S(1)} %get-tuple-element.11), channel_id=1, replica_groups=mesh['zh'=4,'y'=4,'c'=2,'x'=4,'zl'=4] {'x'}, dimensions={0} | all-to-all | bytes 3145728 | tf_op jit(solution)/shard_map/all_to_all | solution.py:22
  27.1 45.0 %all_to_all.56.qg_ref.refs_2_ = bf16[4,2,4,64,384]{4,3,2,1,0:T(8,128)(2,1)S(1)} all-to-all(bf16[4,2,4,64,384]{4,3,2,1,0:T(8,128)(2,1)S(1)} %get-tuple-element.12), channel_id=1, replica_groups=mesh['zh'=4,'y'=4,'c'=2,'x'=4,'zl'=4] {'zl'}, dimensions={0} | all-to-all | bytes 3145728 | tf_op jit(solution)/shard_map/all_to_all | solution.py:22
  72.1 2.2 products.1
  74.3 7.9 %all_to_all.57 = f32[2,4,3,2,64,256]{5,4,3,2,1,0:T(8,128)S(1)} all-to-all(f32[2,4,3,2,64,256]{5,4,3,2,1,0:T(8,128)S(1)} %products.1), channel_id=1, replica_groups=mesh['zh'=4,'y'=4,'c'=2,'x'=4,'zl'=4] {'c'}, dimensions={0} | all-to-all | bytes 6291456 | tf_op jit(solution)/shard_map/all_to_all | solution.py:22
  82.2 0.3 fusion
  82.4 24.0 %all_to_all.58 = f32[4,3,2,64,256]{4,3,2,1,0:T(8,128)} all-to-all(f32[4,3,2,64,256]{4,3,2,1,0:T(8,128)S(1)} %fusion), channel_id=1, replica_groups=mesh['zh'=4,'y'=4,'c'=2,'x'=4,'zl'=4] {'y'}, dimensions={0} | all-to-all | bytes 3145728 | tf_op jit(solution)/shard_map/all_to_all | solution.py:22
  106.4 1.6 reduce_sum.9
  108.0 33.4 %all_to_all.59.refs_0_ = f32[4,3,2,16,256]{4,3,2,1,0:T(8,128)S(1)} all-to-all(f32[4,3,2,16,256]{4,3,2,1,0:T(8,128)S(1)} %bitcast.6), channel_id=1, replica_groups=mesh['zh'=4,'y'=4,'c'=2,'x'=4,'zl'=4] {'zh'}, dimensions={0} | all-to-all | bytes 786432 | tf_op jit(solution)/shard_map/all_to_all | solution.py:22
  141.3 0.2 stats.1
  141.5 11.2 %all_to_all.60.stat_ref = f32[4,3,16,128]{3,2,1,0:T(8,128)S(1)} all-to-all(f32[4,3,16,128]{3,2,1,0:T(8,128)S(1)} %get-tuple-element.13.own_ref), channel_id=1, replica_groups=mesh['zh'=4,'y'=4,'c'=2,'x'=4,'zl'=4] {'zl'}, dimensions={0} | all-to-all | bytes 196608 | tf_op jit(solution)/shard_map/all_to_all | solution.py:22
  152.8 0.2 weights.1
  153.0 17.9 %all_to_all.61 = bf16[4,2,3,16,256]{4,3,2,1,0:T(8,128)(2,1)S(1)} all-to-all(bf16[4,2,3,16,256]{4,3,2,1,0:T(8,128)(2,1)S(1)} %weights.1), channel_id=1, replica_groups=mesh['zh'=4,'y'=4,'c'=2,'x'=4,'zl'=4] {'zh'}, dimensions={0} | all-to-all | bytes 393216 | tf_op jit(solution)/shard_map/all_to_all | solution.py:22
  170.9 0.1 broadcast_in_dim.4
  171.0 10.8 %all_to_all.62 = bf16[4,4,2,3,16,256]{5,4,3,2,1,0:T(8,128)(2,1)S(1)} all-to-all(bf16[4,4,2,3,16,256]{5,4,3,2,1,0:T(8,128)(2,1)S(1)} %broadcast_in_dim.4), channel_id=1, replica_groups=mesh['zh'=4,'y'=4,'c'=2,'x'=4,'zl'=4] {'y'}, dimensions={0} | all-to-all | bytes 1572864 | tf_op jit(solution)/shard_map/all_to_all | solution.py:22
  181.7 0.2 broadcast_in_dim.5
  181.9 9.5 %all_to_all.63.refs_0_ = bf16[2,4,4,2,3,16,256]{6,5,4,3,2,1,0:T(8,128)(2,1)S(1)} all-to-all(bf16[2,4,4,2,3,16,256]{6,5,4,3,2,1,0:T(8,128)(2,1)S(1)} %broadcast_in_dim.5), channel_id=1, replica_groups=mesh['zh'=4,'y'=4,'c'=2,'x'=4,'zl'=4] {'c'}, dimensions={0} | all-to-all | bytes 3145728 | tf_op jit(solution)/shard_map/all_to_all | solution.py:22
  191.4 3.4 %outputs.1 = (bf16[4,2,4,64,384]{4,3,2,1,0:T(8,128)(2,1)S(1)}, bf16[4,2,4,64,384]{4,3,2,1,0:T(8,128)(2,1)S(1)}) custom-call(bf16[2,4,4,2,3,16,256]{6,5,4,3,2,1,0:T(8,128)(2,1)S(1)} %all_to_all.63.refs_0_, bf16[4,2,4,64,384]{4,3,2,1,0:T(8,128)(2,1)S(1)} %all_to_all.55.kv_ref.refs_1_, bf16[4,2,4,64,384]{4,3,2,1,0:T(8,128)(2,1)S(1)} %all_to_all.56.qg_ref.refs_2_), custom_call_target="tpu_custom_call" | custom-call | tf_op jit(solution)/shard_map/outputs/pallas_call | solution.py:171
  194.9 22.9 %all_to_all.64.col_ref = bf16[4,2,4,64,384]{4,3,2,1,0:T(8,128)(2,1)S(1)} all-to-all(bf16[4,2,4,64,384]{4,3,2,1,0:T(8,128)(2,1)S(1)} %get-tuple-element.17), channel_id=1, replica_groups=mesh['zh'=4,'y'=4,'c'=2,'x'=4,'zl'=4] {'x'}, dimensions={0} | all-to-all | bytes 3145728 | tf_op jit(solution)/shard_map/all_to_all | solution.py:22
  217.8 0.0 copy-start.1
  217.8 39.3 %all_to_all.65.row_ref = bf16[4,2,4,64,384]{4,3,2,1,0:T(8,128)(2,1)S(1)} all-to-all(bf16[4,2,4,64,384]{4,3,2,1,0:T(8,128)(2,1)S(1)} %get-tuple-element.16), channel_id=1, replica_groups=mesh['zh'=4,'y'=4,'c'=2,'x'=4,'zl'=4] {'zl'}, dimensions={0} | all-to-all | bytes 3145728 | tf_op jit(solution)/shard_map/all_to_all | solution.py:22
  257.1 0.0 copy-done.1
  257.1 1.5 finish.1
  (1 shorter events, 0.0 us)
Async XLA Ops:
  0.6 1.1 copy-start
  1.7 1.0 copy-start.2
  2.7 0.9 copy-start.3
  3.6 0.9 copy-start.4
  4.5 0.9 copy-start.5
  217.8 39.3 %copy-start.1 = (bf16[384,768]{1,0:T(8,128)(2,1)S(1)}, bf16[384,768]{1,0:T(8,128)(2,1)}, u32[]{:S(2)}) copy-start(bf16[384,768]{1,0:T(8,128)(2,1)} %w_ref.3) | copy-start | bytes 1769476

commit v2 on v1

v2 whole, which is shorter than its diff:
```python
import math

import jax
import jax.numpy as jnp
from jax import lax
from jax.experimental import pallas as pl
from jax.experimental.pallas import tpu as pltpu
from jax.sharding import Mesh, PartitionSpec as P

HEADS = 6
PAIRS = 3
F32 = jnp.float32
BF16 = jnp.bfloat16
VMEM = 40 * 1024 * 1024


def params():
    return pltpu.CompilerParams(vmem_limit_bytes=VMEM)


def exchange(blocks, axis):
    return lax.all_to_all(blocks, axis, 0, 0, tiled=True)


def shift(block, axis, by):
    n = lax.axis_size(axis)
    return lax.ppermute(block, axis, [(i, (i + by) % n) for i in range(n)])


def prep_kernel(q_ref, k_ref, v_ref, w_ref, go_ref, kv_ref, qg_ref):
    kv_ref[0] = k_ref[...]
    kv_ref[1] = v_ref[...]
    for s in range(q_ref.shape[0]):
        ga = lax.dot_general(
            go_ref[s], w_ref[...], (((1,), (1,)), ((), ())), preferred_element_type=F32
        ).astype(BF16)
        for n in range(qg_ref.shape[0]):
            qg_ref[n, 0, s] = q_ref[s]
            qg_ref[n, 1, s] = ga


def columns(refs, which):
    seqs = refs[0].shape[1]
    rows = [jnp.concatenate([ref[which, s] for s in range(seqs)], axis=1) for ref in refs]
    return jnp.concatenate(rows, axis=0)


def head_mask(shape, head):
    lane = lax.broadcasted_iota(jnp.int32, shape, 1)
    return ((lane // 64) % 2) == head


def product_kernel(core_ref, *refs):
    kv_refs, qg_ref, keep_ref, send_ref = refs[:4], refs[4], refs[5], refs[6]
    qg_refs = [qg_ref.at[n] for n in range(4)]
    first = core_ref[0] == 0
    for which in range(2):
        left = columns(qg_refs, which)
        right = columns(kv_refs, which)
        both = []
        for head in range(2):
            own = jnp.where(head_mask(left.shape, head), left, jnp.zeros_like(left))
            both.append(
                lax.dot_general(own, right, (((1,), (1,)), ((), ())), preferred_element_type=F32)
            )
        shape = (keep_ref.shape[0],) + keep_ref.shape[3:]
        keep_ref[:, 0, which] = jnp.where(first, both[0], both[1]).reshape(shape)
        send_ref[:, 0, which] = jnp.where(first, both[1], both[0]).reshape(shape)


def rows_kernel(part_ref, out_ref):
    total = (part_ref[0] + part_ref[1]) + (part_ref[2] + part_ref[3])
    for n in range(16):
        for p in range(PAIRS):
            for which in range(2):
                at = (which * PAIRS + p) * 4
                out_ref[n, at : at + 4] = total[p, which, n * 4 : n * 4 + 4]


def softmax_kernel(scale, part_ref, out_ref):
    tiles = []
    for col in range(4):
        parts = [part_ref[n * 4 + col] for n in range(4)]
        tiles.append((parts[0] + parts[1]) + (parts[2] + parts[3]))
    total = jnp.concatenate(tiles, axis=1)
    logits = total[:12] * scale
    grads = total[12:]
    expo = jnp.exp(logits - jnp.max(logits, axis=-1, keepdims=True))
    weights = expo / jnp.sum(expo, axis=-1, keepdims=True)
    scores = weights * (grads - jnp.sum(weights * grads, axis=-1, keepdims=True))
    pad = jnp.zeros((4, weights.shape[1]), F32)
    full = jnp.concatenate([weights, pad, scores, pad], axis=0).astype(BF16)
    for n in range(16):
        col = n % 4
        out_ref[n] = full[:, col * 256 : (col + 1) * 256]


def unpack_kernel(ws_ref, out_ref, rows_ref):
    for n in range(16):
        block = ws_ref[n].astype(F32)
        for which in range(2):
            for p in range(PAIRS):
                at = which * 16 + p * 4
                rows_ref[which, p, n * 4 : n * 4 + 4] = block[at : at + 4]
    full = rows_ref[...].astype(BF16)
    for n in range(out_ref.shape[0]):
        out_ref[n] = full


def output_kernel(scale, core_ref, mine_ref, other_ref, *refs):
    kv_refs, qg_ref, row_ref, col_refs = refs[:4], refs[4], refs[5], refs[6:10]
    qg_refs = [qg_ref.at[n] for n in range(4)]
    row_refs = [row_ref.at[n] for n in range(4)]
    first = core_ref[0] == 0

    def heads(which):
        mine = mine_ref[:, which, 0].reshape(256, 256)
        other = other_ref[:, which, 0].reshape(256, 256)
        return jnp.where(first, mine, other), jnp.where(first, other, mine)

    def product(mats, side, contract):
        both = [
            lax.dot_general(m, side, (((contract,), (0,)), ((), ())), preferred_element_type=F32)
            for m in mats
        ]
        return jnp.where(head_mask(both[0].shape, 0), both[0], both[1])

    def put(outs, which, value):
        value = value.astype(BF16)
        for n, ref in enumerate(outs):
            _, seqs, res, lanes = ref.shape
            for s in range(seqs):
                ref[which, s] = value[n * res : (n + 1) * res, s * lanes : (s + 1) * lanes]

    weights, scores = heads(0), heads(1)
    put(row_refs, 0, product(weights, columns(kv_refs, 1), 1))
    put(row_refs, 1, product(scores, columns(kv_refs, 0), 1) * scale)
    put(col_refs, 0, product(weights, columns(qg_refs, 1), 0))
    put(col_refs, 1, product(scores, columns(qg_refs, 0), 0) * scale)


def total_of(refs, which, s):
    parts = [ref[which, s].astype(F32) for ref in refs]
    return ((parts[0] + parts[1]) + (parts[2] + parts[3])).astype(BF16)


def finish_kernel(row_ref, *refs):
    col_refs, (w_ref, mixed_ref, gq_ref, gk_ref, gv_ref) = refs[:4], refs[4:]
    row_refs = [row_ref.at[n] for n in range(4)]
    for s in range(mixed_ref.shape[0]):
        attended = total_of(row_refs, 0, s)
        mixed_ref[s] = jnp.dot(attended, w_ref[...], preferred_element_type=F32).astype(BF16)
        gq_ref[s] = total_of(row_refs, 1, s)
        gv_ref[s] = total_of(col_refs, 0, s)
        gk_ref[s] = total_of(col_refs, 1, s)


def on_device(queries, keys, values, out_weight, grad_out):
    seqs, res, width = queries.shape
    model_dim = out_weight.shape[1]
    scale = 1.0 / math.sqrt(width // HEADS * seqs * 32)
    core = lax.axis_index("c").astype(jnp.int32).reshape(1)
    block = jax.ShapeDtypeStruct((2, seqs, res, width), BF16)
    blocks = jax.ShapeDtypeStruct((4, 2, seqs, res, width), BF16)
    smem = pl.BlockSpec(memory_space=pltpu.SMEM)

    kv_own, qg_send = pl.pallas_call(
        prep_kernel, out_shape=(block, blocks), compiler_params=params(), name="prep"
    )(queries, keys, values, out_weight, grad_out)
    qg = exchange(qg_send, "zl")
    kv = [kv_own] + [shift(kv_own, "x", by) for by in (1, 2, 3)]

    slab = pl.BlockSpec((2, seqs, res, 128), lambda p: (0, 0, 0, p))
    slabs = pl.BlockSpec((4, 2, seqs, res, 128), lambda p: (0, 0, 0, 0, p))
    half = jax.ShapeDtypeStruct((4, PAIRS, 2, 64, 256), F32)
    half_slab = pl.BlockSpec((4, 1, 2, 64, 256), lambda p: (0, p, 0, 0, 0))
    keep, send = pl.pallas_call(
        product_kernel,
        grid=(PAIRS,),
        in_specs=[smem] + [slab] * 4 + [slabs],
        out_specs=[half_slab, half_slab],
        out_shape=(half, half),
        compiler_params=params(),
        name="products",
    )(core, *kv, qg)
    partial = exchange(keep + shift(send, "c", 1), "y")
    partial = pl.pallas_call(
        rows_kernel,
        out_shape=jax.ShapeDtypeStruct((16, 8 * PAIRS, 256), F32),
        compiler_params=params(),
        name="rows",
    )(partial)
    partial = exchange(partial, ("zh", "zl"))
    ws = pl.pallas_call(
        lambda *refs: softmax_kernel(scale, *refs),
        out_shape=jax.ShapeDtypeStruct((16, 32, 256), BF16),
        compiler_params=params(),
        name="softmax",
    )(partial)
    ws = exchange(ws, ("zh", "zl"))
    ws = pl.pallas_call(
        unpack_kernel,
        out_shape=jax.ShapeDtypeStruct((4, 2, PAIRS, 64, 256), BF16),
        scratch_shapes=[pltpu.VMEM((2, PAIRS, 64, 256), F32)],
        compiler_params=params(),
        name="unpack",
    )(ws)
    mine = exchange(ws, "y")
    other = shift(mine, "c", 1)

    ws_slab = pl.BlockSpec((4, 2, 1, 64, 256), lambda p: (0, 0, p, 0, 0))
    row, *cols = pl.pallas_call(
        lambda *refs: output_kernel(scale, *refs),
        grid=(PAIRS,),
        in_specs=[smem, ws_slab, ws_slab] + [slab] * 4 + [slabs],
        out_specs=[slabs] + [slab] * 4,
        out_shape=(blocks,) + (block,) * 4,
        compiler_params=params(),
        name="outputs",
    )(core, mine, other, *kv, qg)
    row = exchange(row, "zl")
    cols = [cols[0]] + [shift(cols[by], "x", -by) for by in (1, 2, 3)]
    grad = jax.ShapeDtypeStruct((seqs, res, width), BF16)
    return pl.pallas_call(
        finish_kernel,
        out_shape=(jax.ShapeDtypeStruct((seqs, res, model_dim), BF16), grad, grad, grad),
        compiler_params=params(),
        name="finish",
    )(row, *cols, out_weight)


def solution(mesh):
    grid = Mesh(mesh.devices.reshape(4, 4, 2, 4, 4), ("zh", "y", "c", "x", "zl"))
    placed = P(("zh", "y", "c"), ("x", "zl"), None)
    return jax.shard_map(
        on_device,
        mesh=grid,
        in_specs=(placed, placed, placed, P(), placed),
        out_specs=(placed, placed, placed, placed),
        check_vma=False,
    )
```

time: 259 us -> 212 us (0.82)
  blocking collectives: 243 us -> 88.8 us
  waiting for transfers between devices: 0 us -> 58.4 us
  starting transfers between devices: 0 us -> 43.4 us
  local copies, waits for them, and re-layouts: 5.13 us -> 9.27 us
    all_to_all x11 -> x4, blocking collectives: 243 us -> 88.8 us  [exchange(): return lax.all_to_all(blocks, axis, 0, 0, tiled=True)]
    ppermute x0 -> x8, waiting for transfers between devices: none -> 40.9 us  [shift(): return lax.ppermute(block, axis, [(i, (i + by) % n) for i in range(n)])]
    ppermute x0 -> x8, starting transfers between devices: none -> 31.8 us  [shift(): return lax.ppermute(block, axis, [(i, (i + by) % n) for i in range(n)])]
    all_to_all x0 -> x2, waiting for transfers between devices: none -> 17.5 us  [exchange(): return lax.all_to_all(blocks, axis, 0, 0, tiled=True)]
    all_to_all x0 -> x2, starting transfers between devices: none -> 11.5 us  [exchange(): return lax.all_to_all(blocks, axis, 0, 0, tiled=True)]
    unnamed x12 -> x22, local copies, waits for them, and re-layouts: 4.84 us -> 9.27 us
  transfers between devices with their start and end apart: 0 -> 10, of which waited for: 0 -> 10; matrix products, arithmetic and copies ran while one was open for 0% -> 0% of each run, Pallas kernels for 0% -> 0%
where the time goes in v2:
time: 212 us; the launch traced here: 211 us
  blocking collectives  88.8 us (42%)
  waiting for transfers between devices  58.4 us (28%)
  starting transfers between devices  43.4 us (20%)
  Pallas kernels  10.3 us (5%)
  local copies, waits for them, and re-layouts  9.27 us (4%)
    all_to_all x4, blocking collectives, exchange(): return lax.all_to_all(blocks, axis, 0, 0, tiled=True)  88.8 us
    ppermute x8, waiting for transfers between devices, shift(): return lax.ppermute(block, axis, [(i, (i + by) % n) for i in range(n)])  40.9 us
    ppermute x8, starting transfers between devices, shift(): return lax.ppermute(block, axis, [(i, (i + by) % n) for i in range(n)])  31.8 us
    all_to_all x2, waiting for transfers between devices, exchange(): return lax.all_to_all(blocks, axis, 0, 0, tiled=True)  17.5 us
    all_to_all x2, starting transfers between devices, exchange(): return lax.all_to_all(blocks, axis, 0, 0, tiled=True)  11.5 us
    unnamed x22, local copies, waits for them, and re-layouts  9.27 us
  transfers between devices with their start and end apart: 10, of which 10 were waited for; matrix products, arithmetic and copies ran while one was open for 0% of the time, Pallas kernels for 0%

profile of v2, /device:TPU:1, one launch (start us, length us, event | category | flops | bytes accessed | tf_op | source)
XLA Modules:
  0.0 211.1 jit_solution(10567651345782775369)
XLA Ops:
  0.6 0.0 copy-start
  0.6 1.1 copy-done
  1.7 0.0 copy-start.5
  1.7 1.0 copy-done.5
  2.7 0.0 copy-start.6
  2.7 0.9 copy-done.6
  3.6 0.0 copy-start.7
  3.6 0.9 copy-done.7
  4.5 0.0 copy-start.8
  4.6 0.9 copy-done.8
  5.5 2.0 prep.1
  7.5 6.4 %all-to-all-start = ((bf16[4,2,4,64,384]{4,3,2,1,0:T(8,128)(2,1)}), bf16[4,2,4,64,384]{4,3,2,1,0:T(8,128)(2,1)S(1)}, u32[]{:S(2)}, u32[]{:S(2)}) async-start(bf16[4,2,4,64,384]{4,3,2,1,0:T(8,128)(2,1)} %get-tuple-element.14), calls=%async_computation | async-start | bytes 3145728 | tf_op jit(solution)/shard_map/all_to_all | solution.py:22
  13.9 4.4 %collective-permute-start.2 = (bf16[2,4,64,384]{3,2,1,0:T(8,128)(2,1)S(1)}, bf16[2,4,64,384]{3,2,1,0:T(8,128)(2,1)S(1)}, u32[]{:S(2)}, u32[]{:S(2)}) collective-permute-start(bf16[2,4,64,384]{3,2,1,0:T(8,128)(2,1)S(1)} %get-tuple-element.13.refs_0_.refs_3_), channel_id=1, source_target_pairs={{0,12},{4,0},{8,4},{12,8},{1,13},{5,1},{9,5},{13,9},{2,14},{6,2},{... | collective-permute-start | bytes 1179656 | tf_op jit(solution)/shard_map/ppermute | solution.py:27
  18.3 2.4 %collective-permute-start.1 = (bf16[2,4,64,384]{3,2,1,0:T(8,128)(2,1)S(1)}, bf16[2,4,64,384]{3,2,1,0:T(8,128)(2,1)S(1)}, u32[]{:S(2)}, u32[]{:S(2)}) collective-permute-start(bf16[2,4,64,384]{3,2,1,0:T(8,128)(2,1)S(1)} %get-tuple-element.13.refs_0_.refs_3_), channel_id=1, source_target_pairs={{0,8},{4,12},{8,0},{12,4},{1,9},{5,13},{9,1},{13,5},{2,10},{6,14},... | collective-permute-start | bytes 1179656 | tf_op jit(solution)/shard_map/ppermute | solution.py:27
  20.8 2.5 %collective-permute-start = (bf16[2,4,64,384]{3,2,1,0:T(8,128)(2,1)S(1)}, bf16[2,4,64,384]{3,2,1,0:T(8,128)(2,1)S(1)}, u32[]{:S(2)}, u32[]{:S(2)}) collective-permute-start(bf16[2,4,64,384]{3,2,1,0:T(8,128)(2,1)S(1)} %get-tuple-element.13.refs_0_.refs_3_), channel_id=1, source_target_pairs={{0,4},{4,8},{8,12},{12,0},{1,5},{5,9},{9,13},{13,1},{2,6},{6,10},{... | collective-permute-start | bytes 1179656 | tf_op jit(solution)/shard_map/ppermute | solution.py:27
  23.3 5.7 %collective-permute-done.2.refs_3_.refs_6_ = bf16[2,4,64,384]{3,2,1,0:T(8,128)(2,1)S(1)} collective-permute-done((bf16[2,4,64,384]{3,2,1,0:T(8,128)(2,1)S(1)}, bf16[2,4,64,384]{3,2,1,0:T(8,128)(2,1)S(1)}, u32[]{:S(2)}, u32[]{:S(2)}) %collective-permute-start.2) | collective-permute-done | bytes 393248 | tf_op jit(solution)/shard_map/ppermute | solution.py:27
  29.0 1.8 collective-permute-done.1.refs_2_.refs_5_
  30.8 10.4 %collective-permute-done.refs_1_.refs_4_ = bf16[2,4,64,384]{3,2,1,0:T(8,128)(2,1)S(1)} collective-permute-done((bf16[2,4,64,384]{3,2,1,0:T(8,128)(2,1)S(1)}, bf16[2,4,64,384]{3,2,1,0:T(8,128)(2,1)S(1)}, u32[]{:S(2)}, u32[]{:S(2)}) %collective-permute-start) | collective-permute-done | bytes 393248 | tf_op jit(solution)/shard_map/ppermute | solution.py:27
  41.2 9.2 %all-to-all-done.refs_4_.refs_7_ = bf16[4,2,4,64,384]{4,3,2,1,0:T(8,128)(2,1)S(1)} async-done(((bf16[4,2,4,64,384]{4,3,2,1,0:T(8,128)(2,1)}), bf16[4,2,4,64,384]{4,3,2,1,0:T(8,128)(2,1)S(1)}, u32[]{:S(2)}, u32[]{:S(2)}) %all-to-all-start) | async-done | bytes 1572896 | tf_op jit(solution)/shard_map/all_to_all | solution.py:22
  50.4 2.2 %products.1 = (f32[4,3,2,64,256]{4,3,2,1,0:T(8,128)S(1)}, f32[4,3,2,64,256]{4,3,2,1,0:T(8,128)S(1)}) custom-call(s32[1]{0:T(128)} %bitcast.core_ref.refs_0_, bf16[2,4,64,384]{3,2,1,0:T(8,128)(2,1)S(1)} %get-tuple-element.13.refs_0_.refs_3_, bf16[2,4,64,384]{3,2,1,0:T(8,128)(2,1)S(1)} %collective-permute-done.refs_1_.refs_4_, ...), custom_call_target="tpu_custom_call" | custom-call | tf_op jit(solution)/shard_map/products/pallas_call | solution.py:177
  52.6 3.4 %collective-permute-start.3 = (f32[4,3,2,64,256]{4,3,2,1,0:T(8,128)S(1)}, f32[4,3,2,64,256]{4,3,2,1,0:T(8,128)S(1)}, u32[]{:S(2)}, u32[]{:S(2)}) collective-permute-start(f32[4,3,2,64,256]{4,3,2,1,0:T(8,128)S(1)} %get-tuple-element.16), channel_id=1, source_target_pairs={{0,16},{16,0},{1,17},{17,1},{2,18},{18,2},{3,19},{19,3},{4,20},{20... | collective-permute-start | bytes 4718600 | tf_op jit(solution)/shard_map/ppermute | solution.py:27
  56.0 3.0 %collective-permute-done.3 = f32[4,3,2,64,256]{4,3,2,1,0:T(8,128)S(1)} collective-permute-done((f32[4,3,2,64,256]{4,3,2,1,0:T(8,128)S(1)}, f32[4,3,2,64,256]{4,3,2,1,0:T(8,128)S(1)}, u32[]{:S(2)}, u32[]{:S(2)}) %collective-permute-start.3) | collective-permute-done | bytes 1572896 | tf_op jit(solution)/shard_map/ppermute | solution.py:27
  59.0 0.3 add.3
  59.3 23.8 %all_to_all.30.part_ref = f32[4,3,2,64,256]{4,3,2,1,0:T(8,128)S(1)} all-to-all(f32[4,3,2,64,256]{4,3,2,1,0:T(8,128)S(1)} %add.3), channel_id=1, replica_groups=mesh['zh'=4,'y'=4,'c'=2,'x'=4,'zl'=4] {'y'}, dimensions={0} | all-to-all | bytes 3145728 | tf_op jit(solution)/shard_map/all_to_all | solution.py:22
  83.1 0.1 rows.1
  83.2 30.3 %all_to_all.31.refs_0_ = f32[16,24,256]{2,1,0:T(8,128)S(1)} all-to-all(f32[16,24,256]{2,1,0:T(8,128)S(1)} %rows.1), channel_id=1, replica_groups=mesh['zh'=4,'y'=4,'c'=2,'x'=4,'zl'=4] {'zh','zl'}, dimensions={0} | all-to-all | bytes 786432 | tf_op jit(solution)/shard_map/all_to_all | solution.py:22
  113.6 0.3 softmax.1
  113.9 23.8 %all_to_all.32.ws_ref = bf16[16,32,256]{2,1,0:T(8,128)(2,1)S(1)} all-to-all(bf16[16,32,256]{2,1,0:T(8,128)(2,1)S(1)} %softmax.1), channel_id=1, replica_groups=mesh['zh'=4,'y'=4,'c'=2,'x'=4,'zl'=4] {'zh','zl'}, dimensions={0} | all-to-all | bytes 524288 | tf_op jit(solution)/shard_map/all_to_all | solution.py:22
  137.7 0.1 unpack.1
  137.8 10.7 %all_to_all.33.refs_1_ = bf16[4,2,3,64,256]{4,3,2,1,0:T(8,128)(2,1)S(1)} all-to-all(bf16[4,2,3,64,256]{4,3,2,1,0:T(8,128)(2,1)S(1)} %unpack.1), channel_id=1, replica_groups=mesh['zh'=4,'y'=4,'c'=2,'x'=4,'zl'=4] {'y'}, dimensions={0} | all-to-all | bytes 1572864 | tf_op jit(solution)/shard_map/all_to_all | solution.py:22
  148.6 9.8 %collective-permute-start.4 = (bf16[4,2,3,64,256]{4,3,2,1,0:T(8,128)(2,1)S(1)}, bf16[4,2,3,64,256]{4,3,2,1,0:T(8,128)(2,1)S(1)}, u32[]{:S(2)}, u32[]{:S(2)}) collective-permute-start(bf16[4,2,3,64,256]{4,3,2,1,0:T(8,128)(2,1)S(1)} %all_to_all.33.refs_1_), channel_id=1, source_target_pairs={{0,16},{16,0},{1,17},{17,1},{2,18},{18,2},{3,19},{19,3},{4,20},{20... | collective-permute-start | bytes 2359304 | tf_op jit(solution)/shard_map/ppermute | solution.py:27
  158.4 1.9 collective-permute-done.4.refs_2_
  160.3 4.0 %outputs.1 = (bf16[4,2,4,64,384]{4,3,2,1,0:T(8,128)(2,1)S(1)}, bf16[2,4,64,384]{3,2,1,0:T(8,128)(2,1)S(1)}, bf16[2,4,64,384]{3,2,1,0:T(8,128)(2,1)}, bf16[2,4,64...) custom-call(s32[1]{0:T(128)} %bitcast.core_ref.refs_0_, bf16[4,2,3,64,256]{4,3,2,1,0:T(8,128)(2,1)S(1)} %all_to_all.33.refs_1_, ...), custom_call_target="tpu_custom_call" | custom-call | tf_op jit(solution)/shard_map/outputs/pallas_call | solution.py:212
  164.3 0.0 copy-start.2
  164.3 1.2 copy-done.2
  165.5 0.0 copy-start.9
  165.5 0.8 copy-done.9
  166.3 0.0 copy-start.10
  166.3 0.7 copy-done.10
  167.0 0.0 copy-start.1
  167.0 5.1 %all-to-all-start.5 = ((bf16[4,2,4,64,384]{4,3,2,1,0:T(8,128)(2,1)}), bf16[4,2,4,64,384]{4,3,2,1,0:T(8,128)(2,1)S(1)}, u32[]{:S(2)}, u32[]{:S(2)}) async-start(bf16[4,2,4,64,384]{4,3,2,1,0:T(8,128)(2,1)} %copy-done.2), calls=%async_computation.5 | async-start | bytes 3145728 | tf_op jit(solution)/shard_map/all_to_all | solution.py:22
  172.1 4.4 %collective-permute-start.5 = (bf16[2,4,64,384]{3,2,1,0:T(8,128)(2,1)}, bf16[2,4,64,384]{3,2,1,0:T(8,128)(2,1)S(1)}, u32[]{:S(2)}, u32[]{:S(2)}) collective-permute-start(bf16[2,4,64,384]{3,2,1,0:T(8,128)(2,1)} %get-tuple-element.19), channel_id=1, source_target_pairs={{0,12},{4,0},{8,4},{12,8},{1,13},{5,1},{9,5},{13,9},{2,14},{6,2},{... | collective-permute-start | bytes 1179656 | tf_op jit(solution)/shard_map/ppermute | solution.py:27
  176.5 2.4 %collective-permute-start.6 = (bf16[2,4,64,384]{3,2,1,0:T(8,128)(2,1)}, bf16[2,4,64,384]{3,2,1,0:T(8,128)(2,1)S(1)}, u32[]{:S(2)}, u32[]{:S(2)}) collective-permute-start(bf16[2,4,64,384]{3,2,1,0:T(8,128)(2,1)} %copy-done.10), channel_id=1, source_target_pairs={{0,8},{4,12},{8,0},{12,4},{1,9},{5,13},{9,1},{13,5},{2,10},{6,14},... | collective-permute-start | bytes 1179656 | tf_op jit(solution)/shard_map/ppermute | solution.py:27
  178.9 2.5 %collective-permute-start.7 = (bf16[2,4,64,384]{3,2,1,0:T(8,128)(2,1)}, bf16[2,4,64,384]{3,2,1,0:T(8,128)(2,1)S(1)}, u32[]{:S(2)}, u32[]{:S(2)}) collective-permute-start(bf16[2,4,64,384]{3,2,1,0:T(8,128)(2,1)} %copy-done.9), channel_id=1, source_target_pairs={{0,4},{4,8},{8,12},{12,0},{1,5},{5,9},{9,13},{13,1},{2,6},{6,10},{... | collective-permute-start | bytes 1179656 | tf_op jit(solution)/shard_map/ppermute | solution.py:27
  181.4 3.9 %collective-permute-done.5.refs_1_ = bf16[2,4,64,384]{3,2,1,0:T(8,128)(2,1)S(1)} collective-permute-done((bf16[2,4,64,384]{3,2,1,0:T(8,128)(2,1)}, bf16[2,4,64,384]{3,2,1,0:T(8,128)(2,1)S(1)}, u32[]{:S(2)}, u32[]{:S(2)}) %collective-permute-start.5) | collective-permute-done | bytes 393248 | tf_op jit(solution)/shard_map/ppermute | solution.py:27
  185.4 4.4 %collective-permute-done.6.refs_2_ = bf16[2,4,64,384]{3,2,1,0:T(8,128)(2,1)S(1)} collective-permute-done((bf16[2,4,64,384]{3,2,1,0:T(8,128)(2,1)}, bf16[2,4,64,384]{3,2,1,0:T(8,128)(2,1)S(1)}, u32[]{:S(2)}, u32[]{:S(2)}) %collective-permute-start.6) | collective-permute-done | bytes 393248 | tf_op jit(solution)/shard_map/ppermute | solution.py:27
  189.8 9.7 %collective-permute-done.7.refs_3_ = bf16[2,4,64,384]{3,2,1,0:T(8,128)(2,1)S(1)} collective-permute-done((bf16[2,4,64,384]{3,2,1,0:T(8,128)(2,1)}, bf16[2,4,64,384]{3,2,1,0:T(8,128)(2,1)S(1)}, u32[]{:S(2)}, u32[]{:S(2)}) %collective-permute-start.7) | collective-permute-done | bytes 393248 | tf_op jit(solution)/shard_map/ppermute | solution.py:27
  199.6 0.0 copy-start.3
  199.6 0.7 copy-done.3
  200.3 8.3 %all-to-all-done.5.row_ref = bf16[4,2,4,64,384]{4,3,2,1,0:T(8,128)(2,1)S(1)} async-done(((bf16[4,2,4,64,384]{4,3,2,1,0:T(8,128)(2,1)}), bf16[4,2,4,64,384]{4,3,2,1,0:T(8,128)(2,1)S(1)}, u32[]{:S(2)}, u32[]{:S(2)}) %all-to-all-start.5) | async-done | bytes 1572896 | tf_op jit(solution)/shard_map/all_to_all | solution.py:22
  208.6 0.0 copy-done.1
  208.6 0.0 copy-start.4
  208.6 1.0 copy-done.4
  209.6 1.5 finish.1
Async XLA Ops:
  0.6 1.1 copy-start
  1.7 1.0 copy-start.5
  2.7 0.9 copy-start.6
  3.6 0.9 copy-start.7
  4.5 0.9 copy-start.8
  7.5 42.9 %all-to-all-start = ((bf16[4,2,4,64,384]{4,3,2,1,0:T(8,128)(2,1)}), bf16[4,2,4,64,384]{4,3,2,1,0:T(8,128)(2,1)S(1)}, u32[]{:S(2)}, u32[]{:S(2)}) async-start(bf16[4,2,4,64,384]{4,3,2,1,0:T(8,128)(2,1)} %get-tuple-element.14), calls=%async_computation | async-start | bytes 3145728 | tf_op jit(solution)/shard_map/all_to_all | solution.py:22
  13.9 15.0 %collective-permute-start.2 = (bf16[2,4,64,384]{3,2,1,0:T(8,128)(2,1)S(1)}, bf16[2,4,64,384]{3,2,1,0:T(8,128)(2,1)S(1)}, u32[]{:S(2)}, u32[]{:S(2)}) collective-permute-start(bf16[2,4,64,384]{3,2,1,0:T(8,128)(2,1)S(1)} %get-tuple-element.13.refs_0_.refs_3_), channel_id=1, source_target_pairs={{0,12},{4,0},{8,4},{12,8},{1,13},{5,1},{9,5},{13,9},{2,14},{6,2},{... | collective-permute-start | bytes 1179656 | tf_op jit(solution)/shard_map/ppermute | solution.py:27
  18.3 12.5 %collective-permute-start.1 = (bf16[2,4,64,384]{3,2,1,0:T(8,128)(2,1)S(1)}, bf16[2,4,64,384]{3,2,1,0:T(8,128)(2,1)S(1)}, u32[]{:S(2)}, u32[]{:S(2)}) collective-permute-start(bf16[2,4,64,384]{3,2,1,0:T(8,128)(2,1)S(1)} %get-tuple-element.13.refs_0_.refs_3_), channel_id=1, source_target_pairs={{0,8},{4,12},{8,0},{12,4},{1,9},{5,13},{9,1},{13,5},{2,10},{6,14},... | collective-permute-start | bytes 1179656 | tf_op jit(solution)/shard_map/ppermute | solution.py:27
  20.8 20.4 %collective-permute-start = (bf16[2,4,64,384]{3,2,1,0:T(8,128)(2,1)S(1)}, bf16[2,4,64,384]{3,2,1,0:T(8,128)(2,1)S(1)}, u32[]{:S(2)}, u32[]{:S(2)}) collective-permute-start(bf16[2,4,64,384]{3,2,1,0:T(8,128)(2,1)S(1)} %get-tuple-element.13.refs_0_.refs_3_), channel_id=1, source_target_pairs={{0,4},{4,8},{8,12},{12,0},{1,5},{5,9},{9,13},{13,1},{2,6},{6,10},{... | collective-permute-start | bytes 1179656 | tf_op jit(solution)/shard_map/ppermute | solution.py:27
  52.6 6.4 %collective-permute-start.3 = (f32[4,3,2,64,256]{4,3,2,1,0:T(8,128)S(1)}, f32[4,3,2,64,256]{4,3,2,1,0:T(8,128)S(1)}, u32[]{:S(2)}, u32[]{:S(2)}) collective-permute-start(f32[4,3,2,64,256]{4,3,2,1,0:T(8,128)S(1)} %get-tuple-element.16), channel_id=1, source_target_pairs={{0,16},{16,0},{1,17},{17,1},{2,18},{18,2},{3,19},{19,3},{4,20},{20... | collective-permute-start | bytes 4718600 | tf_op jit(solution)/shard_map/ppermute | solution.py:27
  148.6 11.7 %collective-permute-start.4 = (bf16[4,2,3,64,256]{4,3,2,1,0:T(8,128)(2,1)S(1)}, bf16[4,2,3,64,256]{4,3,2,1,0:T(8,128)(2,1)S(1)}, u32[]{:S(2)}, u32[]{:S(2)}) collective-permute-start(bf16[4,2,3,64,256]{4,3,2,1,0:T(8,128)(2,1)S(1)} %all_to_all.33.refs_1_), channel_id=1, source_target_pairs={{0,16},{16,0},{1,17},{17,1},{2,18},{18,2},{3,19},{19,3},{4,20},{20... | collective-permute-start | bytes 2359304 | tf_op jit(solution)/shard_map/ppermute | solution.py:27
  164.3 1.2 copy-start.2
  165.5 0.8 copy-start.9
  166.3 0.7 copy-start.10
  167.0 41.6 %copy-start.1 = (bf16[384,768]{1,0:T(8,128)(2,1)S(1)}, bf16[384,768]{1,0:T(8,128)(2,1)}, u32[]{:S(2)}) copy-start(bf16[384,768]{1,0:T(8,128)(2,1)} %refs_4_.1) | copy-start | bytes 1769476
  167.0 41.6 %all-to-all-start.5 = ((bf16[4,2,4,64,384]{4,3,2,1,0:T(8,128)(2,1)}), bf16[4,2,4,64,384]{4,3,2,1,0:T(8,128)(2,1)S(1)}, u32[]{:S(2)}, u32[]{:S(2)}) async-start(bf16[4,2,4,64,384]{4,3,2,1,0:T(8,128)(2,1)} %copy-done.2), calls=%async_computation.5 | async-start | bytes 3145728 | tf_op jit(solution)/shard_map/all_to_all | solution.py:22
  172.1 13.3 %collective-permute-start.5 = (bf16[2,4,64,384]{3,2,1,0:T(8,128)(2,1)}, bf16[2,4,64,384]{3,2,1,0:T(8,128)(2,1)S(1)}, u32[]{:S(2)}, u32[]{:S(2)}) collective-permute-start(bf16[2,4,64,384]{3,2,1,0:T(8,128)(2,1)} %get-tuple-element.19), channel_id=1, source_target_pairs={{0,12},{4,0},{8,4},{12,8},{1,13},{5,1},{9,5},{13,9},{2,14},{6,2},{... | collective-permute-start | bytes 1179656 | tf_op jit(solution)/shard_map/ppermute | solution.py:27
  176.5 13.3 %collective-permute-start.6 = (bf16[2,4,64,384]{3,2,1,0:T(8,128)(2,1)}, bf16[2,4,64,384]{3,2,1,0:T(8,128)(2,1)S(1)}, u32[]{:S(2)}, u32[]{:S(2)}) collective-permute-start(bf16[2,4,64,384]{3,2,1,0:T(8,128)(2,1)} %copy-done.10), channel_id=1, source_target_pairs={{0,8},{4,12},{8,0},{12,4},{1,9},{5,13},{9,1},{13,5},{2,10},{6,14},... | collective-permute-start | bytes 1179656 | tf_op jit(solution)/shard_map/ppermute | solution.py:27
  178.9 20.6 %collective-permute-start.7 = (bf16[2,4,64,384]{3,2,1,0:T(8,128)(2,1)}, bf16[2,4,64,384]{3,2,1,0:T(8,128)(2,1)S(1)}, u32[]{:S(2)}, u32[]{:S(2)}) collective-permute-start(bf16[2,4,64,384]{3,2,1,0:T(8,128)(2,1)} %copy-done.9), channel_id=1, source_target_pairs={{0,4},{4,8},{8,12},{12,0},{1,5},{5,9},{9,13},{13,1},{2,6},{6,10},{... | collective-permute-start | bytes 1179656 | tf_op jit(solution)/shard_map/ppermute | solution.py:27
  199.6 0.7 copy-start.3
  208.6 1.0 copy-start.4

commit v3 on v2

v3 whole, which is shorter than its diff:
```python
import math

import jax
import jax.numpy as jnp
from jax import lax
from jax.experimental import pallas as pl
from jax.experimental.pallas import tpu as pltpu
from jax.sharding import Mesh, PartitionSpec as P

HEADS = 6
PAIRS = 3
F32 = jnp.float32
BF16 = jnp.bfloat16
VMEM = 16 * 1024 * 1024


def params():
    return pltpu.CompilerParams(vmem_limit_bytes=VMEM)


def exchange(blocks, axis):
    return lax.all_to_all(blocks, axis, 0, 0, tiled=True)


def shift(block, axis, by):
    n = lax.axis_size(axis)
    return lax.ppermute(block, axis, [(i, (i + by) % n) for i in range(n)])


def grad_kernel(w_ref, go_ref, out_ref):
    for s in range(go_ref.shape[0]):
        ga = lax.dot_general(
            go_ref[s], w_ref[...], (((1,), (1,)), ((), ())), preferred_element_type=F32
        ).astype(BF16)
        for n in range(out_ref.shape[0]):
            out_ref[n, s] = ga


def columns(refs):
    seqs = refs[0].shape[0]
    rows = [jnp.concatenate([ref[s] for s in range(seqs)], axis=1) for ref in refs]
    return jnp.concatenate(rows, axis=0)


def head_mask(shape, head):
    lane = lax.broadcasted_iota(jnp.int32, shape, 1)
    return ((lane // 64) % 2) == head


def product_kernel(core_ref, own_ref, one_ref, two_ref, three_ref, left_ref, keep_ref, send_ref):
    first = core_ref[0] == 0
    left = columns([left_ref.at[n] for n in range(4)])
    right = columns([own_ref, one_ref, two_ref, three_ref])
    both = []
    for head in range(2):
        own = jnp.where(head_mask(left.shape, head), left, jnp.zeros_like(left))
        both.append(lax.dot_general(own, right, (((1,), (1,)), ((), ())), preferred_element_type=F32))
    shape = (keep_ref.shape[0],) + keep_ref.shape[2:]
    keep_ref[:, 0] = jnp.where(first, both[0], both[1]).reshape(shape)
    send_ref[:, 0] = jnp.where(first, both[1], both[0]).reshape(shape)


def split_kernel(core_ref, keep_ref, got_ref, own_ref, one_ref, two_ref, three_ref):
    for by, ref in enumerate((own_ref, one_ref, two_ref, three_ref)):
        at = lax.rem(core_ref[1] + by, 4)
        ref[...] = keep_ref[at] + got_ref[at]


def rows_kernel(own_ref, one_ref, two_ref, three_ref, grad_ref, out_ref):
    logits = (own_ref[...] + one_ref[...]) + (two_ref[...] + three_ref[...])
    grads = (grad_ref[0] + grad_ref[1]) + (grad_ref[2] + grad_ref[3])
    for n in range(16):
        for p in range(PAIRS):
            out_ref[n, p * 4 : p * 4 + 4] = logits[p, n * 4 : n * 4 + 4]
            out_ref[n, 12 + p * 4 : 16 + p * 4] = grads[p, n * 4 : n * 4 + 4]


def softmax_kernel(scale, part_ref, out_ref):
    tiles = []
    for col in range(4):
        parts = [part_ref[n * 4 + col] for n in range(4)]
        tiles.append((parts[0] + parts[1]) + (parts[2] + parts[3]))
    total = jnp.concatenate(tiles, axis=1)
    logits = total[:12] * scale
    grads = total[12:]
    expo = jnp.exp(logits - jnp.max(logits, axis=-1, keepdims=True))
    weights = expo / jnp.sum(expo, axis=-1, keepdims=True)
    scores = weights * (grads - jnp.sum(weights * grads, axis=-1, keepdims=True))
    full = jnp.concatenate([weights, scores], axis=0)
    for col in range(4):
        at = col * 256
        tile = jnp.concatenate([full[:, at : at + 128], full[:, at + 128 : at + 256]], axis=0).astype(BF16)
        for n in range(col, 16, 4):
            out_ref[n] = tile


def unpack_kernel(ws_ref, out_ref, rows_ref):
    for n in range(16):
        block = ws_ref[n].astype(F32)
        for which in range(2):
            for p in range(PAIRS):
                at = which * 12 + p * 4
                rows_ref[which, p, n * 4 : n * 4 + 4, 0:128] = block[at : at + 4]
                rows_ref[which, p, n * 4 : n * 4 + 4, 128:256] = block[24 + at : 28 + at]
    full = rows_ref[...].astype(BF16)
    for n in range(out_ref.shape[0]):
        out_ref[n] = full


def output_kernel(scale, core_ref, mine_ref, other_ref, own_ref, one_ref, two_ref, three_ref, left_ref, row_ref, *col_refs):
    first = core_ref[0] == 0
    mine = mine_ref[:, 0, 0].reshape(256, 256)
    other = other_ref[:, 0, 0].reshape(256, 256)
    mats = (jnp.where(first, mine, other), jnp.where(first, other, mine))

    def product(side, contract):
        both = [
            lax.dot_general(m, side, (((contract,), (0,)), ((), ())), preferred_element_type=F32)
            for m in mats
        ]
        return (jnp.where(head_mask(both[0].shape, 0), both[0], both[1]) * scale).astype(BF16)

    def put(outs, value):
        for n, ref in enumerate(outs):
            seqs, res, lanes = ref.shape
            for s in range(seqs):
                ref[s] = value[n * res : (n + 1) * res, s * lanes : (s + 1) * lanes]

    put([row_ref.at[n] for n in range(4)], product(columns([own_ref, one_ref, two_ref, three_ref]), 1))
    put(col_refs, product(columns([left_ref.at[n] for n in range(4)]), 0))


def total_of(refs, s):
    parts = [ref[s].astype(F32) for ref in refs]
    return ((parts[0] + parts[1]) + (parts[2] + parts[3])).astype(BF16)


def finish_weights_kernel(w_ref, row_ref, own_ref, one_ref, two_ref, three_ref, mixed_ref, gv_ref):
    for s in range(mixed_ref.shape[0]):
        attended = total_of([row_ref.at[n] for n in range(4)], s)
        mixed_ref[s] = jnp.dot(attended, w_ref[...], preferred_element_type=F32).astype(BF16)
        gv_ref[s] = total_of((own_ref, one_ref, two_ref, three_ref), s)


def finish_scores_kernel(row_ref, own_ref, one_ref, two_ref, three_ref, gq_ref, gk_ref):
    for s in range(gq_ref.shape[0]):
        gq_ref[s] = total_of([row_ref.at[n] for n in range(4)], s)
        gk_ref[s] = total_of((own_ref, one_ref, two_ref, three_ref), s)


def on_device(queries, keys, values, out_weight, grad_out):
    seqs, res, width = queries.shape
    model_dim = out_weight.shape[1]
    scale = 1.0 / math.sqrt(width // HEADS * seqs * 32)
    place = jnp.stack([lax.axis_index("c"), lax.axis_index("y")]).astype(jnp.int32)
    block = jax.ShapeDtypeStruct((seqs, res, width), BF16)
    blocks = jax.ShapeDtypeStruct((4, seqs, res, width), BF16)
    half = jax.ShapeDtypeStruct((4, PAIRS, 64, 256), F32)
    quarter = jax.ShapeDtypeStruct((PAIRS, 64, 256), F32)
    smem = pl.BlockSpec(memory_space=pltpu.SMEM)
    slab = pl.BlockSpec((seqs, res, 128), lambda p: (0, 0, p))
    slabs = pl.BlockSpec((4, seqs, res, 128), lambda p: (0, 0, 0, p))
    half_slab = pl.BlockSpec((4, 1, 64, 256), lambda p: (0, p, 0, 0))

    def products(rights, left, name):
        return pl.pallas_call(
            product_kernel,
            grid=(PAIRS,),
            in_specs=[smem] + [slab] * 4 + [slabs],
            out_specs=[half_slab, half_slab],
            out_shape=(half, half),
            compiler_params=params(),
            name=name,
        )(place, *rights, left)

    left_q = exchange(jnp.broadcast_to(queries[None], blocks.shape), "zl")
    rights_k = [keys] + [shift(keys, "x", by) for by in (1, 2, 3)]
    grads = pl.pallas_call(grad_kernel, out_shape=blocks, compiler_params=params(), name="grad_attended")(
        out_weight, grad_out
    )
    rights_v = [values] + [shift(values, "x", by) for by in (1, 2, 3)]
    grads, left_q, rights_k, rights_v = lax.optimization_barrier((grads, left_q, rights_k, rights_v))
    left_g = exchange(grads, "zl")

    keep, send = products(rights_k, left_q, "logits")
    pieces = pl.pallas_call(
        split_kernel,
        in_specs=[smem] + [pl.BlockSpec(memory_space=pltpu.VMEM)] * 2,
        out_shape=(quarter,) * 4,
        compiler_params=params(),
        name="split",
    )(place, keep, shift(send, "c", 1))
    pieces = [pieces[0]] + [shift(pieces[by], "y", by) for by in (1, 2, 3)]

    left_g, pieces = lax.optimization_barrier((left_g, pieces))
    keep, send = products(rights_v, left_g, "weight_grads")
    partial = exchange(keep + shift(send, "c", 1), "y")
    partial = pl.pallas_call(
        rows_kernel,
        out_shape=jax.ShapeDtypeStruct((16, 8 * PAIRS, 256), F32),
        compiler_params=params(),
        name="rows",
    )(*pieces, partial)
    partial = exchange(partial, ("zh", "zl"))
    ws = pl.pallas_call(
        lambda *refs: softmax_kernel(scale, *refs),
        out_shape=jax.ShapeDtypeStruct((16, 48, 128), BF16),
        compiler_params=params(),
        name="softmax",
    )(partial)
    ws = exchange(ws, ("zh", "zl"))
    ws = pl.pallas_call(
        unpack_kernel,
        out_shape=jax.ShapeDtypeStruct((4, 2, PAIRS, 64, 256), BF16),
        scratch_shapes=[pltpu.VMEM((2, PAIRS, 64, 256), F32)],
        compiler_params=params(),
        name="unpack",
    )(ws)
    mine = exchange(ws, "y")
    other = shift(mine, "c", 1)

    def outputs(which, factor, rights, left, name):
        ws_slab = pl.BlockSpec((4, 1, 1, 64, 256), lambda p: (0, which, p, 0, 0))
        return pl.pallas_call(
            lambda *refs: output_kernel(factor, *refs),
            grid=(PAIRS,),
            in_specs=[smem, ws_slab, ws_slab] + [slab] * 4 + [slabs],
            out_specs=[slabs] + [slab] * 4,
            out_shape=(blocks,) + (block,) * 4,
            compiler_params=params(),
            name=name,
        )(place, mine, other, *rights, left)

    row_w, *cols_w = outputs(0, 1.0, rights_v, left_g, "weights_out")
    row_s, *cols_s = outputs(1, scale, rights_k, left_q, "scores_out")
    row_w = exchange(row_w, "zl")
    cols_w = [cols_w[0]] + [shift(cols_w[by], "x", -by) for by in (1, 2, 3)]
    row_s, row_w, cols_w = lax.optimization_barrier((row_s, row_w, cols_w))
    row_s = exchange(row_s, "zl")
    cols_s = [cols_s[0]] + [shift(cols_s[by], "x", -by) for by in (1, 2, 3)]
    mixed, grad_value = pl.pallas_call(
        finish_weights_kernel,
        out_shape=(jax.ShapeDtypeStruct((seqs, res, model_dim), BF16), block),
        compiler_params=params(),
        name="finish_weights",
    )(out_weight, row_w, *cols_w)
    grad_query, grad_key = pl.pallas_call(
        finish_scores_kernel, out_shape=(block, block), compiler_params=params(), name="finish_scores"
    )(row_s, *cols_s)
    return mixed, grad_query, grad_key, grad_value


def solution(mesh):
    grid = Mesh(mesh.devices.reshape(4, 4, 2, 4, 4), ("zh", "y", "c", "x", "zl"))
    placed = P(("zh", "y", "c"), ("x", "zl"), None)
    return jax.shard_map(
        on_device,
        mesh=grid,
        in_specs=(placed, placed, placed, P(), placed),
        out_specs=(placed, placed, placed, placed),
        check_vma=False,
    )
```

time: 212 us -> 220 us (1.038)
  starting transfers between devices: 43.4 us -> 84.4 us
  waiting for transfers between devices: 58.4 us -> 24.5 us
  blocking collectives: 88.8 us -> 80.5 us
  Pallas kernels: 10.3 us -> 14.5 us
  local copies, waits for them, and re-layouts: 9.27 us -> 13.3 us
    ppermute x8 -> x18, starting transfers between devices: 31.8 us -> 64.9 us  [shift(): return lax.ppermute(block, axis, [(i, (i + by) % n) for i in range(n)])]
    ppermute x8 -> x18, waiting for transfers between devices: 40.9 us -> 22.5 us  [shift(): return lax.ppermute(block, axis, [(i, (i + by) % n) for i in range(n)])]
    all_to_all x2 -> x4, waiting for transfers between devices: 17.5 us -> 1.99 us  [exchange(): return lax.all_to_all(blocks, axis, 0, 0, tiled=True)]
    all_to_all x4, blocking collectives: 88.8 us -> 80.5 us  [exchange(): return lax.all_to_all(blocks, axis, 0, 0, tiled=True)]
    all_to_all x2 -> x4, starting transfers between devices: 11.5 us -> 19.4 us  [exchange(): return lax.all_to_all(blocks, axis, 0, 0, tiled=True)]
    pallas_call x4 -> x8, Pallas kernels: 9.76 us -> 14 us  [the longest x2 5.56 us: outputs(): pl.pallas_call(lambda *refs: output_kernel(factor, *refs), grid=(PAIRS,),...]
    unnamed x22 -> x70, local copies, waits for them, and re-layouts: 9.27 us -> 11.4 us
  transfers between devices with their start and end apart: 10 -> 22, of which waited for: 10 -> 12; matrix products, arithmetic and copies ran while one was open for 0% -> 0% of each run, Pallas kernels for 0% -> 4%
where the time goes in v3:
time: 220 us; the launch traced here: 218 us
  starting transfers between devices  84.4 us (38%)
  blocking collectives  80.5 us (37%)
  waiting for transfers between devices  24.5 us (11%)
  Pallas kernels  14.5 us (7%)
  local copies, waits for them, and re-layouts  13.3 us (6%)
    all_to_all x4, blocking collectives, exchange(): return lax.all_to_all(blocks, axis, 0, 0, tiled=True)  80.5 us
    ppermute x18, starting transfers between devices, shift(): return lax.ppermute(block, axis, [(i, (i + by) % n) for i in range(n)])  64.9 us
    ppermute x18, waiting for transfers between devices, shift(): return lax.ppermute(block, axis, [(i, (i + by) % n) for i in range(n)])  22.5 us
    all_to_all x4, starting transfers between devices, exchange(): return lax.all_to_all(blocks, axis, 0, 0, tiled=True)  19.4 us
    unnamed x70, local copies, waits for them, and re-layouts  11.4 us
    pallas_call x2, Pallas kernels, outputs(): pl.pallas_call(lambda *refs: output_kernel(factor, *refs), grid=(PAIRS,),...  5.56 us
  transfers between devices with their start and end apart: 22, of which 12 were waited for; matrix products, arithmetic and copies ran while one was open for 0% of the time, Pallas kernels for 4%

profile of v3, /device:TPU:1, one launch (start us, length us, event | category | flops | bytes accessed | tf_op | source)
XLA Modules:
  0.0 218.4 jit_solution(6981690816933384353)
XLA Ops:
  0.6 1.9 broadcast_in_dim.2
  2.6 6.6 %all-to-all-start = ((bf16[4,4,64,384]{3,2,1,0:T(8,128)(2,1)}), bf16[4,4,64,384]{3,2,1,0:T(8,128)(2,1)S(1)}, u32[]{:S(2)}, u32[]{:S(2)}) async-start(bf16[4,4,64,384]{3,2,1,0:T(8,128)(2,1)} %broadcast_in_dim.2), calls=%async_computation | async-start | bytes 1572864 | tf_op jit(solution)/shard_map/all_to_all | solution.py:22
  9.1 3.1 %collective-permute-start = (bf16[4,64,384]{2,1,0:T(8,128)(2,1)S(1)}, bf16[4,64,384]{2,1,0:T(8,128)(2,1)S(1)}, u32[]{:S(2)}, u32[]{:S(2)}) collective-permute-start(bf16[4,64,384]{2,1,0:T(8,128)(2,1)S(1)} %copy-done.5), channel_id=1, source_target_pairs={{0,4},{4,8},{8,12},{12,0},{1,5},{5,9},{9,13},{13,1},{2,6},{6,10},{... | collective-permute-start | bytes 589832 | tf_op jit(solution)/shard_map/ppermute | solution.py:27
  12.3 4.4 %collective-permute-start.1 = (bf16[4,64,384]{2,1,0:T(8,128)(2,1)S(1)}, bf16[4,64,384]{2,1,0:T(8,128)(2,1)S(1)}, u32[]{:S(2)}, u32[]{:S(2)}) collective-permute-start(bf16[4,64,384]{2,1,0:T(8,128)(2,1)S(1)} %copy-done.5), channel_id=1, source_target_pairs={{0,8},{4,12},{8,0},{12,4},{1,9},{5,13},{9,1},{13,5},{2,10},{6,14},... | collective-permute-start | bytes 589832 | tf_op jit(solution)/shard_map/ppermute | solution.py:27
  16.6 3.1 %collective-permute-start.2 = (bf16[4,64,384]{2,1,0:T(8,128)(2,1)S(1)}, bf16[4,64,384]{2,1,0:T(8,128)(2,1)S(1)}, u32[]{:S(2)}, u32[]{:S(2)}) collective-permute-start(bf16[4,64,384]{2,1,0:T(8,128)(2,1)S(1)} %copy-done.5), channel_id=1, source_target_pairs={{0,12},{4,0},{8,4},{12,8},{1,13},{5,1},{9,5},{13,9},{2,14},{6,2},{... | collective-permute-start | bytes 589832 | tf_op jit(solution)/shard_map/ppermute | solution.py:27
  19.7 2.2 %collective-permute-start.3 = (bf16[4,64,384]{2,1,0:T(8,128)(2,1)S(1)}, bf16[4,64,384]{2,1,0:T(8,128)(2,1)S(1)}, u32[]{:S(2)}, u32[]{:S(2)}) collective-permute-start(bf16[4,64,384]{2,1,0:T(8,128)(2,1)S(1)} %copy-done.4), channel_id=1, source_target_pairs={{0,4},{4,8},{8,12},{12,0},{1,5},{5,9},{9,13},{13,1},{2,6},{6,10},{... | collective-permute-start | bytes 589832 | tf_op jit(solution)/shard_map/ppermute | solution.py:27
  21.9 2.8 %collective-permute-start.4 = (bf16[4,64,384]{2,1,0:T(8,128)(2,1)S(1)}, bf16[4,64,384]{2,1,0:T(8,128)(2,1)S(1)}, u32[]{:S(2)}, u32[]{:S(2)}) collective-permute-start(bf16[4,64,384]{2,1,0:T(8,128)(2,1)S(1)} %copy-done.4), channel_id=1, source_target_pairs={{0,8},{4,12},{8,0},{12,4},{1,9},{5,13},{9,1},{13,5},{2,10},{6,14},... | collective-permute-start | bytes 589832 | tf_op jit(solution)/shard_map/ppermute | solution.py:27
  24.8 3.4 %collective-permute-start.5 = (bf16[4,64,384]{2,1,0:T(8,128)(2,1)S(1)}, bf16[4,64,384]{2,1,0:T(8,128)(2,1)S(1)}, u32[]{:S(2)}, u32[]{:S(2)}) collective-permute-start(bf16[4,64,384]{2,1,0:T(8,128)(2,1)S(1)} %copy-done.4), channel_id=1, source_target_pairs={{0,12},{4,0},{8,4},{12,8},{1,13},{5,1},{9,5},{13,9},{2,14},{6,2},{... | collective-permute-start | bytes 589832 | tf_op jit(solution)/shard_map/ppermute | solution.py:27
  28.2 1.7 grad_attended.1
  30.0 2.0 collective-permute-done.4.two_ref.refs_5_
  31.9 1.3 collective-permute-done.5.three_ref.refs_6_
  33.2 4.3 %all-to-all-start.1 = ((bf16[4,4,64,384]{3,2,1,0:T(8,128)(2,1)}), bf16[4,4,64,384]{3,2,1,0:T(8,128)(2,1)S(1)}, u32[]{:S(2)}, u32[]{:S(2)}) async-start(bf16[4,4,64,384]{3,2,1,0:T(8,128)(2,1)} %grad_attended.1), calls=%async_computation.1 | async-start | bytes 1572864 | tf_op jit(solution)/shard_map/all_to_all | solution.py:22
  37.6 1.9 logits.1
  39.6 6.0 %collective-permute-start.6 = (f32[4,3,64,256]{3,2,1,0:T(8,128)S(1)}, f32[4,3,64,256]{3,2,1,0:T(8,128)S(1)}, u32[]{:S(2)}, u32[]{:S(2)}) collective-permute-start(f32[4,3,64,256]{3,2,1,0:T(8,128)S(1)} %get-tuple-element.54), channel_id=1, source_target_pairs={{0,16},{16,0},{1,17},{17,1},{2,18},{18,2},{3,19},{19,3},{4,20},{20... | collective-permute-start | bytes 2359304 | tf_op jit(solution)/shard_map/ppermute | solution.py:27
  45.6 1.9 collective-permute-done.6.got_ref
  47.5 0.6 split.1
  48.1 3.2 %collective-permute-start.7 = (f32[3,64,256]{2,1,0:T(8,128)S(1)}, f32[3,64,256]{2,1,0:T(8,128)S(1)}, u32[]{:S(2)}, u32[]{:S(2)}) collective-permute-start(f32[3,64,256]{2,1,0:T(8,128)S(1)} %get-tuple-element.56), channel_id=1, source_target_pairs={{0,32},{32,64},{64,96},{96,0},{1,33},{33,65},{65,97},{97,1},{2,34}... | collective-permute-start | bytes 589832 | tf_op jit(solution)/shard_map/ppermute | solution.py:27
  51.3 4.5 %collective-permute-start.8 = (f32[3,64,256]{2,1,0:T(8,128)S(1)}, f32[3,64,256]{2,1,0:T(8,128)S(1)}, u32[]{:S(2)}, u32[]{:S(2)}) collective-permute-start(f32[3,64,256]{2,1,0:T(8,128)S(1)} %get-tuple-element.57), channel_id=1, source_target_pairs={{0,64},{32,96},{64,0},{96,32},{1,65},{33,97},{65,1},{97,33},{2,66}... | collective-permute-start | bytes 589832 | tf_op jit(solution)/shard_map/ppermute | solution.py:27
  55.8 3.0 %collective-permute-start.9 = (f32[3,64,256]{2,1,0:T(8,128)S(1)}, f32[3,64,256]{2,1,0:T(8,128)S(1)}, u32[]{:S(2)}, u32[]{:S(2)}) collective-permute-start(f32[3,64,256]{2,1,0:T(8,128)S(1)} %get-tuple-element.58), channel_id=1, source_target_pairs={{0,96},{32,0},{64,32},{96,64},{1,97},{33,1},{65,33},{97,65},{2,98}... | collective-permute-start | bytes 589832 | tf_op jit(solution)/shard_map/ppermute | solution.py:27
  58.8 3.9 %collective-permute-done.8.two_ref = f32[3,64,256]{2,1,0:T(8,128)S(1)} collective-permute-done((f32[3,64,256]{2,1,0:T(8,128)S(1)}, f32[3,64,256]{2,1,0:T(8,128)S(1)}, u32[]{:S(2)}, u32[]{:S(2)}) %collective-permute-start.8) | collective-permute-done | bytes 196640 | tf_op jit(solution)/shard_map/ppermute | solution.py:27
  62.8 0.9 collective-permute-done.9.three_ref
  63.7 1.9 weight_grads.1
  65.6 3.5 %collective-permute-start.10 = (f32[4,3,64,256]{3,2,1,0:T(8,128)S(1)}, f32[4,3,64,256]{3,2,1,0:T(8,128)S(1)}, u32[]{:S(2)}, u32[]{:S(2)}) collective-permute-start(f32[4,3,64,256]{3,2,1,0:T(8,128)S(1)} %get-tuple-element.69), channel_id=1, source_target_pairs={{0,16},{16,0},{1,17},{17,1},{2,18},{18,2},{3,19},{19,3},{4,20},{20... | collective-permute-start | bytes 2359304 | tf_op jit(solution)/shard_map/ppermute | solution.py:27
  69.1 1.9 collective-permute-done.10
  71.1 15.4 %all_to_all.40.grad_ref = f32[4,3,64,256]{3,2,1,0:T(8,128)S(1)} all-to-all(f32[4,3,64,256]{3,2,1,0:T(8,128)S(1)} %add.3), channel_id=1, replica_groups=mesh['zh'=4,'y'=4,'c'=2,'x'=4,'zl'=4] {'y'}, dimensions={0} | all-to-all | bytes 1572864 | tf_op jit(solution)/shard_map/all_to_all | solution.py:22
  86.5 0.1 rows.1
  86.6 30.9 %all_to_all.41.refs_0_ = f32[16,24,256]{2,1,0:T(8,128)S(1)} all-to-all(f32[16,24,256]{2,1,0:T(8,128)S(1)} %rows.1), channel_id=1, replica_groups=mesh['zh'=4,'y'=4,'c'=2,'x'=4,'zl'=4] {'zh','zl'}, dimensions={0} | all-to-all | bytes 786432 | tf_op jit(solution)/shard_map/all_to_all | solution.py:22
  117.5 0.3 softmax.1
  117.8 23.4 %all_to_all.42.ws_ref = bf16[16,48,128]{2,1,0:T(8,128)(2,1)S(1)} all-to-all(bf16[16,48,128]{2,1,0:T(8,128)(2,1)S(1)} %softmax.1), channel_id=1, replica_groups=mesh['zh'=4,'y'=4,'c'=2,'x'=4,'zl'=4] {'zh','zl'}, dimensions={0} | all-to-all | bytes 393216 | tf_op jit(solution)/shard_map/all_to_all | solution.py:22
  141.3 10.9 %all_to_all.43.refs_1_ = bf16[4,2,3,64,256]{4,3,2,1,0:T(8,128)(2,1)S(1)} all-to-all(bf16[4,2,3,64,256]{4,3,2,1,0:T(8,128)(2,1)S(1)} %unpack.1), channel_id=1, replica_groups=mesh['zh'=4,'y'=4,'c'=2,'x'=4,'zl'=4] {'y'}, dimensions={0} | all-to-all | bytes 1572864 | tf_op jit(solution)/shard_map/all_to_all | solution.py:22
  152.2 8.5 %collective-permute-start.11 = (bf16[4,2,3,64,256]{4,3,2,1,0:T(8,128)(2,1)S(1)}, bf16[4,2,3,64,256]{4,3,2,1,0:T(8,128)(2,1)S(1)}, u32[]{:S(2)}, u32[]{:S(2)}) collective-permute-start(bf16[4,2,3,64,256]{4,3,2,1,0:T(8,128)(2,1)S(1)} %all_to_all.43.refs_1_), channel_id=1, source_target_pairs={{0,16},{16,0},{1,17},{17,1},{2,18},{18,2},{3,19},{19,3},{4,20},{20... | collective-permute-start | bytes 2359304 | tf_op jit(solution)/shard_map/ppermute | solution.py:27
  160.7 1.9 collective-permute-done.11.refs_2_
  162.6 2.5 %weights_out.1 = (bf16[4,4,64,384]{3,2,1,0:T(8,128)(2,1)S(1)}, bf16[4,64,384]{2,1,0:T(8,128)(2,1)S(1)}, bf16[4,64,384]{2,1,0:T(8,128)(2,1)S(1)}, bf16[4,64,384]{2,1,0:T(8,128)(2,1)S(1)}, bf16[4,64,384]{2,1,0:T(8,128)(2,1)S(1)}) custom-call(s32[2]{0:T(128)S(1)} %pad_add_fusion.core_ref.refs_0_, bf16[4,2,3,64,256]{4,3,2,1,0:T(8,128)(2,1)S(1)} %all_to_all.43.refs_1_, ...), custom_call_target="tpu_custom_call" | custom-call | tf_op jit(solution)/shard_map/weights_out/pallas_call | solution.py:224
  165.1 0.9 copy-done.3
  166.0 0.7 copy-done.19
  166.7 0.7 copy-done.32
  167.4 0.7 copy-done.33
  168.0 0.7 copy-done.34
  168.7 4.4 %all-to-all-start.6 = ((bf16[4,4,64,384]{3,2,1,0:T(8,128)(2,1)}), bf16[4,4,64,384]{3,2,1,0:T(8,128)(2,1)S(1)}, u32[]{:S(2)}, u32[]{:S(2)}) async-start(bf16[4,4,64,384]{3,2,1,0:T(8,128)(2,1)} %copy-done.3), calls=%async_computation.6 | async-start | bytes 1572864 | tf_op jit(solution)/shard_map/all_to_all | solution.py:22
  173.1 4.3 %collective-permute-start.12 = (bf16[4,64,384]{2,1,0:T(8,128)(2,1)}, bf16[4,64,384]{2,1,0:T(8,128)(2,1)S(1)}, u32[]{:S(2)}, u32[]{:S(2)}) collective-permute-start(bf16[4,64,384]{2,1,0:T(8,128)(2,1)} %copy-done.34), channel_id=1, source_target_pairs={{0,12},{4,0},{8,4},{12,8},{1,13},{5,1},{9,5},{13,9},{2,14},{6,2},{... | collective-permute-start | bytes 589832 | tf_op jit(solution)/shard_map/ppermute | solution.py:27
  177.4 1.9 collective-permute-start.13
  179.3 2.5 %collective-permute-start.14 = (bf16[4,64,384]{2,1,0:T(8,128)(2,1)}, bf16[4,64,384]{2,1,0:T(8,128)(2,1)S(1)}, u32[]{:S(2)}, u32[]{:S(2)}) collective-permute-start(bf16[4,64,384]{2,1,0:T(8,128)(2,1)} %copy-done.32), channel_id=1, source_target_pairs={{0,4},{4,8},{8,12},{12,0},{1,5},{5,9},{9,13},{13,1},{2,6},{6,10},{... | collective-permute-start | bytes 589832 | tf_op jit(solution)/shard_map/ppermute | solution.py:27
  181.8 0.9 copy-done.9
  182.8 0.9 copy-done.11
  183.7 3.1 %scores_out.1 = (bf16[4,4,64,384]{3,2,1,0:T(8,128)(2,1)S(1)}, bf16[4,64,384]{2,1,0:T(8,128)(2,1)S(1)}, bf16[4,64,384]{2,1,0:T(8,128)(2,1)}, bf16[4,64,384]{2,1,0:T(8,128)(2,1)}, bf16[4,64,384]{2,1,0:T(8,128)(2,1)S(1)}) custom-call(s32[2]{0:T(128)S(1)} %pad_add_fusion.core_ref.refs_0_, bf16[4,2,3,64,256]{4,3,2,1,0:T(8,128)(2,1)S(1)} %all_to_all.43.refs_1_, ...), custom_call_target="tpu_custom_call" | custom-call | tf_op jit(solution)/shard_map/scores_out/pallas_call | solution.py:224
  186.8 0.9 copy-done.2
  187.7 0.7 copy-done.21
  188.3 0.7 copy-done.31
  189.0 0.7 copy-done.23
  189.7 0.7 copy-done.25
  190.4 1.5 collective-permute-done.14.three_ref
  191.9 0.7 copy-done.27
  192.6 0.2 all-to-all-done.6.row_ref
  192.8 4.2 %all-to-all-start.7 = ((bf16[4,4,64,384]{3,2,1,0:T(8,128)(2,1)}), bf16[4,4,64,384]{3,2,1,0:T(8,128)(2,1)S(1)}, u32[]{:S(2)}, u32[]{:S(2)}) async-start(bf16[4,4,64,384]{3,2,1,0:T(8,128)(2,1)} %copy-done.2), calls=%async_computation.7 | async-start | bytes 1572864 | tf_op jit(solution)/shard_map/all_to_all | solution.py:22
  196.9 3.8 %collective-permute-start.15 = (bf16[4,64,384]{2,1,0:T(8,128)(2,1)}, bf16[4,64,384]{2,1,0:T(8,128)(2,1)S(1)}, u32[]{:S(2)}, u32[]{:S(2)}) collective-permute-start(bf16[4,64,384]{2,1,0:T(8,128)(2,1)} %get-tuple-element.84), channel_id=1, source_target_pairs={{0,12},{4,0},{8,4},{12,8},{1,13},{5,1},{9,5},{13,9},{2,14},{6,2},{... | collective-permute-start | bytes 589832 | tf_op jit(solution)/shard_map/ppermute | solution.py:27
  200.7 2.7 %collective-permute-start.16 = (bf16[4,64,384]{2,1,0:T(8,128)(2,1)}, bf16[4,64,384]{2,1,0:T(8,128)(2,1)S(1)}, u32[]{:S(2)}, u32[]{:S(2)}) collective-permute-start(bf16[4,64,384]{2,1,0:T(8,128)(2,1)} %get-tuple-element.85), channel_id=1, source_target_pairs={{0,8},{4,12},{8,0},{12,4},{1,9},{5,13},{9,1},{13,5},{2,10},{6,14},... | collective-permute-start | bytes 589832 | tf_op jit(solution)/shard_map/ppermute | solution.py:27
  203.4 2.1 collective-permute-start.17
  205.5 1.4 finish_weights.1
  206.9 2.0 collective-permute-done.16.two_ref
  208.9 5.2 %collective-permute-done.17.three_ref = bf16[4,64,384]{2,1,0:T(8,128)(2,1)S(1)} collective-permute-done((bf16[4,64,384]{2,1,0:T(8,128)(2,1)}, bf16[4,64,384]{2,1,0:T(8,128)(2,1)S(1)}, u32[]{:S(2)}, u32[]{:S(2)}) %collective-permute-start.17) | collective-permute-done | bytes 196640 | tf_op jit(solution)/shard_map/ppermute | solution.py:27
  214.0 0.7 copy-done.29
  214.7 1.8 all-to-all-done.7.row_ref
  216.6 0.9 copy-done.30
  217.5 0.9 finish_scores.1
  (68 shorter events, 0.4 us)
Async XLA Ops:
  2.5 6.6 %copy-start.5 = (bf16[4,64,384]{2,1,0:T(8,128)(2,1)S(1)}, bf16[4,64,384]{2,1,0:T(8,128)(2,1)}, u32[]{:S(2)}) copy-start(bf16[4,64,384]{2,1,0:T(8,128)(2,1)} %refs_3_) | copy-start | bytes 589828
  2.5 17.2 %copy-start.4 = (bf16[4,64,384]{2,1,0:T(8,128)(2,1)S(1)}, bf16[4,64,384]{2,1,0:T(8,128)(2,1)}, u32[]{:S(2)}) copy-start(bf16[4,64,384]{2,1,0:T(8,128)(2,1)} %refs_3_.1) | copy-start | bytes 589828
  2.5 25.6 %copy-start = (bf16[384,768]{1,0:T(8,128)(2,1)S(1)}, bf16[384,768]{1,0:T(8,128)(2,1)}, u32[]{:S(2)}) copy-start(bf16[384,768]{1,0:T(8,128)(2,1)} %w_ref.3) | copy-start | bytes 1769476
  2.5 25.7 %copy-start.18 = (bf16[4,64,768]{2,1,0:T(8,128)(2,1)S(1)}, bf16[4,64,768]{2,1,0:T(8,128)(2,1)}, u32[]{:S(2)}) copy-start(bf16[4,64,768]{2,1,0:T(8,128)(2,1)} %go_ref.1) | copy-start | bytes 1179652
  2.6 30.7 %all-to-all-start = ((bf16[4,4,64,384]{3,2,1,0:T(8,128)(2,1)}), bf16[4,4,64,384]{3,2,1,0:T(8,128)(2,1)S(1)}, u32[]{:S(2)}, u32[]{:S(2)}) async-start(bf16[4,4,64,384]{3,2,1,0:T(8,128)(2,1)} %broadcast_in_dim.2), calls=%async_computation | async-start | bytes 1572864 | tf_op jit(solution)/shard_map/all_to_all | solution.py:22
  9.1 15.6 %collective-permute-start = (bf16[4,64,384]{2,1,0:T(8,128)(2,1)S(1)}, bf16[4,64,384]{2,1,0:T(8,128)(2,1)S(1)}, u32[]{:S(2)}, u32[]{:S(2)}) collective-permute-start(bf16[4,64,384]{2,1,0:T(8,128)(2,1)S(1)} %copy-done.5), channel_id=1, source_target_pairs={{0,4},{4,8},{8,12},{12,0},{1,5},{5,9},{9,13},{13,1},{2,6},{6,10},{... | collective-permute-start | bytes 589832 | tf_op jit(solution)/shard_map/ppermute | solution.py:27
  12.3 17.7 %collective-permute-start.1 = (bf16[4,64,384]{2,1,0:T(8,128)(2,1)S(1)}, bf16[4,64,384]{2,1,0:T(8,128)(2,1)S(1)}, u32[]{:S(2)}, u32[]{:S(2)}) collective-permute-start(bf16[4,64,384]{2,1,0:T(8,128)(2,1)S(1)} %copy-done.5), channel_id=1, source_target_pairs={{0,8},{4,12},{8,0},{12,4},{1,9},{5,13},{9,1},{13,5},{2,10},{6,14},... | collective-permute-start | bytes 589832 | tf_op jit(solution)/shard_map/ppermute | solution.py:27
  16.6 13.3 %collective-permute-start.2 = (bf16[4,64,384]{2,1,0:T(8,128)(2,1)S(1)}, bf16[4,64,384]{2,1,0:T(8,128)(2,1)S(1)}, u32[]{:S(2)}, u32[]{:S(2)}) collective-permute-start(bf16[4,64,384]{2,1,0:T(8,128)(2,1)S(1)} %copy-done.5), channel_id=1, source_target_pairs={{0,12},{4,0},{8,4},{12,8},{1,13},{5,1},{9,5},{13,9},{2,14},{6,2},{... | collective-permute-start | bytes 589832 | tf_op jit(solution)/shard_map/ppermute | solution.py:27
  19.7 10.3 %collective-permute-start.3 = (bf16[4,64,384]{2,1,0:T(8,128)(2,1)S(1)}, bf16[4,64,384]{2,1,0:T(8,128)(2,1)S(1)}, u32[]{:S(2)}, u32[]{:S(2)}) collective-permute-start(bf16[4,64,384]{2,1,0:T(8,128)(2,1)S(1)} %copy-done.4), channel_id=1, source_target_pairs={{0,4},{4,8},{8,12},{12,0},{1,5},{5,9},{9,13},{13,1},{2,6},{6,10},{... | collective-permute-start | bytes 589832 | tf_op jit(solution)/shard_map/ppermute | solution.py:27
  21.9 10.0 %collective-permute-start.4 = (bf16[4,64,384]{2,1,0:T(8,128)(2,1)S(1)}, bf16[4,64,384]{2,1,0:T(8,128)(2,1)S(1)}, u32[]{:S(2)}, u32[]{:S(2)}) collective-permute-start(bf16[4,64,384]{2,1,0:T(8,128)(2,1)S(1)} %copy-done.4), channel_id=1, source_target_pairs={{0,8},{4,12},{8,0},{12,4},{1,9},{5,13},{9,1},{13,5},{2,10},{6,14},... | collective-permute-start | bytes 589832 | tf_op jit(solution)/shard_map/ppermute | solution.py:27
  24.7 12.9 %copy-start.6 = (bf16[4,64,384]{2,1,0:T(8,128)(2,1)}, bf16[4,64,384]{2,1,0:T(8,128)(2,1)S(1)}, u32[]{:S(2)}) copy-start(bf16[4,64,384]{2,1,0:T(8,128)(2,1)S(1)} %collective-permute-done.one_ref.refs_4_) | copy-start | bytes 589828
  24.8 8.5 %collective-permute-start.5 = (bf16[4,64,384]{2,1,0:T(8,128)(2,1)S(1)}, bf16[4,64,384]{2,1,0:T(8,128)(2,1)S(1)}, u32[]{:S(2)}, u32[]{:S(2)}) collective-permute-start(bf16[4,64,384]{2,1,0:T(8,128)(2,1)S(1)} %copy-done.4), channel_id=1, source_target_pairs={{0,12},{4,0},{8,4},{12,8},{1,13},{5,1},{9,5},{13,9},{2,14},{6,2},{... | collective-permute-start | bytes 589832 | tf_op jit(solution)/shard_map/ppermute | solution.py:27
  29.9 7.7 %copy-start.8 = (bf16[4,64,384]{2,1,0:T(8,128)(2,1)}, bf16[4,64,384]{2,1,0:T(8,128)(2,1)S(1)}, u32[]{:S(2)}) copy-start(bf16[4,64,384]{2,1,0:T(8,128)(2,1)S(1)} %collective-permute-done.1.two_ref.refs_5_) | copy-start | bytes 589828
  29.9 7.7 %copy-start.10 = (bf16[4,64,384]{2,1,0:T(8,128)(2,1)}, bf16[4,64,384]{2,1,0:T(8,128)(2,1)S(1)}, u32[]{:S(2)}) copy-start(bf16[4,64,384]{2,1,0:T(8,128)(2,1)S(1)} %collective-permute-done.2.three_ref.refs_6_) | copy-start | bytes 589828
  30.0 33.7 %copy-start.12 = (bf16[4,64,384]{2,1,0:T(8,128)(2,1)}, bf16[4,64,384]{2,1,0:T(8,128)(2,1)S(1)}, u32[]{:S(2)}) copy-start(bf16[4,64,384]{2,1,0:T(8,128)(2,1)S(1)} %collective-permute-done.3.one_ref.refs_4_) | copy-start | bytes 589828
  31.9 31.7 %copy-start.14 = (bf16[4,64,384]{2,1,0:T(8,128)(2,1)}, bf16[4,64,384]{2,1,0:T(8,128)(2,1)S(1)}, u32[]{:S(2)}) copy-start(bf16[4,64,384]{2,1,0:T(8,128)(2,1)S(1)} %collective-permute-done.4.two_ref.refs_5_) | copy-start | bytes 589828
  33.2 30.5 %copy-start.16 = (bf16[4,64,384]{2,1,0:T(8,128)(2,1)}, bf16[4,64,384]{2,1,0:T(8,128)(2,1)S(1)}, u32[]{:S(2)}) copy-start(bf16[4,64,384]{2,1,0:T(8,128)(2,1)S(1)} %collective-permute-done.5.three_ref.refs_6_) | copy-start | bytes 589828
  33.2 30.4 %all-to-all-start.1 = ((bf16[4,4,64,384]{3,2,1,0:T(8,128)(2,1)}), bf16[4,4,64,384]{3,2,1,0:T(8,128)(2,1)S(1)}, u32[]{:S(2)}, u32[]{:S(2)}) async-start(bf16[4,4,64,384]{3,2,1,0:T(8,128)(2,1)} %grad_attended.1), calls=%async_computation.1 | async-start | bytes 1572864 | tf_op jit(solution)/shard_map/all_to_all | solution.py:22
  39.6 7.9 %collective-permute-start.6 = (f32[4,3,64,256]{3,2,1,0:T(8,128)S(1)}, f32[4,3,64,256]{3,2,1,0:T(8,128)S(1)}, u32[]{:S(2)}, u32[]{:S(2)}) collective-permute-start(f32[4,3,64,256]{3,2,1,0:T(8,128)S(1)} %get-tuple-element.54), channel_id=1, source_target_pairs={{0,16},{16,0},{1,17},{17,1},{2,18},{18,2},{3,19},{19,3},{4,20},{20... | collective-permute-start | bytes 2359304 | tf_op jit(solution)/shard_map/ppermute | solution.py:27
  48.1 10.7 %collective-permute-start.7 = (f32[3,64,256]{2,1,0:T(8,128)S(1)}, f32[3,64,256]{2,1,0:T(8,128)S(1)}, u32[]{:S(2)}, u32[]{:S(2)}) collective-permute-start(f32[3,64,256]{2,1,0:T(8,128)S(1)} %get-tuple-element.56), channel_id=1, source_target_pairs={{0,32},{32,64},{64,96},{96,0},{1,33},{33,65},{65,97},{97,1},{2,34}... | collective-permute-start | bytes 589832 | tf_op jit(solution)/shard_map/ppermute | solution.py:27
  51.3 11.5 %collective-permute-start.8 = (f32[3,64,256]{2,1,0:T(8,128)S(1)}, f32[3,64,256]{2,1,0:T(8,128)S(1)}, u32[]{:S(2)}, u32[]{:S(2)}) collective-permute-start(f32[3,64,256]{2,1,0:T(8,128)S(1)} %get-tuple-element.57), channel_id=1, source_target_pairs={{0,64},{32,96},{64,0},{96,32},{1,65},{33,97},{65,1},{97,33},{2,66}... | collective-permute-start | bytes 589832 | tf_op jit(solution)/shard_map/ppermute | solution.py:27
  55.8 7.8 %collective-permute-start.9 = (f32[3,64,256]{2,1,0:T(8,128)S(1)}, f32[3,64,256]{2,1,0:T(8,128)S(1)}, u32[]{:S(2)}, u32[]{:S(2)}) collective-permute-start(f32[3,64,256]{2,1,0:T(8,128)S(1)} %get-tuple-element.58), channel_id=1, source_target_pairs={{0,96},{32,0},{64,32},{96,64},{1,97},{33,1},{65,33},{97,65},{2,98}... | collective-permute-start | bytes 589832 | tf_op jit(solution)/shard_map/ppermute | solution.py:27
  65.6 5.4 %collective-permute-start.10 = (f32[4,3,64,256]{3,2,1,0:T(8,128)S(1)}, f32[4,3,64,256]{3,2,1,0:T(8,128)S(1)}, u32[]{:S(2)}, u32[]{:S(2)}) collective-permute-start(f32[4,3,64,256]{3,2,1,0:T(8,128)S(1)} %get-tuple-element.69), channel_id=1, source_target_pairs={{0,16},{16,0},{1,17},{17,1},{2,18},{18,2},{3,19},{19,3},{4,20},{20... | collective-permute-start | bytes 2359304 | tf_op jit(solution)/shard_map/ppermute | solution.py:27
  141.3 21.3 %copy-start.13 = (bf16[4,64,384]{2,1,0:T(8,128)(2,1)S(1)}, bf16[4,64,384]{2,1,0:T(8,128)(2,1)}, u32[]{:S(2)}) copy-start(bf16[4,64,384]{2,1,0:T(8,128)(2,1)} %copy-done.12) | copy-start | bytes 589828
  141.3 21.3 %copy-start.15 = (bf16[4,64,384]{2,1,0:T(8,128)(2,1)S(1)}, bf16[4,64,384]{2,1,0:T(8,128)(2,1)}, u32[]{:S(2)}) copy-start(bf16[4,64,384]{2,1,0:T(8,128)(2,1)} %copy-done.14) | copy-start | bytes 589828
  141.3 21.3 %copy-start.17 = (bf16[4,64,384]{2,1,0:T(8,128)(2,1)S(1)}, bf16[4,64,384]{2,1,0:T(8,128)(2,1)}, u32[]{:S(2)}) copy-start(bf16[4,64,384]{2,1,0:T(8,128)(2,1)} %copy-done.16) | copy-start | bytes 589828
  152.2 10.4 %collective-permute-start.11 = (bf16[4,2,3,64,256]{4,3,2,1,0:T(8,128)(2,1)S(1)}, bf16[4,2,3,64,256]{4,3,2,1,0:T(8,128)(2,1)S(1)}, u32[]{:S(2)}, u32[]{:S(2)}) collective-permute-start(bf16[4,2,3,64,256]{4,3,2,1,0:T(8,128)(2,1)S(1)} %all_to_all.43.refs_1_), channel_id=1, source_target_pairs={{0,16},{16,0},{1,17},{17,1},{2,18},{18,2},{3,19},{19,3},{4,20},{20... | collective-permute-start | bytes 2359304 | tf_op jit(solution)/shard_map/ppermute | solution.py:27
  165.1 0.9 copy-start.3
  166.0 0.7 copy-start.19
  166.7 0.7 copy-start.32
  167.4 0.7 copy-start.33
  168.0 0.7 copy-start.34
  168.7 13.1 %copy-start.7 = (bf16[4,64,384]{2,1,0:T(8,128)(2,1)S(1)}, bf16[4,64,384]{2,1,0:T(8,128)(2,1)}, u32[]{:S(2)}) copy-start(bf16[4,64,384]{2,1,0:T(8,128)(2,1)} %copy-done.6) | copy-start | bytes 589828
  168.7 24.0 %all-to-all-start.6 = ((bf16[4,4,64,384]{3,2,1,0:T(8,128)(2,1)}), bf16[4,4,64,384]{3,2,1,0:T(8,128)(2,1)S(1)}, u32[]{:S(2)}, u32[]{:S(2)}) async-start(bf16[4,4,64,384]{3,2,1,0:T(8,128)(2,1)} %copy-done.3), calls=%async_computation.6 | async-start | bytes 1572864 | tf_op jit(solution)/shard_map/all_to_all | solution.py:22
  173.1 15.9 %collective-permute-start.12 = (bf16[4,64,384]{2,1,0:T(8,128)(2,1)}, bf16[4,64,384]{2,1,0:T(8,128)(2,1)S(1)}, u32[]{:S(2)}, u32[]{:S(2)}) collective-permute-start(bf16[4,64,384]{2,1,0:T(8,128)(2,1)} %copy-done.34), channel_id=1, source_target_pairs={{0,12},{4,0},{8,4},{12,8},{1,13},{5,1},{9,5},{13,9},{2,14},{6,2},{... | collective-permute-start | bytes 589832 | tf_op jit(solution)/shard_map/ppermute | solution.py:27
  177.4 12.3 %collective-permute-start.13 = (bf16[4,64,384]{2,1,0:T(8,128)(2,1)}, bf16[4,64,384]{2,1,0:T(8,128)(2,1)S(1)}, u32[]{:S(2)}, u32[]{:S(2)}) collective-permute-start(bf16[4,64,384]{2,1,0:T(8,128)(2,1)} %copy-done.33), channel_id=1, source_target_pairs={{0,8},{4,12},{8,0},{12,4},{1,9},{5,13},{9,1},{13,5},{2,10},{6,14},... | collective-permute-start | bytes 589832 | tf_op jit(solution)/shard_map/ppermute | solution.py:27
  179.3 12.6 %collective-permute-start.14 = (bf16[4,64,384]{2,1,0:T(8,128)(2,1)}, bf16[4,64,384]{2,1,0:T(8,128)(2,1)S(1)}, u32[]{:S(2)}, u32[]{:S(2)}) collective-permute-start(bf16[4,64,384]{2,1,0:T(8,128)(2,1)} %copy-done.32), channel_id=1, source_target_pairs={{0,4},{4,8},{8,12},{12,0},{1,5},{5,9},{9,13},{13,1},{2,6},{6,10},{... | collective-permute-start | bytes 589832 | tf_op jit(solution)/shard_map/ppermute | solution.py:27
  181.8 0.9 copy-start.9
  182.8 0.9 copy-start.11
  186.8 0.9 copy-start.2
  187.7 0.7 copy-start.21
  188.3 0.7 copy-start.31
  189.0 0.7 copy-start.23
  189.7 0.7 copy-start.25
  191.9 0.7 copy-start.27
  192.8 12.7 %copy-start.1 = (bf16[384,768]{1,0:T(8,128)(2,1)S(1)}, bf16[384,768]{1,0:T(8,128)(2,1)}, u32[]{:S(2)}) copy-start(bf16[384,768]{1,0:T(8,128)(2,1)} %w_ref.3) | copy-start | bytes 1769476
  192.8 12.7 %copy-start.20 = (bf16[4,64,384]{2,1,0:T(8,128)(2,1)S(1)}, bf16[4,64,384]{2,1,0:T(8,128)(2,1)}, u32[]{:S(2)}) copy-start(bf16[4,64,384]{2,1,0:T(8,128)(2,1)} %copy-done.19) | copy-start | bytes 589828
  192.8 12.8 %copy-start.24 = (bf16[4,64,384]{2,1,0:T(8,128)(2,1)S(1)}, bf16[4,64,384]{2,1,0:T(8,128)(2,1)}, u32[]{:S(2)}) copy-start(bf16[4,64,384]{2,1,0:T(8,128)(2,1)} %copy-done.23) | copy-start | bytes 589828
  192.8 12.8 %copy-start.26 = (bf16[4,64,384]{2,1,0:T(8,128)(2,1)S(1)}, bf16[4,64,384]{2,1,0:T(8,128)(2,1)}, u32[]{:S(2)}) copy-start(bf16[4,64,384]{2,1,0:T(8,128)(2,1)} %copy-done.25) | copy-start | bytes 589828
  192.8 12.8 %copy-start.28 = (bf16[4,64,384]{2,1,0:T(8,128)(2,1)S(1)}, bf16[4,64,384]{2,1,0:T(8,128)(2,1)}, u32[]{:S(2)}) copy-start(bf16[4,64,384]{2,1,0:T(8,128)(2,1)} %copy-done.27) | copy-start | bytes 589828
  192.8 23.8 %all-to-all-start.7 = ((bf16[4,4,64,384]{3,2,1,0:T(8,128)(2,1)}), bf16[4,4,64,384]{3,2,1,0:T(8,128)(2,1)S(1)}, u32[]{:S(2)}, u32[]{:S(2)}) async-start(bf16[4,4,64,384]{3,2,1,0:T(8,128)(2,1)} %copy-done.2), calls=%async_computation.7 | async-start | bytes 1572864 | tf_op jit(solution)/shard_map/all_to_all | solution.py:22
  196.9 10.0 %collective-permute-start.15 = (bf16[4,64,384]{2,1,0:T(8,128)(2,1)}, bf16[4,64,384]{2,1,0:T(8,128)(2,1)S(1)}, u32[]{:S(2)}, u32[]{:S(2)}) collective-permute-start(bf16[4,64,384]{2,1,0:T(8,128)(2,1)} %get-tuple-element.84), channel_id=1, source_target_pairs={{0,12},{4,0},{8,4},{12,8},{1,13},{5,1},{9,5},{13,9},{2,14},{6,2},{... | collective-permute-start | bytes 589832 | tf_op jit(solution)/shard_map/ppermute | solution.py:27
  200.7 8.1 %collective-permute-start.16 = (bf16[4,64,384]{2,1,0:T(8,128)(2,1)}, bf16[4,64,384]{2,1,0:T(8,128)(2,1)S(1)}, u32[]{:S(2)}, u32[]{:S(2)}) collective-permute-start(bf16[4,64,384]{2,1,0:T(8,128)(2,1)} %get-tuple-element.85), channel_id=1, source_target_pairs={{0,8},{4,12},{8,0},{12,4},{1,9},{5,13},{9,1},{13,5},{2,10},{6,14},... | collective-permute-start | bytes 589832 | tf_op jit(solution)/shard_map/ppermute | solution.py:27
  203.4 13.1 %copy-start.22 = (bf16[4,64,384]{2,1,0:T(8,128)(2,1)S(1)}, bf16[4,64,384]{2,1,0:T(8,128)(2,1)}, u32[]{:S(2)}) copy-start(bf16[4,64,384]{2,1,0:T(8,128)(2,1)} %copy-done.21) | copy-start | bytes 589828
  203.4 10.6 %collective-permute-start.17 = (bf16[4,64,384]{2,1,0:T(8,128)(2,1)}, bf16[4,64,384]{2,1,0:T(8,128)(2,1)S(1)}, u32[]{:S(2)}, u32[]{:S(2)}) collective-permute-start(bf16[4,64,384]{2,1,0:T(8,128)(2,1)} %copy-done.31), channel_id=1, source_target_pairs={{0,4},{4,8},{8,12},{12,0},{1,5},{5,9},{9,13},{13,1},{2,6},{6,10},{... | collective-permute-start | bytes 589832 | tf_op jit(solution)/shard_map/ppermute | solution.py:27
  214.0 0.7 copy-start.29
  216.6 0.9 copy-start.30

commit v4 on v3

--- a/solution.py
+++ b/solution.py
@@ -25,6 +25,19 @@
 def shift(block, axis, by):
     n = lax.axis_size(axis)
     return lax.ppermute(block, axis, [(i, (i + by) % n) for i in range(n)])
+
+
+def prep_kernel(q_ref, k_ref, v_ref, kv_ref, send_ref, sems):
+    copies = [
+        pltpu.make_async_copy(k_ref, kv_ref.at[0], sems.at[0]),
+        pltpu.make_async_copy(v_ref, kv_ref.at[1], sems.at[1]),
+    ]
+    for n in range(4):
+        copies.append(pltpu.make_async_copy(q_ref, send_ref.at[n], sems.at[2 + n]))
+    for copy in copies:
+        copy.start()
+    for copy in copies:
+        copy.wait()
 
 
 def grad_kernel(w_ref, go_ref, out_ref):
@@ -50,7 +63,7 @@
 def product_kernel(core_ref, own_ref, one_ref, two_ref, three_ref, left_ref, keep_ref, send_ref):
     first = core_ref[0] == 0
     left = columns([left_ref.at[n] for n in range(4)])
-    right = columns([own_ref, one_ref, two_ref, three_ref])
+    right = columns([ref.at[0] for ref in (own_ref, one_ref, two_ref, three_ref)])
     both = []
     for head in range(2):
         own = jnp.where(head_mask(left.shape, head), left, jnp.zeros_like(left))
@@ -107,45 +120,53 @@
         out_ref[n] = full
 
 
-def output_kernel(scale, core_ref, mine_ref, other_ref, own_ref, one_ref, two_ref, three_ref, left_ref, row_ref, *col_refs):
+def output_kernel(scale, core_ref, mine_ref, other_ref, *refs):
+    kv_refs, q_ref, g_ref, row_ref, col_refs = refs[:4], refs[4], refs[5], refs[6], refs[7:11]
     first = core_ref[0] == 0
-    mine = mine_ref[:, 0, 0].reshape(256, 256)
-    other = other_ref[:, 0, 0].reshape(256, 256)
-    mats = (jnp.where(first, mine, other), jnp.where(first, other, mine))
-
-    def product(side, contract):
+    row_refs = [row_ref.at[n] for n in range(4)]
+
+    def heads(which):
+        mine = mine_ref[:, which, 0].reshape(256, 256)
+        other = other_ref[:, which, 0].reshape(256, 256)
+        return jnp.where(first, mine, other), jnp.where(first, other, mine)
+
+    def product(mats, side, contract):
         both = [
             lax.dot_general(m, side, (((contract,), (0,)), ((), ())), preferred_element_type=F32)
             for m in mats
         ]
-        return (jnp.where(head_mask(both[0].shape, 0), both[0], both[1]) * scale).astype(BF16)
-
-    def put(outs, value):
+        return jnp.where(head_mask(both[0].shape, 0), both[0], both[1])
+
+    def put(outs, which, value):
+        value = value.astype(BF16)
         for n, ref in enumerate(outs):
-            seqs, res, lanes = ref.shape
+            _, seqs, res, lanes = ref.shape
             for s in range(seqs):
-                ref[s] = value[n * res : (n + 1) * res, s * lanes : (s + 1) * lanes]
-
-    put([row_ref.at[n] for n in range(4)], product(columns([own_ref, one_ref, two_ref, three_ref]), 1))
-    put(col_refs, product(columns([left_ref.at[n] for n in range(4)]), 0))
-
-
-def total_of(refs, s):
-    parts = [ref[s].astype(F32) for ref in refs]
+                ref[which, s] = value[n * res : (n + 1) * res, s * lanes : (s + 1) * lanes]
+
+    weights, scores = heads(0), heads(1)
+    left_q = columns([q_ref.at[n] for n in range(4)])
+    left_g = columns([g_ref.at[n] for n in range(4)])
+    put(row_refs, 0, product(weights, columns([ref.at[1] for ref in kv_refs]), 1))
+    put(row_refs, 1, product(scores, columns([ref.at[0] for ref in kv_refs]), 1) * scale)
+    put(col_refs, 0, product(weights, left_g, 0))
+    put(col_refs, 1, product(scores, left_q, 0) * scale)
+
+
+def total_of(refs, which, s):
+    parts = [ref[which, s].astype(F32) for ref in refs]
     return ((parts[0] + parts[1]) + (parts[2] + parts[3])).astype(BF16)
 
 
-def finish_weights_kernel(w_ref, row_ref, own_ref, one_ref, two_ref, three_ref, mixed_ref, gv_ref):
+def finish_kernel(row_ref, *refs):
+    col_refs, (w_ref, mixed_ref, gq_ref, gk_ref, gv_ref) = refs[:4], refs[4:]
+    row_refs = [row_ref.at[n] for n in range(4)]
     for s in range(mixed_ref.shape[0]):
-        attended = total_of([row_ref.at[n] for n in range(4)], s)
+        attended = total_of(row_refs, 0, s)
         mixed_ref[s] = jnp.dot(attended, w_ref[...], preferred_element_type=F32).astype(BF16)
-        gv_ref[s] = total_of((own_ref, one_ref, two_ref, three_ref), s)
-
-
-def finish_scores_kernel(row_ref, own_ref, one_ref, two_ref, three_ref, gq_ref, gk_ref):
-    for s in range(gq_ref.shape[0]):
-        gq_ref[s] = total_of([row_ref.at[n] for n in range(4)], s)
-        gk_ref[s] = total_of((own_ref, one_ref, two_ref, three_ref), s)
+        gq_ref[s] = total_of(row_refs, 1, s)
+        gv_ref[s] = total_of(col_refs, 0, s)
+        gk_ref[s] = total_of(col_refs, 1, s)
 
 
 def on_device(queries, keys, values, out_weight, grad_out):
@@ -158,11 +179,13 @@
     half = jax.ShapeDtypeStruct((4, PAIRS, 64, 256), F32)
     quarter = jax.ShapeDtypeStruct((PAIRS, 64, 256), F32)
     smem = pl.BlockSpec(memory_space=pltpu.SMEM)
-    slab = pl.BlockSpec((seqs, res, 128), lambda p: (0, 0, p))
+    hbm = pl.BlockSpec(memory_space=pltpu.HBM)
     slabs = pl.BlockSpec((4, seqs, res, 128), lambda p: (0, 0, 0, p))
+    stack_slab = pl.BlockSpec((2, seqs, res, 128), lambda p: (0, 0, 0, p))
     half_slab = pl.BlockSpec((4, 1, 64, 256), lambda p: (0, p, 0, 0))
 
-    def products(rights, left, name):
+    def products(which, rights, left, name):
+        slab = pl.BlockSpec((1, seqs, res, 128), lambda p: (which, 0, 0, p))
         return pl.pallas_call(
             product_kernel,
             grid=(PAIRS,),
@@ -173,16 +196,27 @@
             name=name,
         )(place, *rights, left)
 
-    left_q = exchange(jnp.broadcast_to(queries[None], blocks.shape), "zl")
-    rights_k = [keys] + [shift(keys, "x", by) for by in (1, 2, 3)]
-    grads = pl.pallas_call(grad_kernel, out_shape=blocks, compiler_params=params(), name="grad_attended")(
-        out_weight, grad_out
-    )
-    rights_v = [values] + [shift(values, "x", by) for by in (1, 2, 3)]
-    grads, left_q, rights_k, rights_v = lax.optimization_barrier((grads, left_q, rights_k, rights_v))
+    kv_own, q_send = pl.pallas_call(
+        prep_kernel,
+        in_specs=[hbm] * 3,
+        out_specs=[hbm] * 2,
+        out_shape=(pltpu.HBM((2, seqs, res, width), BF16), pltpu.HBM((4, seqs, res, width), BF16)),
+        scratch_shapes=[pltpu.SemaphoreType.DMA((6,))],
+        compiler_params=params(),
+        name="prep",
+    )(*(pltpu.with_memory_space_constraint(a, pltpu.HBM) for a in (queries, keys, values)))
+    left_q = exchange(q_send, "zl")
+    rights = [kv_own] + [shift(kv_own, "x", by) for by in (1, 2, 3)]
+    grads = pl.pallas_call(
+        grad_kernel,
+        out_shape=pltpu.HBM((4, seqs, res, width), BF16),
+        compiler_params=params(),
+        name="grad_attended",
+    )(out_weight, grad_out)
+    grads, left_q, rights = lax.optimization_barrier((grads, left_q, rights))
     left_g = exchange(grads, "zl")
 
-    keep, send = products(rights_k, left_q, "logits")
+    keep, send = products(0, rights, left_q, "logits")
     pieces = pl.pallas_call(
         split_kernel,
         in_specs=[smem] + [pl.BlockSpec(memory_space=pltpu.VMEM)] * 2,
@@ -190,10 +224,11 @@
         compiler_params=params(),
         name="split",
     )(place, keep, shift(send, "c", 1))
+    _, left_g = lax.optimization_barrier((pieces, left_g))
+    keep, send = products(1, rights, left_g, "weight_grads")
     pieces = [pieces[0]] + [shift(pieces[by], "y", by) for by in (1, 2, 3)]
-
-    left_g, pieces = lax.optimization_barrier((left_g, pieces))
-    keep, send = products(rights_v, left_g, "weight_grads")
+    send, pieces = lax.optimization_barrier((send, pieces))
+
     partial = exchange(keep + shift(send, "c", 1), "y")
     partial = pl.pallas_call(
         rows_kernel,
@@ -219,35 +254,25 @@
     mine = exchange(ws, "y")
     other = shift(mine, "c", 1)
 
-    def outputs(which, factor, rights, left, name):
-        ws_slab = pl.BlockSpec((4, 1, 1, 64, 256), lambda p: (0, which, p, 0, 0))
-        return pl.pallas_call(
-            lambda *refs: output_kernel(factor, *refs),
-            grid=(PAIRS,),
-            in_specs=[smem, ws_slab, ws_slab] + [slab] * 4 + [slabs],
-            out_specs=[slabs] + [slab] * 4,
-            out_shape=(blocks,) + (block,) * 4,
-            compiler_params=params(),
-            name=name,
-        )(place, mine, other, *rights, left)
-
-    row_w, *cols_w = outputs(0, 1.0, rights_v, left_g, "weights_out")
-    row_s, *cols_s = outputs(1, scale, rights_k, left_q, "scores_out")
-    row_w = exchange(row_w, "zl")
-    cols_w = [cols_w[0]] + [shift(cols_w[by], "x", -by) for by in (1, 2, 3)]
-    row_s, row_w, cols_w = lax.optimization_barrier((row_s, row_w, cols_w))
-    row_s = exchange(row_s, "zl")
-    cols_s = [cols_s[0]] + [shift(cols_s[by], "x", -by) for by in (1, 2, 3)]
-    mixed, grad_value = pl.pallas_call(
-        finish_weights_kernel,
-        out_shape=(jax.ShapeDtypeStruct((seqs, res, model_dim), BF16), block),
-        compiler_params=params(),
-        name="finish_weights",
-    )(out_weight, row_w, *cols_w)
-    grad_query, grad_key = pl.pallas_call(
-        finish_scores_kernel, out_shape=(block, block), compiler_params=params(), name="finish_scores"
-    )(row_s, *cols_s)
-    return mixed, grad_query, grad_key, grad_value
+    ws_slab = pl.BlockSpec((4, 2, 1, 64, 256), lambda p: (0, 0, p, 0, 0))
+    row, *cols = pl.pallas_call(
+        lambda *refs: output_kernel(scale, *refs),
+        grid=(PAIRS,),
+        in_specs=[smem, ws_slab, ws_slab] + [stack_slab] * 4 + [slabs] * 2,
+        out_specs=[pl.BlockSpec((4, 2, seqs, res, 128), lambda p: (0, 0, 0, 0, p))] + [stack_slab] * 4,
+        out_shape=(pltpu.HBM((4, 2, seqs, res, width), BF16),)
+        + (pltpu.HBM((2, seqs, res, width), BF16),) * 4,
+        compiler_params=params(),
+        name="outputs",
+    )(place, mine, other, *rights, left_q, left_g)
+    row = exchange(row, "zl")
+    cols = [cols[0]] + [shift(cols[by], "x", -by) for by in (1, 2, 3)]
+    return pl.pallas_call(
+        finish_kernel,
+        out_shape=(jax.ShapeDtypeStruct((seqs, res, model_dim), BF16), block, block, block),
+        compiler_params=params(),
+        name="finish",
+    )(row, *cols, out_weight)
 
 
 def solution(mesh):

time: 220 us -> 246 us (1.12)
  Pallas kernels: 14.5 us -> 50.9 us
  waiting for transfers between devices: 24.5 us -> 53.6 us
  starting transfers between devices: 84.4 us -> 57.4 us
  local copies, waits for them, and re-layouts: 13.3 us -> 1.8 us
    pallas_call x5 -> x4, Pallas kernels: 9.56 us -> 44.1 us  [the longest x1 36.9 us: on_device(): pl.pallas_call(prep_kernel, in_specs=[hbm] * 3, out_specs=[hbm] * 2, out_...]
    ppermute x18 -> x12, starting transfers between devices: 64.9 us -> 41.9 us  [shift(): return lax.ppermute(block, axis, [(i, (i + by) % n) for i in range(n)])]
    ppermute x18 -> x12, waiting for transfers between devices: 22.5 us -> 42.2 us  [shift(): return lax.ppermute(block, axis, [(i, (i + by) % n) for i in range(n)])]
    unnamed x70 -> x14, local copies, waits for them, and re-layouts: 11.4 us -> 1.8 us
    all_to_all x4 -> x3, waiting for transfers between devices: 1.99 us -> 11.4 us  [exchange(): return lax.all_to_all(blocks, axis, 0, 0, tiled=True)]
    all_to_all x4 -> x3, starting transfers between devices: 19.4 us -> 15.5 us  [exchange(): return lax.all_to_all(blocks, axis, 0, 0, tiled=True)]
  transfers between devices with their start and end apart: 22 -> 15, of which waited for: 12 -> 13; matrix products, arithmetic and copies ran while one was open for 0% -> 0% of each run, Pallas kernels for 4% -> 3%
where the time goes in v4:
time: 246 us; the launch traced here: 245 us
  blocking collectives  80.4 us (33%)
  starting transfers between devices  57.4 us (23%)
  waiting for transfers between devices  53.6 us (22%)
  Pallas kernels  50.9 us (21%)
    all_to_all x4, blocking collectives, exchange(): return lax.all_to_all(blocks, axis, 0, 0, tiled=True)  80.4 us
    ppermute x12, waiting for transfers between devices, shift(): return lax.ppermute(block, axis, [(i, (i + by) % n) for i in range(n)])  42.2 us
    ppermute x12, starting transfers between devices, shift(): return lax.ppermute(block, axis, [(i, (i + by) % n) for i in range(n)])  41.9 us
    pallas_call x1, Pallas kernels, on_device(): pl.pallas_call(prep_kernel, in_specs=[hbm] * 3, out_specs=[hbm] * 2, out_...  36.9 us
    all_to_all x3, starting transfers between devices, exchange(): return lax.all_to_all(blocks, axis, 0, 0, tiled=True)  15.5 us
    all_to_all x3, waiting for transfers between devices, exchange(): return lax.all_to_all(blocks, axis, 0, 0, tiled=True)  11.4 us
  transfers between devices with their start and end apart: 15, of which 13 were waited for; matrix products, arithmetic and copies ran while one was open for 0% of the time, Pallas kernels for 3%

profile of v4, /device:TPU:1, one launch (start us, length us, event | category | flops | bytes accessed | tf_op | source)
XLA Modules:
  0.0 245.1 jit_solution(11939079731148233649)
XLA Ops:
  0.6 0.0 copy-start.1
  0.6 0.0 copy-start.3
  0.7 36.9 %prep.1 = (bf16[2,4,64,384]{3,2,1,0:T(8,128)(2,1)}, bf16[4,4,64,384]{3,2,1,0:T(8,128)(2,1)}) custom-call(bf16[4,64,384]{2,1,0:T(8,128)(2,1)} %q_ref.1, bf16[4,64,384]{2,1,0:T(8,128)(2,1)} %k_ref.1, bf16[4,64,384]{2,1,0:T(8,128)(2,1)} %v_ref.1), custom_call_target="tpu_custom_call" | custom-call | tf_op jit(solution)/shard_map/prep/pallas_call | solution.py:199
  37.6 0.0 copy-start
  37.6 6.6 %all-to-all-start = ((bf16[4,4,64,384]{3,2,1,0:T(8,128)(2,1)}), bf16[4,4,64,384]{3,2,1,0:T(8,128)(2,1)S(1)}, u32[]{:S(2)}, u32[]{:S(2)}) async-start(bf16[4,4,64,384]{3,2,1,0:T(8,128)(2,1)} %get-tuple-element.31), calls=%async_computation | async-start | bytes 1572864 | tf_op jit(solution)/shard_map/all_to_all | solution.py:22
  44.2 0.0 copy-done
  44.2 4.4 %collective-permute-start.2 = (bf16[2,4,64,384]{3,2,1,0:T(8,128)(2,1)S(1)}, bf16[2,4,64,384]{3,2,1,0:T(8,128)(2,1)S(1)}, u32[]{:S(2)}, u32[]{:S(2)}) collective-permute-start(bf16[2,4,64,384]{3,2,1,0:T(8,128)(2,1)S(1)} %copy-done), channel_id=1, source_target_pairs={{0,12},{4,0},{8,4},{12,8},{1,13},{5,1},{9,5},{13,9},{2,14},{6,2},{... | collective-permute-start | bytes 1179656 | tf_op jit(solution)/shard_map/ppermute | solution.py:27
  48.5 2.4 collective-permute-start.1
  51.0 2.5 %collective-permute-start = (bf16[2,4,64,384]{3,2,1,0:T(8,128)(2,1)S(1)}, bf16[2,4,64,384]{3,2,1,0:T(8,128)(2,1)S(1)}, u32[]{:S(2)}, u32[]{:S(2)}) collective-permute-start(bf16[2,4,64,384]{3,2,1,0:T(8,128)(2,1)S(1)} %copy-done), channel_id=1, source_target_pairs={{0,4},{4,8},{8,12},{12,0},{1,5},{5,9},{9,13},{13,1},{2,6},{6,10},{... | collective-permute-start | bytes 1179656 | tf_op jit(solution)/shard_map/ppermute | solution.py:27
  53.5 0.0 copy-done.1
  53.5 0.0 copy-done.3
  53.5 1.7 grad_attended.1
  55.2 4.0 %collective-permute-done.2.three_ref.refs_6_ = bf16[2,4,64,384]{3,2,1,0:T(8,128)(2,1)S(1)} collective-permute-done((bf16[2,4,64,384]{3,2,1,0:T(8,128)(2,1)S(1)}, bf16[2,4,64,384]{3,2,1,0:T(8,128)(2,1)S(1)}, u32[]{:S(2)}, u32[]{:S(2)}) %collective-permute-start.2) | collective-permute-done | bytes 393248 | tf_op jit(solution)/shard_map/ppermute | solution.py:27
  59.2 1.8 collective-permute-done.1.two_ref.refs_5_
  61.1 10.3 %collective-permute-done.one_ref.refs_4_ = bf16[2,4,64,384]{3,2,1,0:T(8,128)(2,1)S(1)} collective-permute-done((bf16[2,4,64,384]{3,2,1,0:T(8,128)(2,1)S(1)}, bf16[2,4,64,384]{3,2,1,0:T(8,128)(2,1)S(1)}, u32[]{:S(2)}, u32[]{:S(2)}) %collective-permute-start) | collective-permute-done | bytes 393248 | tf_op jit(solution)/shard_map/ppermute | solution.py:27
  71.4 0.0 all-to-all-done.left_ref.refs_7_
  71.4 4.5 %all-to-all-start.1 = ((bf16[4,4,64,384]{3,2,1,0:T(8,128)(2,1)}), bf16[4,4,64,384]{3,2,1,0:T(8,128)(2,1)S(1)}, u32[]{:S(2)}, u32[]{:S(2)}) async-start(bf16[4,4,64,384]{3,2,1,0:T(8,128)(2,1)} %grad_attended.1), calls=%async_computation.1 | async-start | bytes 1572864 | tf_op jit(solution)/shard_map/all_to_all | solution.py:22
  75.9 0.1 pad_add_fusion.core_ref.refs_0_
  76.0 1.9 logits.1
  77.9 2.7 %collective-permute-start.3 = (f32[4,3,64,256]{3,2,1,0:T(8,128)S(1)}, f32[4,3,64,256]{3,2,1,0:T(8,128)S(1)}, u32[]{:S(2)}, u32[]{:S(2)}) collective-permute-start(f32[4,3,64,256]{3,2,1,0:T(8,128)S(1)} %get-tuple-element.39), channel_id=1, source_target_pairs={{0,16},{16,0},{1,17},{17,1},{2,18},{18,2},{3,19},{19,3},{4,20},{20... | collective-permute-start | bytes 2359304 | tf_op jit(solution)/shard_map/ppermute | solution.py:27
  80.6 1.9 collective-permute-done.3.got_ref
  82.5 1.4 split.1
  83.9 3.2 %collective-permute-start.4 = (f32[3,64,256]{2,1,0:T(8,128)}, f32[3,64,256]{2,1,0:T(8,128)S(1)}, u32[]{:S(2)}, u32[]{:S(2)}) collective-permute-start(f32[3,64,256]{2,1,0:T(8,128)} %get-tuple-element.41), channel_id=1, source_target_pairs={{0,32},{32,64},{64,96},{96,0},{1,33},{33,65},{65,97},{97,1},{2,34}... | collective-permute-start | bytes 589832 | tf_op jit(solution)/shard_map/ppermute | solution.py:27
  87.1 4.5 %collective-permute-start.5 = (f32[3,64,256]{2,1,0:T(8,128)}, f32[3,64,256]{2,1,0:T(8,128)}, u32[]{:S(2)}, u32[]{:S(2)}) collective-permute-start(f32[3,64,256]{2,1,0:T(8,128)} %get-tuple-element.42), channel_id=1, source_target_pairs={{0,64},{32,96},{64,0},{96,32},{1,65},{33,97},{65,1},{97,33},{2,66}... | collective-permute-start | bytes 589832 | tf_op jit(solution)/shard_map/ppermute | solution.py:27
  91.6 3.0 %collective-permute-start.6 = (f32[3,64,256]{2,1,0:T(8,128)}, f32[3,64,256]{2,1,0:T(8,128)}, u32[]{:S(2)}, u32[]{:S(2)}) collective-permute-start(f32[3,64,256]{2,1,0:T(8,128)} %get-tuple-element.43), channel_id=1, source_target_pairs={{0,96},{32,0},{64,32},{96,64},{1,97},{33,1},{65,33},{97,65},{2,98}... | collective-permute-start | bytes 589832 | tf_op jit(solution)/shard_map/ppermute | solution.py:27
  94.6 0.9 all-to-all-done.1.left_ref.refs_8_
  95.6 1.9 weight_grads.1
  97.5 0.0 collective-permute-done.4.one_ref
  97.5 1.4 collective-permute-done.5.two_ref
  98.9 0.9 collective-permute-done.6.three_ref
  99.8 3.5 %collective-permute-start.7 = (f32[4,3,64,256]{3,2,1,0:T(8,128)S(1)}, f32[4,3,64,256]{3,2,1,0:T(8,128)S(1)}, u32[]{:S(2)}, u32[]{:S(2)}) collective-permute-start(f32[4,3,64,256]{3,2,1,0:T(8,128)S(1)} %get-tuple-element.52), channel_id=1, source_target_pairs={{0,16},{16,0},{1,17},{17,1},{2,18},{18,2},{3,19},{19,3},{4,20},{20... | collective-permute-start | bytes 2359304 | tf_op jit(solution)/shard_map/ppermute | solution.py:27
  103.3 1.9 collective-permute-done.7
  105.2 0.1 add.3
  105.3 15.4 %all_to_all.35.grad_ref = f32[4,3,64,256]{3,2,1,0:T(8,128)S(1)} all-to-all(f32[4,3,64,256]{3,2,1,0:T(8,128)S(1)} %add.3), channel_id=1, replica_groups=mesh['zh'=4,'y'=4,'c'=2,'x'=4,'zl'=4] {'y'}, dimensions={0} | all-to-all | bytes 1572864 | tf_op jit(solution)/shard_map/all_to_all | solution.py:22
  120.7 1.1 rows.1
  121.8 30.9 %all_to_all.36.refs_0_ = f32[16,24,256]{2,1,0:T(8,128)S(1)} all-to-all(f32[16,24,256]{2,1,0:T(8,128)S(1)} %rows.1), channel_id=1, replica_groups=mesh['zh'=4,'y'=4,'c'=2,'x'=4,'zl'=4] {'zh','zl'}, dimensions={0} | all-to-all | bytes 786432 | tf_op jit(solution)/shard_map/all_to_all | solution.py:22
  152.7 0.3 softmax.1
  153.0 23.4 %all_to_all.37.ws_ref = bf16[16,48,128]{2,1,0:T(8,128)(2,1)S(1)} all-to-all(bf16[16,48,128]{2,1,0:T(8,128)(2,1)S(1)} %softmax.1), channel_id=1, replica_groups=mesh['zh'=4,'y'=4,'c'=2,'x'=4,'zl'=4] {'zh','zl'}, dimensions={0} | all-to-all | bytes 393216 | tf_op jit(solution)/shard_map/all_to_all | solution.py:22
  176.4 0.1 unpack.1
  176.5 10.7 %all_to_all.38.refs_1_ = bf16[4,2,3,64,256]{4,3,2,1,0:T(8,128)(2,1)S(1)} all-to-all(bf16[4,2,3,64,256]{4,3,2,1,0:T(8,128)(2,1)S(1)} %unpack.1), channel_id=1, replica_groups=mesh['zh'=4,'y'=4,'c'=2,'x'=4,'zl'=4] {'y'}, dimensions={0} | all-to-all | bytes 1572864 | tf_op jit(solution)/shard_map/all_to_all | solution.py:22
  187.2 8.5 %collective-permute-start.8 = (bf16[4,2,3,64,256]{4,3,2,1,0:T(8,128)(2,1)S(1)}, bf16[4,2,3,64,256]{4,3,2,1,0:T(8,128)(2,1)S(1)}, u32[]{:S(2)}, u32[]{:S(2)}) collective-permute-start(bf16[4,2,3,64,256]{4,3,2,1,0:T(8,128)(2,1)S(1)} %all_to_all.38.refs_1_), channel_id=1, source_target_pairs={{0,16},{16,0},{1,17},{17,1},{2,18},{18,2},{3,19},{19,3},{4,20},{20... | collective-permute-start | bytes 2359304 | tf_op jit(solution)/shard_map/ppermute | solution.py:27
  195.8 1.9 collective-permute-done.8.refs_2_
  197.6 4.0 %outputs.1 = (bf16[4,2,4,64,384]{4,3,2,1,0:T(8,128)(2,1)}, bf16[2,4,64,384]{3,2,1,0:T(8,128)(2,1)}, bf16[2,4,64,384]{3,2,1,0:T(8,128)(2,1)}, bf16[2,4,64,384]{3,2,1,0:T(8,128)(2,1)}, bf16[2,4,64,384]{3,2,1,0:T(8,128)(2,1)}) custom-call(s32[2]{0:T(128)S(1)} %pad_add_fusion.core_ref.refs_0_, bf16[4,2,3,64,256]{4,3,2,1,0:T(8,128)(2,1)S(1)} %all_to_all.38.refs_1_, ...), custom_call_target="tpu_custom_call" | custom-call | tf_op jit(solution)/shard_map/outputs/pallas_call | solution.py:258
  201.7 0.0 copy-start.2
  201.7 0.0 copy-start.4
  201.7 4.4 %all-to-all-start.6 = ((bf16[4,2,4,64,384]{4,3,2,1,0:T(8,128)(2,1)}), bf16[4,2,4,64,384]{4,3,2,1,0:T(8,128)(2,1)S(1)}, u32[]{:S(2)}, u32[]{:S(2)}) async-start(bf16[4,2,4,64,384]{4,3,2,1,0:T(8,128)(2,1)} %get-tuple-element.53), calls=%async_computation.6 | async-start | bytes 3145728 | tf_op jit(solution)/shard_map/all_to_all | solution.py:22
  206.1 2.2 collective-permute-start.9
  208.3 2.4 collective-permute-start.10
  210.7 2.5 %collective-permute-start.11 = (bf16[2,4,64,384]{3,2,1,0:T(8,128)(2,1)}, bf16[2,4,64,384]{3,2,1,0:T(8,128)(2,1)S(1)}, u32[]{:S(2)}, u32[]{:S(2)}) collective-permute-start(bf16[2,4,64,384]{3,2,1,0:T(8,128)(2,1)} %get-tuple-element.57), channel_id=1, source_target_pairs={{0,4},{4,8},{8,12},{12,0},{1,5},{5,9},{9,13},{13,1},{2,6},{6,10},{... | collective-permute-start | bytes 1179656 | tf_op jit(solution)/shard_map/ppermute | solution.py:27
  213.3 4.9 %collective-permute-done.9.refs_1_ = bf16[2,4,64,384]{3,2,1,0:T(8,128)(2,1)S(1)} collective-permute-done((bf16[2,4,64,384]{3,2,1,0:T(8,128)(2,1)}, bf16[2,4,64,384]{3,2,1,0:T(8,128)(2,1)S(1)}, u32[]{:S(2)}, u32[]{:S(2)}) %collective-permute-start.9) | collective-permute-done | bytes 393248 | tf_op jit(solution)/shard_map/ppermute | solution.py:27
  218.2 3.5 %collective-permute-done.10.refs_2_ = bf16[2,4,64,384]{3,2,1,0:T(8,128)(2,1)S(1)} collective-permute-done((bf16[2,4,64,384]{3,2,1,0:T(8,128)(2,1)}, bf16[2,4,64,384]{3,2,1,0:T(8,128)(2,1)S(1)}, u32[]{:S(2)}, u32[]{:S(2)}) %collective-permute-start.10) | collective-permute-done | bytes 393248 | tf_op jit(solution)/shard_map/ppermute | solution.py:27
  221.6 9.7 %collective-permute-done.11.refs_3_ = bf16[2,4,64,384]{3,2,1,0:T(8,128)(2,1)S(1)} collective-permute-done((bf16[2,4,64,384]{3,2,1,0:T(8,128)(2,1)}, bf16[2,4,64,384]{3,2,1,0:T(8,128)(2,1)S(1)}, u32[]{:S(2)}, u32[]{:S(2)}) %collective-permute-start.11) | collective-permute-done | bytes 393248 | tf_op jit(solution)/shard_map/ppermute | solution.py:27
  231.4 0.0 copy-start.5
  231.4 0.8 copy-done.5
  232.2 10.4 %all-to-all-done.6.row_ref = bf16[4,2,4,64,384]{4,3,2,1,0:T(8,128)(2,1)S(1)} async-done(((bf16[4,2,4,64,384]{4,3,2,1,0:T(8,128)(2,1)}), bf16[4,2,4,64,384]{4,3,2,1,0:T(8,128)(2,1)S(1)}, u32[]{:S(2)}, u32[]{:S(2)}) %all-to-all-start.6) | async-done | bytes 1572896 | tf_op jit(solution)/shard_map/all_to_all | solution.py:22
  242.6 0.0 copy-done.2
  242.6 0.0 copy-done.4
  242.6 0.0 copy-start.6
  242.6 1.0 copy-done.6
  243.6 1.5 finish.1
Async XLA Ops:
  0.6 52.9 %copy-start.1 = (bf16[384,768]{1,0:T(8,128)(2,1)S(1)}, bf16[384,768]{1,0:T(8,128)(2,1)}, u32[]{:S(2)}) copy-start(bf16[384,768]{1,0:T(8,128)(2,1)} %refs_4_.1) | copy-start | bytes 1769476
  0.6 52.9 %copy-start.3 = (bf16[4,64,768]{2,1,0:T(8,128)(2,1)S(1)}, bf16[4,64,768]{2,1,0:T(8,128)(2,1)}, u32[]{:S(2)}) copy-start(bf16[4,64,768]{2,1,0:T(8,128)(2,1)} %go_ref.1) | copy-start | bytes 1179652
  37.6 6.6 %copy-start = (bf16[2,4,64,384]{3,2,1,0:T(8,128)(2,1)S(1)}, bf16[2,4,64,384]{3,2,1,0:T(8,128)(2,1)}, u32[]{:S(2)}) copy-start(bf16[2,4,64,384]{3,2,1,0:T(8,128)(2,1)} %get-tuple-element.33.own_ref.refs_3_) | copy-start | bytes 1179652
  37.6 33.8 %all-to-all-start = ((bf16[4,4,64,384]{3,2,1,0:T(8,128)(2,1)}), bf16[4,4,64,384]{3,2,1,0:T(8,128)(2,1)S(1)}, u32[]{:S(2)}, u32[]{:S(2)}) async-start(bf16[4,4,64,384]{3,2,1,0:T(8,128)(2,1)} %get-tuple-element.31), calls=%async_computation | async-start | bytes 1572864 | tf_op jit(solution)/shard_map/all_to_all | solution.py:22
  44.2 15.1 %collective-permute-start.2 = (bf16[2,4,64,384]{3,2,1,0:T(8,128)(2,1)S(1)}, bf16[2,4,64,384]{3,2,1,0:T(8,128)(2,1)S(1)}, u32[]{:S(2)}, u32[]{:S(2)}) collective-permute-start(bf16[2,4,64,384]{3,2,1,0:T(8,128)(2,1)S(1)} %copy-done), channel_id=1, source_target_pairs={{0,12},{4,0},{8,4},{12,8},{1,13},{5,1},{9,5},{13,9},{2,14},{6,2},{... | collective-permute-start | bytes 1179656 | tf_op jit(solution)/shard_map/ppermute | solution.py:27
  48.5 12.6 %collective-permute-start.1 = (bf16[2,4,64,384]{3,2,1,0:T(8,128)(2,1)S(1)}, bf16[2,4,64,384]{3,2,1,0:T(8,128)(2,1)S(1)}, u32[]{:S(2)}, u32[]{:S(2)}) collective-permute-start(bf16[2,4,64,384]{3,2,1,0:T(8,128)(2,1)S(1)} %copy-done), channel_id=1, source_target_pairs={{0,8},{4,12},{8,0},{12,4},{1,9},{5,13},{9,1},{13,5},{2,10},{6,14},... | collective-permute-start | bytes 1179656 | tf_op jit(solution)/shard_map/ppermute | solution.py:27
  51.0 20.4 %collective-permute-start = (bf16[2,4,64,384]{3,2,1,0:T(8,128)(2,1)S(1)}, bf16[2,4,64,384]{3,2,1,0:T(8,128)(2,1)S(1)}, u32[]{:S(2)}, u32[]{:S(2)}) collective-permute-start(bf16[2,4,64,384]{3,2,1,0:T(8,128)(2,1)S(1)} %copy-done), channel_id=1, source_target_pairs={{0,4},{4,8},{8,12},{12,0},{1,5},{5,9},{9,13},{13,1},{2,6},{6,10},{... | collective-permute-start | bytes 1179656 | tf_op jit(solution)/shard_map/ppermute | solution.py:27
  71.4 24.2 %all-to-all-start.1 = ((bf16[4,4,64,384]{3,2,1,0:T(8,128)(2,1)}), bf16[4,4,64,384]{3,2,1,0:T(8,128)(2,1)S(1)}, u32[]{:S(2)}, u32[]{:S(2)}) async-start(bf16[4,4,64,384]{3,2,1,0:T(8,128)(2,1)} %grad_attended.1), calls=%async_computation.1 | async-start | bytes 1572864 | tf_op jit(solution)/shard_map/all_to_all | solution.py:22
  77.9 4.6 %collective-permute-start.3 = (f32[4,3,64,256]{3,2,1,0:T(8,128)S(1)}, f32[4,3,64,256]{3,2,1,0:T(8,128)S(1)}, u32[]{:S(2)}, u32[]{:S(2)}) collective-permute-start(f32[4,3,64,256]{3,2,1,0:T(8,128)S(1)} %get-tuple-element.39), channel_id=1, source_target_pairs={{0,16},{16,0},{1,17},{17,1},{2,18},{18,2},{3,19},{19,3},{4,20},{20... | collective-permute-start | bytes 2359304 | tf_op jit(solution)/shard_map/ppermute | solution.py:27
  83.9 13.6 %collective-permute-start.4 = (f32[3,64,256]{2,1,0:T(8,128)}, f32[3,64,256]{2,1,0:T(8,128)S(1)}, u32[]{:S(2)}, u32[]{:S(2)}) collective-permute-start(f32[3,64,256]{2,1,0:T(8,128)} %get-tuple-element.41), channel_id=1, source_target_pairs={{0,32},{32,64},{64,96},{96,0},{1,33},{33,65},{65,97},{97,1},{2,34}... | collective-permute-start | bytes 589832 | tf_op jit(solution)/shard_map/ppermute | solution.py:27
  87.1 11.8 %collective-permute-start.5 = (f32[3,64,256]{2,1,0:T(8,128)}, f32[3,64,256]{2,1,0:T(8,128)}, u32[]{:S(2)}, u32[]{:S(2)}) collective-permute-start(f32[3,64,256]{2,1,0:T(8,128)} %get-tuple-element.42), channel_id=1, source_target_pairs={{0,64},{32,96},{64,0},{96,32},{1,65},{33,97},{65,1},{97,33},{2,66}... | collective-permute-start | bytes 589832 | tf_op jit(solution)/shard_map/ppermute | solution.py:27
  91.6 8.2 %collective-permute-start.6 = (f32[3,64,256]{2,1,0:T(8,128)}, f32[3,64,256]{2,1,0:T(8,128)}, u32[]{:S(2)}, u32[]{:S(2)}) collective-permute-start(f32[3,64,256]{2,1,0:T(8,128)} %get-tuple-element.43), channel_id=1, source_target_pairs={{0,96},{32,0},{64,32},{96,64},{1,97},{33,1},{65,33},{97,65},{2,98}... | collective-permute-start | bytes 589832 | tf_op jit(solution)/shard_map/ppermute | solution.py:27
  99.8 5.4 %collective-permute-start.7 = (f32[4,3,64,256]{3,2,1,0:T(8,128)S(1)}, f32[4,3,64,256]{3,2,1,0:T(8,128)S(1)}, u32[]{:S(2)}, u32[]{:S(2)}) collective-permute-start(f32[4,3,64,256]{3,2,1,0:T(8,128)S(1)} %get-tuple-element.52), channel_id=1, source_target_pairs={{0,16},{16,0},{1,17},{17,1},{2,18},{18,2},{3,19},{19,3},{4,20},{20... | collective-permute-start | bytes 2359304 | tf_op jit(solution)/shard_map/ppermute | solution.py:27
  187.2 10.4 %collective-permute-start.8 = (bf16[4,2,3,64,256]{4,3,2,1,0:T(8,128)(2,1)S(1)}, bf16[4,2,3,64,256]{4,3,2,1,0:T(8,128)(2,1)S(1)}, u32[]{:S(2)}, u32[]{:S(2)}) collective-permute-start(bf16[4,2,3,64,256]{4,3,2,1,0:T(8,128)(2,1)S(1)} %all_to_all.38.refs_1_), channel_id=1, source_target_pairs={{0,16},{16,0},{1,17},{17,1},{2,18},{18,2},{3,19},{19,3},{4,20},{20... | collective-permute-start | bytes 2359304 | tf_op jit(solution)/shard_map/ppermute | solution.py:27
  201.7 40.9 %copy-start.2 = (bf16[384,768]{1,0:T(8,128)(2,1)S(1)}, bf16[384,768]{1,0:T(8,128)(2,1)}, u32[]{:S(2)}) copy-start(bf16[384,768]{1,0:T(8,128)(2,1)} %refs_4_.1) | copy-start | bytes 1769476
  201.7 40.9 %copy-start.4 = (bf16[2,4,64,384]{3,2,1,0:T(8,128)(2,1)S(1)}, bf16[2,4,64,384]{3,2,1,0:T(8,128)(2,1)}, u32[]{:S(2)}) copy-start(bf16[2,4,64,384]{3,2,1,0:T(8,128)(2,1)} %get-tuple-element.54.refs_0_) | copy-start | bytes 1179652
  201.7 40.9 %all-to-all-start.6 = ((bf16[4,2,4,64,384]{4,3,2,1,0:T(8,128)(2,1)}), bf16[4,2,4,64,384]{4,3,2,1,0:T(8,128)(2,1)S(1)}, u32[]{:S(2)}, u32[]{:S(2)}) async-start(bf16[4,2,4,64,384]{4,3,2,1,0:T(8,128)(2,1)} %get-tuple-element.53), calls=%async_computation.6 | async-start | bytes 3145728 | tf_op jit(solution)/shard_map/all_to_all | solution.py:22
  206.1 12.1 %collective-permute-start.9 = (bf16[2,4,64,384]{3,2,1,0:T(8,128)(2,1)}, bf16[2,4,64,384]{3,2,1,0:T(8,128)(2,1)S(1)}, u32[]{:S(2)}, u32[]{:S(2)}) collective-permute-start(bf16[2,4,64,384]{3,2,1,0:T(8,128)(2,1)} %get-tuple-element.55), channel_id=1, source_target_pairs={{0,12},{4,0},{8,4},{12,8},{1,13},{5,1},{9,5},{13,9},{2,14},{6,2},{... | collective-permute-start | bytes 1179656 | tf_op jit(solution)/shard_map/ppermute | solution.py:27
  208.3 13.3 %collective-permute-start.10 = (bf16[2,4,64,384]{3,2,1,0:T(8,128)(2,1)}, bf16[2,4,64,384]{3,2,1,0:T(8,128)(2,1)S(1)}, u32[]{:S(2)}, u32[]{:S(2)}) collective-permute-start(bf16[2,4,64,384]{3,2,1,0:T(8,128)(2,1)} %get-tuple-element.56), channel_id=1, source_target_pairs={{0,8},{4,12},{8,0},{12,4},{1,9},{5,13},{9,1},{13,5},{2,10},{6,14},... | collective-permute-start | bytes 1179656 | tf_op jit(solution)/shard_map/ppermute | solution.py:27
  210.7 20.6 %collective-permute-start.11 = (bf16[2,4,64,384]{3,2,1,0:T(8,128)(2,1)}, bf16[2,4,64,384]{3,2,1,0:T(8,128)(2,1)S(1)}, u32[]{:S(2)}, u32[]{:S(2)}) collective-permute-start(bf16[2,4,64,384]{3,2,1,0:T(8,128)(2,1)} %get-tuple-element.57), channel_id=1, source_target_pairs={{0,4},{4,8},{8,12},{12,0},{1,5},{5,9},{9,13},{13,1},{2,6},{6,10},{... | collective-permute-start | bytes 1179656 | tf_op jit(solution)/shard_map/ppermute | solution.py:27
  231.4 0.8 copy-start.5
  242.6 1.0 copy-start.6

commit v5 on v2

v5 whole, which is shorter than its diff:
```python
import math

import jax
import jax.numpy as jnp
from jax import lax
from jax.experimental import pallas as pl
from jax.experimental.pallas import tpu as pltpu
from jax.sharding import Mesh, PartitionSpec as P

HEADS = 6
LOCAL = 3
F32 = jnp.float32
BF16 = jnp.bfloat16
VMEM = 16 * 1024 * 1024


def params():
    return pltpu.CompilerParams(vmem_limit_bytes=VMEM)


def exchange(blocks, axis):
    return lax.all_to_all(blocks, axis, 0, 0, tiled=True)


def shift(block, axis, by):
    n = lax.axis_size(axis)
    return lax.ppermute(block, axis, [(i, (i + by) % n) for i in range(n)])


def gather(block, axis):
    return lax.all_gather(block, axis)


def stack_kernel(q_hbm, k_hbm, v_hbm, w_hbm, go_hbm, out_ref, w_ref, go_ref, sems):
    loads = [
        pltpu.make_async_copy(w_hbm, w_ref, sems.at[0]),
        pltpu.make_async_copy(go_hbm, go_ref, sems.at[1]),
        pltpu.make_async_copy(q_hbm, out_ref.at[0], sems.at[2]),
        pltpu.make_async_copy(k_hbm, out_ref.at[1], sems.at[3]),
        pltpu.make_async_copy(v_hbm, out_ref.at[2], sems.at[4]),
    ]
    for load in loads:
        load.start()
    loads[0].wait()
    loads[1].wait()
    for s in range(go_ref.shape[0]):
        out_ref[3, s] = lax.dot_general(
            go_ref[s], w_ref[...], (((1,), (1,)), ((), ())), preferred_element_type=F32
        ).astype(BF16)
    for load in loads[2:]:
        load.wait()


def merge(first, own, other):
    half = own.shape[1] // 2
    swapped = jnp.concatenate([other[:, half:], other[:, :half]], axis=1)
    low = lax.broadcasted_iota(jnp.int32, own.shape, 1) < half
    return jnp.where(first, jnp.where(low, own, swapped), jnp.where(low, swapped, own))


def trade_kernel(place_ref, own_ref, other_ref, q_ref, g_ref, kv_ref):
    first = place_ref[0] == 0
    for s in range(q_ref.shape[0]):
        q_ref[s] = merge(first, own_ref[0, s], other_ref[0, s])
        g_ref[s] = merge(first, own_ref[3, s], other_ref[3, s])
        for which in range(2):
            block = merge(first, own_ref[1 + which, s], other_ref[1 + which, s])
            for n in range(kv_ref.shape[0]):
                kv_ref[n, which, s] = block


def columns(refs):
    seqs = refs[0].shape[0]
    rows = [jnp.concatenate([ref[s] for s in range(seqs)], axis=1) for ref in refs]
    return jnp.concatenate(rows, axis=0)


def lefts(ref):
    return columns([ref.at[n] for n in range(4)])


def rights(place_ref, ref, which):
    return columns([ref.at[lax.rem(place_ref[1] + 4 - n, 4), which] for n in range(4)])


def odd_chunk(shape):
    return (lax.broadcasted_iota(jnp.int32, shape, 1) // 64) % 2


def product_kernel(place_ref, q0_ref, q1_ref, g0_ref, g1_ref, kv0_ref, kv1_ref, out_ref):
    odd = lax.rem(pl.program_id(0), 2)
    for which, (left0, left1) in enumerate(((q0_ref, q1_ref), (g0_ref, g1_ref))):
        left = []
        for ref, parity in ((left0, odd), (left1, 1 - odd)):
            cols = lefts(ref)
            left.append(jnp.where(odd_chunk(cols.shape) == parity, cols, jnp.zeros_like(cols)))
        left = jnp.concatenate(left, axis=1)
        right = jnp.concatenate([rights(place_ref, kv0_ref, which), rights(place_ref, kv1_ref, which)], axis=1)
        full = lax.dot_general(left, right, (((1,), (1,)), ((), ())), preferred_element_type=F32)
        out_ref[:, 0, which] = full.reshape(out_ref.shape[0], out_ref.shape[3], out_ref.shape[4])


def rows_kernel(part_ref, out_ref):
    total = (part_ref[0] + part_ref[1]) + (part_ref[2] + part_ref[3])
    for n in range(16):
        for t in range(LOCAL):
            for which in range(2):
                at = (which * LOCAL + t) * 4
                out_ref[n, at : at + 4] = total[t, which, n * 4 : n * 4 + 4]


def softmax_kernel(scale, part_ref, out_ref):
    tiles = []
    for col in range(4):
        parts = [part_ref[n * 4 + col] for n in range(4)]
        tiles.append((parts[0] + parts[1]) + (parts[2] + parts[3]))
    total = jnp.concatenate(tiles, axis=1)
    logits = total[:12] * scale
    grads = total[12:]
    expo = jnp.exp(logits - jnp.max(logits, axis=-1, keepdims=True))
    weights = expo / jnp.sum(expo, axis=-1, keepdims=True)
    scores = weights * (grads - jnp.sum(weights * grads, axis=-1, keepdims=True))
    full = jnp.concatenate([weights, scores], axis=0)
    for col in range(4):
        at = col * 256
        tile = jnp.concatenate([full[:, at : at + 128], full[:, at + 128 : at + 256]], axis=0).astype(BF16)
        for n in range(col, 16, 4):
            out_ref[n] = tile


def unpack_kernel(ws_ref, out_ref, rows_ref):
    for n in range(16):
        block = ws_ref[n].astype(F32)
        for which in range(2):
            for t in range(LOCAL):
                at = which * 12 + t * 4
                rows_ref[which, t, n * 4 : n * 4 + 4, 0:128] = block[at : at + 4]
                rows_ref[which, t, n * 4 : n * 4 + 4, 128:256] = block[24 + at : 28 + at]
    full = rows_ref[...].astype(BF16)
    for n in range(out_ref.shape[0]):
        out_ref[n] = full


def output_kernel(scale, place_ref, even_ref, odd_ref, q_ref, g_ref, kv_ref, row_ref, *col_refs):
    row_refs = [row_ref.at[n] for n in range(4)]

    def product(kind, side, contract):
        both = [
            lax.dot_general(
                ref[:, kind, 0].reshape(256, 256), side, (((contract,), (0,)), ((), ())), preferred_element_type=F32
            )
            for ref in (even_ref, odd_ref)
        ]
        return jnp.where(odd_chunk(both[0].shape) == 0, both[0], both[1])

    def put(outs, which, value):
        value = value.astype(BF16)
        for n, ref in enumerate(outs):
            _, seqs, res, lanes = ref.shape
            for s in range(seqs):
                ref[which, s] = value[n * res : (n + 1) * res, s * lanes : (s + 1) * lanes]

    put(row_refs, 0, product(0, rights(place_ref, kv_ref, 1), 1))
    put(row_refs, 1, product(1, rights(place_ref, kv_ref, 0), 1) * scale)
    put(col_refs, 0, product(0, lefts(g_ref), 0))
    put(col_refs, 1, product(1, lefts(q_ref), 0) * scale)


def total_kernel(*refs):
    parts, out_ref = refs[:-1], refs[-1]
    for which in range(out_ref.shape[0]):
        for s in range(out_ref.shape[1]):
            p = [ref[which, s].astype(F32) for ref in parts]
            out_ref[which, s] = ((p[0] + p[1]) + (p[2] + p[3])).astype(BF16)


def total_blocks_kernel(part_ref, out_ref):
    total_kernel(*[part_ref.at[n] for n in range(4)], out_ref)


def finish_kernel(place_ref, row_ref, row_other_ref, col_ref, col_other_ref, w_ref, mixed_ref, gq_ref, gk_ref, gv_ref):
    first = place_ref[0] == 0
    for s in range(mixed_ref.shape[0]):
        attended = merge(first, row_ref[0, s], row_other_ref[0, s])
        mixed_ref[s] = jnp.dot(attended, w_ref[...], preferred_element_type=F32).astype(BF16)
        gq_ref[s] = merge(first, row_ref[1, s], row_other_ref[1, s])
        gv_ref[s] = merge(first, col_ref[0, s], col_other_ref[0, s])
        gk_ref[s] = merge(first, col_ref[1, s], col_other_ref[1, s])


def on_device(queries, keys, values, out_weight, grad_out):
    seqs, res, width = queries.shape
    model_dim = out_weight.shape[1]
    scale = 1.0 / math.sqrt(width // HEADS * seqs * 32)
    place = jnp.stack([lax.axis_index("c"), lax.axis_index("x")]).astype(jnp.int32)
    block = (seqs, res, width)
    smem = pl.BlockSpec(memory_space=pltpu.SMEM)
    vmem = pl.BlockSpec(memory_space=pltpu.VMEM)
    hbm = pl.BlockSpec(memory_space=pltpu.HBM)

    def array(shape, dtype=BF16):
        return jax.ShapeDtypeStruct(shape, dtype)

    args = (queries, keys, values, out_weight, grad_out)
    own = pl.pallas_call(
        stack_kernel,
        in_specs=[hbm] * 5,
        out_specs=vmem,
        out_shape=array((4,) + block),
        scratch_shapes=[
            pltpu.VMEM(out_weight.shape, BF16),
            pltpu.VMEM(grad_out.shape, BF16),
            pltpu.SemaphoreType.DMA((5,)),
        ],
        compiler_params=params(),
        name="stack",
    )(*(pltpu.with_memory_space_constraint(arg, pltpu.HBM) for arg in args))
    q, g, kv = pl.pallas_call(
        trade_kernel,
        in_specs=[smem, vmem, vmem],
        out_shape=(array(block), array(block), array((4, 2) + block)),
        compiler_params=params(),
        name="trade",
    )(place, own, shift(own, "c", 1))
    kv = exchange(kv, "x")
    q = gather(q, "zl")
    g = gather(g, "zl")

    def slab(at):
        return pl.BlockSpec((4, seqs, res, 128), lambda t: (0, 0, 0, at(t)))

    def kv_slab(at):
        return pl.BlockSpec((4, 2, seqs, res, 128), lambda t: (0, 0, 0, 0, at(t)))

    low, high, same = (lambda t: t // 2), (lambda t: (t + 3) // 2), (lambda t: t)
    partial = pl.pallas_call(
        product_kernel,
        grid=(LOCAL,),
        in_specs=[smem, slab(low), slab(high), slab(low), slab(high), kv_slab(low), kv_slab(high)],
        out_specs=pl.BlockSpec((4, 1, 2, 64, 256), lambda t: (0, t, 0, 0, 0)),
        out_shape=array((4, LOCAL, 2, 64, 256), F32),
        compiler_params=params(),
        name="products",
    )(place, q, q, g, g, kv, kv)
    partial = exchange(partial, "y")
    partial = pl.pallas_call(
        rows_kernel, out_shape=array((16, 8 * LOCAL, 256), F32), compiler_params=params(), name="rows"
    )(partial)
    partial = exchange(partial, ("zh", "zl"))
    ws = pl.pallas_call(
        lambda *refs: softmax_kernel(scale, *refs),
        out_shape=array((16, 48, 128)),
        compiler_params=params(),
        name="softmax",
    )(partial)
    ws = exchange(ws, ("zh", "zl"))
    ws = pl.pallas_call(
        unpack_kernel,
        out_shape=array((4, 2, LOCAL, 64, 256)),
        scratch_shapes=[pltpu.VMEM((2, LOCAL, 64, 256), F32)],
        compiler_params=params(),
        name="unpack",
    )(ws)
    ws = exchange(ws, "y")

    def ws_slab(add):
        return pl.BlockSpec((4, 2, 1, 64, 256), lambda p: (0, 0, (2 * p + add) % 3, 0, 0))

    row, *cols = pl.pallas_call(
        lambda *refs: output_kernel(scale, *refs),
        grid=(3,),
        in_specs=[smem, ws_slab(0), ws_slab(1), slab(same), slab(same), kv_slab(same)],
        out_specs=[kv_slab(same)] + [pl.BlockSpec((2, seqs, res, 128), lambda p: (0, 0, 0, p))] * 4,
        out_shape=(pltpu.HBM((4, 2) + block, BF16),) + (pltpu.HBM((2,) + block, BF16),) * 4,
        compiler_params=params(),
        name="outputs",
    )(place, ws, ws, q, g, kv)
    row = exchange(row, "zl")
    cols = [cols[0]] + [shift(cols[by], "x", -by) for by in (1, 2, 3)]
    col = pl.pallas_call(
        total_kernel, out_shape=array((2,) + block), compiler_params=params(), name="total_columns"
    )(*cols)
    col_other = shift(col, "c", 1)
    row = pl.pallas_call(
        total_blocks_kernel, out_shape=array((2,) + block), compiler_params=params(), name="total_rows"
    )(row)
    return pl.pallas_call(
        finish_kernel,
        in_specs=[smem] + [vmem] * 5,
        out_shape=(array((seqs, res, model_dim)), array(block), array(block), array(block)),
        compiler_params=params(),
        name="finish",
    )(place, row, shift(row, "c", 1), col, col_other, out_weight)


def solution(mesh):
    grid = Mesh(mesh.devices.reshape(4, 4, 2, 4, 4), ("zh", "y", "c", "x", "zl"))
    placed = P(("zh", "y", "c"), ("x", "zl"), None)
    return jax.shard_map(
        on_device,
        mesh=grid,
        in_specs=(placed, placed, placed, P(), placed),
        out_specs=(placed, placed, placed, placed),
        check_vma=False,
    )
```

time: 212 us -> 183 us (0.86)
  waiting for transfers between devices: 58.4 us -> 14.1 us
  blocking collectives: 88.8 us -> 109 us
  local copies, waits for them, and re-layouts: 9.27 us -> 0.02 us
  Pallas kernels: 10.3 us -> 13.9 us
    all_gather x0 -> x2, blocking collectives: none -> 31.6 us  [gather(): return lax.all_gather(block, axis)]
    ppermute x8 -> x6, waiting for transfers between devices: 40.9 us -> 12.7 us  [shift(): return lax.ppermute(block, axis, [(i, (i + by) % n) for i in range(n)])]
    all_to_all x2, waiting for transfers between devices: 17.5 us -> 1.47 us  [exchange(): return lax.all_to_all(blocks, axis, 0, 0, tiled=True)]
    all_to_all x4, blocking collectives: 88.8 us -> 77 us  [exchange(): return lax.all_to_all(blocks, axis, 0, 0, tiled=True)]
    unnamed x22 -> x10, local copies, waits for them, and re-layouts: 9.27 us -> 0.02 us
    ppermute x8 -> x6, starting transfers between devices: 31.8 us -> 37.3 us  [shift(): return lax.ppermute(block, axis, [(i, (i + by) % n) for i in range(n)])]
    all_to_all x2, starting transfers between devices: 11.5 us -> 7.75 us  [exchange(): return lax.all_to_all(blocks, axis, 0, 0, tiled=True)]
    pallas_call x7 -> x10, Pallas kernels: 10.3 us -> 13.9 us  [the longest x1 4.04 us: on_device(): pl.pallas_call(lambda *refs: output_kernel(scale, *refs), grid=(3,), in_s...]
  transfers between devices with their start and end apart: 10 -> 8, of which waited for: 10 -> 6; matrix products, arithmetic and copies ran while one was open for 0% -> 0% of each run, Pallas kernels for 0% -> 0%
where the time goes in v5:
time: 183 us
  blocking collectives  109 us (60%)
  starting transfers between devices  45.1 us (25%)
  waiting for transfers between devices  14.1 us (8%)
  Pallas kernels  13.9 us (8%)
    all_to_all x4, blocking collectives, exchange(): return lax.all_to_all(blocks, axis, 0, 0, tiled=True)  77 us
    ppermute x6, starting transfers between devices, shift(): return lax.ppermute(block, axis, [(i, (i + by) % n) for i in range(n)])  37.3 us
    all_gather x2, blocking collectives, gather(): return lax.all_gather(block, axis)  31.6 us
    ppermute x6, waiting for transfers between devices, shift(): return lax.ppermute(block, axis, [(i, (i + by) % n) for i in range(n)])  12.7 us
    all_to_all x2, starting transfers between devices, exchange(): return lax.all_to_all(blocks, axis, 0, 0, tiled=True)  7.75 us
    pallas_call x1, Pallas kernels, on_device(): pl.pallas_call(lambda *refs: output_kernel(scale, *refs), grid=(3,), in_s...  4.04 us
  transfers between devices with their start and end apart: 8, of which 6 were waited for; matrix products, arithmetic and copies ran while one was open for 0% of the time, Pallas kernels for 0%

profile of v5, /device:TPU:1, one launch (start us, length us, event | category | flops | bytes accessed | tf_op | source)
XLA Modules:
  0.0 182.6 jit_solution(2949922198147217482)
XLA Ops:
  0.6 2.0 %stack.13.own_ref = bf16[4,4,64,384]{3,2,1,0:T(8,128)(2,1)S(1)} custom-call(bf16[4,64,384]{2,1,0:T(8,128)(2,1)} %q_hbm.1, bf16[4,64,384]{2,1,0:T(8,128)(2,1)} %k_hbm.1, bf16[4,64,384]{2,1,0:T(8,128)(2,1)} %v_hbm.1, bf16[384,768]{1,0:T(8,128)(2,1)} %w_ref.1, bf16[4,64,768]{2,1,0:T(8,128)(2,1)} %go_hbm.1), custom_call_target="tpu_custom_call" | custom-call | tf_op jit(solution)/shard_map/stack/pallas_call | solution.py:205
  2.7 8.8 %collective-permute-start = (bf16[4,4,64,384]{3,2,1,0:T(8,128)(2,1)S(1)}, bf16[4,4,64,384]{3,2,1,0:T(8,128)(2,1)S(1)}, u32[]{:S(2)}, u32[]{:S(2)}) collective-permute-start(bf16[4,4,64,384]{3,2,1,0:T(8,128)(2,1)S(1)} %stack.13.own_ref), channel_id=1, source_target_pairs={{0,16},{16,0},{1,17},{17,1},{2,18},{18,2},{3,19},{19,3},{4,20},{20... | collective-permute-start | bytes 2359304 | tf_op jit(solution)/shard_map/ppermute | solution.py:27
  11.5 0.1 pad_add_fusion.place_ref.refs_0_
  11.6 1.8 collective-permute-done.other_ref
  13.4 2.1 %trade.1 = (bf16[4,64,384]{2,1,0:T(8,128)(2,1)S(1)}, bf16[4,64,384]{2,1,0:T(8,128)(2,1)S(1)}, bf16[4,2,4,64,384]{4,3,2,1,0:T(8,128)(2,1)}) custom-call(s32[2]{0:T(128)S(1)} %pad_add_fusion.place_ref.refs_0_, bf16[4,4,64,384]{3,2,1,0:T(8,128)(2,1)S(1)} %stack.13.own_ref, bf16[4,4,64,384]{3,2,1,0:T(8,128)(2,1)S(1)} %collective-permute-done.other_ref), custom_call_target="tpu_custom_call" | custom-call | tf_op jit(solution)/shard_map/trade/pallas_call | solution.py:218
  15.5 3.6 %all-to-all-start = ((bf16[4,2,4,64,384]{4,3,2,1,0:T(8,128)(2,1)}), bf16[4,2,4,64,384]{4,3,2,1,0:T(8,128)(2,1)S(1)}, u32[]{:S(2)}, u32[]{:S(2)}) async-start(bf16[4,2,4,64,384]{4,3,2,1,0:T(8,128)(2,1)} %get-tuple-element.14), calls=%async_computation | async-start | bytes 3145728 | tf_op jit(solution)/shard_map/all_to_all | solution.py:22
  19.0 16.5 %all-gather = bf16[16,64,384]{2,1,0:T(8,128)(2,1)S(1)} all-gather(bf16[4,64,384]{2,1,0:T(8,128)(2,1)S(1)} %get-tuple-element.12), channel_id=2, replica_groups=mesh['zh'=4,'y'=4,'c'=2,'x'=4,'zl'=4] {'zl'}, dimensions={0}, use_global_device_ids=true | all-gather | bytes 983040 | tf_op jit(solution)/shard_map/all_gather | solution.py:31
  35.5 15.1 %all-gather.1 = bf16[16,64,384]{2,1,0:T(8,128)(2,1)S(1)} all-gather(bf16[4,64,384]{2,1,0:T(8,128)(2,1)S(1)} %get-tuple-element.13), channel_id=3, replica_groups=mesh['zh'=4,'y'=4,'c'=2,'x'=4,'zl'=4] {'zl'}, dimensions={0}, use_global_device_ids=true | all-gather | bytes 983040 | tf_op jit(solution)/shard_map/all_gather | solution.py:31
  50.6 0.0 all-to-all-done.kv0_ref.kv1_ref.refs_5_
  50.6 2.8 %products.1 = f32[4,3,2,64,256]{4,3,2,1,0:T(8,128)S(1)} custom-call(s32[2]{0:T(128)S(1)} %pad_add_fusion.place_ref.refs_0_, bf16[4,4,64,384]{3,2,1,0:T(8,128)(2,1)S(1)} %bitcast.4, bf16[4,4,64,384]{3,2,1,0:T(8,128)(2,1)S(1)} %bitcast.5, bf16[4,4,64,384]{3,2,1,0:T(8,128)(2,1)S(1)} %bitcast.7, bf16[4,4,64,384]{3,2,1,0:T(8,128)(2,1)S(1)} %bitcast.8, ...), custom_call_target="tpu_custom_call" | custom-call | tf_op jit(solution)/shard_map/products/pallas_call | solution.py:236
  53.4 18.7 %all_to_all.30.part_ref = f32[4,3,2,64,256]{4,3,2,1,0:T(8,128)S(1)} all-to-all(f32[4,3,2,64,256]{4,3,2,1,0:T(8,128)S(1)} %products.1), channel_id=1, replica_groups=mesh['zh'=4,'y'=4,'c'=2,'x'=4,'zl'=4] {'y'}, dimensions={0} | all-to-all | bytes 3145728 | tf_op jit(solution)/shard_map/all_to_all | solution.py:22
  72.1 0.1 rows.1
  72.2 25.4 %all_to_all.31.refs_0_ = f32[16,24,256]{2,1,0:T(8,128)S(1)} all-to-all(f32[16,24,256]{2,1,0:T(8,128)S(1)} %rows.1), channel_id=1, replica_groups=mesh['zh'=4,'y'=4,'c'=2,'x'=4,'zl'=4] {'zh','zl'}, dimensions={0} | all-to-all | bytes 786432 | tf_op jit(solution)/shard_map/all_to_all | solution.py:22
  97.6 0.3 softmax.1
  97.9 22.2 %all_to_all.32.ws_ref = bf16[16,48,128]{2,1,0:T(8,128)(2,1)S(1)} all-to-all(bf16[16,48,128]{2,1,0:T(8,128)(2,1)S(1)} %softmax.1), channel_id=1, replica_groups=mesh['zh'=4,'y'=4,'c'=2,'x'=4,'zl'=4] {'zh','zl'}, dimensions={0} | all-to-all | bytes 393216 | tf_op jit(solution)/shard_map/all_to_all | solution.py:22
  120.1 0.1 unpack.1
  120.2 10.7 %all_to_all.33.refs_1_.refs_2_ = bf16[4,2,3,64,256]{4,3,2,1,0:T(8,128)(2,1)S(1)} all-to-all(bf16[4,2,3,64,256]{4,3,2,1,0:T(8,128)(2,1)S(1)} %unpack.1), channel_id=1, replica_groups=mesh['zh'=4,'y'=4,'c'=2,'x'=4,'zl'=4] {'y'}, dimensions={0} | all-to-all | bytes 1572864 | tf_op jit(solution)/shard_map/all_to_all | solution.py:22
  130.9 4.0 %outputs.1 = (bf16[4,2,4,64,384]{4,3,2,1,0:T(8,128)(2,1)}, bf16[2,4,64,384]{3,2,1,0:T(8,128)(2,1)}, bf16[2,4,64,384]{3,2,1,0:T(8,128)(2,1)}, bf16[2,4,64,384]{3,2,1,0:T(8,128)(2,1)}, bf16[2,4,64,384]{3,2,1,0:T(8,128)(2,1)}) custom-call(s32[2]{0:T(128)S(1)} %pad_add_fusion.place_ref.refs_0_, bf16[4,2,3,64,256]{4,3,2,1,0:T(8,128)(2,1)S(1)} %all_to_all.33.refs_1_.refs_2_, ...), custom_call_target="tpu_custom_call" | custom-call | tf_op jit(solution)/shard_map/outputs/pallas_call | solution.py:269
  135.0 0.0 copy-start.4
  135.0 0.0 copy-start.3
  135.0 0.0 copy-start.2
  135.0 0.0 copy-start.1
  135.0 4.2 %all-to-all-start.5 = ((bf16[4,2,4,64,384]{4,3,2,1,0:T(8,128)(2,1)}), bf16[4,2,4,64,384]{4,3,2,1,0:T(8,128)(2,1)S(1)}, u32[]{:S(2)}, u32[]{:S(2)}) async-start(bf16[4,2,4,64,384]{4,3,2,1,0:T(8,128)(2,1)} %get-tuple-element.15), calls=%async_computation.5 | async-start | bytes 3145728 | tf_op jit(solution)/shard_map/all_to_all | solution.py:22
  139.2 0.0 copy-done.4
  139.2 5.1 %collective-permute-start.2 = (bf16[2,4,64,384]{3,2,1,0:T(8,128)(2,1)S(1)}, bf16[2,4,64,384]{3,2,1,0:T(8,128)(2,1)S(1)}, u32[]{:S(2)}, u32[]{:S(2)}) collective-permute-start(bf16[2,4,64,384]{3,2,1,0:T(8,128)(2,1)S(1)} %copy-done.4), channel_id=1, source_target_pairs={{0,12},{4,0},{8,4},{12,8},{1,13},{5,1},{9,5},{13,9},{2,14},{6,2},{... | collective-permute-start | bytes 1179656 | tf_op jit(solution)/shard_map/ppermute | solution.py:27
  144.3 0.0 copy-done.3
  144.3 2.5 %collective-permute-start.3 = (bf16[2,4,64,384]{3,2,1,0:T(8,128)(2,1)S(1)}, bf16[2,4,64,384]{3,2,1,0:T(8,128)(2,1)S(1)}, u32[]{:S(2)}, u32[]{:S(2)}) collective-permute-start(bf16[2,4,64,384]{3,2,1,0:T(8,128)(2,1)S(1)} %copy-done.3), channel_id=1, source_target_pairs={{0,8},{4,12},{8,0},{12,4},{1,9},{5,13},{9,1},{13,5},{2,10},{6,14},... | collective-permute-start | bytes 1179656 | tf_op jit(solution)/shard_map/ppermute | solution.py:27
  146.8 0.0 copy-done.2
  146.8 2.5 %collective-permute-start.4 = (bf16[2,4,64,384]{3,2,1,0:T(8,128)(2,1)S(1)}, bf16[2,4,64,384]{3,2,1,0:T(8,128)(2,1)S(1)}, u32[]{:S(2)}, u32[]{:S(2)}) collective-permute-start(bf16[2,4,64,384]{3,2,1,0:T(8,128)(2,1)S(1)} %copy-done.2), channel_id=1, source_target_pairs={{0,4},{4,8},{8,12},{12,0},{1,5},{5,9},{9,13},{13,1},{2,6},{6,10},{... | collective-permute-start | bytes 1179656 | tf_op jit(solution)/shard_map/ppermute | solution.py:27
  149.3 3.9 %collective-permute-done.2.refs_1_ = bf16[2,4,64,384]{3,2,1,0:T(8,128)(2,1)S(1)} collective-permute-done((bf16[2,4,64,384]{3,2,1,0:T(8,128)(2,1)S(1)}, bf16[2,4,64,384]{3,2,1,0:T(8,128)(2,1)S(1)}, u32[]{:S(2)}, u32[]{:S(2)}) %collective-permute-start.2) | collective-permute-done | bytes 393248 | tf_op jit(solution)/shard_map/ppermute | solution.py:27
  153.2 1.3 collective-permute-done.3.refs_2_
  154.5 4.3 %collective-permute-done.4.refs_3_ = bf16[2,4,64,384]{3,2,1,0:T(8,128)(2,1)S(1)} collective-permute-done((bf16[2,4,64,384]{3,2,1,0:T(8,128)(2,1)S(1)}, bf16[2,4,64,384]{3,2,1,0:T(8,128)(2,1)S(1)}, u32[]{:S(2)}, u32[]{:S(2)}) %collective-permute-start.4) | collective-permute-done | bytes 393248 | tf_op jit(solution)/shard_map/ppermute | solution.py:27
  158.8 0.0 copy-done.1
  158.8 0.0 copy-start
  158.8 0.2 total_columns.1.col_ref
  159.0 11.2 %collective-permute-start.5 = (bf16[2,4,64,384]{3,2,1,0:T(8,128)(2,1)S(1)}, bf16[2,4,64,384]{3,2,1,0:T(8,128)(2,1)S(1)}, u32[]{:S(2)}, u32[]{:S(2)}) collective-permute-start(bf16[2,4,64,384]{3,2,1,0:T(8,128)(2,1)S(1)} %total_columns.1.col_ref), channel_id=1, source_target_pairs={{0,16},{16,0},{1,17},{17,1},{2,18},{18,2},{3,19},{19,3},{4,20},{20... | collective-permute-start | bytes 1179656 | tf_op jit(solution)/shard_map/ppermute | solution.py:27
  170.2 1.5 all-to-all-done.5.part_ref
  171.6 0.2 total_rows.1.row_ref
  171.8 7.4 %collective-permute-start.1 = (bf16[2,4,64,384]{3,2,1,0:T(8,128)(2,1)S(1)}, bf16[2,4,64,384]{3,2,1,0:T(8,128)(2,1)S(1)}, u32[]{:S(2)}, u32[]{:S(2)}) collective-permute-start(bf16[2,4,64,384]{3,2,1,0:T(8,128)(2,1)S(1)} %total_rows.1.row_ref), channel_id=1, source_target_pairs={{0,16},{16,0},{1,17},{17,1},{2,18},{18,2},{3,19},{19,3},{4,20},{20... | collective-permute-start | bytes 1179656 | tf_op jit(solution)/shard_map/ppermute | solution.py:27
  179.2 0.0 collective-permute-done.5.col_other_ref
  179.2 1.3 collective-permute-done.1.row_other_ref
  180.5 0.0 copy-done
  180.6 2.0 %finish.1 = (bf16[4,64,768]{2,1,0:T(8,128)(2,1)}, bf16[4,64,384]{2,1,0:T(8,128)(2,1)}, bf16[4,64,384]{2,1,0:T(8,128)(2,1)}, bf16[4,64,384]{2,1,0:T(8,128)(2,1)}) custom-call(s32[2]{0:T(128)S(1)} %pad_add_fusion.place_ref.refs_0_, bf16[2,4,64,384]{3,2,1,0:T(8,128)(2,1)S(1)} %total_rows.1.row_ref, ...), custom_call_target="tpu_custom_call" | custom-call | tf_op jit(solution)/shard_map/finish/pallas_call | solution.py:287
Async XLA Ops:
  2.7 10.7 %collective-permute-start = (bf16[4,4,64,384]{3,2,1,0:T(8,128)(2,1)S(1)}, bf16[4,4,64,384]{3,2,1,0:T(8,128)(2,1)S(1)}, u32[]{:S(2)}, u32[]{:S(2)}) collective-permute-start(bf16[4,4,64,384]{3,2,1,0:T(8,128)(2,1)S(1)} %stack.13.own_ref), channel_id=1, source_target_pairs={{0,16},{16,0},{1,17},{17,1},{2,18},{18,2},{3,19},{19,3},{4,20},{20... | collective-permute-start | bytes 2359304 | tf_op jit(solution)/shard_map/ppermute | solution.py:27
  15.5 35.1 %all-to-all-start = ((bf16[4,2,4,64,384]{4,3,2,1,0:T(8,128)(2,1)}), bf16[4,2,4,64,384]{4,3,2,1,0:T(8,128)(2,1)S(1)}, u32[]{:S(2)}, u32[]{:S(2)}) async-start(bf16[4,2,4,64,384]{4,3,2,1,0:T(8,128)(2,1)} %get-tuple-element.14), calls=%async_computation | async-start | bytes 3145728 | tf_op jit(solution)/shard_map/all_to_all | solution.py:22
  135.0 4.2 %copy-start.4 = (bf16[2,4,64,384]{3,2,1,0:T(8,128)(2,1)S(1)}, bf16[2,4,64,384]{3,2,1,0:T(8,128)(2,1)}, u32[]{:S(2)}) copy-start(bf16[2,4,64,384]{3,2,1,0:T(8,128)(2,1)} %get-tuple-element.17) | copy-start | bytes 1179652
  135.0 9.3 %copy-start.3 = (bf16[2,4,64,384]{3,2,1,0:T(8,128)(2,1)S(1)}, bf16[2,4,64,384]{3,2,1,0:T(8,128)(2,1)}, u32[]{:S(2)}) copy-start(bf16[2,4,64,384]{3,2,1,0:T(8,128)(2,1)} %get-tuple-element.18) | copy-start | bytes 1179652
  135.0 11.8 %copy-start.2 = (bf16[2,4,64,384]{3,2,1,0:T(8,128)(2,1)S(1)}, bf16[2,4,64,384]{3,2,1,0:T(8,128)(2,1)}, u32[]{:S(2)}) copy-start(bf16[2,4,64,384]{3,2,1,0:T(8,128)(2,1)} %get-tuple-element.19) | copy-start | bytes 1179652
  135.0 23.8 %copy-start.1 = (bf16[2,4,64,384]{3,2,1,0:T(8,128)(2,1)S(1)}, bf16[2,4,64,384]{3,2,1,0:T(8,128)(2,1)}, u32[]{:S(2)}) copy-start(bf16[2,4,64,384]{3,2,1,0:T(8,128)(2,1)} %get-tuple-element.16.refs_0_) | copy-start | bytes 1179652
  135.0 36.6 %all-to-all-start.5 = ((bf16[4,2,4,64,384]{4,3,2,1,0:T(8,128)(2,1)}), bf16[4,2,4,64,384]{4,3,2,1,0:T(8,128)(2,1)S(1)}, u32[]{:S(2)}, u32[]{:S(2)}) async-start(bf16[4,2,4,64,384]{4,3,2,1,0:T(8,128)(2,1)} %get-tuple-element.15), calls=%async_computation.5 | async-start | bytes 3145728 | tf_op jit(solution)/shard_map/all_to_all | solution.py:22
  139.2 14.0 %collective-permute-start.2 = (bf16[2,4,64,384]{3,2,1,0:T(8,128)(2,1)S(1)}, bf16[2,4,64,384]{3,2,1,0:T(8,128)(2,1)S(1)}, u32[]{:S(2)}, u32[]{:S(2)}) collective-permute-start(bf16[2,4,64,384]{3,2,1,0:T(8,128)(2,1)S(1)} %copy-done.4), channel_id=1, source_target_pairs={{0,12},{4,0},{8,4},{12,8},{1,13},{5,1},{9,5},{13,9},{2,14},{6,2},{... | collective-permute-start | bytes 1179656 | tf_op jit(solution)/shard_map/ppermute | solution.py:27
  144.3 10.2 %collective-permute-start.3 = (bf16[2,4,64,384]{3,2,1,0:T(8,128)(2,1)S(1)}, bf16[2,4,64,384]{3,2,1,0:T(8,128)(2,1)S(1)}, u32[]{:S(2)}, u32[]{:S(2)}) collective-permute-start(bf16[2,4,64,384]{3,2,1,0:T(8,128)(2,1)S(1)} %copy-done.3), channel_id=1, source_target_pairs={{0,8},{4,12},{8,0},{12,4},{1,9},{5,13},{9,1},{13,5},{2,10},{6,14},... | collective-permute-start | bytes 1179656 | tf_op jit(solution)/shard_map/ppermute | solution.py:27
  146.8 12.0 %collective-permute-start.4 = (bf16[2,4,64,384]{3,2,1,0:T(8,128)(2,1)S(1)}, bf16[2,4,64,384]{3,2,1,0:T(8,128)(2,1)S(1)}, u32[]{:S(2)}, u32[]{:S(2)}) collective-permute-start(bf16[2,4,64,384]{3,2,1,0:T(8,128)(2,1)S(1)} %copy-done.2), channel_id=1, source_target_pairs={{0,4},{4,8},{8,12},{12,0},{1,5},{5,9},{9,13},{13,1},{2,6},{6,10},{... | collective-permute-start | bytes 1179656 | tf_op jit(solution)/shard_map/ppermute | solution.py:27
  158.8 21.8 %copy-start = (bf16[384,768]{1,0:T(8,128)(2,1)S(1)}, bf16[384,768]{1,0:T(8,128)(2,1)}, u32[]{:S(2)}) copy-start(bf16[384,768]{1,0:T(8,128)(2,1)} %w_ref.1) | copy-start | bytes 1769476
  159.0 20.2 %collective-permute-start.5 = (bf16[2,4,64,384]{3,2,1,0:T(8,128)(2,1)S(1)}, bf16[2,4,64,384]{3,2,1,0:T(8,128)(2,1)S(1)}, u32[]{:S(2)}, u32[]{:S(2)}) collective-permute-start(bf16[2,4,64,384]{3,2,1,0:T(8,128)(2,1)S(1)} %total_columns.1.col_ref), channel_id=1, source_target_pairs={{0,16},{16,0},{1,17},{17,1},{2,18},{18,2},{3,19},{19,3},{4,20},{20... | collective-permute-start | bytes 1179656 | tf_op jit(solution)/shard_map/ppermute | solution.py:27
  171.8 8.7 %collective-permute-start.1 = (bf16[2,4,64,384]{3,2,1,0:T(8,128)(2,1)S(1)}, bf16[2,4,64,384]{3,2,1,0:T(8,128)(2,1)S(1)}, u32[]{:S(2)}, u32[]{:S(2)}) collective-permute-start(bf16[2,4,64,384]{3,2,1,0:T(8,128)(2,1)S(1)} %total_rows.1.row_ref), channel_id=1, source_target_pairs={{0,16},{16,0},{1,17},{17,1},{2,18},{18,2},{3,19},{19,3},{4,20},{20... | collective-permute-start | bytes 1179656 | tf_op jit(solution)/shard_map/ppermute | solution.py:27

commit v6 on v5

v6 whole, which is shorter than its diff:
```python
import math

import jax
import jax.numpy as jnp
from jax import lax
from jax.experimental import pallas as pl
from jax.experimental.pallas import tpu as pltpu
from jax.sharding import Mesh, PartitionSpec as P

HEADS = 6
F32 = jnp.float32
BF16 = jnp.bfloat16
VMEM = 16 * 1024 * 1024


def params():
    return pltpu.CompilerParams(vmem_limit_bytes=VMEM)


def exchange(blocks, axis):
    return lax.all_to_all(blocks, axis, 0, 0, tiled=True)


def shift(block, axis, by):
    n = lax.axis_size(axis)
    return lax.ppermute(block, axis, [(i, (i + by) % n) for i in range(n)])


def halves(one, two):
    half = one.shape[1] // 2
    return (
        jnp.concatenate([one[:, :half], two[:, :half]], axis=1),
        jnp.concatenate([one[:, half:], two[:, half:]], axis=1),
    )


def pack_kernel(place_ref, q_hbm, k_hbm, v_hbm, w_hbm, go_hbm, own_ref, send_ref, right_ref, q_ref, k_ref, v_ref, w_ref, go_ref, sems):
    loads = [
        pltpu.make_async_copy(src, dst, sems.at[n])
        for n, (src, dst) in enumerate(
            ((w_hbm, w_ref), (go_hbm, go_ref), (q_hbm, q_ref), (k_hbm, k_ref), (v_hbm, v_ref))
        )
    ]
    for load in loads:
        load.start()
    for load in loads:
        load.wait()
    first = place_ref[0] == 0
    for s in range(q_ref.shape[0]):
        grads = lax.dot_general(
            go_ref[s], w_ref[...], (((1,), (1,)), ((), ())), preferred_element_type=F32
        ).astype(BF16)
        low, high = halves(q_ref[s], grads)
        own_ref[s] = jnp.where(first, low, high)
        send_ref[s] = jnp.where(first, high, low)
        for core, part in enumerate(halves(k_ref[s], v_ref[s])):
            for n in range(right_ref.shape[0]):
                right_ref[n, core, s] = part


def columns(blocks):
    rows = [jnp.concatenate([ref[s] for ref in row for s in range(ref.shape[0])], axis=1) for row in blocks]
    return jnp.concatenate(rows, axis=0)


def lefts(own_ref, other_ref):
    return columns([(own_ref.at[n], other_ref.at[n]) for n in range(4)])


def rights(place_ref, ref):
    core = place_ref[0]
    x = [lax.rem(place_ref[1] + 4 - n, 4) for n in range(4)]
    return columns([(ref.at[x[n], core], ref.at[x[n], 1 - core]) for n in range(4)])


def odd_chunk(shape):
    return (lax.broadcasted_iota(jnp.int32, shape, 1) // 64) % 2 == 1


def product_kernel(place_ref, own_ref, other_ref, right_ref, out_ref):
    left = lefts(own_ref, other_ref)
    right = rights(place_ref, right_ref)
    odd = odd_chunk(left.shape)
    zero = jnp.zeros_like(left)
    for parity, part in enumerate((jnp.where(odd, zero, left), jnp.where(odd, left, zero))):
        full = lax.dot_general(part, right, (((1,), (1,)), ((), ())), preferred_element_type=F32)
        out_ref[:, parity] = full.reshape(out_ref.shape[0], out_ref.shape[2], out_ref.shape[3])


def rows_kernel(part_ref, out_ref):
    total = (part_ref[0] + part_ref[1]) + (part_ref[2] + part_ref[3])
    for n in range(16):
        for j in range(6):
            out_ref[n, j * 4 : j * 4 + 4] = total[j, n * 4 : n * 4 + 4]


def softmax_kernel(scale, part_ref, out_ref):
    tiles = []
    for col in range(4):
        parts = [part_ref[n * 4 + col] for n in range(4)]
        tiles.append((parts[0] + parts[1]) + (parts[2] + parts[3]))
    total = jnp.concatenate(tiles, axis=1)
    logits = total[:12] * scale
    grads = total[12:]
    expo = jnp.exp(logits - jnp.max(logits, axis=-1, keepdims=True))
    weights = expo / jnp.sum(expo, axis=-1, keepdims=True)
    scores = weights * (grads - jnp.sum(weights * grads, axis=-1, keepdims=True))
    full = jnp.concatenate([scores, weights], axis=0)
    for col in range(4):
        at = col * 256
        tile = jnp.concatenate([full[:, at : at + 128], full[:, at + 128 : at + 256]], axis=0).astype(BF16)
        for n in range(col, 16, 4):
            out_ref[n] = tile


def unpack_kernel(mats_ref, out_ref, rows_ref):
    for n in range(16):
        block = mats_ref[n].astype(F32)
        for j in range(6):
            rows_ref[j, n * 4 : n * 4 + 4, 0:128] = block[j * 4 : j * 4 + 4]
            rows_ref[j, n * 4 : n * 4 + 4, 128:256] = block[24 + j * 4 : 28 + j * 4]
    full = rows_ref[...].astype(BF16)
    for n in range(out_ref.shape[0]):
        out_ref[n] = full


def output_kernel(scale, place_ref, mats_ref, own_ref, other_ref, right_ref, row_ref, *col_refs):
    core = place_ref[0]
    seqs, res, lanes = own_ref.shape[1:]
    mats = [mats_ref[:, parity].reshape(256, 256) for parity in range(2)]

    def product(side, contract):
        both = [
            lax.dot_general(m, side, (((contract,), (0,)), ((), ())), preferred_element_type=F32) for m in mats
        ]
        odd = odd_chunk(both[0].shape)
        chunk = 2 * pl.program_id(0) + odd.astype(jnp.int32)
        return (jnp.where(odd, both[1], both[0]) * jnp.where(chunk < 3, scale, 1.0)).astype(BF16)

    def piece(value, n, core_slot, s):
        at = (core_slot * seqs + s) * lanes
        return value[n * res : (n + 1) * res, at : at + lanes]

    row = product(rights(place_ref, right_ref), 1)
    col = product(lefts(own_ref, other_ref), 0)
    for n in range(4):
        for s in range(seqs):
            row_ref[n, core, s] = piece(row, n, 0, s)
            row_ref[n, 1 - core, s] = piece(row, n, 1, s)
            col_refs[n][0, s] = piece(col, n, 0, s)
            col_refs[n][1, s] = piece(col, n, 1, s)


def four(refs, s):
    p = [ref[s].astype(F32) for ref in refs]
    return ((p[0] + p[1]) + (p[2] + p[3])).astype(BF16)


def columns_total_kernel(zero_ref, one_ref, two_ref, three_ref, keep_ref, send_ref):
    refs = (zero_ref, one_ref, two_ref, three_ref)
    for s in range(keep_ref.shape[0]):
        keep_ref[s] = four([ref.at[0] for ref in refs], s)
        send_ref[s] = four([ref.at[1] for ref in refs], s)


def finish_kernel(place_ref, row_ref, col_ref, got_ref, w_ref, mixed_ref, gq_ref, gk_ref, gv_ref):
    first = place_ref[0] == 0
    for s in range(mixed_ref.shape[0]):
        cores = [four([row_ref.at[n, core] for n in range(4)], s) for core in range(2)]
        gq_ref[s], attended = halves(*cores)
        mixed_ref[s] = jnp.dot(attended, w_ref[...], preferred_element_type=F32).astype(BF16)
        low, high = jnp.where(first, col_ref[s], got_ref[s]), jnp.where(first, got_ref[s], col_ref[s])
        gk_ref[s], gv_ref[s] = halves(low, high)


def on_device(queries, keys, values, out_weight, grad_out):
    seqs, res, width = queries.shape
    model_dim = out_weight.shape[1]
    scale = 1.0 / math.sqrt(width // HEADS * seqs * 32)
    place = jnp.stack([lax.axis_index("c"), lax.axis_index("x")]).astype(jnp.int32)
    block = (seqs, res, width)
    smem = pl.BlockSpec(memory_space=pltpu.SMEM)
    vmem = pl.BlockSpec(memory_space=pltpu.VMEM)
    hbm = pl.BlockSpec(memory_space=pltpu.HBM)

    def array(shape, dtype=BF16):
        return jax.ShapeDtypeStruct(shape, dtype)

    args = (queries, keys, values, out_weight, grad_out)
    own, send, right = pl.pallas_call(
        pack_kernel,
        in_specs=[smem] + [hbm] * 5,
        out_specs=[vmem] * 3,
        out_shape=(array(block), array(block), array((4, 2) + block)),
        scratch_shapes=[pltpu.VMEM(a.shape, BF16) for a in (queries, keys, values, out_weight, grad_out)]
        + [pltpu.SemaphoreType.DMA((5,))],
        compiler_params=params(),
        name="pack",
    )(place, *(pltpu.with_memory_space_constraint(arg, pltpu.HBM) for arg in args))
    right = exchange(right.reshape((8,) + block), ("x", "c")).reshape((4, 2) + block)
    other = shift(send, "c", 1)
    own = lax.all_gather(own, "zl")
    other = lax.all_gather(other, "zl")

    left_slab = pl.BlockSpec((4, seqs, res, 128), lambda p: (0, 0, 0, p))
    right_slab = pl.BlockSpec((4, 2, seqs, res, 128), lambda p: (0, 0, 0, 0, p))
    mats_slab = pl.BlockSpec((4, 2, 64, 256), lambda p: (0, p, 0, 0))
    partial = pl.pallas_call(
        product_kernel,
        grid=(3,),
        in_specs=[smem, left_slab, left_slab, right_slab],
        out_specs=mats_slab,
        out_shape=array((4, 6, 64, 256), F32),
        compiler_params=params(),
        name="products",
    )(place, own, other, right)
    partial = exchange(partial, "y")
    partial = pl.pallas_call(
        rows_kernel, out_shape=array((16, 24, 256), F32), compiler_params=params(), name="rows"
    )(partial)
    partial = exchange(partial, ("zh", "zl"))
    mats = pl.pallas_call(
        lambda *refs: softmax_kernel(scale, *refs),
        out_shape=array((16, 48, 128)),
        compiler_params=params(),
        name="softmax",
    )(partial)
    mats = exchange(mats, ("zh", "zl"))
    mats = pl.pallas_call(
        unpack_kernel,
        out_shape=array((4, 6, 64, 256)),
        scratch_shapes=[pltpu.VMEM((6, 64, 256), F32)],
        compiler_params=params(),
        name="unpack",
    )(mats)
    mats = exchange(mats, "y")

    row, *cols = pl.pallas_call(
        lambda *refs: output_kernel(scale, *refs),
        grid=(3,),
        in_specs=[smem, mats_slab, left_slab, left_slab, right_slab],
        out_specs=[right_slab] + [pl.BlockSpec((2, seqs, res, 128), lambda p: (0, 0, 0, p))] * 4,
        out_shape=(pltpu.HBM((4, 2) + block, BF16),) + (pltpu.HBM((2,) + block, BF16),) * 4,
        compiler_params=params(),
        name="outputs",
    )(place, mats, own, other, right)
    row = exchange(row.reshape((8,) + block), ("zl", "c")).reshape((4, 2) + block)
    cols = [cols[0]] + [shift(cols[by], "x", -by) for by in (1, 2, 3)]
    keep, send = pl.pallas_call(
        columns_total_kernel, out_shape=(array(block), array(block)), compiler_params=params(), name="columns_total"
    )(*cols)
    return pl.pallas_call(
        finish_kernel,
        in_specs=[smem] + [vmem] * 4,
        out_shape=(array((seqs, res, model_dim)), array(block), array(block), array(block)),
        compiler_params=params(),
        name="finish",
    )(place, row, keep, shift(send, "c", 1), out_weight)


def solution(mesh):
    grid = Mesh(mesh.devices.reshape(4, 4, 2, 4, 4), ("zh", "y", "c", "x", "zl"))
    placed = P(("zh", "y", "c"), ("x", "zl"), None)
    return jax.shard_map(
        on_device,
        mesh=grid,
        in_specs=(placed, placed, placed, P(), placed),
        out_specs=(placed, placed, placed, placed),
        check_vma=False,
    )
```

time: 183 us -> 188 us (1.027)
  the two profiles are of different devices: /device:TPU:1 before, /device:TPU:2 now
where the time goes in v6:
time: 188 us
  blocking collectives  121 us (64%)
  starting transfers between devices  27.7 us (15%)
  waiting for transfers between devices  25 us (13%)
  Pallas kernels  13.2 us (7%)
    all_to_all x4, blocking collectives, exchange(): return lax.all_to_all(blocks, axis, 0, 0, tiled=True)  85.2 us
    all_gather x1, blocking collectives, on_device(): other = lax.all_gather(other, 'zl')  18.1 us
    all_gather x1, blocking collectives, on_device(): own = lax.all_gather(own, 'zl')  17.8 us
    ppermute x5, waiting for transfers between devices, shift(): return lax.ppermute(block, axis, [(i, (i + by) % n) for i in range(n)])  16.4 us
    ppermute x5, starting transfers between devices, shift(): return lax.ppermute(block, axis, [(i, (i + by) % n) for i in range(n)])  14.6 us
    all_to_all x2, starting transfers between devices, exchange(): return lax.all_to_all(blocks, axis, 0, 0, tiled=True)  13.1 us
    all_to_all x2, waiting for transfers between devices, exchange(): return lax.all_to_all(blocks, axis, 0, 0, tiled=True)  8.59 us
    pallas_call x1, Pallas kernels, on_device(): pl.pallas_call(pack_kernel, in_specs=[smem] + [hbm] * 5, out_specs=[vmem]...  4 us
  transfers between devices with their start and end apart: 7, of which 5 were waited for; matrix products, arithmetic and copies ran while one was open for 0% of the time, Pallas kernels for 0%

profile of v6, /device:TPU:2, one launch (start us, length us, event | category | flops | bytes accessed | tf_op | source)
XLA Modules:
  0.0 187.8 jit_solution(16964101518487205339)
XLA Ops:
  0.6 0.1 pad_add_fusion.place_ref.refs_0_
  0.7 4.0 %pack.1 = (bf16[4,64,384]{2,1,0:T(8,128)(2,1)S(1)}, bf16[4,64,384]{2,1,0:T(8,128)(2,1)S(1)}, bf16[4,2,4,64,384]{4,3,2,1,0:T(8,128)(2,1)}) custom-call(s32[2]{0:T(128)S(1)} %pad_add_fusion.place_ref.refs_0_, bf16[4,64,384]{2,1,0:T(8,128)(2,1)} %q_hbm.1, bf16[4,64,384]{2,1,0:T(8,128)(2,1)} %k_hbm.1, bf16[4,64,384]{2,1,0:T(8,128)(2,1)} %v_hbm.1, ...), custom_call_target="tpu_custom_call" | custom-call | tf_op jit(solution)/shard_map/pack/pallas_call | solution.py:190
  4.7 9.4 %all-to-all-start = ((bf16[8,4,64,384]{3,2,1,0:T(8,128)(2,1)}), bf16[8,4,64,384]{3,2,1,0:T(8,128)(2,1)S(1)}, u32[]{:S(2)}, u32[]{:S(2)}) async-start(bf16[8,4,64,384]{3,2,1,0:T(8,128)(2,1)} %bitcast.4), calls=%async_computation | async-start | bytes 3145728 | tf_op jit(solution)/shard_map/all_to_all | solution.py:21
  14.1 2.0 %collective-permute-start = (bf16[4,64,384]{2,1,0:T(8,128)(2,1)S(1)}, bf16[4,64,384]{2,1,0:T(8,128)(2,1)S(1)}, u32[]{:S(2)}, u32[]{:S(2)}) collective-permute-start(bf16[4,64,384]{2,1,0:T(8,128)(2,1)S(1)} %get-tuple-element.15), channel_id=1, source_target_pairs={{0,16},{16,0},{1,17},{17,1},{2,18},{18,2},{3,19},{19,3},{4,20},{20... | collective-permute-start | bytes 589832 | tf_op jit(solution)/shard_map/ppermute | solution.py:26
  16.2 17.8 %all-gather = bf16[16,64,384]{2,1,0:T(8,128)(2,1)S(1)} all-gather(bf16[4,64,384]{2,1,0:T(8,128)(2,1)S(1)} %get-tuple-element.14), channel_id=2, replica_groups=mesh['zh'=4,'y'=4,'c'=2,'x'=4,'zl'=4] {'zl'}, dimensions={0}, use_global_device_ids=true | all-gather | bytes 983040 | tf_op jit(solution)/shard_map/all_gather | solution.py:202
  34.0 0.0 collective-permute-done
  34.0 18.1 %all-gather.1 = bf16[16,64,384]{2,1,0:T(8,128)(2,1)S(1)} all-gather(bf16[4,64,384]{2,1,0:T(8,128)(2,1)S(1)} %collective-permute-done), channel_id=3, replica_groups=mesh['zh'=4,'y'=4,'c'=2,'x'=4,'zl'=4] {'zl'}, dimensions={0}, use_global_device_ids=true | all-gather | bytes 983040 | tf_op jit(solution)/shard_map/all_gather | solution.py:203
  52.0 0.0 all-to-all-done
  52.0 2.5 %products.1 = f32[4,6,64,256]{3,2,1,0:T(8,128)S(1)} custom-call(s32[2]{0:T(128)S(1)} %pad_add_fusion.place_ref.refs_0_, bf16[4,4,64,384]{3,2,1,0:T(8,128)(2,1)S(1)} %bitcast.10, bf16[4,4,64,384]{3,2,1,0:T(8,128)(2,1)S(1)} %bitcast.12, bf16[4,2,4,64,384]{4,3,2,1,0:T(8,128)(2,1)S(1)} %bitcast.8), custom_call_target="tpu_custom_call" | custom-call | tf_op jit(solution)/shard_map/products/pallas_call | solution.py:208
  54.5 20.0 %all_to_all.30.part_ref = f32[4,6,64,256]{3,2,1,0:T(8,128)S(1)} all-to-all(f32[4,6,64,256]{3,2,1,0:T(8,128)S(1)} %products.1), channel_id=1, replica_groups=mesh['zh'=4,'y'=4,'c'=2,'x'=4,'zl'=4] {'y'}, dimensions={0} | all-to-all | bytes 3145728 | tf_op jit(solution)/shard_map/all_to_all | solution.py:21
  74.5 0.1 rows.1
  74.6 31.6 %all_to_all.31.refs_0_ = f32[16,24,256]{2,1,0:T(8,128)S(1)} all-to-all(f32[16,24,256]{2,1,0:T(8,128)S(1)} %rows.1), channel_id=1, replica_groups=mesh['zh'=4,'y'=4,'c'=2,'x'=4,'zl'=4] {'zh','zl'}, dimensions={0} | all-to-all | bytes 786432 | tf_op jit(solution)/shard_map/all_to_all | solution.py:21
  106.2 0.3 softmax.1
  106.5 21.7 %all_to_all.32.mats_ref = bf16[16,48,128]{2,1,0:T(8,128)(2,1)S(1)} all-to-all(bf16[16,48,128]{2,1,0:T(8,128)(2,1)S(1)} %softmax.1), channel_id=1, replica_groups=mesh['zh'=4,'y'=4,'c'=2,'x'=4,'zl'=4] {'zh','zl'}, dimensions={0} | all-to-all | bytes 393216 | tf_op jit(solution)/shard_map/all_to_all | solution.py:21
  128.2 0.1 unpack.1
  128.4 11.9 %all_to_all.33.refs_1_ = bf16[4,6,64,256]{3,2,1,0:T(8,128)(2,1)S(1)} all-to-all(bf16[4,6,64,256]{3,2,1,0:T(8,128)(2,1)S(1)} %unpack.1), channel_id=1, replica_groups=mesh['zh'=4,'y'=4,'c'=2,'x'=4,'zl'=4] {'y'}, dimensions={0} | all-to-all | bytes 1572864 | tf_op jit(solution)/shard_map/all_to_all | solution.py:21
  140.3 4.0 %outputs.1 = (bf16[4,2,4,64,384]{4,3,2,1,0:T(8,128)(2,1)}, bf16[2,4,64,384]{3,2,1,0:T(8,128)(2,1)}, bf16[2,4,64,384]{3,2,1,0:T(8,128)(2,1)}, bf16[2,4,64,384]{3,2,1,0:T(8,128)(2,1)}, bf16[2,4,64,384]{3,2,1,0:T(8,128)(2,1)}) custom-call(s32[2]{0:T(128)S(1)} %pad_add_fusion.place_ref.refs_0_, bf16[4,6,64,256]{3,2,1,0:T(8,128)(2,1)S(1)} %all_to_all.33.refs_1_, ...), custom_call_target="tpu_custom_call" | custom-call | tf_op jit(solution)/shard_map/outputs/pallas_call | solution.py:238
  144.2 0.0 copy-start.3
  144.2 0.0 copy-start.2
  144.3 0.0 copy-start.1
  144.3 3.7 %all-to-all-start.5 = ((bf16[8,4,64,384]{3,2,1,0:T(8,128)(2,1)}), bf16[8,4,64,384]{3,2,1,0:T(8,128)(2,1)S(1)}, u32[]{:S(2)}, u32[]{:S(2)}) async-start(bf16[8,4,64,384]{3,2,1,0:T(8,128)(2,1)} %bitcast.15), calls=%async_computation.5 | async-start | bytes 3145728 | tf_op jit(solution)/shard_map/all_to_all | solution.py:21
  148.0 0.0 copy-start
  148.0 2.1 %collective-permute-start.1 = (bf16[2,4,64,384]{3,2,1,0:T(8,128)(2,1)}, bf16[2,4,64,384]{3,2,1,0:T(8,128)(2,1)S(1)}, u32[]{:S(2)}, u32[]{:S(2)}) collective-permute-start(bf16[2,4,64,384]{3,2,1,0:T(8,128)(2,1)} %get-tuple-element.19), channel_id=1, source_target_pairs={{0,12},{4,0},{8,4},{12,8},{1,13},{5,1},{9,5},{13,9},{2,14},{6,2},{... | collective-permute-start | bytes 1179656 | tf_op jit(solution)/shard_map/ppermute | solution.py:26
  150.1 0.0 copy-done.3
  150.1 4.8 %collective-permute-start.2 = (bf16[2,4,64,384]{3,2,1,0:T(8,128)(2,1)S(1)}, bf16[2,4,64,384]{3,2,1,0:T(8,128)(2,1)S(1)}, u32[]{:S(2)}, u32[]{:S(2)}) collective-permute-start(bf16[2,4,64,384]{3,2,1,0:T(8,128)(2,1)S(1)} %copy-done.3), channel_id=1, source_target_pairs={{0,8},{4,12},{8,0},{12,4},{1,9},{5,13},{9,1},{13,5},{2,10},{6,14},... | collective-permute-start | bytes 1179656 | tf_op jit(solution)/shard_map/ppermute | solution.py:26
  154.9 0.0 copy-done.2
  154.9 3.7 %collective-permute-start.3 = (bf16[2,4,64,384]{3,2,1,0:T(8,128)(2,1)S(1)}, bf16[2,4,64,384]{3,2,1,0:T(8,128)(2,1)S(1)}, u32[]{:S(2)}, u32[]{:S(2)}) collective-permute-start(bf16[2,4,64,384]{3,2,1,0:T(8,128)(2,1)S(1)} %copy-done.2), channel_id=1, source_target_pairs={{0,4},{4,8},{8,12},{12,0},{1,5},{5,9},{9,13},{13,1},{2,6},{6,10},{... | collective-permute-start | bytes 1179656 | tf_op jit(solution)/shard_map/ppermute | solution.py:26
  158.6 3.0 %collective-permute-done.1.one_ref = bf16[2,4,64,384]{3,2,1,0:T(8,128)(2,1)S(1)} collective-permute-done((bf16[2,4,64,384]{3,2,1,0:T(8,128)(2,1)}, bf16[2,4,64,384]{3,2,1,0:T(8,128)(2,1)S(1)}, u32[]{:S(2)}, u32[]{:S(2)}) %collective-permute-start.1) | collective-permute-done | bytes 393248 | tf_op jit(solution)/shard_map/ppermute | solution.py:26
  161.6 9.3 %collective-permute-done.2.two_ref = bf16[2,4,64,384]{3,2,1,0:T(8,128)(2,1)S(1)} collective-permute-done((bf16[2,4,64,384]{3,2,1,0:T(8,128)(2,1)S(1)}, bf16[2,4,64,384]{3,2,1,0:T(8,128)(2,1)S(1)}, u32[]{:S(2)}, u32[]{:S(2)}) %collective-permute-start.2) | collective-permute-done | bytes 393248 | tf_op jit(solution)/shard_map/ppermute | solution.py:26
  171.0 2.6 %collective-permute-done.3.three_ref = bf16[2,4,64,384]{3,2,1,0:T(8,128)(2,1)S(1)} collective-permute-done((bf16[2,4,64,384]{3,2,1,0:T(8,128)(2,1)S(1)}, bf16[2,4,64,384]{3,2,1,0:T(8,128)(2,1)S(1)}, u32[]{:S(2)}, u32[]{:S(2)}) %collective-permute-start.3) | collective-permute-done | bytes 393248 | tf_op jit(solution)/shard_map/ppermute | solution.py:26
  173.6 0.0 copy-done.1
  173.6 0.2 columns_total.1
  173.8 1.9 %collective-permute-start.4 = (bf16[4,64,384]{2,1,0:T(8,128)(2,1)S(1)}, bf16[4,64,384]{2,1,0:T(8,128)(2,1)S(1)}, u32[]{:S(2)}, u32[]{:S(2)}) collective-permute-start(bf16[4,64,384]{2,1,0:T(8,128)(2,1)S(1)} %get-tuple-element.23), channel_id=1, source_target_pairs={{0,16},{16,0},{1,17},{17,1},{2,18},{18,2},{3,19},{19,3},{4,20},{20... | collective-permute-start | bytes 589832 | tf_op jit(solution)/shard_map/ppermute | solution.py:26
  175.7 1.4 collective-permute-done.4.got_ref
  177.2 8.6 %all-to-all-done.5 = bf16[8,4,64,384]{3,2,1,0:T(8,128)(2,1)S(1)} async-done(((bf16[8,4,64,384]{3,2,1,0:T(8,128)(2,1)}), bf16[8,4,64,384]{3,2,1,0:T(8,128)(2,1)S(1)}, u32[]{:S(2)}, u32[]{:S(2)}) %all-to-all-start.5) | async-done | bytes 1572896 | tf_op jit(solution)/shard_map/all_to_all | solution.py:21
  185.7 0.0 copy-done
  185.7 2.0 %finish.1 = (bf16[4,64,768]{2,1,0:T(8,128)(2,1)}, bf16[4,64,384]{2,1,0:T(8,128)(2,1)}, bf16[4,64,384]{2,1,0:T(8,128)(2,1)}, bf16[4,64,384]{2,1,0:T(8,128)(2,1)}) custom-call(s32[2]{0:T(128)S(1)} %pad_add_fusion.place_ref.refs_0_, bf16[4,2,4,64,384]{4,3,2,1,0:T(8,128)(2,1)S(1)} %bitcast.14, bf16[4,64,384]{2,1,0:T(8,128)(2,1)S(1)} %get-tuple-element.22.col_ref, ...), custom_call_target="tpu_custom_call" | custom-call | tf_op jit(solution)/shard_map/finish/pallas_call | solution.py:252
Async XLA Ops:
  4.7 47.3 %all-to-all-start = ((bf16[8,4,64,384]{3,2,1,0:T(8,128)(2,1)}), bf16[8,4,64,384]{3,2,1,0:T(8,128)(2,1)S(1)}, u32[]{:S(2)}, u32[]{:S(2)}) async-start(bf16[8,4,64,384]{3,2,1,0:T(8,128)(2,1)} %bitcast.4), calls=%async_computation | async-start | bytes 3145728 | tf_op jit(solution)/shard_map/all_to_all | solution.py:21
  14.1 19.8 %collective-permute-start = (bf16[4,64,384]{2,1,0:T(8,128)(2,1)S(1)}, bf16[4,64,384]{2,1,0:T(8,128)(2,1)S(1)}, u32[]{:S(2)}, u32[]{:S(2)}) collective-permute-start(bf16[4,64,384]{2,1,0:T(8,128)(2,1)S(1)} %get-tuple-element.15), channel_id=1, source_target_pairs={{0,16},{16,0},{1,17},{17,1},{2,18},{18,2},{3,19},{19,3},{4,20},{20... | collective-permute-start | bytes 589832 | tf_op jit(solution)/shard_map/ppermute | solution.py:26
  144.2 5.8 %copy-start.3 = (bf16[2,4,64,384]{3,2,1,0:T(8,128)(2,1)S(1)}, bf16[2,4,64,384]{3,2,1,0:T(8,128)(2,1)}, u32[]{:S(2)}) copy-start(bf16[2,4,64,384]{3,2,1,0:T(8,128)(2,1)} %get-tuple-element.20) | copy-start | bytes 1179652
  144.2 10.7 %copy-start.2 = (bf16[2,4,64,384]{3,2,1,0:T(8,128)(2,1)S(1)}, bf16[2,4,64,384]{3,2,1,0:T(8,128)(2,1)}, u32[]{:S(2)}) copy-start(bf16[2,4,64,384]{3,2,1,0:T(8,128)(2,1)} %get-tuple-element.21) | copy-start | bytes 1179652
  144.3 29.4 %copy-start.1 = (bf16[2,4,64,384]{3,2,1,0:T(8,128)(2,1)S(1)}, bf16[2,4,64,384]{3,2,1,0:T(8,128)(2,1)}, u32[]{:S(2)}) copy-start(bf16[2,4,64,384]{3,2,1,0:T(8,128)(2,1)} %get-tuple-element.18.zero_ref) | copy-start | bytes 1179652
  144.3 41.5 %all-to-all-start.5 = ((bf16[8,4,64,384]{3,2,1,0:T(8,128)(2,1)}), bf16[8,4,64,384]{3,2,1,0:T(8,128)(2,1)S(1)}, u32[]{:S(2)}, u32[]{:S(2)}) async-start(bf16[8,4,64,384]{3,2,1,0:T(8,128)(2,1)} %bitcast.15), calls=%async_computation.5 | async-start | bytes 3145728 | tf_op jit(solution)/shard_map/all_to_all | solution.py:21
  148.0 37.8 %copy-start = (bf16[384,768]{1,0:T(8,128)(2,1)S(1)}, bf16[384,768]{1,0:T(8,128)(2,1)}, u32[]{:S(2)}) copy-start(bf16[384,768]{1,0:T(8,128)(2,1)} %w_ref.1) | copy-start | bytes 1769476
  148.0 13.6 %collective-permute-start.1 = (bf16[2,4,64,384]{3,2,1,0:T(8,128)(2,1)}, bf16[2,4,64,384]{3,2,1,0:T(8,128)(2,1)S(1)}, u32[]{:S(2)}, u32[]{:S(2)}) collective-permute-start(bf16[2,4,64,384]{3,2,1,0:T(8,128)(2,1)} %get-tuple-element.19), channel_id=1, source_target_pairs={{0,12},{4,0},{8,4},{12,8},{1,13},{5,1},{9,5},{13,9},{2,14},{6,2},{... | collective-permute-start | bytes 1179656 | tf_op jit(solution)/shard_map/ppermute | solution.py:26
  150.1 20.9 %collective-permute-start.2 = (bf16[2,4,64,384]{3,2,1,0:T(8,128)(2,1)S(1)}, bf16[2,4,64,384]{3,2,1,0:T(8,128)(2,1)S(1)}, u32[]{:S(2)}, u32[]{:S(2)}) collective-permute-start(bf16[2,4,64,384]{3,2,1,0:T(8,128)(2,1)S(1)} %copy-done.3), channel_id=1, source_target_pairs={{0,8},{4,12},{8,0},{12,4},{1,9},{5,13},{9,1},{13,5},{2,10},{6,14},... | collective-permute-start | bytes 1179656 | tf_op jit(solution)/shard_map/ppermute | solution.py:26
  154.9 18.7 %collective-permute-start.3 = (bf16[2,4,64,384]{3,2,1,0:T(8,128)(2,1)S(1)}, bf16[2,4,64,384]{3,2,1,0:T(8,128)(2,1)S(1)}, u32[]{:S(2)}, u32[]{:S(2)}) collective-permute-start(bf16[2,4,64,384]{3,2,1,0:T(8,128)(2,1)S(1)} %copy-done.2), channel_id=1, source_target_pairs={{0,4},{4,8},{8,12},{12,0},{1,5},{5,9},{9,13},{13,1},{2,6},{6,10},{... | collective-permute-start | bytes 1179656 | tf_op jit(solution)/shard_map/ppermute | solution.py:26
  173.8 3.3 %collective-permute-start.4 = (bf16[4,64,384]{2,1,0:T(8,128)(2,1)S(1)}, bf16[4,64,384]{2,1,0:T(8,128)(2,1)S(1)}, u32[]{:S(2)}, u32[]{:S(2)}) collective-permute-start(bf16[4,64,384]{2,1,0:T(8,128)(2,1)S(1)} %get-tuple-element.23), channel_id=1, source_target_pairs={{0,16},{16,0},{1,17},{17,1},{2,18},{18,2},{3,19},{19,3},{4,20},{20... | collective-permute-start | bytes 589832 | tf_op jit(solution)/shard_map/ppermute | solution.py:26

commit v7 on v6

--- a/solution.py
+++ b/solution.py
@@ -38,39 +38,49 @@
     loads = [
         pltpu.make_async_copy(src, dst, sems.at[n])
         for n, (src, dst) in enumerate(
-            ((w_hbm, w_ref), (go_hbm, go_ref), (q_hbm, q_ref), (k_hbm, k_ref), (v_hbm, v_ref))
+            ((k_hbm, k_ref), (v_hbm, v_ref), (w_hbm, w_ref), (go_hbm, go_ref), (q_hbm, q_ref))
         )
     ]
     for load in loads:
         load.start()
-    for load in loads:
-        load.wait()
     first = place_ref[0] == 0
-    for s in range(q_ref.shape[0]):
-        grads = lax.dot_general(
-            go_ref[s], w_ref[...], (((1,), (1,)), ((), ())), preferred_element_type=F32
-        ).astype(BF16)
-        low, high = halves(q_ref[s], grads)
-        own_ref[s] = jnp.where(first, low, high)
-        send_ref[s] = jnp.where(first, high, low)
+    loads[0].wait()
+    loads[1].wait()
+    seqs, res, _ = q_ref.shape
+    for s in range(seqs):
         for core, part in enumerate(halves(k_ref[s], v_ref[s])):
             for n in range(right_ref.shape[0]):
                 right_ref[n, core, s] = part
-
-
-def columns(blocks):
-    rows = [jnp.concatenate([ref[s] for ref in row for s in range(ref.shape[0])], axis=1) for row in blocks]
+    for load in loads[2:]:
+        load.wait()
+    grads = lax.dot_general(
+        go_ref[...].reshape(seqs * res, go_ref.shape[2]),
+        w_ref[...],
+        (((1,), (1,)), ((), ())),
+        preferred_element_type=F32,
+    ).astype(BF16)
+    for s in range(seqs):
+        low, high = halves(q_ref[s], grads[s * res : (s + 1) * res])
+        own_ref[s] = jnp.where(first, low, high)
+        send_ref[s] = jnp.where(first, high, low)
+
+
+def slab(blocks, p):
+    at = slice(p * 128, p * 128 + 128)
+    rows = [
+        jnp.concatenate([ref[s, :, at] for ref in row for s in range(ref.shape[0])], axis=1) for row in blocks
+    ]
     return jnp.concatenate(rows, axis=0)
 
 
 def lefts(own_ref, other_ref):
-    return columns([(own_ref.at[n], other_ref.at[n]) for n in range(4)])
+    return [(own_ref.at[n], other_ref.at[n]) for n in range(4)]
 
 
 def rights(place_ref, ref):
     core = place_ref[0]
     x = [lax.rem(place_ref[1] + 4 - n, 4) for n in range(4)]
-    return columns([(ref.at[x[n], core], ref.at[x[n], 1 - core]) for n in range(4)])
+    return [(ref.at[x[n], core], ref.at[x[n], 1 - core]) for n in range(4)]
 
 
 def odd_chunk(shape):
@@ -78,13 +88,14 @@
 
 
 def product_kernel(place_ref, own_ref, other_ref, right_ref, out_ref):
-    left = lefts(own_ref, other_ref)
-    right = rights(place_ref, right_ref)
-    odd = odd_chunk(left.shape)
-    zero = jnp.zeros_like(left)
-    for parity, part in enumerate((jnp.where(odd, zero, left), jnp.where(odd, left, zero))):
-        full = lax.dot_general(part, right, (((1,), (1,)), ((), ())), preferred_element_type=F32)
-        out_ref[:, parity] = full.reshape(out_ref.shape[0], out_ref.shape[2], out_ref.shape[3])
+    for p in range(3):
+        left = slab(lefts(own_ref, other_ref), p)
+        right = slab(rights(place_ref, right_ref), p)
+        odd = odd_chunk(left.shape)
+        zero = jnp.zeros_like(left)
+        for parity, part in enumerate((jnp.where(odd, zero, left), jnp.where(odd, left, zero))):
+            full = lax.dot_general(part, right, (((1,), (1,)), ((), ())), preferred_element_type=F32)
+            out_ref[:, 2 * p + parity] = full.reshape(out_ref.shape[0], out_ref.shape[2], out_ref.shape[3])
 
 
 def rows_kernel(part_ref, out_ref):
@@ -124,31 +135,40 @@
         out_ref[n] = full
 
 
-def output_kernel(scale, place_ref, mats_ref, own_ref, other_ref, right_ref, row_ref, *col_refs):
-    core = place_ref[0]
-    seqs, res, lanes = own_ref.shape[1:]
-    mats = [mats_ref[:, parity].reshape(256, 256) for parity in range(2)]
-
-    def product(side, contract):
-        both = [
+def output_kernel(scale, place_ref, mats_ref, own_ref, other_ref, right_ref, row_hbm, *refs):
+    col_hbms, row_ref, col_ref, sems = refs[:4], refs[4], refs[5], refs[6]
+    seqs, res = own_ref.shape[1:3]
+
+    def put(ref, value, p):
+        for n in range(4):
+            for slot in range(2):
+                for s in range(seqs):
+                    at = (slot * seqs + s) * 128
+                    ref[n, slot, s, :, p * 128 : p * 128 + 128] = value[n * res : (n + 1) * res, at : at + 128]
+
+    def product(side, contract, p):
+        mats = [mats_ref[:, 2 * p + parity].reshape(256, 256) for parity in range(2)]
+        even, odd = (
             lax.dot_general(m, side, (((contract,), (0,)), ((), ())), preferred_element_type=F32) for m in mats
-        ]
-        odd = odd_chunk(both[0].shape)
-        chunk = 2 * pl.program_id(0) + odd.astype(jnp.int32)
-        return (jnp.where(odd, both[1], both[0]) * jnp.where(chunk < 3, scale, 1.0)).astype(BF16)
-
-    def piece(value, n, core_slot, s):
-        at = (core_slot * seqs + s) * lanes
-        return value[n * res : (n + 1) * res, at : at + lanes]
-
-    row = product(rights(place_ref, right_ref), 1)
-    col = product(lefts(own_ref, other_ref), 0)
-    for n in range(4):
-        for s in range(seqs):
-            row_ref[n, core, s] = piece(row, n, 0, s)
-            row_ref[n, 1 - core, s] = piece(row, n, 1, s)
-            col_refs[n][0, s] = piece(col, n, 0, s)
-            col_refs[n][1, s] = piece(col, n, 1, s)
+        )
+        if 2 * p < 3:
+            even = even * scale
+        if 2 * p + 1 < 3:
+            odd = odd * scale
+        return jnp.where(odd_chunk(even.shape), odd, even).astype(BF16)
+
+    for p in range(3):
+        put(row_ref, product(slab(rights(place_ref, right_ref), p), 1, p), p)
+    row_copy = pltpu.make_async_copy(row_ref, row_hbm, sems.at[4])
+    row_copy.start()
+    for p in range(3):
+        put(col_ref, product(slab(lefts(own_ref, other_ref), p), 0, p), p)
+    col_copies = [pltpu.make_async_copy(col_ref.at[n], col_hbms[n], sems.at[n]) for n in range(4)]
+    for copy in col_copies:
+        copy.start()
+    row_copy.wait()
+    for copy in col_copies:
+        copy.wait()
 
 
 def four(refs, s):
@@ -156,21 +176,32 @@
     return ((p[0] + p[1]) + (p[2] + p[3])).astype(BF16)
 
 
-def columns_total_kernel(zero_ref, one_ref, two_ref, three_ref, keep_ref, send_ref):
+def total_kernel(zero_ref, one_ref, two_ref, three_ref, keep_ref, send_ref):
     refs = (zero_ref, one_ref, two_ref, three_ref)
     for s in range(keep_ref.shape[0]):
         keep_ref[s] = four([ref.at[0] for ref in refs], s)
         send_ref[s] = four([ref.at[1] for ref in refs], s)
 
 
-def finish_kernel(place_ref, row_ref, col_ref, got_ref, w_ref, mixed_ref, gq_ref, gk_ref, gv_ref):
+def total_blocks_kernel(part_ref, keep_ref, send_ref):
+    total_kernel(*[part_ref.at[n] for n in range(4)], keep_ref, send_ref)
+
+
+def unpacked(first, keep, got):
+    return halves(jnp.where(first, keep, got), jnp.where(first, got, keep))
+
+
+def finish_columns_kernel(place_ref, keep_ref, got_ref, gk_ref, gv_ref):
     first = place_ref[0] == 0
-    for s in range(mixed_ref.shape[0]):
-        cores = [four([row_ref.at[n, core] for n in range(4)], s) for core in range(2)]
-        gq_ref[s], attended = halves(*cores)
+    for s in range(keep_ref.shape[0]):
+        gk_ref[s], gv_ref[s] = unpacked(first, keep_ref[s], got_ref[s])
+
+
+def finish_rows_kernel(place_ref, keep_ref, got_ref, w_ref, mixed_ref, gq_ref):
+    first = place_ref[0] == 0
+    for s in range(keep_ref.shape[0]):
+        gq_ref[s], attended = unpacked(first, keep_ref[s], got_ref[s])
         mixed_ref[s] = jnp.dot(attended, w_ref[...], preferred_element_type=F32).astype(BF16)
-        low, high = jnp.where(first, col_ref[s], got_ref[s]), jnp.where(first, got_ref[s], col_ref[s])
-        gk_ref[s], gv_ref[s] = halves(low, high)
 
 
 def on_device(queries, keys, values, out_weight, grad_out):
@@ -202,14 +233,9 @@
     own = lax.all_gather(own, "zl")
     other = lax.all_gather(other, "zl")
 
-    left_slab = pl.BlockSpec((4, seqs, res, 128), lambda p: (0, 0, 0, p))
-    right_slab = pl.BlockSpec((4, 2, seqs, res, 128), lambda p: (0, 0, 0, 0, p))
-    mats_slab = pl.BlockSpec((4, 2, 64, 256), lambda p: (0, p, 0, 0))
     partial = pl.pallas_call(
         product_kernel,
-        grid=(3,),
-        in_specs=[smem, left_slab, left_slab, right_slab],
-        out_specs=mats_slab,
+        in_specs=[smem] + [vmem] * 3,
         out_shape=array((4, 6, 64, 256), F32),
         compiler_params=params(),
         name="products",
@@ -237,25 +263,36 @@
 
     row, *cols = pl.pallas_call(
         lambda *refs: output_kernel(scale, *refs),
-        grid=(3,),
-        in_specs=[smem, mats_slab, left_slab, left_slab, right_slab],
-        out_specs=[right_slab] + [pl.BlockSpec((2, seqs, res, 128), lambda p: (0, 0, 0, p))] * 4,
+        in_specs=[smem] + [vmem] * 4,
+        out_specs=[hbm] * 5,
         out_shape=(pltpu.HBM((4, 2) + block, BF16),) + (pltpu.HBM((2,) + block, BF16),) * 4,
+        scratch_shapes=[pltpu.VMEM((4, 2) + block, BF16)] * 2 + [pltpu.SemaphoreType.DMA((5,))],
         compiler_params=params(),
         name="outputs",
     )(place, mats, own, other, right)
-    row = exchange(row.reshape((8,) + block), ("zl", "c")).reshape((4, 2) + block)
+    row = exchange(row, "zl")
     cols = [cols[0]] + [shift(cols[by], "x", -by) for by in (1, 2, 3)]
     keep, send = pl.pallas_call(
-        columns_total_kernel, out_shape=(array(block), array(block)), compiler_params=params(), name="columns_total"
+        total_kernel, out_shape=(array(block), array(block)), compiler_params=params(), name="total_columns"
     )(*cols)
-    return pl.pallas_call(
-        finish_kernel,
-        in_specs=[smem] + [vmem] * 4,
-        out_shape=(array((seqs, res, model_dim)), array(block), array(block), array(block)),
-        compiler_params=params(),
-        name="finish",
-    )(place, row, keep, shift(send, "c", 1), out_weight)
+    grad_key, grad_value = pl.pallas_call(
+        finish_columns_kernel,
+        in_specs=[smem, vmem, vmem],
+        out_shape=(array(block), array(block)),
+        compiler_params=params(),
+        name="finish_columns",
+    )(place, keep, shift(send, "c", 1))
+    keep, send = pl.pallas_call(
+        total_blocks_kernel, out_shape=(array(block), array(block)), compiler_params=params(), name="total_rows"
+    )(row)
+    mixed, grad_query = pl.pallas_call(
+        finish_rows_kernel,
+        in_specs=[smem] + [vmem] * 3,
+        out_shape=(array((seqs, res, model_dim)), array(block)),
+        compiler_params=params(),
+        name="finish_rows",
+    )(place, keep, shift(send, "c", 1), out_weight)
+    return mixed, grad_query, grad_key, grad_value
 
 
 def solution(mesh):

time: 188 us -> 184 us (0.979)
  the two profiles are of different devices: /device:TPU:2 before, /device:TPU:3 now
where the time goes in v7:
time: 184 us
  blocking collectives  114 us (62%)
  starting transfers between devices  41.4 us (22%)
  waiting for transfers between devices  14.8 us (8%)
  Pallas kernels  13.1 us (7%)
    all_to_all x4, blocking collectives, exchange(): return lax.all_to_all(blocks, axis, 0, 0, tiled=True)  81.7 us
    ppermute x6, starting transfers between devices, shift(): return lax.ppermute(block, axis, [(i, (i + by) % n) for i in range(n)])  27 us
    all_gather x1, blocking collectives, on_device(): own = lax.all_gather(own, 'zl')  16.7 us
    all_gather x1, blocking collectives, on_device(): other = lax.all_gather(other, 'zl')  15.1 us
    all_to_all x2, starting transfers between devices, exchange(): return lax.all_to_all(blocks, axis, 0, 0, tiled=True)  14.4 us
    ppermute x6, waiting for transfers between devices, shift(): return lax.ppermute(block, axis, [(i, (i + by) % n) for i in range(n)])  8.02 us
    all_to_all x2, waiting for transfers between devices, exchange(): return lax.all_to_all(blocks, axis, 0, 0, tiled=True)  6.82 us
    pallas_call x1, Pallas kernels, on_device(): pl.pallas_call(lambda *refs: output_kernel(scale, *refs), in_specs=[smem]...  4.18 us
  transfers between devices with their start and end apart: 8, of which 3 were waited for; matrix products, arithmetic and copies ran while one was open for 0% of the time, Pallas kernels for 1%

profile of v7, /device:TPU:3, one launch (start us, length us, event | category | flops | bytes accessed | tf_op | source)
XLA Modules:
  0.0 183.8 jit_solution(2860059645678327073)
XLA Ops:
  0.6 0.1 pad_add_fusion.place_ref.refs_0_
  0.7 3.2 %pack.1 = (bf16[4,64,384]{2,1,0:T(8,128)(2,1)S(1)}, bf16[4,64,384]{2,1,0:T(8,128)(2,1)S(1)}, bf16[4,2,4,64,384]{4,3,2,1,0:T(8,128)(2,1)}) custom-call(s32[2]{0:T(128)S(1)} %pad_add_fusion.place_ref.refs_0_, bf16[4,64,384]{2,1,0:T(8,128)(2,1)} %q_hbm.1, bf16[4,64,384]{2,1,0:T(8,128)(2,1)} %k_hbm.1, bf16[4,64,384]{2,1,0:T(8,128)(2,1)} %v_hbm.1, ...), custom_call_target="tpu_custom_call" | custom-call | tf_op jit(solution)/shard_map/pack/pallas_call | solution.py:221
  3.9 9.7 %all-to-all-start = ((bf16[8,4,64,384]{3,2,1,0:T(8,128)(2,1)}), bf16[8,4,64,384]{3,2,1,0:T(8,128)(2,1)S(1)}, u32[]{:S(2)}, u32[]{:S(2)}) async-start(bf16[8,4,64,384]{3,2,1,0:T(8,128)(2,1)} %bitcast.4), calls=%async_computation | async-start | bytes 3145728 | tf_op jit(solution)/shard_map/all_to_all | solution.py:21
  13.6 2.3 %collective-permute-start = (bf16[4,64,384]{2,1,0:T(8,128)(2,1)S(1)}, bf16[4,64,384]{2,1,0:T(8,128)(2,1)S(1)}, u32[]{:S(2)}, u32[]{:S(2)}) collective-permute-start(bf16[4,64,384]{2,1,0:T(8,128)(2,1)S(1)} %get-tuple-element.21), channel_id=1, source_target_pairs={{0,16},{16,0},{1,17},{17,1},{2,18},{18,2},{3,19},{19,3},{4,20},{20... | collective-permute-start | bytes 589832 | tf_op jit(solution)/shard_map/ppermute | solution.py:26
  15.9 16.7 %all-gather = bf16[16,64,384]{2,1,0:T(8,128)(2,1)S(1)} all-gather(bf16[4,64,384]{2,1,0:T(8,128)(2,1)S(1)} %get-tuple-element.20), channel_id=2, replica_groups=mesh['zh'=4,'y'=4,'c'=2,'x'=4,'zl'=4] {'zl'}, dimensions={0}, use_global_device_ids=true | all-gather | bytes 983040 | tf_op jit(solution)/shard_map/all_gather | solution.py:233
  32.6 0.0 collective-permute-done
  32.6 15.1 %all-gather.1 = bf16[16,64,384]{2,1,0:T(8,128)(2,1)S(1)} all-gather(bf16[4,64,384]{2,1,0:T(8,128)(2,1)S(1)} %collective-permute-done), channel_id=3, replica_groups=mesh['zh'=4,'y'=4,'c'=2,'x'=4,'zl'=4] {'zl'}, dimensions={0}, use_global_device_ids=true | all-gather | bytes 983040 | tf_op jit(solution)/shard_map/all_gather | solution.py:234
  47.7 0.0 all-to-all-done
  47.7 1.5 products.1
  49.3 18.6 %all_to_all.30.part_ref = f32[4,6,64,256]{3,2,1,0:T(8,128)S(1)} all-to-all(f32[4,6,64,256]{3,2,1,0:T(8,128)S(1)} %products.1), channel_id=1, replica_groups=mesh['zh'=4,'y'=4,'c'=2,'x'=4,'zl'=4] {'y'}, dimensions={0} | all-to-all | bytes 3145728 | tf_op jit(solution)/shard_map/all_to_all | solution.py:21
  67.9 0.1 rows.1
  68.0 27.7 %all_to_all.31.refs_0_ = f32[16,24,256]{2,1,0:T(8,128)S(1)} all-to-all(f32[16,24,256]{2,1,0:T(8,128)S(1)} %rows.1), channel_id=1, replica_groups=mesh['zh'=4,'y'=4,'c'=2,'x'=4,'zl'=4] {'zh','zl'}, dimensions={0} | all-to-all | bytes 786432 | tf_op jit(solution)/shard_map/all_to_all | solution.py:21
  95.7 0.3 softmax.1
  96.0 24.6 %all_to_all.32.mats_ref = bf16[16,48,128]{2,1,0:T(8,128)(2,1)S(1)} all-to-all(bf16[16,48,128]{2,1,0:T(8,128)(2,1)S(1)} %softmax.1), channel_id=1, replica_groups=mesh['zh'=4,'y'=4,'c'=2,'x'=4,'zl'=4] {'zh','zl'}, dimensions={0} | all-to-all | bytes 393216 | tf_op jit(solution)/shard_map/all_to_all | solution.py:21
  120.6 0.1 unpack.1
  120.7 10.7 %all_to_all.33.refs_1_ = bf16[4,6,64,256]{3,2,1,0:T(8,128)(2,1)S(1)} all-to-all(bf16[4,6,64,256]{3,2,1,0:T(8,128)(2,1)S(1)} %unpack.1), channel_id=1, replica_groups=mesh['zh'=4,'y'=4,'c'=2,'x'=4,'zl'=4] {'y'}, dimensions={0} | all-to-all | bytes 1572864 | tf_op jit(solution)/shard_map/all_to_all | solution.py:21
  131.5 4.2 %outputs.1 = (bf16[4,2,4,64,384]{4,3,2,1,0:T(8,128)(2,1)}, bf16[2,4,64,384]{3,2,1,0:T(8,128)(2,1)}, bf16[2,4,64,384]{3,2,1,0:T(8,128)(2,1)}, bf16[2,4,64,384]{3,2,1,0:T(8,128)(2,1)}, bf16[2,4,64,384]{3,2,1,0:T(8,128)(2,1)}) custom-call(s32[2]{0:T(128)S(1)} %pad_add_fusion.place_ref.refs_0_, bf16[4,6,64,256]{3,2,1,0:T(8,128)(2,1)S(1)} %all_to_all.33.refs_1_, ...), custom_call_target="tpu_custom_call" | custom-call | tf_op jit(solution)/shard_map/outputs/pallas_call | solution.py:264
  135.7 0.0 copy-start.4
  135.7 0.0 copy-start.3
  135.7 0.0 copy-start.2
  135.7 0.0 copy-start.1
  135.7 4.7 %all-to-all-start.5 = ((bf16[4,2,4,64,384]{4,3,2,1,0:T(8,128)(2,1)}), bf16[4,2,4,64,384]{4,3,2,1,0:T(8,128)(2,1)S(1)}, u32[]{:S(2)}, u32[]{:S(2)}) async-start(bf16[4,2,4,64,384]{4,3,2,1,0:T(8,128)(2,1)} %get-tuple-element.23), calls=%async_computation.5 | async-start | bytes 3145728 | tf_op jit(solution)/shard_map/all_to_all | solution.py:21
  140.4 0.0 copy-done.4
  140.4 1.9 %collective-permute-start.2 = (bf16[2,4,64,384]{3,2,1,0:T(8,128)(2,1)S(1)}, bf16[2,4,64,384]{3,2,1,0:T(8,128)(2,1)S(1)}, u32[]{:S(2)}, u32[]{:S(2)}) collective-permute-start(bf16[2,4,64,384]{3,2,1,0:T(8,128)(2,1)S(1)} %copy-done.4), channel_id=1, source_target_pairs={{0,12},{4,0},{8,4},{12,8},{1,13},{5,1},{9,5},{13,9},{2,14},{6,2},{... | collective-permute-start | bytes 1179656 | tf_op jit(solution)/shard_map/ppermute | solution.py:26
  142.3 0.0 copy-done.3
  142.3 4.3 %collective-permute-start.3 = (bf16[2,4,64,384]{3,2,1,0:T(8,128)(2,1)S(1)}, bf16[2,4,64,384]{3,2,1,0:T(8,128)(2,1)S(1)}, u32[]{:S(2)}, u32[]{:S(2)}) collective-permute-start(bf16[2,4,64,384]{3,2,1,0:T(8,128)(2,1)S(1)} %copy-done.3), channel_id=1, source_target_pairs={{0,8},{4,12},{8,0},{12,4},{1,9},{5,13},{9,1},{13,5},{2,10},{6,14},... | collective-permute-start | bytes 1179656 | tf_op jit(solution)/shard_map/ppermute | solution.py:26
  146.6 0.0 copy-done.2
  146.6 3.4 %collective-permute-start.4 = (bf16[2,4,64,384]{3,2,1,0:T(8,128)(2,1)S(1)}, bf16[2,4,64,384]{3,2,1,0:T(8,128)(2,1)S(1)}, u32[]{:S(2)}, u32[]{:S(2)}) collective-permute-start(bf16[2,4,64,384]{3,2,1,0:T(8,128)(2,1)S(1)} %copy-done.2), channel_id=1, source_target_pairs={{0,4},{4,8},{8,12},{12,0},{1,5},{5,9},{9,13},{13,1},{2,6},{6,10},{... | collective-permute-start | bytes 1179656 | tf_op jit(solution)/shard_map/ppermute | solution.py:26
  150.0 0.0 collective-permute-done.2.one_ref
  150.0 5.5 %collective-permute-done.3.two_ref = bf16[2,4,64,384]{3,2,1,0:T(8,128)(2,1)S(1)} collective-permute-done((bf16[2,4,64,384]{3,2,1,0:T(8,128)(2,1)S(1)}, bf16[2,4,64,384]{3,2,1,0:T(8,128)(2,1)S(1)}, u32[]{:S(2)}, u32[]{:S(2)}) %collective-permute-start.3) | collective-permute-done | bytes 393248 | tf_op jit(solution)/shard_map/ppermute | solution.py:26
  155.5 2.5 %collective-permute-done.4.three_ref = bf16[2,4,64,384]{3,2,1,0:T(8,128)(2,1)S(1)} collective-permute-done((bf16[2,4,64,384]{3,2,1,0:T(8,128)(2,1)S(1)}, bf16[2,4,64,384]{3,2,1,0:T(8,128)(2,1)S(1)}, u32[]{:S(2)}, u32[]{:S(2)}) %collective-permute-start.4) | collective-permute-done | bytes 393248 | tf_op jit(solution)/shard_map/ppermute | solution.py:26
  158.0 0.0 copy-done.1
  158.0 0.0 copy-start
  158.1 0.2 total_columns.1
  158.3 9.9 %collective-permute-start.5 = (bf16[4,64,384]{2,1,0:T(8,128)(2,1)S(1)}, bf16[4,64,384]{2,1,0:T(8,128)(2,1)S(1)}, u32[]{:S(2)}, u32[]{:S(2)}) collective-permute-start(bf16[4,64,384]{2,1,0:T(8,128)(2,1)S(1)} %get-tuple-element.33), channel_id=1, source_target_pairs={{0,16},{16,0},{1,17},{17,1},{2,18},{18,2},{3,19},{19,3},{4,20},{20... | collective-permute-start | bytes 589832 | tf_op jit(solution)/shard_map/ppermute | solution.py:26
  168.1 6.8 %all-to-all-done.5.part_ref = bf16[4,2,4,64,384]{4,3,2,1,0:T(8,128)(2,1)S(1)} async-done(((bf16[4,2,4,64,384]{4,3,2,1,0:T(8,128)(2,1)}), bf16[4,2,4,64,384]{4,3,2,1,0:T(8,128)(2,1)S(1)}, u32[]{:S(2)}, u32[]{:S(2)}) %all-to-all-start.5) | async-done | bytes 1572896 | tf_op jit(solution)/shard_map/all_to_all | solution.py:21
  175.0 0.2 total_rows.1
  175.2 5.3 %collective-permute-start.1 = (bf16[4,64,384]{2,1,0:T(8,128)(2,1)S(1)}, bf16[4,64,384]{2,1,0:T(8,128)(2,1)S(1)}, u32[]{:S(2)}, u32[]{:S(2)}) collective-permute-start(bf16[4,64,384]{2,1,0:T(8,128)(2,1)S(1)} %get-tuple-element.25), channel_id=1, source_target_pairs={{0,16},{16,0},{1,17},{17,1},{2,18},{18,2},{3,19},{19,3},{4,20},{20... | collective-permute-start | bytes 589832 | tf_op jit(solution)/shard_map/ppermute | solution.py:26
  180.4 0.0 collective-permute-done.5.got_ref
  180.5 1.4 finish_columns.1
  181.9 0.0 collective-permute-done.1.got_ref
  181.9 0.0 copy-done
  181.9 1.9 %finish_rows.1 = (bf16[4,64,768]{2,1,0:T(8,128)(2,1)}, bf16[4,64,384]{2,1,0:T(8,128)(2,1)}) custom-call(s32[2]{0:T(128)S(1)} %pad_add_fusion.place_ref.refs_0_, bf16[4,64,384]{2,1,0:T(8,128)(2,1)S(1)} %get-tuple-element.24.keep_ref, bf16[4,64,384]{2,1,0:T(8,128)(2,1)S(1)} %collective-permute-done.1.got_ref, bf16[384,768]{1,0:T(8,128)(2,1)S(1)} %copy-done), custom_call_target="tpu_custom_call" | custom-call | tf_op jit(solution)/shard_map/finish_rows/pallas_call | solution.py:288
Async XLA Ops:
  3.9 43.8 %all-to-all-start = ((bf16[8,4,64,384]{3,2,1,0:T(8,128)(2,1)}), bf16[8,4,64,384]{3,2,1,0:T(8,128)(2,1)S(1)}, u32[]{:S(2)}, u32[]{:S(2)}) async-start(bf16[8,4,64,384]{3,2,1,0:T(8,128)(2,1)} %bitcast.4), calls=%async_computation | async-start | bytes 3145728 | tf_op jit(solution)/shard_map/all_to_all | solution.py:21
  13.6 19.0 %collective-permute-start = (bf16[4,64,384]{2,1,0:T(8,128)(2,1)S(1)}, bf16[4,64,384]{2,1,0:T(8,128)(2,1)S(1)}, u32[]{:S(2)}, u32[]{:S(2)}) collective-permute-start(bf16[4,64,384]{2,1,0:T(8,128)(2,1)S(1)} %get-tuple-element.21), channel_id=1, source_target_pairs={{0,16},{16,0},{1,17},{17,1},{2,18},{18,2},{3,19},{19,3},{4,20},{20... | collective-permute-start | bytes 589832 | tf_op jit(solution)/shard_map/ppermute | solution.py:26
  135.7 4.8 %copy-start.4 = (bf16[2,4,64,384]{3,2,1,0:T(8,128)(2,1)S(1)}, bf16[2,4,64,384]{3,2,1,0:T(8,128)(2,1)}, u32[]{:S(2)}) copy-start(bf16[2,4,64,384]{3,2,1,0:T(8,128)(2,1)} %get-tuple-element.29) | copy-start | bytes 1179652
  135.7 6.7 %copy-start.3 = (bf16[2,4,64,384]{3,2,1,0:T(8,128)(2,1)S(1)}, bf16[2,4,64,384]{3,2,1,0:T(8,128)(2,1)}, u32[]{:S(2)}) copy-start(bf16[2,4,64,384]{3,2,1,0:T(8,128)(2,1)} %get-tuple-element.30) | copy-start | bytes 1179652
  135.7 10.9 %copy-start.2 = (bf16[2,4,64,384]{3,2,1,0:T(8,128)(2,1)S(1)}, bf16[2,4,64,384]{3,2,1,0:T(8,128)(2,1)}, u32[]{:S(2)}) copy-start(bf16[2,4,64,384]{3,2,1,0:T(8,128)(2,1)} %get-tuple-element.31) | copy-start | bytes 1179652
  135.7 22.4 %copy-start.1 = (bf16[2,4,64,384]{3,2,1,0:T(8,128)(2,1)S(1)}, bf16[2,4,64,384]{3,2,1,0:T(8,128)(2,1)}, u32[]{:S(2)}) copy-start(bf16[2,4,64,384]{3,2,1,0:T(8,128)(2,1)} %get-tuple-element.28.zero_ref) | copy-start | bytes 1179652
  135.7 39.2 %all-to-all-start.5 = ((bf16[4,2,4,64,384]{4,3,2,1,0:T(8,128)(2,1)}), bf16[4,2,4,64,384]{4,3,2,1,0:T(8,128)(2,1)S(1)}, u32[]{:S(2)}, u32[]{:S(2)}) async-start(bf16[4,2,4,64,384]{4,3,2,1,0:T(8,128)(2,1)} %get-tuple-element.23), calls=%async_computation.5 | async-start | bytes 3145728 | tf_op jit(solution)/shard_map/all_to_all | solution.py:21
  140.4 9.6 %collective-permute-start.2 = (bf16[2,4,64,384]{3,2,1,0:T(8,128)(2,1)S(1)}, bf16[2,4,64,384]{3,2,1,0:T(8,128)(2,1)S(1)}, u32[]{:S(2)}, u32[]{:S(2)}) collective-permute-start(bf16[2,4,64,384]{3,2,1,0:T(8,128)(2,1)S(1)} %copy-done.4), channel_id=1, source_target_pairs={{0,12},{4,0},{8,4},{12,8},{1,13},{5,1},{9,5},{13,9},{2,14},{6,2},{... | collective-permute-start | bytes 1179656 | tf_op jit(solution)/shard_map/ppermute | solution.py:26
  142.3 13.2 %collective-permute-start.3 = (bf16[2,4,64,384]{3,2,1,0:T(8,128)(2,1)S(1)}, bf16[2,4,64,384]{3,2,1,0:T(8,128)(2,1)S(1)}, u32[]{:S(2)}, u32[]{:S(2)}) collective-permute-start(bf16[2,4,64,384]{3,2,1,0:T(8,128)(2,1)S(1)} %copy-done.3), channel_id=1, source_target_pairs={{0,8},{4,12},{8,0},{12,4},{1,9},{5,13},{9,1},{13,5},{2,10},{6,14},... | collective-permute-start | bytes 1179656 | tf_op jit(solution)/shard_map/ppermute | solution.py:26
  146.6 11.4 %collective-permute-start.4 = (bf16[2,4,64,384]{3,2,1,0:T(8,128)(2,1)S(1)}, bf16[2,4,64,384]{3,2,1,0:T(8,128)(2,1)S(1)}, u32[]{:S(2)}, u32[]{:S(2)}) collective-permute-start(bf16[2,4,64,384]{3,2,1,0:T(8,128)(2,1)S(1)} %copy-done.2), channel_id=1, source_target_pairs={{0,4},{4,8},{8,12},{12,0},{1,5},{5,9},{9,13},{13,1},{2,6},{6,10},{... | collective-permute-start | bytes 1179656 | tf_op jit(solution)/shard_map/ppermute | solution.py:26
  158.0 23.8 %copy-start = (bf16[384,768]{1,0:T(8,128)(2,1)S(1)}, bf16[384,768]{1,0:T(8,128)(2,1)}, u32[]{:S(2)}) copy-start(bf16[384,768]{1,0:T(8,128)(2,1)} %w_ref.1) | copy-start | bytes 1769476
  158.3 22.2 %collective-permute-start.5 = (bf16[4,64,384]{2,1,0:T(8,128)(2,1)S(1)}, bf16[4,64,384]{2,1,0:T(8,128)(2,1)S(1)}, u32[]{:S(2)}, u32[]{:S(2)}) collective-permute-start(bf16[4,64,384]{2,1,0:T(8,128)(2,1)S(1)} %get-tuple-element.33), channel_id=1, source_target_pairs={{0,16},{16,0},{1,17},{17,1},{2,18},{18,2},{3,19},{19,3},{4,20},{20... | collective-permute-start | bytes 589832 | tf_op jit(solution)/shard_map/ppermute | solution.py:26
  175.2 6.7 %collective-permute-start.1 = (bf16[4,64,384]{2,1,0:T(8,128)(2,1)S(1)}, bf16[4,64,384]{2,1,0:T(8,128)(2,1)S(1)}, u32[]{:S(2)}, u32[]{:S(2)}) collective-permute-start(bf16[4,64,384]{2,1,0:T(8,128)(2,1)S(1)} %get-tuple-element.25), channel_id=1, source_target_pairs={{0,16},{16,0},{1,17},{17,1},{2,18},{18,2},{3,19},{19,3},{4,20},{20... | collective-permute-start | bytes 589832 | tf_op jit(solution)/shard_map/ppermute | solution.py:26

commit v8 on v7

v8 whole, which is shorter than its diff:
```python
import math

import jax
import jax.numpy as jnp
from jax import lax
from jax.experimental import pallas as pl
from jax.experimental.pallas import tpu as pltpu
from jax.sharding import Mesh, PartitionSpec as P

HEADS = 6
F32 = jnp.float32
BF16 = jnp.bfloat16
VMEM = 16 * 1024 * 1024


def params():
    return pltpu.CompilerParams(vmem_limit_bytes=VMEM)


def exchange(blocks, axis):
    return lax.all_to_all(blocks, axis, 0, 0, tiled=True)


def shift(block, axis, by):
    n = lax.axis_size(axis)
    return lax.ppermute(block, axis, [(i, (i + by) % n) for i in range(n)])


def halves(one, two):
    half = one.shape[1] // 2
    return (
        jnp.concatenate([one[:, :half], two[:, :half]], axis=1),
        jnp.concatenate([one[:, half:], two[:, half:]], axis=1),
    )


def low_lanes(shape):
    return lax.broadcasted_iota(jnp.int32, shape, 1) < shape[1] // 2


def pack_kernel(place_ref, q_hbm, k_hbm, v_hbm, w_hbm, go_hbm, own_ref, send_ref, right_ref, q_ref, k_ref, v_ref, w_ref, go_ref, sems):
    loads = [
        pltpu.make_async_copy(src, dst, sems.at[n])
        for n, (src, dst) in enumerate(
            ((w_hbm, w_ref), (go_hbm, go_ref), (k_hbm, k_ref), (v_hbm, v_ref), (q_hbm, q_ref))
        )
    ]
    for load in loads:
        load.start()
    first = place_ref[0] == 0
    loads[0].wait()
    loads[1].wait()
    seqs, res, _ = q_ref.shape
    grads = lax.dot_general(
        go_ref[...].reshape(seqs * res, go_ref.shape[2]),
        w_ref[...],
        (((1,), (1,)), ((), ())),
        preferred_element_type=F32,
    ).astype(BF16)
    for load in loads[2:]:
        load.wait()
    for s in range(seqs):
        kv = halves(k_ref[s], v_ref[s])
        vk = halves(v_ref[s], k_ref[s])
        for core, part in enumerate((jnp.where(first, kv[0], vk[0]), jnp.where(first, vk[1], kv[1]))):
            for n in range(right_ref.shape[0]):
                right_ref[n, core, s] = part
        q, g = q_ref[s], grads[s * res : (s + 1) * res]
        qg, gq = halves(q, g), halves(g, q)
        own_ref[s] = jnp.where(first, qg[0], qg[1])
        send_ref[s] = jnp.where(first, gq[1], gq[0])


def mix_kernel(own_ref, got_ref, low_ref, high_ref):
    for s in range(own_ref.shape[0]):
        low = low_lanes(own_ref.shape[1:])
        low_ref[s] = jnp.where(low, own_ref[s], got_ref[s])
        high_ref[s] = jnp.where(low, got_ref[s], own_ref[s])


def slab(blocks, p):
    at = slice(p * 128, p * 128 + 128)
    rows = [
        jnp.concatenate([ref[s, :, at] for ref in row for s in range(ref.shape[0])], axis=1) for row in blocks
    ]
    return jnp.concatenate(rows, axis=0)


def lefts(ref):
    return [(ref.at[n],) for n in range(4)]


def rights(place_ref, ref, slot):
    core = place_ref[0] if slot == 0 else 1 - place_ref[0]
    return [(ref.at[lax.rem(place_ref[1] + 4 - n, 4), core],) for n in range(4)]


def odd_chunk(shape):
    return (lax.broadcasted_iota(jnp.int32, shape, 1) // 64) % 2 == 1


def product_kernel(own_first, place_ref, left_ref, right_ref, out_ref):
    own, other = (0, 1) if own_first else (1, 0)
    left = [slab(lefts(left_ref), p) for p in range(3)]
    right = [[slab(rights(place_ref, right_ref, slot), p) for p in range(3)] for slot in range(2)]
    odd = odd_chunk(left[0].shape)
    zero = jnp.zeros_like(left[0])
    for t in range(3):
        ones, others = [], []
        for chunk, slot in ((t, own), (t + 3, other)):
            part = left[chunk // 2]
            ones.append(jnp.where(odd, part, zero) if chunk % 2 else jnp.where(odd, zero, part))
            others.append(right[slot][chunk // 2])
        full = lax.dot_general(
            jnp.concatenate(ones, axis=1),
            jnp.concatenate(others, axis=1),
            (((1,), (1,)), ((), ())),
            preferred_element_type=F32,
        )
        out_ref[:, t] = full.reshape(out_ref.shape[0], out_ref.shape[2], out_ref.shape[3])


def rows_kernel(logit_ref, grad_ref, out_ref):
    for which, ref in enumerate((logit_ref, grad_ref)):
        total = (ref[0] + ref[1]) + (ref[2] + ref[3])
        for n in range(16):
            for t in range(3):
                at = (which * 3 + t) * 4
                out_ref[n, at : at + 4] = total[t, n * 4 : n * 4 + 4]


def softmax_kernel(scale, part_ref, out_ref):
    tiles = []
    for col in range(4):
        parts = [part_ref[n * 4 + col] for n in range(4)]
        tiles.append((parts[0] + parts[1]) + (parts[2] + parts[3]))
    total = jnp.concatenate(tiles, axis=1)
    logits = total[:12] * scale
    grads = total[12:]
    expo = jnp.exp(logits - jnp.max(logits, axis=-1, keepdims=True))
    weights = expo / jnp.sum(expo, axis=-1, keepdims=True)
    scores = weights * (grads - jnp.sum(weights * grads, axis=-1, keepdims=True))
    full = jnp.concatenate([scores, weights], axis=0)
    for col in range(4):
        at = col * 256
        tile = jnp.concatenate([full[:, at : at + 128], full[:, at + 128 : at + 256]], axis=0).astype(BF16)
        for n in range(col, 16, 4):
            out_ref[n] = tile


def unpack_kernel(mats_ref, out_ref, rows_ref):
    for n in range(16):
        block = mats_ref[n].astype(F32)
        for j in range(6):
            rows_ref[j, n * 4 : n * 4 + 4, 0:128] = block[j * 4 : j * 4 + 4]
            rows_ref[j, n * 4 : n * 4 + 4, 128:256] = block[24 + j * 4 : 28 + j * 4]
    full = rows_ref[...].astype(BF16)
    for n in range(out_ref.shape[0]):
        out_ref[n] = full


def product(mats_ref, heads, side, contract):
    even, odd = (
        lax.dot_general(
            mats_ref[:, j].reshape(256, 256), side, (((contract,), (0,)), ((), ())), preferred_element_type=F32
        )
        for j in heads
    )
    return jnp.where(odd_chunk(even.shape), odd, even)


def scaled(value, scale, p, scores):
    chunk = 2 * p + odd_chunk(value.shape).astype(jnp.int32)
    return (value * jnp.where((chunk < 3) == scores, scale, 1.0)).astype(BF16)


def put(refs, value, p):
    for n, ref in enumerate(refs):
        seqs, res, _ = ref.shape
        for s in range(seqs):
            ref[s, :, p * 128 : p * 128 + 128] = value[n * res : (n + 1) * res, s * 128 : s * 128 + 128]


def row_kernel(scale, place_ref, mats_ref, right_ref, row_hbm, row_ref, sems):
    copies = [pltpu.make_async_copy(row_ref.at[:, slot], row_hbm.at[:, slot], sems.at[slot]) for slot in range(2)]
    for slot in range(2):
        for p in range(3):
            heads = [(j + 3 * slot) % 6 for j in (2 * p, 2 * p + 1)]
            value = product(mats_ref, heads, slab(rights(place_ref, right_ref, slot), p), 1)
            put([row_ref.at[n, slot] for n in range(4)], scaled(value, scale, p, slot == 0), p)
        copies[slot].start()
    for copy in copies:
        copy.wait()


def col_kernel(scale, mats_ref, q_ref, g_ref, *refs):
    col_hbms, col_ref, sems = refs[:4], refs[4], refs[5]
    for which, ref in enumerate((q_ref, g_ref)):
        for p in range(3):
            heads = [j % 3 + 3 * which for j in (2 * p, 2 * p + 1)]
            value = product(mats_ref, heads, slab(lefts(ref), p), 0)
            put([col_ref.at[n, which] for n in range(4)], (value * scale if which == 0 else value).astype(BF16), p)
    copies = [pltpu.make_async_copy(col_ref.at[n], col_hbms[n], sems.at[n]) for n in range(4)]
    for copy in copies:
        copy.start()
    for copy in copies:
        copy.wait()


def four(refs, s):
    p = [ref[s].astype(F32) for ref in refs]
    return ((p[0] + p[1]) + (p[2] + p[3])).astype(BF16)


def total_columns_kernel(zero_ref, one_ref, two_ref, three_ref, keep_ref, send_ref):
    refs = (zero_ref, one_ref, two_ref, three_ref)
    low = low_lanes(keep_ref.shape[1:])
    for s in range(keep_ref.shape[0]):
        keys = four([ref.at[0] for ref in refs], s)
        values = four([ref.at[1] for ref in refs], s)
        keep_ref[s] = jnp.where(low, keys, values)
        send_ref[s] = jnp.where(low, values, keys)


def total_rows_kernel(row_ref, keep_ref, send_ref):
    for s in range(keep_ref.shape[0]):
        keep_ref[s] = four([row_ref.at[n, 0] for n in range(4)], s)
        send_ref[s] = four([row_ref.at[n, 1] for n in range(4)], s)


def unpacked(first, keep, got):
    low = low_lanes(keep.shape)
    one, two = jnp.where(low, keep, got), jnp.where(low, got, keep)
    half = keep.shape[1] // 2
    turned = [jnp.concatenate([a[:, half:], a[:, :half]], axis=1) for a in (one, two)]
    return jnp.where(first, one, turned[0]), jnp.where(first, turned[1], two)


def finish_columns_kernel(place_ref, keep_ref, got_ref, gk_ref, gv_ref):
    first = place_ref[0] == 0
    for s in range(keep_ref.shape[0]):
        gk_ref[s], gv_ref[s] = unpacked(first, keep_ref[s], got_ref[s])


def finish_rows_kernel(place_ref, keep_ref, got_ref, w_ref, mixed_ref, gq_ref):
    seqs, res, width = keep_ref.shape
    keep, got = keep_ref[...].reshape(seqs * res, width), got_ref[...].reshape(seqs * res, width)
    grad_query, attended = unpacked(place_ref[0] == 0, keep, got)
    gq_ref[...] = grad_query.reshape(seqs, res, width)
    mixed = jnp.dot(attended, w_ref[...], preferred_element_type=F32).astype(BF16)
    mixed_ref[...] = mixed.reshape(mixed_ref.shape)


def on_device(queries, keys, values, out_weight, grad_out):
    seqs, res, width = queries.shape
    model_dim = out_weight.shape[1]
    scale = 1.0 / math.sqrt(width // HEADS * seqs * 32)
    place = jnp.stack([lax.axis_index("c"), lax.axis_index("x")]).astype(jnp.int32)
    block = (seqs, res, width)
    smem = pl.BlockSpec(memory_space=pltpu.SMEM)
    vmem = pl.BlockSpec(memory_space=pltpu.VMEM)
    hbm = pl.BlockSpec(memory_space=pltpu.HBM)

    def array(shape, dtype=BF16):
        return jax.ShapeDtypeStruct(shape, dtype)

    args = (queries, keys, values, out_weight, grad_out)
    own, send, right = pl.pallas_call(
        pack_kernel,
        in_specs=[smem] + [hbm] * 5,
        out_specs=[vmem] * 3,
        out_shape=(array(block), array(block), array((4, 2) + block)),
        scratch_shapes=[pltpu.VMEM(a.shape, BF16) for a in (queries, keys, values, out_weight, grad_out)]
        + [pltpu.SemaphoreType.DMA((5,))],
        compiler_params=params(),
        name="pack",
    )(place, *(pltpu.with_memory_space_constraint(arg, pltpu.HBM) for arg in args))
    right = exchange(right.reshape((8,) + block), ("x", "c")).reshape((4, 2) + block)
    left_q, left_g = pl.pallas_call(
        mix_kernel, out_shape=(array(block), array(block)), compiler_params=params(), name="mix"
    )(own, shift(send, "c", 1))

    def products(own_first, left, name):
        return pl.pallas_call(
            lambda *refs: product_kernel(own_first, *refs),
            in_specs=[smem] + [vmem] * 2,
            out_shape=array((4, 3, 64, 256), F32),
            compiler_params=params(),
            name=name,
        )(place, left, right)

    left_q = lax.all_gather(left_q, "zl")
    logits = products(True, left_q, "logits")
    left_g, logits = lax.optimization_barrier((left_g, logits))
    logits = exchange(logits, "y")
    left_g = lax.all_gather(left_g, "zl")
    weight_grads = exchange(products(False, left_g, "weight_grads"), "y")
    partial = pl.pallas_call(
        rows_kernel, out_shape=array((16, 24, 256), F32), compiler_params=params(), name="rows"
    )(logits, weight_grads)
    partial = exchange(partial, ("zh", "zl"))
    mats = pl.pallas_call(
        lambda *refs: softmax_kernel(scale, *refs),
        out_shape=array((16, 48, 128)),
        compiler_params=params(),
        name="softmax",
    )(partial)
    mats = exchange(mats, ("zh", "zl"))
    mats = pl.pallas_call(
        unpack_kernel,
        out_shape=array((4, 6, 64, 256)),
        scratch_shapes=[pltpu.VMEM((6, 64, 256), F32)],
        compiler_params=params(),
        name="unpack",
    )(mats)
    mats = exchange(mats, "y")

    (row,) = pl.pallas_call(
        lambda *refs: row_kernel(scale, *refs),
        in_specs=[smem] + [vmem] * 2,
        out_specs=[hbm],
        out_shape=(pltpu.HBM((4, 2) + block, BF16),),
        scratch_shapes=[pltpu.VMEM((4, 2) + block, BF16), pltpu.SemaphoreType.DMA((2,))],
        compiler_params=params(),
        name="row_products",
    )(place, mats, right)
    cols = pl.pallas_call(
        lambda *refs: col_kernel(scale, *refs),
        in_specs=[vmem] * 3,
        out_specs=[hbm] * 4,
        out_shape=(pltpu.HBM((2,) + block, BF16),) * 4,
        scratch_shapes=[pltpu.VMEM((4, 2) + block, BF16), pltpu.SemaphoreType.DMA((4,))],
        compiler_params=params(),
        name="col_products",
    )(mats, left_q, left_g)
    row = exchange(row, "zl")
    cols = [cols[0]] + [shift(cols[by], "x", -by) for by in (1, 2, 3)]
    keep, send = pl.pallas_call(
        total_columns_kernel, out_shape=(array(block), array(block)), compiler_params=params(), name="total_columns"
    )(*cols)
    grad_key, grad_value = pl.pallas_call(
        finish_columns_kernel,
        in_specs=[smem, vmem, vmem],
        out_shape=(array(block), array(block)),
        compiler_params=params(),
        name="finish_columns",
    )(place, keep, shift(send, "c", 1))
    keep, send = pl.pallas_call(
        total_rows_kernel, out_shape=(array(block), array(block)), compiler_params=params(), name="total_rows"
    )(row)
    mixed, grad_query = pl.pallas_call(
        finish_rows_kernel,
        in_specs=[smem] + [vmem] * 3,
        out_shape=(array((seqs, res, model_dim)), array(block)),
        compiler_params=params(),
        name="finish_rows",
    )(place, keep, shift(send, "c", 1), out_weight)
    return mixed, grad_query, grad_key, grad_value


def solution(mesh):
    grid = Mesh(mesh.devices.reshape(4, 4, 2, 4, 4), ("zh", "y", "c", "x", "zl"))
    placed = P(("zh", "y", "c"), ("x", "zl"), None)
    return jax.shard_map(
        on_device,
        mesh=grid,
        in_specs=(placed, placed, placed, P(), placed),
        out_specs=(placed, placed, placed, placed),
        check_vma=False,
    )
```

time: 184 us -> 185 us (level)
  the two profiles are of different devices: /device:TPU:3 before, /device:TPU:1 now
where the time goes in v8:
time: 185 us; the launch traced here: 184 us
  blocking collectives  104 us (56%)
  starting transfers between devices  44.9 us (24%)
  Pallas kernels  18.2 us (10%)
  waiting for transfers between devices  14.5 us (8%)
  local copies, waits for them, and re-layouts  1.88 us (1%)
    all_to_all x4, blocking collectives, exchange(): return lax.all_to_all(blocks, axis, 0, 0, tiled=True)  71.6 us
    ppermute x6, starting transfers between devices, shift(): return lax.ppermute(block, axis, [(i, (i + by) % n) for i in range(n)])  25.9 us
    all_to_all x3, starting transfers between devices, exchange(): return lax.all_to_all(blocks, axis, 0, 0, tiled=True)  19 us
    all_gather x1, blocking collectives, on_device(): left_q = lax.all_gather(left_q, 'zl')  16.7 us
    all_gather x1, blocking collectives, on_device(): left_g = lax.all_gather(left_g, 'zl')  15.6 us
    ppermute x6, waiting for transfers between devices, shift(): return lax.ppermute(block, axis, [(i, (i + by) % n) for i in range(n)])  11.1 us
  transfers between devices with their start and end apart: 9, of which 6 were waited for; matrix products, arithmetic and copies ran while one was open for 0% of the time, Pallas kernels for 4%

profile of v8, /device:TPU:1, one launch (start us, length us, event | category | flops | bytes accessed | tf_op | source)
XLA Modules:
  0.0 184.2 jit_solution(289529240513599980)
XLA Ops:
  0.6 0.1 pad_add_fusion.place_ref.refs_0_
  0.7 3.6 %pack.1 = (bf16[4,64,384]{2,1,0:T(8,128)(2,1)S(1)}, bf16[4,64,384]{2,1,0:T(8,128)(2,1)S(1)}, bf16[4,2,4,64,384]{4,3,2,1,0:T(8,128)(2,1)}) custom-call(s32[2]{0:T(128)S(1)} %pad_add_fusion.place_ref.refs_0_, bf16[4,64,384]{2,1,0:T(8,128)(2,1)} %q_hbm.1, bf16[4,64,384]{2,1,0:T(8,128)(2,1)} %k_hbm.1, bf16[4,64,384]{2,1,0:T(8,128)(2,1)} %v_hbm.1, ...), custom_call_target="tpu_custom_call" | custom-call | tf_op jit(solution)/shard_map/pack/pallas_call | solution.py:268
  4.3 10.4 %all-to-all-start = ((bf16[8,4,64,384]{3,2,1,0:T(8,128)(2,1)}), bf16[8,4,64,384]{3,2,1,0:T(8,128)(2,1)S(1)}, u32[]{:S(2)}, u32[]{:S(2)}) async-start(bf16[8,4,64,384]{3,2,1,0:T(8,128)(2,1)} %bitcast.3), calls=%async_computation | async-start | bytes 3145728 | tf_op jit(solution)/shard_map/all_to_all | solution.py:21
  14.7 2.0 %collective-permute-start = (bf16[4,64,384]{2,1,0:T(8,128)(2,1)S(1)}, bf16[4,64,384]{2,1,0:T(8,128)(2,1)S(1)}, u32[]{:S(2)}, u32[]{:S(2)}) collective-permute-start(bf16[4,64,384]{2,1,0:T(8,128)(2,1)S(1)} %get-tuple-element.24), channel_id=1, source_target_pairs={{0,16},{16,0},{1,17},{17,1},{2,18},{18,2},{3,19},{19,3},{4,20},{20... | collective-permute-start | bytes 589832 | tf_op jit(solution)/shard_map/ppermute | solution.py:26
  16.7 1.3 collective-permute-done.got_ref
  18.1 16.7 %all-gather = bf16[16,64,384]{2,1,0:T(8,128)(2,1)S(1)} all-gather(bf16[4,64,384]{2,1,0:T(8,128)(2,1)S(1)} %get-tuple-element.26), channel_id=2, replica_groups=mesh['zh'=4,'y'=4,'c'=2,'x'=4,'zl'=4] {'zl'}, dimensions={0}, use_global_device_ids=true | all-gather | bytes 983040 | tf_op jit(solution)/shard_map/all_gather | solution.py:292
  34.8 0.7 all-to-all-done
  35.4 2.1 %logits.1 = f32[4,3,64,256]{3,2,1,0:T(8,128)} custom-call(s32[2]{0:T(128)S(1)} %pad_add_fusion.place_ref.refs_0_, bf16[4,4,64,384]{3,2,1,0:T(8,128)(2,1)S(1)} %bitcast.9, bf16[4,2,4,64,384]{4,3,2,1,0:T(8,128)(2,1)S(1)} %bitcast.6), custom_call_target="tpu_custom_call" | custom-call | tf_op jit(solution)/shard_map/logits/pallas_call | solution.py:284
  37.5 4.2 %all-to-all-start.1 = ((f32[4,3,64,256]{3,2,1,0:T(8,128)}), f32[4,3,64,256]{3,2,1,0:T(8,128)}, u32[]{:S(2)}, u32[]{:S(2)}) async-start(f32[4,3,64,256]{3,2,1,0:T(8,128)} %logits.1), calls=%async_computation.1 | async-start | bytes 1572864 | tf_op jit(solution)/shard_map/all_to_all | solution.py:21
  41.7 15.6 %all-gather.1 = bf16[16,64,384]{2,1,0:T(8,128)(2,1)S(1)} all-gather(bf16[4,64,384]{2,1,0:T(8,128)(2,1)S(1)} %get-tuple-element.29), channel_id=3, replica_groups=mesh['zh'=4,'y'=4,'c'=2,'x'=4,'zl'=4] {'zl'}, dimensions={0}, use_global_device_ids=true | all-gather | bytes 983040 | tf_op jit(solution)/shard_map/all_gather | solution.py:296
  57.3 0.0 copy-start
  57.3 1.1 weight_grads.1
  58.5 0.0 copy-done
  58.5 0.0 copy-start.2
  58.5 0.9 copy-done.2
  59.3 0.0 all-to-all-done.1.logit_ref
  59.4 12.8 %all_to_all.35.grad_ref = f32[4,3,64,256]{3,2,1,0:T(8,128)S(1)} all-to-all(f32[4,3,64,256]{3,2,1,0:T(8,128)} %copy-done.2), channel_id=1, replica_groups=mesh['zh'=4,'y'=4,'c'=2,'x'=4,'zl'=4] {'y'}, dimensions={0} | all-to-all | bytes 1572864 | tf_op jit(solution)/shard_map/all_to_all | solution.py:21
  72.1 1.2 rows.1
  73.4 24.0 %all_to_all.36.refs_0_ = f32[16,24,256]{2,1,0:T(8,128)S(1)} all-to-all(f32[16,24,256]{2,1,0:T(8,128)S(1)} %rows.1), channel_id=1, replica_groups=mesh['zh'=4,'y'=4,'c'=2,'x'=4,'zl'=4] {'zh','zl'}, dimensions={0} | all-to-all | bytes 786432 | tf_op jit(solution)/shard_map/all_to_all | solution.py:21
  97.3 0.3 softmax.1
  97.6 24.1 %all_to_all.37.mats_ref = bf16[16,48,128]{2,1,0:T(8,128)(2,1)S(1)} all-to-all(bf16[16,48,128]{2,1,0:T(8,128)(2,1)S(1)} %softmax.1), channel_id=1, replica_groups=mesh['zh'=4,'y'=4,'c'=2,'x'=4,'zl'=4] {'zh','zl'}, dimensions={0} | all-to-all | bytes 393216 | tf_op jit(solution)/shard_map/all_to_all | solution.py:21
  121.7 0.1 unpack.1
  121.8 10.7 %all_to_all.38.refs_1_.refs_0_ = bf16[4,6,64,256]{3,2,1,0:T(8,128)(2,1)S(1)} all-to-all(bf16[4,6,64,256]{3,2,1,0:T(8,128)(2,1)S(1)} %unpack.1), channel_id=1, replica_groups=mesh['zh'=4,'y'=4,'c'=2,'x'=4,'zl'=4] {'y'}, dimensions={0} | all-to-all | bytes 1572864 | tf_op jit(solution)/shard_map/all_to_all | solution.py:21
  132.5 2.5 %row_products.1 = bf16[4,2,4,64,384]{4,3,2,1,0:T(8,128)(2,1)} custom-call(s32[2]{0:T(128)S(1)} %pad_add_fusion.place_ref.refs_0_, bf16[4,6,64,256]{3,2,1,0:T(8,128)(2,1)S(1)} %all_to_all.38.refs_1_.refs_0_, bf16[4,2,4,64,384]{4,3,2,1,0:T(8,128)(2,1)S(1)} %bitcast.8), custom_call_target="tpu_custom_call" | custom-call | tf_op jit(solution)/shard_map/row_products/pallas_call | solution.py:318
  135.1 0.0 copy-start.1
  135.1 4.5 %all-to-all-start.6 = ((bf16[4,2,4,64,384]{4,3,2,1,0:T(8,128)(2,1)}), bf16[4,2,4,64,384]{4,3,2,1,0:T(8,128)(2,1)}, u32[]{:S(2)}, u32[]{:S(2)}) async-start(bf16[4,2,4,64,384]{4,3,2,1,0:T(8,128)(2,1)} %row_products.1), calls=%async_computation.6 | async-start | bytes 3145728 | tf_op jit(solution)/shard_map/all_to_all | solution.py:21
  139.6 0.0 copy-done.1
  139.6 2.2 %col_products.1 = (bf16[2,4,64,384]{3,2,1,0:T(8,128)(2,1)}, bf16[2,4,64,384]{3,2,1,0:T(8,128)(2,1)}, bf16[2,4,64,384]{3,2,1,0:T(8,128)(2,1)}, bf16[2,4,64,384]{3,2,1,0:T(8,128)(2,1)}) custom-call(bf16[4,6,64,256]{3,2,1,0:T(8,128)(2,1)S(1)} %all_to_all.38.refs_1_.refs_0_, bf16[4,4,64,384]{3,2,1,0:T(8,128)(2,1)S(1)} %bitcast.10, ...), custom_call_target="tpu_custom_call" | custom-call | tf_op jit(solution)/shard_map/col_products/pallas_call | solution.py:327
  141.8 2.2 %collective-permute-start.2 = (bf16[2,4,64,384]{3,2,1,0:T(8,128)(2,1)}, bf16[2,4,64,384]{3,2,1,0:T(8,128)(2,1)S(1)}, u32[]{:S(2)}, u32[]{:S(2)}) collective-permute-start(bf16[2,4,64,384]{3,2,1,0:T(8,128)(2,1)} %get-tuple-element.35), channel_id=1, source_target_pairs={{0,12},{4,0},{8,4},{12,8},{1,13},{5,1},{9,5},{13,9},{2,14},{6,2},{... | collective-permute-start | bytes 1179656 | tf_op jit(solution)/shard_map/ppermute | solution.py:26
  144.1 2.4 %collective-permute-start.3 = (bf16[2,4,64,384]{3,2,1,0:T(8,128)(2,1)}, bf16[2,4,64,384]{3,2,1,0:T(8,128)(2,1)S(1)}, u32[]{:S(2)}, u32[]{:S(2)}) collective-permute-start(bf16[2,4,64,384]{3,2,1,0:T(8,128)(2,1)} %get-tuple-element.36), channel_id=1, source_target_pairs={{0,8},{4,12},{8,0},{12,4},{1,9},{5,13},{9,1},{13,5},{2,10},{6,14},... | collective-permute-start | bytes 1179656 | tf_op jit(solution)/shard_map/ppermute | solution.py:26
  146.5 2.6 %collective-permute-start.4 = (bf16[2,4,64,384]{3,2,1,0:T(8,128)(2,1)}, bf16[2,4,64,384]{3,2,1,0:T(8,128)(2,1)S(1)}, u32[]{:S(2)}, u32[]{:S(2)}) collective-permute-start(bf16[2,4,64,384]{3,2,1,0:T(8,128)(2,1)} %get-tuple-element.37), channel_id=1, source_target_pairs={{0,4},{4,8},{8,12},{12,0},{1,5},{5,9},{9,13},{13,1},{2,6},{6,10},{... | collective-permute-start | bytes 1179656 | tf_op jit(solution)/shard_map/ppermute | solution.py:26
  149.1 1.8 collective-permute-done.2.one_ref
  150.9 3.6 %collective-permute-done.3.two_ref = bf16[2,4,64,384]{3,2,1,0:T(8,128)(2,1)S(1)} collective-permute-done((bf16[2,4,64,384]{3,2,1,0:T(8,128)(2,1)}, bf16[2,4,64,384]{3,2,1,0:T(8,128)(2,1)S(1)}, u32[]{:S(2)}, u32[]{:S(2)}) %collective-permute-start.3) | collective-permute-done | bytes 393248 | tf_op jit(solution)/shard_map/ppermute | solution.py:26
  154.6 4.3 %collective-permute-done.4.three_ref = bf16[2,4,64,384]{3,2,1,0:T(8,128)(2,1)S(1)} collective-permute-done((bf16[2,4,64,384]{3,2,1,0:T(8,128)(2,1)}, bf16[2,4,64,384]{3,2,1,0:T(8,128)(2,1)S(1)}, u32[]{:S(2)}, u32[]{:S(2)}) %collective-permute-start.4) | collective-permute-done | bytes 393248 | tf_op jit(solution)/shard_map/ppermute | solution.py:26
  158.9 0.0 copy-start.4
  158.9 1.0 copy-done.4
  159.9 0.0 copy-start.3
  159.9 0.2 total_columns.1
  160.1 11.2 %collective-permute-start.5 = (bf16[4,64,384]{2,1,0:T(8,128)(2,1)S(1)}, bf16[4,64,384]{2,1,0:T(8,128)(2,1)S(1)}, u32[]{:S(2)}, u32[]{:S(2)}) collective-permute-start(bf16[4,64,384]{2,1,0:T(8,128)(2,1)S(1)} %get-tuple-element.39), channel_id=1, source_target_pairs={{0,16},{16,0},{1,17},{17,1},{2,18},{18,2},{3,19},{19,3},{4,20},{20... | collective-permute-start | bytes 589832 | tf_op jit(solution)/shard_map/ppermute | solution.py:26
  171.4 2.7 %all-to-all-done.6.row_ref = bf16[4,2,4,64,384]{4,3,2,1,0:T(8,128)(2,1)} async-done(((bf16[4,2,4,64,384]{4,3,2,1,0:T(8,128)(2,1)}), bf16[4,2,4,64,384]{4,3,2,1,0:T(8,128)(2,1)}, u32[]{:S(2)}, u32[]{:S(2)}) %all-to-all-start.6) | async-done | bytes 1572896 | tf_op jit(solution)/shard_map/all_to_all | solution.py:21
  174.1 1.6 total_rows.1
  175.7 5.4 %collective-permute-start.1 = (bf16[4,64,384]{2,1,0:T(8,128)(2,1)S(1)}, bf16[4,64,384]{2,1,0:T(8,128)(2,1)S(1)}, u32[]{:S(2)}, u32[]{:S(2)}) collective-permute-start(bf16[4,64,384]{2,1,0:T(8,128)(2,1)S(1)} %get-tuple-element.31), channel_id=1, source_target_pairs={{0,16},{16,0},{1,17},{17,1},{2,18},{18,2},{3,19},{19,3},{4,20},{20... | collective-permute-start | bytes 589832 | tf_op jit(solution)/shard_map/ppermute | solution.py:26
  181.1 0.0 collective-permute-done.5.got_ref
  181.1 1.4 finish_columns.1
  182.5 0.0 collective-permute-done.1.got_ref
  182.5 0.0 copy-done.3
  182.5 1.7 finish_rows.1
  (1 shorter events, 0.0 us)
Async XLA Ops:
  4.3 31.1 %all-to-all-start = ((bf16[8,4,64,384]{3,2,1,0:T(8,128)(2,1)}), bf16[8,4,64,384]{3,2,1,0:T(8,128)(2,1)S(1)}, u32[]{:S(2)}, u32[]{:S(2)}) async-start(bf16[8,4,64,384]{3,2,1,0:T(8,128)(2,1)} %bitcast.3), calls=%async_computation | async-start | bytes 3145728 | tf_op jit(solution)/shard_map/all_to_all | solution.py:21
  14.7 3.3 %collective-permute-start = (bf16[4,64,384]{2,1,0:T(8,128)(2,1)S(1)}, bf16[4,64,384]{2,1,0:T(8,128)(2,1)S(1)}, u32[]{:S(2)}, u32[]{:S(2)}) collective-permute-start(bf16[4,64,384]{2,1,0:T(8,128)(2,1)S(1)} %get-tuple-element.24), channel_id=1, source_target_pairs={{0,16},{16,0},{1,17},{17,1},{2,18},{18,2},{3,19},{19,3},{4,20},{20... | collective-permute-start | bytes 589832 | tf_op jit(solution)/shard_map/ppermute | solution.py:26
  37.5 21.8 %all-to-all-start.1 = ((f32[4,3,64,256]{3,2,1,0:T(8,128)}), f32[4,3,64,256]{3,2,1,0:T(8,128)}, u32[]{:S(2)}, u32[]{:S(2)}) async-start(f32[4,3,64,256]{3,2,1,0:T(8,128)} %logits.1), calls=%async_computation.1 | async-start | bytes 1572864 | tf_op jit(solution)/shard_map/all_to_all | solution.py:21
  57.3 1.2 copy-start
  58.5 0.9 copy-start.2
  135.1 4.5 %copy-start.1 = (bf16[16,64,384]{2,1,0:T(8,128)(2,1)S(1)}, bf16[16,64,384]{2,1,0:T(8,128)(2,1)}, u32[]{:S(2)}) copy-start(bf16[16,64,384]{2,1,0:T(8,128)(2,1)} %copy-done) | copy-start | bytes 2359300
  135.1 39.0 %all-to-all-start.6 = ((bf16[4,2,4,64,384]{4,3,2,1,0:T(8,128)(2,1)}), bf16[4,2,4,64,384]{4,3,2,1,0:T(8,128)(2,1)}, u32[]{:S(2)}, u32[]{:S(2)}) async-start(bf16[4,2,4,64,384]{4,3,2,1,0:T(8,128)(2,1)} %row_products.1), calls=%async_computation.6 | async-start | bytes 3145728 | tf_op jit(solution)/shard_map/all_to_all | solution.py:21
  141.8 9.1 %collective-permute-start.2 = (bf16[2,4,64,384]{3,2,1,0:T(8,128)(2,1)}, bf16[2,4,64,384]{3,2,1,0:T(8,128)(2,1)S(1)}, u32[]{:S(2)}, u32[]{:S(2)}) collective-permute-start(bf16[2,4,64,384]{3,2,1,0:T(8,128)(2,1)} %get-tuple-element.35), channel_id=1, source_target_pairs={{0,12},{4,0},{8,4},{12,8},{1,13},{5,1},{9,5},{13,9},{2,14},{6,2},{... | collective-permute-start | bytes 1179656 | tf_op jit(solution)/shard_map/ppermute | solution.py:26
  144.1 10.5 %collective-permute-start.3 = (bf16[2,4,64,384]{3,2,1,0:T(8,128)(2,1)}, bf16[2,4,64,384]{3,2,1,0:T(8,128)(2,1)S(1)}, u32[]{:S(2)}, u32[]{:S(2)}) collective-permute-start(bf16[2,4,64,384]{3,2,1,0:T(8,128)(2,1)} %get-tuple-element.36), channel_id=1, source_target_pairs={{0,8},{4,12},{8,0},{12,4},{1,9},{5,13},{9,1},{13,5},{2,10},{6,14},... | collective-permute-start | bytes 1179656 | tf_op jit(solution)/shard_map/ppermute | solution.py:26
  146.5 12.4 %collective-permute-start.4 = (bf16[2,4,64,384]{3,2,1,0:T(8,128)(2,1)}, bf16[2,4,64,384]{3,2,1,0:T(8,128)(2,1)S(1)}, u32[]{:S(2)}, u32[]{:S(2)}) collective-permute-start(bf16[2,4,64,384]{3,2,1,0:T(8,128)(2,1)} %get-tuple-element.37), channel_id=1, source_target_pairs={{0,4},{4,8},{8,12},{12,0},{1,5},{5,9},{9,13},{13,1},{2,6},{6,10},{... | collective-permute-start | bytes 1179656 | tf_op jit(solution)/shard_map/ppermute | solution.py:26
  158.9 1.0 copy-start.4
  159.9 22.6 %copy-start.3 = (bf16[384,768]{1,0:T(8,128)(2,1)S(1)}, bf16[384,768]{1,0:T(8,128)(2,1)}, u32[]{:S(2)}) copy-start(bf16[384,768]{1,0:T(8,128)(2,1)} %w_ref.1) | copy-start | bytes 1769476
  160.1 20.9 %collective-permute-start.5 = (bf16[4,64,384]{2,1,0:T(8,128)(2,1)S(1)}, bf16[4,64,384]{2,1,0:T(8,128)(2,1)S(1)}, u32[]{:S(2)}, u32[]{:S(2)}) collective-permute-start(bf16[4,64,384]{2,1,0:T(8,128)(2,1)S(1)} %get-tuple-element.39), channel_id=1, source_target_pairs={{0,16},{16,0},{1,17},{17,1},{2,18},{18,2},{3,19},{19,3},{4,20},{20... | collective-permute-start | bytes 589832 | tf_op jit(solution)/shard_map/ppermute | solution.py:26
  175.7 6.8 %collective-permute-start.1 = (bf16[4,64,384]{2,1,0:T(8,128)(2,1)S(1)}, bf16[4,64,384]{2,1,0:T(8,128)(2,1)S(1)}, u32[]{:S(2)}, u32[]{:S(2)}) collective-permute-start(bf16[4,64,384]{2,1,0:T(8,128)(2,1)S(1)} %get-tuple-element.31), channel_id=1, source_target_pairs={{0,16},{16,0},{1,17},{17,1},{2,18},{18,2},{3,19},{19,3},{4,20},{20... | collective-permute-start | bytes 589832 | tf_op jit(solution)/shard_map/ppermute | solution.py:26

commit v9 on v8

v9 whole, which is shorter than its diff:
```python
import math

import jax
import jax.numpy as jnp
from jax import lax
from jax.experimental import pallas as pl
from jax.experimental.pallas import tpu as pltpu
from jax.sharding import Mesh, PartitionSpec as P

HEADS = 6
F32 = jnp.float32
BF16 = jnp.bfloat16
VMEM = 16 * 1024 * 1024


def params():
    return pltpu.CompilerParams(vmem_limit_bytes=VMEM)


def exchange(blocks, axis):
    return lax.all_to_all(blocks, axis, 0, 0, tiled=True)


def shift(block, axis, by):
    n = lax.axis_size(axis)
    return lax.ppermute(block, axis, [(i, (i + by) % n) for i in range(n)])


def halves(one, two):
    half = one.shape[1] // 2
    return (
        jnp.concatenate([one[:, :half], two[:, :half]], axis=1),
        jnp.concatenate([one[:, half:], two[:, half:]], axis=1),
    )


def low_lanes(shape):
    return lax.broadcasted_iota(jnp.int32, shape, 1) < shape[1] // 2


def pack_kernel(place_ref, q_hbm, k_hbm, v_hbm, w_hbm, go_hbm, own_ref, send_ref, right_ref, q_ref, k_ref, v_ref, w_ref, go_ref, sems):
    loads = [
        pltpu.make_async_copy(src, dst, sems.at[n])
        for n, (src, dst) in enumerate(
            ((w_hbm, w_ref), (go_hbm, go_ref), (k_hbm, k_ref), (v_hbm, v_ref), (q_hbm, q_ref))
        )
    ]
    for load in loads:
        load.start()
    first = place_ref[0] == 0
    loads[0].wait()
    loads[1].wait()
    seqs, res, _ = q_ref.shape
    grads = lax.dot_general(
        go_ref[...].reshape(seqs * res, go_ref.shape[2]),
        w_ref[...],
        (((1,), (1,)), ((), ())),
        preferred_element_type=F32,
    ).astype(BF16)
    for load in loads[2:]:
        load.wait()
    for s in range(seqs):
        kv = halves(k_ref[s], v_ref[s])
        vk = halves(v_ref[s], k_ref[s])
        for core, part in enumerate((jnp.where(first, kv[0], vk[0]), jnp.where(first, vk[1], kv[1]))):
            for n in range(right_ref.shape[0]):
                right_ref[n, core, s] = part
        q, g = q_ref[s], grads[s * res : (s + 1) * res]
        qg, gq = halves(q, g), halves(g, q)
        own_ref[s] = jnp.where(first, qg[0], qg[1])
        send_ref[s] = jnp.where(first, gq[1], gq[0])


def mix_kernel(own_ref, got_ref, low_ref, high_ref):
    for s in range(own_ref.shape[0]):
        low = low_lanes(own_ref.shape[1:])
        low_ref[s] = jnp.where(low, own_ref[s], got_ref[s])
        high_ref[s] = jnp.where(low, got_ref[s], own_ref[s])


def slab(blocks, p):
    at = slice(p * 128, p * 128 + 128)
    rows = [
        jnp.concatenate([ref[s, :, at] for ref in row for s in range(ref.shape[0])], axis=1) for row in blocks
    ]
    return jnp.concatenate(rows, axis=0)


def lefts(ref):
    return [(ref.at[n],) for n in range(4)]


def rights(place_ref, ref, slot):
    core = place_ref[0] if slot == 0 else 1 - place_ref[0]
    return [(ref.at[lax.rem(place_ref[1] + 4 - n, 4), core],) for n in range(4)]


def odd_chunk(shape):
    return (lax.broadcasted_iota(jnp.int32, shape, 1) // 64) % 2 == 1


def tile_products(own_first, place_ref, left_ref, right_ref, out_ref):
    own, other = (0, 1) if own_first else (1, 0)
    left = [slab(lefts(left_ref), p) for p in range(3)]
    right = [[slab(rights(place_ref, right_ref, slot), p) for p in range(3)] for slot in range(2)]
    odd = odd_chunk(left[0].shape)
    zero = jnp.zeros_like(left[0])
    for t in range(3):
        ones, others = [], []
        for chunk, slot in ((t, own), (t + 3, other)):
            part = left[chunk // 2]
            ones.append(jnp.where(odd, part, zero) if chunk % 2 else jnp.where(odd, zero, part))
            others.append(right[slot][chunk // 2])
        full = lax.dot_general(
            jnp.concatenate(ones, axis=1),
            jnp.concatenate(others, axis=1),
            (((1,), (1,)), ((), ())),
            preferred_element_type=F32,
        )
        out_ref[:, t] = full.reshape(out_ref.shape[0], out_ref.shape[2], out_ref.shape[3])


def logits_kernel(place_ref, left_ref, right_ref, out_ref):
    tile_products(True, place_ref, left_ref, right_ref, out_ref)


def weight_grads_kernel(place_ref, left_ref, right_ref, own_hbm, one_hbm, two_hbm, three_hbm, all_ref, sems):
    tile_products(False, place_ref, left_ref, right_ref, all_ref)
    copies = []
    for by, hbm in enumerate((own_hbm, one_hbm, two_hbm, three_hbm)):
        copies.append(pltpu.make_async_copy(all_ref.at[lax.rem(place_ref[2] + by, 4)], hbm, sems.at[by]))
    for copy in copies:
        copy.start()
    for copy in copies:
        copy.wait()


def cut_rows(total, out_ref):
    for n in range(16):
        for t in range(3):
            rows = total[t, n * 4 : n * 4 + 4]
            out_ref[n, t * 4 : t * 4 + 4] = rows[:, :128]
            out_ref[n, 12 + t * 4 : 16 + t * 4] = rows[:, 128:]


def logit_rows_kernel(part_ref, out_ref):
    cut_rows((part_ref[0] + part_ref[1]) + (part_ref[2] + part_ref[3]), out_ref)


def grad_rows_kernel(own_ref, one_ref, two_ref, three_ref, out_ref):
    cut_rows((own_ref[...] + one_ref[...]) + (two_ref[...] + three_ref[...]), out_ref)


def whole_rows(part_ref):
    tiles = []
    for col in range(4):
        parts = [part_ref[n * 4 + col] for n in range(4)]
        total = (parts[0] + parts[1]) + (parts[2] + parts[3])
        tiles += [total[:12], total[12:]]
    return jnp.concatenate(tiles, axis=1)


def deal_rows(value, out_ref):
    for col in range(4):
        at = col * 256
        tile = jnp.concatenate([value[:, at : at + 128], value[:, at + 128 : at + 256]], axis=0).astype(BF16)
        for n in range(col, 16, 4):
            out_ref[n] = tile


def weights_kernel(scale, part_ref, weights_ref, out_ref):
    logits = whole_rows(part_ref) * scale
    expo = jnp.exp(logits - jnp.max(logits, axis=-1, keepdims=True))
    weights = expo / jnp.sum(expo, axis=-1, keepdims=True)
    weights_ref[...] = weights
    deal_rows(weights, out_ref)


def scores_kernel(weights_ref, part_ref, out_ref):
    weights, grads = weights_ref[...], whole_rows(part_ref)
    deal_rows(weights * (grads - jnp.sum(weights * grads, axis=-1, keepdims=True)), out_ref)


def unpack_rows(rows_in_ref, rows_ref):
    for n in range(16):
        block = rows_in_ref[n].astype(F32)
        for t in range(3):
            rows_ref[t, n * 4 : n * 4 + 4, 0:128] = block[t * 4 : t * 4 + 4]
            rows_ref[t, n * 4 : n * 4 + 4, 128:256] = block[12 + t * 4 : 16 + t * 4]
    return rows_ref[...].astype(BF16)


def unpack_kernel(rows_in_ref, out_ref, rows_ref):
    out_ref[...] = unpack_rows(rows_in_ref, rows_ref)


def unpack_copies_kernel(rows_in_ref, out_ref, rows_ref):
    full = unpack_rows(rows_in_ref, rows_ref)
    for n in range(out_ref.shape[0]):
        out_ref[n] = full


def product(mats_ref, heads, side, contract):
    even, odd = (
        lax.dot_general(
            mats_ref[:, j].reshape(256, 256), side, (((contract,), (0,)), ((), ())), preferred_element_type=F32
        )
        for j in heads
    )
    return jnp.where(odd_chunk(even.shape), odd, even)


def put(refs, value, p):
    for n, ref in enumerate(refs):
        seqs, res, _ = ref.shape
        for s in range(seqs):
            ref[s, :, p * 128 : p * 128 + 128] = value[n * res : (n + 1) * res, s * 128 : s * 128 + 128]


def mixed_rights(place_ref, right_ref, low_slot, p):
    low, high = (slab(rights(place_ref, right_ref, slot), p) for slot in (low_slot, 1 - low_slot))
    if p == 1:
        return jnp.where(odd_chunk(low.shape), high, low)
    return low if p == 0 else high


def rows_into(factor, low_slot, place_ref, mats_ref, right_ref, row_ref):
    for p in range(3):
        value = product(mats_ref, [j % 3 for j in (2 * p, 2 * p + 1)], mixed_rights(place_ref, right_ref, low_slot, p), 1)
        put([row_ref.at[n] for n in range(4)], (value if factor is None else value * factor).astype(BF16), p)


def attended_kernel(place_ref, mats_ref, right_ref, own_hbm, one_hbm, two_hbm, three_hbm, row_ref, sems):
    rows_into(None, 1, place_ref, mats_ref, right_ref, row_ref)
    copies = []
    for by, hbm in enumerate((own_hbm, one_hbm, two_hbm, three_hbm)):
        copies.append(pltpu.make_async_copy(row_ref.at[lax.rem(place_ref[3] + by, 4)], hbm, sems.at[by]))
    for copy in copies:
        copy.start()
    for copy in copies:
        copy.wait()


def grad_query_kernel(scale, place_ref, mats_ref, right_ref, row_hbm, row_ref, sem):
    rows_into(scale, 0, place_ref, mats_ref, right_ref, row_ref)
    copy = pltpu.make_async_copy(row_ref, row_hbm, sem)
    copy.start()
    copy.wait()


def col_kernel(factor, mats_ref, left_ref, *refs):
    col_hbms, col_ref, sems = refs[:4], refs[4], refs[5]
    for p in range(3):
        value = product(mats_ref, [j % 3 for j in (2 * p, 2 * p + 1)], slab(lefts(left_ref), p), 0)
        put([col_ref.at[n] for n in range(4)], (value if factor is None else value * factor).astype(BF16), p)
    copies = [pltpu.make_async_copy(col_ref.at[n], col_hbms[n], sems.at[n]) for n in range(4)]
    for copy in copies:
        copy.start()
    for copy in copies:
        copy.wait()


def four(refs, s):
    p = [ref[s].astype(F32) for ref in refs]
    return ((p[0] + p[1]) + (p[2] + p[3])).astype(BF16)


def total_kernel(zero_ref, one_ref, two_ref, three_ref, out_ref):
    for s in range(out_ref.shape[0]):
        out_ref[s] = four((zero_ref, one_ref, two_ref, three_ref), s)


def total_blocks_kernel(part_ref, out_ref):
    total_kernel(*[part_ref.at[n] for n in range(4)], out_ref)


def turned(array):
    half = array.shape[1] // 2
    return jnp.concatenate([array[:, half:], array[:, :half]], axis=1)


def flat(ref):
    return ref[...].reshape(ref.shape[0] * ref.shape[1], ref.shape[2])


def own_first(first, own, got):
    both = jnp.where(low_lanes(own.shape), own, got)
    return jnp.where(first, both, turned(both))


def own_last(first, own, got):
    both = jnp.where(low_lanes(own.shape), got, own)
    return jnp.where(first, turned(both), both)


def finish_mixed_kernel(place_ref, own_ref, got_ref, w_ref, mixed_ref):
    attended = own_last(place_ref[0] == 0, flat(own_ref), flat(got_ref))
    mixed = jnp.dot(attended, w_ref[...], preferred_element_type=F32).astype(BF16)
    mixed_ref[...] = mixed.reshape(mixed_ref.shape)


def finish_last_kernel(place_ref, own_ref, got_ref, out_ref):
    out_ref[...] = own_last(place_ref[0] == 0, flat(own_ref), flat(got_ref)).reshape(out_ref.shape)


def finish_first_kernel(place_ref, own_ref, got_ref, out_ref):
    out_ref[...] = own_first(place_ref[0] == 0, flat(own_ref), flat(got_ref)).reshape(out_ref.shape)


def on_device(queries, keys, values, out_weight, grad_out):
    seqs, res, width = queries.shape
    model_dim = out_weight.shape[1]
    scale = 1.0 / math.sqrt(width // HEADS * seqs * 32)
    place = jnp.stack([lax.axis_index(axis) for axis in ("c", "x", "y", "zl")]).astype(jnp.int32)
    block = (seqs, res, width)
    smem = pl.BlockSpec(memory_space=pltpu.SMEM)
    vmem = pl.BlockSpec(memory_space=pltpu.VMEM)
    hbm = pl.BlockSpec(memory_space=pltpu.HBM)

    def array(shape, dtype=BF16):
        return jax.ShapeDtypeStruct(shape, dtype)

    args = (queries, keys, values, out_weight, grad_out)
    own, send, right = pl.pallas_call(
        pack_kernel,
        in_specs=[smem] + [hbm] * 5,
        out_specs=[vmem] * 3,
        out_shape=(array(block), array(block), array((4, 2) + block)),
        scratch_shapes=[pltpu.VMEM(a.shape, BF16) for a in (queries, keys, values, out_weight, grad_out)]
        + [pltpu.SemaphoreType.DMA((5,))],
        compiler_params=params(),
        name="pack",
    )(place, *(pltpu.with_memory_space_constraint(arg, pltpu.HBM) for arg in args))
    right = exchange(right.reshape((8,) + block), ("x", "c")).reshape((4, 2) + block)
    left_q, left_g = pl.pallas_call(
        mix_kernel, out_shape=(array(block), array(block)), compiler_params=params(), name="mix"
    )(own, shift(send, "c", 1))

    def call(kernel, out_shape, name, *operands, **more):
        specs = [smem if a is place else vmem for a in operands]
        return pl.pallas_call(
            kernel, in_specs=specs, out_shape=out_shape, compiler_params=params(), name=name, **more
        )(*operands)

    dealt_wide, dealt = array((16, 24, 128), F32), pltpu.HBM((16, 24, 128), BF16)
    unpacking = dict(scratch_shapes=[pltpu.VMEM((3, 64, 256), F32)])
    four_hbm = dict(
        out_specs=[hbm] * 4, scratch_shapes=[pltpu.VMEM((4,) + block, BF16), pltpu.SemaphoreType.DMA((4,))]
    )
    four_blocks = (pltpu.HBM(block, BF16),) * 4

    left_q = lax.all_gather(left_q, "zl")
    logits = call(logits_kernel, array((4, 3, 64, 256), F32), "logits", place, left_q, right)
    left_g, logits = lax.optimization_barrier((left_g, logits))
    logits = exchange(logits, "y")
    left_g = lax.all_gather(left_g, "zl")
    logits = call(logit_rows_kernel, dealt_wide, "logit_rows", logits)
    left_g, logits = lax.optimization_barrier((left_g, logits))
    logits = exchange(logits, ("zh", "zl"))
    grads = call(
        weight_grads_kernel,
        (pltpu.HBM((3, 64, 256), F32),) * 4,
        "weight_grads",
        place,
        left_g,
        right,
        out_specs=[hbm] * 4,
        scratch_shapes=[pltpu.VMEM((4, 3, 64, 256), F32), pltpu.SemaphoreType.DMA((4,))],
    )
    logits, _ = lax.optimization_barrier((logits, grads))
    grads = [grads[0]] + [shift(grads[by], "y", by) for by in (1, 2, 3)]
    weights, dealt_weights = call(
        lambda *refs: weights_kernel(scale, *refs), (pltpu.HBM((12, 1024), F32), dealt), "weights", logits
    )
    dealt_weights = exchange(dealt_weights, ("zh", "zl"))
    grads = call(grad_rows_kernel, dealt_wide, "grad_rows", *grads)
    dealt_weights, grads = lax.optimization_barrier((dealt_weights, grads))
    grads = exchange(grads, ("zh", "zl"))
    mats = lax.all_gather(call(unpack_kernel, array((3, 64, 256)), "unpack_weights", dealt_weights, **unpacking), "y")
    rows = call(attended_kernel, four_blocks, "attended", place, mats, right, **four_hbm)
    grads, _ = lax.optimization_barrier((grads, rows))
    rows = [rows[0]] + [shift(rows[by], "zl", by) for by in (1, 2, 3)]
    cols_made = call(lambda *refs: col_kernel(None, *refs), four_blocks, "grad_value", mats, left_g, **four_hbm)
    cols = [cols_made[0]] + [shift(cols_made[by], "x", -by) for by in (1, 2, 3)]

    scores = exchange(call(scores_kernel, dealt, "scores", weights, grads), ("zh", "zl"))
    scores, _, _ = lax.optimization_barrier((scores, cols_made, rows[1]))
    mats = exchange(call(unpack_copies_kernel, array((4, 3, 64, 256)), "unpack_scores", scores, **unpacking), "y")
    (row,) = call(
        lambda *refs: grad_query_kernel(scale, *refs),
        (pltpu.HBM((4,) + block, BF16),),
        "grad_query",
        place,
        mats,
        right,
        out_specs=[hbm],
        scratch_shapes=[pltpu.VMEM((4,) + block, BF16), pltpu.SemaphoreType.DMA],
    )
    row, rows = lax.optimization_barrier((row, rows))
    row = exchange(row, "zl")
    key_cols = call(lambda *refs: col_kernel(scale, *refs), four_blocks, "grad_key", mats, left_q, **four_hbm)
    key_cols = [key_cols[0]] + [shift(key_cols[by], "x", -by) for by in (1, 2, 3)]

    attended = call(total_kernel, array(block), "total_attended", *rows)
    mixed = call(
        finish_mixed_kernel,
        array((seqs, res, model_dim)),
        "finish_mixed",
        place,
        attended,
        shift(attended, "c", 1),
        out_weight,
    )
    value = call(total_kernel, array(block), "total_grad_value", *cols)
    grad_value = call(finish_last_kernel, array(block), "finish_grad_value", place, value, shift(value, "c", 1))
    key = call(total_kernel, array(block), "total_grad_key", *key_cols)
    grad_key = call(finish_first_kernel, array(block), "finish_grad_key", place, key, shift(key, "c", 1))
    query = call(total_blocks_kernel, array(block), "total_grad_query", row)
    grad_query = call(finish_first_kernel, array(block), "finish_grad_query", place, query, shift(query, "c", 1))
    return mixed, grad_query, grad_key, grad_value


def solution(mesh):
    grid = Mesh(mesh.devices.reshape(4, 4, 2, 4, 4), ("zh", "y", "c", "x", "zl"))
    placed = P(("zh", "y", "c"), ("x", "zl"), None)
    return jax.shard_map(
        on_device,
        mesh=grid,
        in_specs=(placed, placed, placed, P(), placed),
        out_specs=(placed, placed, placed, placed),
        check_vma=False,
    )
```

time: 185 us -> 234 us (1.26)
  starting transfers between devices: 44.9 us -> 132 us
  blocking collectives: 104 us -> 41.9 us
  waiting for transfers between devices: 14.5 us -> 25.9 us
  Pallas kernels: 18.2 us -> 28.9 us
    all_to_all x4 -> x0, blocking collectives: 71.6 us -> none  [exchange(): return lax.all_to_all(blocks, axis, 0, 0, tiled=True)]
    ppermute x6 -> x17, starting transfers between devices: 25.9 us -> 72.4 us  [shift(): return lax.ppermute(block, axis, [(i, (i + by) % n) for i in range(n)])]
    all_to_all x3 -> x8, starting transfers between devices: 19 us -> 59.4 us  [exchange(): return lax.all_to_all(blocks, axis, 0, 0, tiled=True)]
    pallas_call x11 -> x20, Pallas kernels: 14.6 us -> 25.2 us  [call(): pl.pallas_call(kernel, in_specs=specs, out_shape=out_shape, compiler_para...]
    all_to_all x3 -> x8, waiting for transfers between devices: 3.37 us -> 13.2 us  [exchange(): return lax.all_to_all(blocks, axis, 0, 0, tiled=True)]
    all_gather x0 -> x1, blocking collectives: none -> 9.63 us  [on_device(): lax.all_gather(call(unpack_kernel, array((3, 64, 256)), 'unpack_weights',...]
    ppermute x6 -> x17, waiting for transfers between devices: 11.1 us -> 12.7 us  [shift(): return lax.ppermute(block, axis, [(i, (i + by) % n) for i in range(n)])]
  transfers between devices with their start and end apart: 9 -> 25, of which waited for: 6 -> 10; matrix products, arithmetic and copies ran while one was open for 0% -> 0% of each run, Pallas kernels for 4% -> 7%
where the time goes in v9:
time: 234 us; the launch traced here: 232 us
  starting transfers between devices  132 us (56%)
  blocking collectives  41.9 us (18%)
  Pallas kernels  28.9 us (12%)
  waiting for transfers between devices  25.9 us (11%)
  local copies, waits for them, and re-layouts  2.48 us (1%)
    ppermute x17, starting transfers between devices, shift(): return lax.ppermute(block, axis, [(i, (i + by) % n) for i in range(n)])  72.4 us
    all_to_all x8, starting transfers between devices, exchange(): return lax.all_to_all(blocks, axis, 0, 0, tiled=True)  59.4 us
    pallas_call x20, Pallas kernels, call(): pl.pallas_call(kernel, in_specs=specs, out_shape=out_shape, compiler_para...  25.2 us
    all_gather x1, blocking collectives, on_device(): left_q = lax.all_gather(left_q, 'zl')  16.7 us
    all_gather x1, blocking collectives, on_device(): left_g = lax.all_gather(left_g, 'zl')  15.6 us
    all_to_all x8, waiting for transfers between devices, exchange(): return lax.all_to_all(blocks, axis, 0, 0, tiled=True)  13.2 us
    ppermute x17, waiting for transfers between devices, shift(): return lax.ppermute(block, axis, [(i, (i + by) % n) for i in range(n)])  12.7 us
    all_gather x1, blocking collectives, on_device(): lax.all_gather(call(unpack_kernel, array((3, 64, 256)), 'unpack_weights',...  9.63 us
  transfers between devices with their start and end apart: 25, of which 10 were waited for; matrix products, arithmetic and copies ran while one was open for 0% of the time, Pallas kernels for 7%

profile of v9, /device:TPU:1, one launch (start us, length us, event | category | flops | bytes accessed | tf_op | source)
XLA Modules:
  0.0 232.2 jit_solution(2788786535412428905)
XLA Ops:
  0.6 0.1 pad_add_fusion.place_ref.refs_0_
  0.7 3.6 %pack.1 = (bf16[4,64,384]{2,1,0:T(8,128)(2,1)S(1)}, bf16[4,64,384]{2,1,0:T(8,128)(2,1)S(1)}, bf16[4,2,4,64,384]{4,3,2,1,0:T(8,128)(2,1)}) custom-call(s32[4]{0:T(128)S(1)} %pad_add_fusion.place_ref.refs_0_, bf16[4,64,384]{2,1,0:T(8,128)(2,1)} %q_hbm.1, bf16[4,64,384]{2,1,0:T(8,128)(2,1)} %k_hbm.1, bf16[4,64,384]{2,1,0:T(8,128)(2,1)} %v_hbm.1, ...), custom_call_target="tpu_custom_call" | custom-call | tf_op jit(solution)/shard_map/pack/pallas_call | solution.py:324
  4.3 10.4 %all-to-all-start = ((bf16[8,4,64,384]{3,2,1,0:T(8,128)(2,1)}), bf16[8,4,64,384]{3,2,1,0:T(8,128)(2,1)S(1)}, u32[]{:S(2)}, u32[]{:S(2)}) async-start(bf16[8,4,64,384]{3,2,1,0:T(8,128)(2,1)} %bitcast.5), calls=%async_computation | async-start | bytes 3145728 | tf_op jit(solution)/shard_map/all_to_all | solution.py:21
  14.7 2.0 collective-permute-start
  16.7 1.3 collective-permute-done.got_ref
  18.1 16.7 %all-gather = bf16[16,64,384]{2,1,0:T(8,128)(2,1)S(1)} all-gather(bf16[4,64,384]{2,1,0:T(8,128)(2,1)S(1)} %get-tuple-element.44), channel_id=2, replica_groups=mesh['zh'=4,'y'=4,'c'=2,'x'=4,'zl'=4] {'zl'}, dimensions={0}, use_global_device_ids=true | all-gather | bytes 983040 | tf_op jit(solution)/shard_map/all_gather | solution.py:352
  34.8 0.7 all-to-all-done
  35.5 2.0 logits.1
  37.5 4.2 %all-to-all-start.1 = ((f32[4,3,64,256]{3,2,1,0:T(8,128)}), f32[4,3,64,256]{3,2,1,0:T(8,128)}, u32[]{:S(2)}, u32[]{:S(2)}) async-start(f32[4,3,64,256]{3,2,1,0:T(8,128)} %logits.1), calls=%async_computation.1 | async-start | bytes 1572864 | tf_op jit(solution)/shard_map/all_to_all | solution.py:21
  41.7 15.6 %all-gather.1 = bf16[16,64,384]{2,1,0:T(8,128)(2,1)S(1)} all-gather(bf16[4,64,384]{2,1,0:T(8,128)(2,1)S(1)} %get-tuple-element.46), channel_id=3, replica_groups=mesh['zh'=4,'y'=4,'c'=2,'x'=4,'zl'=4] {'zl'}, dimensions={0}, use_global_device_ids=true | all-gather | bytes 983040 | tf_op jit(solution)/shard_map/all_gather | solution.py:356
  57.3 1.9 logit_rows.1
  59.2 10.1 %all-to-all-start.2 = ((f32[16,24,128]{2,1,0:T(8,128)}), f32[16,24,128]{2,1,0:T(8,128)S(1)}, u32[]{:S(2)}, u32[]{:S(2)}) async-start(f32[16,24,128]{2,1,0:T(8,128)} %logit_rows.1), calls=%async_computation.2 | async-start | bytes 393216 | tf_op jit(solution)/shard_map/all_to_all | solution.py:21
  69.2 2.1 weight_grads.1
  71.3 10.2 %all-to-all-done.2.refs_0_ = f32[16,24,128]{2,1,0:T(8,128)S(1)} async-done(((f32[16,24,128]{2,1,0:T(8,128)}), f32[16,24,128]{2,1,0:T(8,128)S(1)}, u32[]{:S(2)}, u32[]{:S(2)}) %all-to-all-start.2) | async-done | bytes 196640 | tf_op jit(solution)/shard_map/all_to_all | solution.py:21
  81.6 0.9 weights.1
  82.4 5.1 %all-to-all-start.3 = ((bf16[16,24,128]{2,1,0:T(8,128)(2,1)}), bf16[16,24,128]{2,1,0:T(8,128)(2,1)S(1)}, u32[]{:S(2)}, u32[]{:S(2)}) async-start(bf16[16,24,128]{2,1,0:T(8,128)(2,1)} %get-tuple-element.56), calls=%async_computation.3 | async-start | bytes 196608 | tf_op jit(solution)/shard_map/all_to_all | solution.py:21
  87.5 3.1 %collective-permute-start.1 = (f32[3,64,256]{2,1,0:T(8,128)}, f32[3,64,256]{2,1,0:T(8,128)S(1)}, u32[]{:S(2)}, u32[]{:S(2)}) collective-permute-start(f32[3,64,256]{2,1,0:T(8,128)} %get-tuple-element.51), channel_id=1, source_target_pairs={{0,32},{32,64},{64,96},{96,0},{1,33},{33,65},{65,97},{97,1},{2,34}... | collective-permute-start | bytes 589832 | tf_op jit(solution)/shard_map/ppermute | solution.py:26
  90.6 4.6 %collective-permute-start.2 = (f32[3,64,256]{2,1,0:T(8,128)}, f32[3,64,256]{2,1,0:T(8,128)S(1)}, u32[]{:S(2)}, u32[]{:S(2)}) collective-permute-start(f32[3,64,256]{2,1,0:T(8,128)} %get-tuple-element.52), channel_id=1, source_target_pairs={{0,64},{32,96},{64,0},{96,32},{1,65},{33,97},{65,1},{97,33},{2,66}... | collective-permute-start | bytes 589832 | tf_op jit(solution)/shard_map/ppermute | solution.py:26
  95.3 2.8 %collective-permute-start.3 = (f32[3,64,256]{2,1,0:T(8,128)}, f32[3,64,256]{2,1,0:T(8,128)S(1)}, u32[]{:S(2)}, u32[]{:S(2)}) collective-permute-start(f32[3,64,256]{2,1,0:T(8,128)} %get-tuple-element.53), channel_id=1, source_target_pairs={{0,96},{32,0},{64,32},{96,64},{1,97},{33,1},{65,33},{97,65},{2,98}... | collective-permute-start | bytes 589832 | tf_op jit(solution)/shard_map/ppermute | solution.py:26
  98.0 1.0 collective-permute-done.2.two_ref
  99.0 3.1 %collective-permute-done.3.three_ref = f32[3,64,256]{2,1,0:T(8,128)S(1)} collective-permute-done((f32[3,64,256]{2,1,0:T(8,128)}, f32[3,64,256]{2,1,0:T(8,128)S(1)}, u32[]{:S(2)}, u32[]{:S(2)}) %collective-permute-start.3) | collective-permute-done | bytes 196640 | tf_op jit(solution)/shard_map/ppermute | solution.py:26
  102.2 0.9 copy-done.6
  103.1 0.7 grad_rows.1
  103.8 11.2 %all-to-all-start.4 = ((f32[16,24,128]{2,1,0:T(8,128)}), f32[16,24,128]{2,1,0:T(8,128)}, u32[]{:S(2)}, u32[]{:S(2)}) async-start(f32[16,24,128]{2,1,0:T(8,128)} %grad_rows.1), calls=%async_computation.4 | async-start | bytes 393216 | tf_op jit(solution)/shard_map/all_to_all | solution.py:21
  115.1 9.6 %all-gather.2 = bf16[12,64,256]{2,1,0:T(8,128)(2,1)S(1)} all-gather(bf16[3,64,256]{2,1,0:T(8,128)(2,1)S(1)} %unpack_weights.1), channel_id=4, replica_groups=mesh['zh'=4,'y'=4,'c'=2,'x'=4,'zl'=4] {'y'}, dimensions={0}, use_global_device_ids=true | all-gather | bytes 491520 | tf_op jit(solution)/shard_map/all_gather | solution.py:379
  124.7 2.1 attended.1
  126.8 0.7 all-to-all-done.4.part_ref
  127.5 0.8 copy-done.7
  128.4 1.7 scores.1
  130.0 11.5 %all-to-all-start.5 = ((bf16[16,24,128]{2,1,0:T(8,128)(2,1)}), bf16[16,24,128]{2,1,0:T(8,128)(2,1)}, u32[]{:S(2)}, u32[]{:S(2)}) async-start(bf16[16,24,128]{2,1,0:T(8,128)(2,1)} %scores.1), calls=%async_computation.5 | async-start | bytes 196608 | tf_op jit(solution)/shard_map/all_to_all | solution.py:21
  141.6 3.2 %collective-permute-start.4 = (bf16[4,64,384]{2,1,0:T(8,128)(2,1)}, bf16[4,64,384]{2,1,0:T(8,128)(2,1)S(1)}, u32[]{:S(2)}, u32[]{:S(2)}) collective-permute-start(bf16[4,64,384]{2,1,0:T(8,128)(2,1)} %get-tuple-element.60), channel_id=1, source_target_pairs={{0,1},{1,2},{2,3},{3,0},{4,5},{5,6},{6,7},{7,4},{8,9},{9,10},{10,1... | collective-permute-start | bytes 589832 | tf_op jit(solution)/shard_map/ppermute | solution.py:26
  144.8 1.5 grad_value.1
  146.3 5.0 %collective-permute-done.4.one_ref = bf16[4,64,384]{2,1,0:T(8,128)(2,1)S(1)} collective-permute-done((bf16[4,64,384]{2,1,0:T(8,128)(2,1)}, bf16[4,64,384]{2,1,0:T(8,128)(2,1)S(1)}, u32[]{:S(2)}, u32[]{:S(2)}) %collective-permute-start.4) | collective-permute-done | bytes 196640 | tf_op jit(solution)/shard_map/ppermute | solution.py:26
  151.3 0.7 copy-done.2
  152.0 1.6 all-to-all-done.5.rows_in_ref
  153.6 1.7 unpack_scores.1
  155.2 3.5 %all-to-all-start.6 = ((bf16[4,3,64,256]{3,2,1,0:T(8,128)(2,1)}), bf16[4,3,64,256]{3,2,1,0:T(8,128)(2,1)S(1)}, u32[]{:S(2)}, u32[]{:S(2)}) async-start(bf16[4,3,64,256]{3,2,1,0:T(8,128)(2,1)} %unpack_scores.1), calls=%async_computation.6 | async-start | bytes 786432 | tf_op jit(solution)/shard_map/all_to_all | solution.py:21
  158.7 2.9 %collective-permute-start.5 = (bf16[4,64,384]{2,1,0:T(8,128)(2,1)}, bf16[4,64,384]{2,1,0:T(8,128)(2,1)S(1)}, u32[]{:S(2)}, u32[]{:S(2)}) collective-permute-start(bf16[4,64,384]{2,1,0:T(8,128)(2,1)} %get-tuple-element.61), channel_id=1, source_target_pairs={{0,2},{1,3},{2,0},{3,1},{4,6},{5,7},{6,4},{7,5},{8,10},{9,11},{10,... | collective-permute-start | bytes 589832 | tf_op jit(solution)/shard_map/ppermute | solution.py:26
  161.7 3.9 %collective-permute-start.6 = (bf16[4,64,384]{2,1,0:T(8,128)(2,1)}, bf16[4,64,384]{2,1,0:T(8,128)(2,1)}, u32[]{:S(2)}, u32[]{:S(2)}) collective-permute-start(bf16[4,64,384]{2,1,0:T(8,128)(2,1)} %get-tuple-element.62), channel_id=1, source_target_pairs={{0,3},{1,0},{2,1},{3,2},{4,7},{5,4},{6,5},{7,6},{8,11},{9,8},{10,9... | collective-permute-start | bytes 589832 | tf_op jit(solution)/shard_map/ppermute | solution.py:26
  165.6 2.1 grad_query.1
  167.7 0.0 copy-start.1
  167.7 0.0 copy-start.3
  167.7 1.0 collective-permute-done.5.two_ref
  168.7 1.3 collective-permute-done.6.three_ref
  170.0 3.5 %all-to-all-start.7 = ((bf16[4,4,64,384]{3,2,1,0:T(8,128)(2,1)}), bf16[4,4,64,384]{3,2,1,0:T(8,128)(2,1)S(1)}, u32[]{:S(2)}, u32[]{:S(2)}) async-start(bf16[4,4,64,384]{3,2,1,0:T(8,128)(2,1)} %grad_query.1), calls=%async_computation.7 | async-start | bytes 1572864 | tf_op jit(solution)/shard_map/all_to_all | solution.py:21
  173.5 3.8 %collective-permute-start.13 = (bf16[4,64,384]{2,1,0:T(8,128)(2,1)S(1)}, bf16[4,64,384]{2,1,0:T(8,128)(2,1)S(1)}, u32[]{:S(2)}, u32[]{:S(2)}) collective-permute-start(bf16[4,64,384]{2,1,0:T(8,128)(2,1)S(1)} %copy-done.10), channel_id=1, source_target_pairs={{0,12},{4,0},{8,4},{12,8},{1,13},{5,1},{9,5},{13,9},{2,14},{6,2},{... | collective-permute-start | bytes 589832 | tf_op jit(solution)/shard_map/ppermute | solution.py:26
  177.3 2.5 %collective-permute-start.14 = (bf16[4,64,384]{2,1,0:T(8,128)(2,1)S(1)}, bf16[4,64,384]{2,1,0:T(8,128)(2,1)S(1)}, u32[]{:S(2)}, u32[]{:S(2)}) collective-permute-start(bf16[4,64,384]{2,1,0:T(8,128)(2,1)S(1)} %copy-done.9), channel_id=1, source_target_pairs={{0,8},{4,12},{8,0},{12,4},{1,9},{5,13},{9,1},{13,5},{2,10},{6,14},... | collective-permute-start | bytes 589832 | tf_op jit(solution)/shard_map/ppermute | solution.py:26
  179.8 2.5 %collective-permute-start.15 = (bf16[4,64,384]{2,1,0:T(8,128)(2,1)S(1)}, bf16[4,64,384]{2,1,0:T(8,128)(2,1)S(1)}, u32[]{:S(2)}, u32[]{:S(2)}) collective-permute-start(bf16[4,64,384]{2,1,0:T(8,128)(2,1)S(1)} %copy-done.8), channel_id=1, source_target_pairs={{0,4},{4,8},{8,12},{12,0},{1,5},{5,9},{9,13},{13,1},{2,6},{6,10},{... | collective-permute-start | bytes 589832 | tf_op jit(solution)/shard_map/ppermute | solution.py:26
  182.4 1.5 grad_key.1
  183.9 4.1 %collective-permute-start.9 = (bf16[4,64,384]{2,1,0:T(8,128)(2,1)}, bf16[4,64,384]{2,1,0:T(8,128)(2,1)S(1)}, u32[]{:S(2)}, u32[]{:S(2)}) collective-permute-start(bf16[4,64,384]{2,1,0:T(8,128)(2,1)} %get-tuple-element.75), channel_id=1, source_target_pairs={{0,12},{4,0},{8,4},{12,8},{1,13},{5,1},{9,5},{13,9},{2,14},{6,2},{... | collective-permute-start | bytes 589832 | tf_op jit(solution)/shard_map/ppermute | solution.py:26
  188.0 3.1 %collective-permute-start.10 = (bf16[4,64,384]{2,1,0:T(8,128)(2,1)}, bf16[4,64,384]{2,1,0:T(8,128)(2,1)S(1)}, u32[]{:S(2)}, u32[]{:S(2)}) collective-permute-start(bf16[4,64,384]{2,1,0:T(8,128)(2,1)} %get-tuple-element.76), channel_id=1, source_target_pairs={{0,8},{4,12},{8,0},{12,4},{1,9},{5,13},{9,1},{13,5},{2,10},{6,14},... | collective-permute-start | bytes 589832 | tf_op jit(solution)/shard_map/ppermute | solution.py:26
  191.1 1.9 collective-permute-start.11
  193.1 0.1 total_grad_value.1.own_ref
  193.2 24.3 %collective-permute-start.16 = (bf16[4,64,384]{2,1,0:T(8,128)(2,1)S(1)}, bf16[4,64,384]{2,1,0:T(8,128)(2,1)S(1)}, u32[]{:S(2)}, u32[]{:S(2)}) collective-permute-start(bf16[4,64,384]{2,1,0:T(8,128)(2,1)S(1)} %total_grad_value.1.own_ref), channel_id=1, source_target_pairs={{0,16},{16,0},{1,17},{17,1},{2,18},{18,2},{3,19},{19,3},{4,20},{20... | collective-permute-start | bytes 589832 | tf_op jit(solution)/shard_map/ppermute | solution.py:26
  217.5 1.1 total_attended.1.own_ref
  218.6 1.9 collective-permute-start.7
  220.6 0.1 total_grad_key.1.own_ref
  220.7 3.7 %collective-permute-start.12 = (bf16[4,64,384]{2,1,0:T(8,128)(2,1)S(1)}, bf16[4,64,384]{2,1,0:T(8,128)(2,1)S(1)}, u32[]{:S(2)}, u32[]{:S(2)}) collective-permute-start(bf16[4,64,384]{2,1,0:T(8,128)(2,1)S(1)} %total_grad_key.1.own_ref), channel_id=1, source_target_pairs={{0,16},{16,0},{1,17},{17,1},{2,18},{18,2},{3,19},{19,3},{4,20},{20... | collective-permute-start | bytes 589832 | tf_op jit(solution)/shard_map/ppermute | solution.py:26
  224.4 0.1 total_grad_query.1.own_ref
  224.5 1.9 collective-permute-start.8
  226.5 1.3 finish_grad_value.1
  227.8 1.7 finish_mixed.1
  229.5 1.3 finish_grad_key.1
  230.9 1.3 finish_grad_query.1
  (34 shorter events, 0.2 us)
Async XLA Ops:
  4.3 31.1 %all-to-all-start = ((bf16[8,4,64,384]{3,2,1,0:T(8,128)(2,1)}), bf16[8,4,64,384]{3,2,1,0:T(8,128)(2,1)S(1)}, u32[]{:S(2)}, u32[]{:S(2)}) async-start(bf16[8,4,64,384]{3,2,1,0:T(8,128)(2,1)} %bitcast.5), calls=%async_computation | async-start | bytes 3145728 | tf_op jit(solution)/shard_map/all_to_all | solution.py:21
  14.7 3.3 %collective-permute-start = (bf16[4,64,384]{2,1,0:T(8,128)(2,1)S(1)}, bf16[4,64,384]{2,1,0:T(8,128)(2,1)S(1)}, u32[]{:S(2)}, u32[]{:S(2)}) collective-permute-start(bf16[4,64,384]{2,1,0:T(8,128)(2,1)S(1)} %get-tuple-element.42), channel_id=1, source_target_pairs={{0,16},{16,0},{1,17},{17,1},{2,18},{18,2},{3,19},{19,3},{4,20},{20... | collective-permute-start | bytes 589832 | tf_op jit(solution)/shard_map/ppermute | solution.py:26
  37.5 19.8 %all-to-all-start.1 = ((f32[4,3,64,256]{3,2,1,0:T(8,128)}), f32[4,3,64,256]{3,2,1,0:T(8,128)}, u32[]{:S(2)}, u32[]{:S(2)}) async-start(f32[4,3,64,256]{3,2,1,0:T(8,128)} %logits.1), calls=%async_computation.1 | async-start | bytes 1572864 | tf_op jit(solution)/shard_map/all_to_all | solution.py:21
  59.2 22.4 %all-to-all-start.2 = ((f32[16,24,128]{2,1,0:T(8,128)}), f32[16,24,128]{2,1,0:T(8,128)S(1)}, u32[]{:S(2)}, u32[]{:S(2)}) async-start(f32[16,24,128]{2,1,0:T(8,128)} %logit_rows.1), calls=%async_computation.2 | async-start | bytes 393216 | tf_op jit(solution)/shard_map/all_to_all | solution.py:21
  82.4 21.4 %all-to-all-start.3 = ((bf16[16,24,128]{2,1,0:T(8,128)(2,1)}), bf16[16,24,128]{2,1,0:T(8,128)(2,1)S(1)}, u32[]{:S(2)}, u32[]{:S(2)}) async-start(bf16[16,24,128]{2,1,0:T(8,128)(2,1)} %get-tuple-element.56), calls=%async_computation.3 | async-start | bytes 196608 | tf_op jit(solution)/shard_map/all_to_all | solution.py:21
  87.5 10.5 %collective-permute-start.1 = (f32[3,64,256]{2,1,0:T(8,128)}, f32[3,64,256]{2,1,0:T(8,128)S(1)}, u32[]{:S(2)}, u32[]{:S(2)}) collective-permute-start(f32[3,64,256]{2,1,0:T(8,128)} %get-tuple-element.51), channel_id=1, source_target_pairs={{0,32},{32,64},{64,96},{96,0},{1,33},{33,65},{65,97},{97,1},{2,34}... | collective-permute-start | bytes 589832 | tf_op jit(solution)/shard_map/ppermute | solution.py:26
  90.6 8.4 %collective-permute-start.2 = (f32[3,64,256]{2,1,0:T(8,128)}, f32[3,64,256]{2,1,0:T(8,128)S(1)}, u32[]{:S(2)}, u32[]{:S(2)}) collective-permute-start(f32[3,64,256]{2,1,0:T(8,128)} %get-tuple-element.52), channel_id=1, source_target_pairs={{0,64},{32,96},{64,0},{96,32},{1,65},{33,97},{65,1},{97,33},{2,66}... | collective-permute-start | bytes 589832 | tf_op jit(solution)/shard_map/ppermute | solution.py:26
  95.3 6.9 %collective-permute-start.3 = (f32[3,64,256]{2,1,0:T(8,128)}, f32[3,64,256]{2,1,0:T(8,128)S(1)}, u32[]{:S(2)}, u32[]{:S(2)}) collective-permute-start(f32[3,64,256]{2,1,0:T(8,128)} %get-tuple-element.53), channel_id=1, source_target_pairs={{0,96},{32,0},{64,32},{96,64},{1,97},{33,1},{65,33},{97,65},{2,98}... | collective-permute-start | bytes 589832 | tf_op jit(solution)/shard_map/ppermute | solution.py:26
  102.2 0.9 copy-start.6
  103.8 23.7 %all-to-all-start.4 = ((f32[16,24,128]{2,1,0:T(8,128)}), f32[16,24,128]{2,1,0:T(8,128)}, u32[]{:S(2)}, u32[]{:S(2)}) async-start(f32[16,24,128]{2,1,0:T(8,128)} %grad_rows.1), calls=%async_computation.4 | async-start | bytes 393216 | tf_op jit(solution)/shard_map/all_to_all | solution.py:21
  127.5 0.8 copy-start.7
  130.0 23.5 %all-to-all-start.5 = ((bf16[16,24,128]{2,1,0:T(8,128)(2,1)}), bf16[16,24,128]{2,1,0:T(8,128)(2,1)}, u32[]{:S(2)}, u32[]{:S(2)}) async-start(bf16[16,24,128]{2,1,0:T(8,128)(2,1)} %scores.1), calls=%async_computation.5 | async-start | bytes 196608 | tf_op jit(solution)/shard_map/all_to_all | solution.py:21
  141.6 9.7 %collective-permute-start.4 = (bf16[4,64,384]{2,1,0:T(8,128)(2,1)}, bf16[4,64,384]{2,1,0:T(8,128)(2,1)S(1)}, u32[]{:S(2)}, u32[]{:S(2)}) collective-permute-start(bf16[4,64,384]{2,1,0:T(8,128)(2,1)} %get-tuple-element.60), channel_id=1, source_target_pairs={{0,1},{1,2},{2,3},{3,0},{4,5},{5,6},{6,7},{7,4},{8,9},{9,10},{10,1... | collective-permute-start | bytes 589832 | tf_op jit(solution)/shard_map/ppermute | solution.py:26
  151.3 0.7 copy-start.2
  155.2 10.4 %all-to-all-start.6 = ((bf16[4,3,64,256]{3,2,1,0:T(8,128)(2,1)}), bf16[4,3,64,256]{3,2,1,0:T(8,128)(2,1)S(1)}, u32[]{:S(2)}, u32[]{:S(2)}) async-start(bf16[4,3,64,256]{3,2,1,0:T(8,128)(2,1)} %unpack_scores.1), calls=%async_computation.6 | async-start | bytes 786432 | tf_op jit(solution)/shard_map/all_to_all | solution.py:21
  158.7 14.8 %copy-start.10 = (bf16[4,64,384]{2,1,0:T(8,128)(2,1)S(1)}, bf16[4,64,384]{2,1,0:T(8,128)(2,1)}, u32[]{:S(2)}) copy-start(bf16[4,64,384]{2,1,0:T(8,128)(2,1)} %get-tuple-element.65) | copy-start | bytes 589828
  158.7 18.6 %copy-start.9 = (bf16[4,64,384]{2,1,0:T(8,128)(2,1)S(1)}, bf16[4,64,384]{2,1,0:T(8,128)(2,1)}, u32[]{:S(2)}) copy-start(bf16[4,64,384]{2,1,0:T(8,128)(2,1)} %get-tuple-element.66) | copy-start | bytes 589828
  158.7 21.1 %copy-start.8 = (bf16[4,64,384]{2,1,0:T(8,128)(2,1)S(1)}, bf16[4,64,384]{2,1,0:T(8,128)(2,1)}, u32[]{:S(2)}) copy-start(bf16[4,64,384]{2,1,0:T(8,128)(2,1)} %get-tuple-element.67) | copy-start | bytes 589828
  158.7 9.9 %collective-permute-start.5 = (bf16[4,64,384]{2,1,0:T(8,128)(2,1)}, bf16[4,64,384]{2,1,0:T(8,128)(2,1)S(1)}, u32[]{:S(2)}, u32[]{:S(2)}) collective-permute-start(bf16[4,64,384]{2,1,0:T(8,128)(2,1)} %get-tuple-element.61), channel_id=1, source_target_pairs={{0,2},{1,3},{2,0},{3,1},{4,6},{5,7},{6,4},{7,5},{8,10},{9,11},{10,... | collective-permute-start | bytes 589832 | tf_op jit(solution)/shard_map/ppermute | solution.py:26
  161.7 8.3 %collective-permute-start.6 = (bf16[4,64,384]{2,1,0:T(8,128)(2,1)}, bf16[4,64,384]{2,1,0:T(8,128)(2,1)}, u32[]{:S(2)}, u32[]{:S(2)}) collective-permute-start(bf16[4,64,384]{2,1,0:T(8,128)(2,1)} %get-tuple-element.62), channel_id=1, source_target_pairs={{0,3},{1,0},{2,1},{3,2},{4,7},{5,4},{6,5},{7,6},{8,11},{9,8},{10,9... | collective-permute-start | bytes 589832 | tf_op jit(solution)/shard_map/ppermute | solution.py:26
  167.7 25.4 %copy-start.4 = (bf16[4,64,384]{2,1,0:T(8,128)(2,1)S(1)}, bf16[4,64,384]{2,1,0:T(8,128)(2,1)}, u32[]{:S(2)}) copy-start(bf16[4,64,384]{2,1,0:T(8,128)(2,1)} %get-tuple-element.64.zero_ref) | copy-start | bytes 589828
  167.7 49.8 %copy-start.1 = (bf16[4,64,384]{2,1,0:T(8,128)(2,1)S(1)}, bf16[4,64,384]{2,1,0:T(8,128)(2,1)}, u32[]{:S(2)}) copy-start(bf16[4,64,384]{2,1,0:T(8,128)(2,1)} %get-tuple-element.69.zero_ref) | copy-start | bytes 589828
  167.7 49.8 %copy-start.3 = (bf16[4,64,384]{2,1,0:T(8,128)(2,1)S(1)}, bf16[4,64,384]{2,1,0:T(8,128)(2,1)}, u32[]{:S(2)}) copy-start(bf16[4,64,384]{2,1,0:T(8,128)(2,1)} %copy-done.2) | copy-start | bytes 589828
  170.0 54.4 %all-to-all-start.7 = ((bf16[4,4,64,384]{3,2,1,0:T(8,128)(2,1)}), bf16[4,4,64,384]{3,2,1,0:T(8,128)(2,1)S(1)}, u32[]{:S(2)}, u32[]{:S(2)}) async-start(bf16[4,4,64,384]{3,2,1,0:T(8,128)(2,1)} %grad_query.1), calls=%async_computation.7 | async-start | bytes 1572864 | tf_op jit(solution)/shard_map/all_to_all | solution.py:21
  173.5 17.6 %collective-permute-start.13 = (bf16[4,64,384]{2,1,0:T(8,128)(2,1)S(1)}, bf16[4,64,384]{2,1,0:T(8,128)(2,1)S(1)}, u32[]{:S(2)}, u32[]{:S(2)}) collective-permute-start(bf16[4,64,384]{2,1,0:T(8,128)(2,1)S(1)} %copy-done.10), channel_id=1, source_target_pairs={{0,12},{4,0},{8,4},{12,8},{1,13},{5,1},{9,5},{13,9},{2,14},{6,2},{... | collective-permute-start | bytes 589832 | tf_op jit(solution)/shard_map/ppermute | solution.py:26
  177.3 15.7 %collective-permute-start.14 = (bf16[4,64,384]{2,1,0:T(8,128)(2,1)S(1)}, bf16[4,64,384]{2,1,0:T(8,128)(2,1)S(1)}, u32[]{:S(2)}, u32[]{:S(2)}) collective-permute-start(bf16[4,64,384]{2,1,0:T(8,128)(2,1)S(1)} %copy-done.9), channel_id=1, source_target_pairs={{0,8},{4,12},{8,0},{12,4},{1,9},{5,13},{9,1},{13,5},{2,10},{6,14},... | collective-permute-start | bytes 589832 | tf_op jit(solution)/shard_map/ppermute | solution.py:26
  179.8 13.2 %collective-permute-start.15 = (bf16[4,64,384]{2,1,0:T(8,128)(2,1)S(1)}, bf16[4,64,384]{2,1,0:T(8,128)(2,1)S(1)}, u32[]{:S(2)}, u32[]{:S(2)}) collective-permute-start(bf16[4,64,384]{2,1,0:T(8,128)(2,1)S(1)} %copy-done.8), channel_id=1, source_target_pairs={{0,4},{4,8},{8,12},{12,0},{1,5},{5,9},{9,13},{13,1},{2,6},{6,10},{... | collective-permute-start | bytes 589832 | tf_op jit(solution)/shard_map/ppermute | solution.py:26
  183.9 36.7 %copy-start.5 = (bf16[4,64,384]{2,1,0:T(8,128)(2,1)S(1)}, bf16[4,64,384]{2,1,0:T(8,128)(2,1)}, u32[]{:S(2)}) copy-start(bf16[4,64,384]{2,1,0:T(8,128)(2,1)} %get-tuple-element.74.zero_ref) | copy-start | bytes 589828
  183.9 36.6 %collective-permute-start.9 = (bf16[4,64,384]{2,1,0:T(8,128)(2,1)}, bf16[4,64,384]{2,1,0:T(8,128)(2,1)S(1)}, u32[]{:S(2)}, u32[]{:S(2)}) collective-permute-start(bf16[4,64,384]{2,1,0:T(8,128)(2,1)} %get-tuple-element.75), channel_id=1, source_target_pairs={{0,12},{4,0},{8,4},{12,8},{1,13},{5,1},{9,5},{13,9},{2,14},{6,2},{... | collective-permute-start | bytes 589832 | tf_op jit(solution)/shard_map/ppermute | solution.py:26
  188.0 32.6 %collective-permute-start.10 = (bf16[4,64,384]{2,1,0:T(8,128)(2,1)}, bf16[4,64,384]{2,1,0:T(8,128)(2,1)S(1)}, u32[]{:S(2)}, u32[]{:S(2)}) collective-permute-start(bf16[4,64,384]{2,1,0:T(8,128)(2,1)} %get-tuple-element.76), channel_id=1, source_target_pairs={{0,8},{4,12},{8,0},{12,4},{1,9},{5,13},{9,1},{13,5},{2,10},{6,14},... | collective-permute-start | bytes 589832 | tf_op jit(solution)/shard_map/ppermute | solution.py:26
  191.1 29.4 %collective-permute-start.11 = (bf16[4,64,384]{2,1,0:T(8,128)(2,1)}, bf16[4,64,384]{2,1,0:T(8,128)(2,1)S(1)}, u32[]{:S(2)}, u32[]{:S(2)}) collective-permute-start(bf16[4,64,384]{2,1,0:T(8,128)(2,1)} %get-tuple-element.77), channel_id=1, source_target_pairs={{0,4},{4,8},{8,12},{12,0},{1,5},{5,9},{9,13},{13,1},{2,6},{6,10},{... | collective-permute-start | bytes 589832 | tf_op jit(solution)/shard_map/ppermute | solution.py:26
  193.2 34.6 %copy-start = (bf16[384,768]{1,0:T(8,128)(2,1)S(1)}, bf16[384,768]{1,0:T(8,128)(2,1)}, u32[]{:S(2)}) copy-start(bf16[384,768]{1,0:T(8,128)(2,1)} %w_ref.1) | copy-start | bytes 1769476
  193.2 33.3 %collective-permute-start.16 = (bf16[4,64,384]{2,1,0:T(8,128)(2,1)S(1)}, bf16[4,64,384]{2,1,0:T(8,128)(2,1)S(1)}, u32[]{:S(2)}, u32[]{:S(2)}) collective-permute-start(bf16[4,64,384]{2,1,0:T(8,128)(2,1)S(1)} %total_grad_value.1.own_ref), channel_id=1, source_target_pairs={{0,16},{16,0},{1,17},{17,1},{2,18},{18,2},{3,19},{19,3},{4,20},{20... | collective-permute-start | bytes 589832 | tf_op jit(solution)/shard_map/ppermute | solution.py:26
  218.6 9.2 %collective-permute-start.7 = (bf16[4,64,384]{2,1,0:T(8,128)(2,1)S(1)}, bf16[4,64,384]{2,1,0:T(8,128)(2,1)S(1)}, u32[]{:S(2)}, u32[]{:S(2)}) collective-permute-start(bf16[4,64,384]{2,1,0:T(8,128)(2,1)S(1)} %total_attended.1.own_ref), channel_id=1, source_target_pairs={{0,16},{16,0},{1,17},{17,1},{2,18},{18,2},{3,19},{19,3},{4,20},{20... | collective-permute-start | bytes 589832 | tf_op jit(solution)/shard_map/ppermute | solution.py:26
  220.7 8.8 %collective-permute-start.12 = (bf16[4,64,384]{2,1,0:T(8,128)(2,1)S(1)}, bf16[4,64,384]{2,1,0:T(8,128)(2,1)S(1)}, u32[]{:S(2)}, u32[]{:S(2)}) collective-permute-start(bf16[4,64,384]{2,1,0:T(8,128)(2,1)S(1)} %total_grad_key.1.own_ref), channel_id=1, source_target_pairs={{0,16},{16,0},{1,17},{17,1},{2,18},{18,2},{3,19},{19,3},{4,20},{20... | collective-permute-start | bytes 589832 | tf_op jit(solution)/shard_map/ppermute | solution.py:26
  224.5 6.3 %collective-permute-start.8 = (bf16[4,64,384]{2,1,0:T(8,128)(2,1)S(1)}, bf16[4,64,384]{2,1,0:T(8,128)(2,1)S(1)}, u32[]{:S(2)}, u32[]{:S(2)}) collective-permute-start(bf16[4,64,384]{2,1,0:T(8,128)(2,1)S(1)} %total_grad_query.1.own_ref), channel_id=1, source_target_pairs={{0,16},{16,0},{1,17},{17,1},{2,18},{18,2},{3,19},{19,3},{4,20},{20... | collective-permute-start | bytes 589832 | tf_op jit(solution)/shard_map/ppermute | solution.py:26

commit v10 on v7

--- a/solution.py
+++ b/solution.py
@@ -34,7 +34,9 @@
     )
 
 
-def pack_kernel(place_ref, q_hbm, k_hbm, v_hbm, w_hbm, go_hbm, own_ref, send_ref, right_ref, q_ref, k_ref, v_ref, w_ref, go_ref, sems):
+def pack_kernel(
+    place_ref, q_hbm, k_hbm, v_hbm, w_hbm, go_hbm, own_ref, send_ref, right_hbm, q_ref, k_ref, v_ref, w_ref, go_ref, kv_ref, sems
+):
     loads = [
         pltpu.make_async_copy(src, dst, sems.at[n])
         for n, (src, dst) in enumerate(
@@ -44,13 +46,14 @@
     for load in loads:
         load.start()
     first = place_ref[0] == 0
+    seqs, res, _ = q_ref.shape
     loads[0].wait()
     loads[1].wait()
-    seqs, res, _ = q_ref.shape
     for s in range(seqs):
-        for core, part in enumerate(halves(k_ref[s], v_ref[s])):
-            for n in range(right_ref.shape[0]):
-                right_ref[n, core, s] = part
+        kv_ref[0, s], kv_ref[1, s] = halves(k_ref[s], v_ref[s])
+    stores = [pltpu.make_async_copy(kv_ref, right_hbm.at[n], sems.at[5 + n]) for n in range(4)]
+    for store in stores:
+        store.start()
     for load in loads[2:]:
         load.wait()
     grads = lax.dot_general(
@@ -63,6 +66,8 @@
         low, high = halves(q_ref[s], grads[s * res : (s + 1) * res])
         own_ref[s] = jnp.where(first, low, high)
         send_ref[s] = jnp.where(first, high, low)
+    for store in stores:
+        store.wait()
 
 
 def slab(blocks, p):
@@ -135,39 +140,52 @@
         out_ref[n] = full
 
 
-def output_kernel(scale, place_ref, mats_ref, own_ref, other_ref, right_ref, row_hbm, *refs):
-    col_hbms, row_ref, col_ref, sems = refs[:4], refs[4], refs[5], refs[6]
-    seqs, res = own_ref.shape[1:3]
-
-    def put(ref, value, p):
-        for n in range(4):
-            for slot in range(2):
-                for s in range(seqs):
-                    at = (slot * seqs + s) * 128
-                    ref[n, slot, s, :, p * 128 : p * 128 + 128] = value[n * res : (n + 1) * res, at : at + 128]
-
-    def product(side, contract, p):
-        mats = [mats_ref[:, 2 * p + parity].reshape(256, 256) for parity in range(2)]
-        even, odd = (
-            lax.dot_general(m, side, (((contract,), (0,)), ((), ())), preferred_element_type=F32) for m in mats
+def product(mats_ref, p, side, contract, scale):
+    even, odd = (
+        lax.dot_general(
+            mats_ref[:, j].reshape(256, 256), side, (((contract,), (0,)), ((), ())), preferred_element_type=F32
         )
-        if 2 * p < 3:
-            even = even * scale
-        if 2 * p + 1 < 3:
-            odd = odd * scale
-        return jnp.where(odd_chunk(even.shape), odd, even).astype(BF16)
-
-    for p in range(3):
-        put(row_ref, product(slab(rights(place_ref, right_ref), p), 1, p), p)
-    row_copy = pltpu.make_async_copy(row_ref, row_hbm, sems.at[4])
-    row_copy.start()
-    for p in range(3):
-        put(col_ref, product(slab(lefts(own_ref, other_ref), p), 0, p), p)
-    col_copies = [pltpu.make_async_copy(col_ref.at[n], col_hbms[n], sems.at[n]) for n in range(4)]
-    for copy in col_copies:
+        for j in (2 * p, 2 * p + 1)
+    )
+    if 2 * p < 3:
+        even = even * scale
+    if 2 * p + 1 < 3:
+        odd = odd * scale
+    return jnp.where(odd_chunk(even.shape), odd, even).astype(BF16)
+
+
+def put(refs, value, p):
+    for n, ref in enumerate(refs):
+        seqs, res, _ = ref.shape
+        for s in range(seqs):
+            ref[s, :, p * 128 : p * 128 + 128] = value[n * res : (n + 1) * res, s * 128 : s * 128 + 128]
+
+
+def row_kernel(scale, place_ref, mats_ref, right_ref, row_hbm, mats_hbm, row_ref, sems):
+    handed = pltpu.make_async_copy(mats_ref, mats_hbm, sems.at[2])
+    handed.start()
+    copies = [pltpu.make_async_copy(row_ref.at[:, slot], row_hbm.at[:, slot], sems.at[slot]) for slot in range(2)]
+    blocks = rights(place_ref, right_ref)
+    for slot in range(2):
+        for p in range(3):
+            side = slab([(pair[slot],) for pair in blocks], p)
+            put([row_ref.at[n, slot] for n in range(4)], product(mats_ref, p, side, 1, scale), p)
+        copies[slot].start()
+    handed.wait()
+    for copy in copies:
+        copy.wait()
+
+
+def col_kernel(scale, mats_ref, own_ref, other_ref, *refs):
+    col_hbms, col_ref, sems = refs[:4], refs[4], refs[5]
+    for slot, ref in enumerate((own_ref, other_ref)):
+        for p in range(3):
+            side = slab([(ref.at[n],) for n in range(4)], p)
+            put([col_ref.at[n, slot] for n in range(4)], product(mats_ref, p, side, 0, scale), p)
+    copies = [pltpu.make_async_copy(col_ref.at[n], col_hbms[n], sems.at[n]) for n in range(4)]
+    for copy in copies:
         copy.start()
-    row_copy.wait()
-    for copy in col_copies:
+    for copy in copies:
         copy.wait()
 
 
@@ -198,10 +216,12 @@
 
 
 def finish_rows_kernel(place_ref, keep_ref, got_ref, w_ref, mixed_ref, gq_ref):
-    first = place_ref[0] == 0
-    for s in range(keep_ref.shape[0]):
-        gq_ref[s], attended = unpacked(first, keep_ref[s], got_ref[s])
-        mixed_ref[s] = jnp.dot(attended, w_ref[...], preferred_element_type=F32).astype(BF16)
+    seqs, res, width = keep_ref.shape
+    keep, got = keep_ref[...].reshape(seqs * res, width), got_ref[...].reshape(seqs * res, width)
+    grad_query, attended = unpacked(place_ref[0] == 0, keep, got)
+    gq_ref[...] = grad_query.reshape(seqs, res, width)
+    mixed = jnp.dot(attended, w_ref[...], preferred_element_type=F32).astype(BF16)
+    mixed_ref[...] = mixed.reshape(mixed_ref.shape)
 
 
 def on_device(queries, keys, values, out_weight, grad_out):
@@ -221,10 +241,10 @@
     own, send, right = pl.pallas_call(
         pack_kernel,
         in_specs=[smem] + [hbm] * 5,
-        out_specs=[vmem] * 3,
-        out_shape=(array(block), array(block), array((4, 2) + block)),
+        out_specs=[vmem, vmem, hbm],
+        out_shape=(array(block), array(block), pltpu.HBM((4, 2) + block, BF16)),
         scratch_shapes=[pltpu.VMEM(a.shape, BF16) for a in (queries, keys, values, out_weight, grad_out)]
-        + [pltpu.SemaphoreType.DMA((5,))],
+        + [pltpu.VMEM((2,) + block, BF16), pltpu.SemaphoreType.DMA((9,))],
         compiler_params=params(),
         name="pack",
     )(place, *(pltpu.with_memory_space_constraint(arg, pltpu.HBM) for arg in args))
@@ -261,15 +281,24 @@
     )(mats)
     mats = exchange(mats, "y")
 
-    row, *cols = pl.pallas_call(
-        lambda *refs: output_kernel(scale, *refs),
-        in_specs=[smem] + [vmem] * 4,
-        out_specs=[hbm] * 5,
-        out_shape=(pltpu.HBM((4, 2) + block, BF16),) + (pltpu.HBM((2,) + block, BF16),) * 4,
-        scratch_shapes=[pltpu.VMEM((4, 2) + block, BF16)] * 2 + [pltpu.SemaphoreType.DMA((5,))],
-        compiler_params=params(),
-        name="outputs",
-    )(place, mats, own, other, right)
+    row, mats = pl.pallas_call(
+        lambda *refs: row_kernel(scale, *refs),
+        in_specs=[smem] + [vmem] * 2,
+        out_specs=[hbm] * 2,
+        out_shape=(pltpu.HBM((4, 2) + block, BF16), pltpu.HBM(mats.shape, BF16)),
+        scratch_shapes=[pltpu.VMEM((4, 2) + block, BF16), pltpu.SemaphoreType.DMA((3,))],
+        compiler_params=params(),
+        name="row_products",
+    )(place, mats, right)
+    cols = pl.pallas_call(
+        lambda *refs: col_kernel(scale, *refs),
+        in_specs=[vmem] * 3,
+        out_specs=[hbm] * 4,
+        out_shape=(pltpu.HBM((2,) + block, BF16),) * 4,
+        scratch_shapes=[pltpu.VMEM((4, 2) + block, BF16), pltpu.SemaphoreType.DMA((4,))],
+        compiler_params=params(),
+        name="col_products",
+    )(mats, own, other)
     row = exchange(row, "zl")
     cols = [cols[0]] + [shift(cols[by], "x", -by) for by in (1, 2, 3)]
     keep, send = pl.pallas_call(
@@ -282,6 +311,7 @@
         compiler_params=params(),
         name="finish_columns",
     )(place, keep, shift(send, "c", 1))
+    row, grad_key, grad_value = lax.optimization_barrier((row, grad_key, grad_value))
     keep, send = pl.pallas_call(
         total_blocks_kernel, out_shape=(array(block), array(block)), compiler_params=params(), name="total_rows"
     )(row)

time: 184 us -> 182 us (0.989)
  the two profiles are of different devices: /device:TPU:3 before, /device:TPU:1 now
where the time goes in v10:
time: 182 us; the launch traced here: 181 us
  blocking collectives  109 us (60%)
  starting transfers between devices  43.5 us (24%)
  Pallas kernels  13.4 us (7%)
  waiting for transfers between devices  12.8 us (7%)
  local copies, waits for them, and re-layouts  2.13 us (1%)
    all_to_all x4, blocking collectives, exchange(): return lax.all_to_all(blocks, axis, 0, 0, tiled=True)  77.2 us
    ppermute x6, starting transfers between devices, shift(): return lax.ppermute(block, axis, [(i, (i + by) % n) for i in range(n)])  29 us
    all_gather x1, blocking collectives, on_device(): own = lax.all_gather(own, 'zl')  16.4 us
    all_gather x1, blocking collectives, on_device(): other = lax.all_gather(other, 'zl')  15.3 us
    all_to_all x2, starting transfers between devices, exchange(): return lax.all_to_all(blocks, axis, 0, 0, tiled=True)  14.5 us
    ppermute x6, waiting for transfers between devices, shift(): return lax.ppermute(block, axis, [(i, (i + by) % n) for i in range(n)])  12.8 us
  transfers between devices with their start and end apart: 8, of which 5 were waited for; matrix products, arithmetic and copies ran while one was open for 0% of the time, Pallas kernels for 2%

profile of v10, /device:TPU:1, one launch (start us, length us, event | category | flops | bytes accessed | tf_op | source)
XLA Modules:
  0.0 181.5 jit_solution(16321376007015142962)
XLA Ops:
  0.6 0.1 pad_add_fusion.place_ref.refs_0_
  0.7 3.0 %pack.1 = (bf16[4,64,384]{2,1,0:T(8,128)(2,1)S(1)}, bf16[4,64,384]{2,1,0:T(8,128)(2,1)S(1)}, bf16[4,2,4,64,384]{4,3,2,1,0:T(8,128)(2,1)}) custom-call(s32[2]{0:T(128)S(1)} %pad_add_fusion.place_ref.refs_0_, bf16[4,64,384]{2,1,0:T(8,128)(2,1)} %q_hbm.1, bf16[4,64,384]{2,1,0:T(8,128)(2,1)} %k_hbm.1, bf16[4,64,384]{2,1,0:T(8,128)(2,1)} %v_hbm.1, ...), custom_call_target="tpu_custom_call" | custom-call | tf_op jit(solution)/shard_map/pack/pallas_call | solution.py:241
  3.7 10.4 %all-to-all-start = ((bf16[8,4,64,384]{3,2,1,0:T(8,128)(2,1)}), bf16[8,4,64,384]{3,2,1,0:T(8,128)(2,1)S(1)}, u32[]{:S(2)}, u32[]{:S(2)}) async-start(bf16[8,4,64,384]{3,2,1,0:T(8,128)(2,1)} %bitcast.12), calls=%async_computation | async-start | bytes 3145728 | tf_op jit(solution)/shard_map/all_to_all | solution.py:21
  14.0 2.0 %collective-permute-start = (bf16[4,64,384]{2,1,0:T(8,128)(2,1)S(1)}, bf16[4,64,384]{2,1,0:T(8,128)(2,1)S(1)}, u32[]{:S(2)}, u32[]{:S(2)}) collective-permute-start(bf16[4,64,384]{2,1,0:T(8,128)(2,1)S(1)} %get-tuple-element.25), channel_id=1, source_target_pairs={{0,16},{16,0},{1,17},{17,1},{2,18},{18,2},{3,19},{19,3},{4,20},{20... | collective-permute-start | bytes 589832 | tf_op jit(solution)/shard_map/ppermute | solution.py:26
  16.1 16.4 %all-gather = bf16[16,64,384]{2,1,0:T(8,128)(2,1)S(1)} all-gather(bf16[4,64,384]{2,1,0:T(8,128)(2,1)S(1)} %get-tuple-element.24), channel_id=2, replica_groups=mesh['zh'=4,'y'=4,'c'=2,'x'=4,'zl'=4] {'zl'}, dimensions={0}, use_global_device_ids=true | all-gather | bytes 983040 | tf_op jit(solution)/shard_map/all_gather | solution.py:253
  32.5 0.0 collective-permute-done
  32.5 15.3 %all-gather.1 = bf16[16,64,384]{2,1,0:T(8,128)(2,1)S(1)} all-gather(bf16[4,64,384]{2,1,0:T(8,128)(2,1)S(1)} %collective-permute-done), channel_id=3, replica_groups=mesh['zh'=4,'y'=4,'c'=2,'x'=4,'zl'=4] {'zl'}, dimensions={0}, use_global_device_ids=true | all-gather | bytes 983040 | tf_op jit(solution)/shard_map/all_gather | solution.py:254
  47.8 0.0 all-to-all-done
  47.8 1.6 products.1
  49.3 18.7 %all_to_all.30.part_ref = f32[4,6,64,256]{3,2,1,0:T(8,128)S(1)} all-to-all(f32[4,6,64,256]{3,2,1,0:T(8,128)S(1)} %products.1), channel_id=1, replica_groups=mesh['zh'=4,'y'=4,'c'=2,'x'=4,'zl'=4] {'y'}, dimensions={0} | all-to-all | bytes 3145728 | tf_op jit(solution)/shard_map/all_to_all | solution.py:21
  68.1 0.1 rows.1
  68.2 25.3 %all_to_all.31.refs_0_ = f32[16,24,256]{2,1,0:T(8,128)S(1)} all-to-all(f32[16,24,256]{2,1,0:T(8,128)S(1)} %rows.1), channel_id=1, replica_groups=mesh['zh'=4,'y'=4,'c'=2,'x'=4,'zl'=4] {'zh','zl'}, dimensions={0} | all-to-all | bytes 786432 | tf_op jit(solution)/shard_map/all_to_all | solution.py:21
  93.5 0.3 softmax.1
  93.8 22.4 %all_to_all.32.mats_ref = bf16[16,48,128]{2,1,0:T(8,128)(2,1)S(1)} all-to-all(bf16[16,48,128]{2,1,0:T(8,128)(2,1)S(1)} %softmax.1), channel_id=1, replica_groups=mesh['zh'=4,'y'=4,'c'=2,'x'=4,'zl'=4] {'zh','zl'}, dimensions={0} | all-to-all | bytes 393216 | tf_op jit(solution)/shard_map/all_to_all | solution.py:21
  116.2 0.1 unpack.1
  116.3 10.7 %all_to_all.33.refs_1_ = bf16[4,6,64,256]{3,2,1,0:T(8,128)(2,1)S(1)} all-to-all(bf16[4,6,64,256]{3,2,1,0:T(8,128)(2,1)S(1)} %unpack.1), channel_id=1, replica_groups=mesh['zh'=4,'y'=4,'c'=2,'x'=4,'zl'=4] {'y'}, dimensions={0} | all-to-all | bytes 1572864 | tf_op jit(solution)/shard_map/all_to_all | solution.py:21
  127.0 2.6 %row_products.1 = (bf16[4,2,4,64,384]{4,3,2,1,0:T(8,128)(2,1)}, bf16[4,6,64,256]{3,2,1,0:T(8,128)(2,1)}) custom-call(s32[2]{0:T(128)S(1)} %pad_add_fusion.place_ref.refs_0_, bf16[4,6,64,256]{3,2,1,0:T(8,128)(2,1)S(1)} %all_to_all.33.refs_1_, bf16[4,2,4,64,384]{4,3,2,1,0:T(8,128)(2,1)S(1)} %bitcast.7), custom_call_target="tpu_custom_call" | custom-call | tf_op jit(solution)/shard_map/row_products/pallas_call | solution.py:284
  129.6 4.1 %all-to-all-start.5 = ((bf16[4,2,4,64,384]{4,3,2,1,0:T(8,128)(2,1)}), bf16[4,2,4,64,384]{4,3,2,1,0:T(8,128)(2,1)S(1)}, u32[]{:S(2)}, u32[]{:S(2)}) async-start(bf16[4,2,4,64,384]{4,3,2,1,0:T(8,128)(2,1)} %get-tuple-element.27), calls=%async_computation.5 | async-start | bytes 3145728 | tf_op jit(solution)/shard_map/all_to_all | solution.py:21
  133.7 0.0 copy-start.1
  133.7 1.1 copy-done.1
  134.9 2.3 %col_products.1 = (bf16[2,4,64,384]{3,2,1,0:T(8,128)(2,1)}, bf16[2,4,64,384]{3,2,1,0:T(8,128)(2,1)}, bf16[2,4,64,384]{3,2,1,0:T(8,128)(2,1)}, bf16[2,4,64,384]{3,2,1,0:T(8,128)(2,1)}) custom-call(bf16[4,6,64,256]{3,2,1,0:T(8,128)(2,1)S(1)} %copy-done.1, bf16[4,4,64,384]{3,2,1,0:T(8,128)(2,1)S(1)} %bitcast.9, bf16[4,4,64,384]{3,2,1,0:T(8,128)(2,1)S(1)} %bitcast.11), custom_call_target="tpu_custom_call" | custom-call | tf_op jit(solution)/shard_map/col_products/pallas_call | solution.py:293
  137.2 9.9 %collective-permute-start.1 = (bf16[2,4,64,384]{3,2,1,0:T(8,128)(2,1)}, bf16[2,4,64,384]{3,2,1,0:T(8,128)(2,1)S(1)}, u32[]{:S(2)}, u32[]{:S(2)}) collective-permute-start(bf16[2,4,64,384]{3,2,1,0:T(8,128)(2,1)} %get-tuple-element.30), channel_id=1, source_target_pairs={{0,12},{4,0},{8,4},{12,8},{1,13},{5,1},{9,5},{13,9},{2,14},{6,2},{... | collective-permute-start | bytes 1179656 | tf_op jit(solution)/shard_map/ppermute | solution.py:26
  147.0 2.5 %collective-permute-start.2 = (bf16[2,4,64,384]{3,2,1,0:T(8,128)(2,1)}, bf16[2,4,64,384]{3,2,1,0:T(8,128)(2,1)S(1)}, u32[]{:S(2)}, u32[]{:S(2)}) collective-permute-start(bf16[2,4,64,384]{3,2,1,0:T(8,128)(2,1)} %get-tuple-element.31), channel_id=1, source_target_pairs={{0,8},{4,12},{8,0},{12,4},{1,9},{5,13},{9,1},{13,5},{2,10},{6,14},... | collective-permute-start | bytes 1179656 | tf_op jit(solution)/shard_map/ppermute | solution.py:26
  149.5 2.5 %collective-permute-start.3 = (bf16[2,4,64,384]{3,2,1,0:T(8,128)(2,1)}, bf16[2,4,64,384]{3,2,1,0:T(8,128)(2,1)S(1)}, u32[]{:S(2)}, u32[]{:S(2)}) collective-permute-start(bf16[2,4,64,384]{3,2,1,0:T(8,128)(2,1)} %get-tuple-element.32), channel_id=1, source_target_pairs={{0,4},{4,8},{8,12},{12,0},{1,5},{5,9},{9,13},{13,1},{2,6},{6,10},{... | collective-permute-start | bytes 1179656 | tf_op jit(solution)/shard_map/ppermute | solution.py:26
  152.0 4.5 %collective-permute-done.1.one_ref = bf16[2,4,64,384]{3,2,1,0:T(8,128)(2,1)S(1)} collective-permute-done((bf16[2,4,64,384]{3,2,1,0:T(8,128)(2,1)}, bf16[2,4,64,384]{3,2,1,0:T(8,128)(2,1)S(1)}, u32[]{:S(2)}, u32[]{:S(2)}) %collective-permute-start.1) | collective-permute-done | bytes 393248 | tf_op jit(solution)/shard_map/ppermute | solution.py:26
  156.5 0.9 collective-permute-done.2.two_ref
  157.4 5.3 %collective-permute-done.3.three_ref = bf16[2,4,64,384]{3,2,1,0:T(8,128)(2,1)S(1)} collective-permute-done((bf16[2,4,64,384]{3,2,1,0:T(8,128)(2,1)}, bf16[2,4,64,384]{3,2,1,0:T(8,128)(2,1)S(1)}, u32[]{:S(2)}, u32[]{:S(2)}) %collective-permute-start.3) | collective-permute-done | bytes 393248 | tf_op jit(solution)/shard_map/ppermute | solution.py:26
  162.7 0.0 copy-start.2
  162.7 1.0 copy-done.2
  163.7 0.0 copy-start
  163.7 0.2 total_columns.1
  163.9 9.8 %collective-permute-start.4 = (bf16[4,64,384]{2,1,0:T(8,128)(2,1)S(1)}, bf16[4,64,384]{2,1,0:T(8,128)(2,1)S(1)}, u32[]{:S(2)}, u32[]{:S(2)}) collective-permute-start(bf16[4,64,384]{2,1,0:T(8,128)(2,1)S(1)} %get-tuple-element.34), channel_id=1, source_target_pairs={{0,16},{16,0},{1,17},{17,1},{2,18},{18,2},{3,19},{19,3},{4,20},{20... | collective-permute-start | bytes 589832 | tf_op jit(solution)/shard_map/ppermute | solution.py:26
  173.8 1.0 collective-permute-done.4.got_ref
  174.8 1.4 finish_columns.1
  176.2 0.0 all-to-all-done.5.part_ref
  176.2 0.2 total_rows.1
  176.4 2.3 %collective-permute-start.5 = (bf16[4,64,384]{2,1,0:T(8,128)(2,1)S(1)}, bf16[4,64,384]{2,1,0:T(8,128)(2,1)S(1)}, u32[]{:S(2)}, u32[]{:S(2)}) collective-permute-start(bf16[4,64,384]{2,1,0:T(8,128)(2,1)S(1)} %get-tuple-element.39), channel_id=1, source_target_pairs={{0,16},{16,0},{1,17},{17,1},{2,18},{18,2},{3,19},{19,3},{4,20},{20... | collective-permute-start | bytes 589832 | tf_op jit(solution)/shard_map/ppermute | solution.py:26
  178.7 1.0 collective-permute-done.5.got_ref
  179.8 0.0 copy-done
  179.8 1.7 finish_rows.1
Async XLA Ops:
  3.7 44.1 %all-to-all-start = ((bf16[8,4,64,384]{3,2,1,0:T(8,128)(2,1)}), bf16[8,4,64,384]{3,2,1,0:T(8,128)(2,1)S(1)}, u32[]{:S(2)}, u32[]{:S(2)}) async-start(bf16[8,4,64,384]{3,2,1,0:T(8,128)(2,1)} %bitcast.12), calls=%async_computation | async-start | bytes 3145728 | tf_op jit(solution)/shard_map/all_to_all | solution.py:21
  14.0 18.5 %collective-permute-start = (bf16[4,64,384]{2,1,0:T(8,128)(2,1)S(1)}, bf16[4,64,384]{2,1,0:T(8,128)(2,1)S(1)}, u32[]{:S(2)}, u32[]{:S(2)}) collective-permute-start(bf16[4,64,384]{2,1,0:T(8,128)(2,1)S(1)} %get-tuple-element.25), channel_id=1, source_target_pairs={{0,16},{16,0},{1,17},{17,1},{2,18},{18,2},{3,19},{19,3},{4,20},{20... | collective-permute-start | bytes 589832 | tf_op jit(solution)/shard_map/ppermute | solution.py:26
  129.6 46.6 %all-to-all-start.5 = ((bf16[4,2,4,64,384]{4,3,2,1,0:T(8,128)(2,1)}), bf16[4,2,4,64,384]{4,3,2,1,0:T(8,128)(2,1)S(1)}, u32[]{:S(2)}, u32[]{:S(2)}) async-start(bf16[4,2,4,64,384]{4,3,2,1,0:T(8,128)(2,1)} %get-tuple-element.27), calls=%async_computation.5 | async-start | bytes 3145728 | tf_op jit(solution)/shard_map/all_to_all | solution.py:21
  133.7 1.1 copy-start.1
  137.2 19.3 %collective-permute-start.1 = (bf16[2,4,64,384]{3,2,1,0:T(8,128)(2,1)}, bf16[2,4,64,384]{3,2,1,0:T(8,128)(2,1)S(1)}, u32[]{:S(2)}, u32[]{:S(2)}) collective-permute-start(bf16[2,4,64,384]{3,2,1,0:T(8,128)(2,1)} %get-tuple-element.30), channel_id=1, source_target_pairs={{0,12},{4,0},{8,4},{12,8},{1,13},{5,1},{9,5},{13,9},{2,14},{6,2},{... | collective-permute-start | bytes 1179656 | tf_op jit(solution)/shard_map/ppermute | solution.py:26
  147.0 10.3 %collective-permute-start.2 = (bf16[2,4,64,384]{3,2,1,0:T(8,128)(2,1)}, bf16[2,4,64,384]{3,2,1,0:T(8,128)(2,1)S(1)}, u32[]{:S(2)}, u32[]{:S(2)}) collective-permute-start(bf16[2,4,64,384]{3,2,1,0:T(8,128)(2,1)} %get-tuple-element.31), channel_id=1, source_target_pairs={{0,8},{4,12},{8,0},{12,4},{1,9},{5,13},{9,1},{13,5},{2,10},{6,14},... | collective-permute-start | bytes 1179656 | tf_op jit(solution)/shard_map/ppermute | solution.py:26
  149.5 13.2 %collective-permute-start.3 = (bf16[2,4,64,384]{3,2,1,0:T(8,128)(2,1)}, bf16[2,4,64,384]{3,2,1,0:T(8,128)(2,1)S(1)}, u32[]{:S(2)}, u32[]{:S(2)}) collective-permute-start(bf16[2,4,64,384]{3,2,1,0:T(8,128)(2,1)} %get-tuple-element.32), channel_id=1, source_target_pairs={{0,4},{4,8},{8,12},{12,0},{1,5},{5,9},{9,13},{13,1},{2,6},{6,10},{... | collective-permute-start | bytes 1179656 | tf_op jit(solution)/shard_map/ppermute | solution.py:26
  162.7 1.0 copy-start.2
  163.7 16.1 %copy-start = (bf16[384,768]{1,0:T(8,128)(2,1)S(1)}, bf16[384,768]{1,0:T(8,128)(2,1)}, u32[]{:S(2)}) copy-start(bf16[384,768]{1,0:T(8,128)(2,1)} %w_ref.1) | copy-start | bytes 1769476
  163.9 10.9 %collective-permute-start.4 = (bf16[4,64,384]{2,1,0:T(8,128)(2,1)S(1)}, bf16[4,64,384]{2,1,0:T(8,128)(2,1)S(1)}, u32[]{:S(2)}, u32[]{:S(2)}) collective-permute-start(bf16[4,64,384]{2,1,0:T(8,128)(2,1)S(1)} %get-tuple-element.34), channel_id=1, source_target_pairs={{0,16},{16,0},{1,17},{17,1},{2,18},{18,2},{3,19},{19,3},{4,20},{20... | collective-permute-start | bytes 589832 | tf_op jit(solution)/shard_map/ppermute | solution.py:26
  176.4 3.3 %collective-permute-start.5 = (bf16[4,64,384]{2,1,0:T(8,128)(2,1)S(1)}, bf16[4,64,384]{2,1,0:T(8,128)(2,1)S(1)}, u32[]{:S(2)}, u32[]{:S(2)}) collective-permute-start(bf16[4,64,384]{2,1,0:T(8,128)(2,1)S(1)} %get-tuple-element.39), channel_id=1, source_target_pairs={{0,16},{16,0},{1,17},{17,1},{2,18},{18,2},{3,19},{19,3},{4,20},{20... | collective-permute-start | bytes 589832 | tf_op jit(solution)/shard_map/ppermute | solution.py:26

commit v11 on v10

--- a/solution.py
+++ b/solution.py
@@ -176,13 +176,23 @@
         copy.wait()
 
 
-def col_kernel(scale, mats_ref, own_ref, other_ref, *refs):
-    col_hbms, col_ref, sems = refs[:4], refs[4], refs[5]
+def col_kernel(scale, mats_ref, own_ref, other_ref, own_hbm, down_hbm, far_low_hbm, far_high_hbm, up_hbm, col_ref, sems):
     for slot, ref in enumerate((own_ref, other_ref)):
         for p in range(3):
             side = slab([(ref.at[n],) for n in range(4)], p)
             put([col_ref.at[n, slot] for n in range(4)], product(mats_ref, p, side, 0, scale), p)
-    copies = [pltpu.make_async_copy(col_ref.at[n], col_hbms[n], sems.at[n]) for n in range(4)]
+    copies = [
+        pltpu.make_async_copy(src, dst, sems.at[n])
+        for n, (src, dst) in enumerate(
+            (
+                (col_ref.at[2, 0], far_low_hbm),
+                (col_ref.at[2, 1], far_high_hbm),
+                (col_ref.at[0], own_hbm),
+                (col_ref.at[1], down_hbm),
+                (col_ref.at[3], up_hbm),
+            )
+        )
+    ]
     for copy in copies:
         copy.start()
     for copy in copies:
@@ -194,15 +204,35 @@
     return ((p[0] + p[1]) + (p[2] + p[3])).astype(BF16)
 
 
-def total_kernel(zero_ref, one_ref, two_ref, three_ref, keep_ref, send_ref):
-    refs = (zero_ref, one_ref, two_ref, three_ref)
-    for s in range(keep_ref.shape[0]):
-        keep_ref[s] = four([ref.at[0] for ref in refs], s)
-        send_ref[s] = four([ref.at[1] for ref in refs], s)
+def relay_kernel(down_ref, up_ref, down_got_ref, up_got_ref, down_hbm, up_hbm, down_sum, up_sum, sems):
+    copies = [
+        pltpu.make_async_copy(down_ref.at[0], down_hbm.at[0], sems.at[0]),
+        pltpu.make_async_copy(up_ref.at[1], up_hbm.at[1], sems.at[1]),
+        pltpu.make_async_copy(down_sum, down_hbm.at[1], sems.at[2]),
+        pltpu.make_async_copy(up_sum, up_hbm.at[0], sems.at[3]),
+    ]
+    copies[0].start()
+    copies[1].start()
+    for s in range(down_sum.shape[0]):
+        down_sum[s] = (down_ref[1, s].astype(F32) + down_got_ref[s].astype(F32)).astype(BF16)
+        up_sum[s] = (up_ref[0, s].astype(F32) + up_got_ref[s].astype(F32)).astype(BF16)
+    copies[2].start()
+    copies[3].start()
+    for copy in copies:
+        copy.wait()
+
+
+def total_columns_kernel(own_ref, down_ref, up_ref, keep_ref, send_ref):
+    for slot, out_ref in enumerate((keep_ref, send_ref)):
+        for s in range(out_ref.shape[0]):
+            own, down, up = (ref[slot, s].astype(F32) for ref in (own_ref, down_ref, up_ref))
+            out_ref[s] = (own + down + up).astype(BF16)
 
 
 def total_blocks_kernel(part_ref, keep_ref, send_ref):
-    total_kernel(*[part_ref.at[n] for n in range(4)], keep_ref, send_ref)
+    for slot, out_ref in enumerate((keep_ref, send_ref)):
+        for s in range(out_ref.shape[0]):
+            out_ref[s] = four([part_ref.at[n, slot] for n in range(4)], s)
 
 
 def unpacked(first, keep, got):
@@ -290,20 +320,30 @@
         compiler_params=params(),
         name="row_products",
     )(place, mats, right)
-    cols = pl.pallas_call(
+    pair = pltpu.HBM((2,) + block, BF16)
+    single = pltpu.HBM(block, BF16)
+    col, down, far_low, far_high, up = pl.pallas_call(
         lambda *refs: col_kernel(scale, *refs),
         in_specs=[vmem] * 3,
-        out_specs=[hbm] * 4,
-        out_shape=(pltpu.HBM((2,) + block, BF16),) * 4,
-        scratch_shapes=[pltpu.VMEM((4, 2) + block, BF16), pltpu.SemaphoreType.DMA((4,))],
+        out_specs=[hbm] * 5,
+        out_shape=(pair, pair, single, single, pair),
+        scratch_shapes=[pltpu.VMEM((4, 2) + block, BF16), pltpu.SemaphoreType.DMA((5,))],
         compiler_params=params(),
         name="col_products",
     )(mats, own, other)
     row = exchange(row, "zl")
-    cols = [cols[0]] + [shift(cols[by], "x", -by) for by in (1, 2, 3)]
+    down, up = pl.pallas_call(
+        relay_kernel,
+        in_specs=[vmem] * 4,
+        out_specs=[hbm] * 2,
+        out_shape=(pair, pair),
+        scratch_shapes=[pltpu.VMEM(block, BF16)] * 2 + [pltpu.SemaphoreType.DMA((4,))],
+        compiler_params=params(),
+        name="relay",
+    )(down, up, shift(far_high, "x", -1), shift(far_low, "x", 1))
     keep, send = pl.pallas_call(
-        total_kernel, out_shape=(array(block), array(block)), compiler_params=params(), name="total_columns"
-    )(*cols)
+        total_columns_kernel, out_shape=(array(block), array(block)), compiler_params=params(), name="total_columns"
+    )(col, shift(down, "x", -1), shift(up, "x", 1))
     grad_key, grad_value = pl.pallas_call(
         finish_columns_kernel,
         in_specs=[smem, vmem, vmem],
@@ -311,7 +351,6 @@
         compiler_params=params(),
         name="finish_columns",
     )(place, keep, shift(send, "c", 1))
-    row, grad_key, grad_value = lax.optimization_barrier((row, grad_key, grad_value))
     keep, send = pl.pallas_call(
         total_blocks_kernel, out_shape=(array(block), array(block)), compiler_params=params(), name="total_rows"
     )(row)

time: 182 us -> 188 us (1.033)
  starting transfers between devices: 43.5 us -> 46.3 us
  local copies, waits for them, and re-layouts: 2.13 us -> 4.12 us
    ppermute x6 -> x7, starting transfers between devices: 29 us -> 31.9 us  [shift(): return lax.ppermute(block, axis, [(i, (i + by) % n) for i in range(n)])]
    unnamed x6 -> x10, local copies, waits for them, and re-layouts: 2.13 us -> 4.12 us
    ppermute x6 -> x7, waiting for transfers between devices: 12.8 us -> 12.9 us  [shift(): return lax.ppermute(block, axis, [(i, (i + by) % n) for i in range(n)])]
  transfers between devices with their start and end apart: 8 -> 9, of which waited for: 5 -> 4; matrix products, arithmetic and copies ran while one was open for 0% -> 0% of each run, Pallas kernels for 2% -> 3%
where the time goes in v11:
time: 188 us; the launch traced here: 187 us
  blocking collectives  109 us (58%)
  starting transfers between devices  46.3 us (25%)
  Pallas kernels  14.3 us (8%)
  waiting for transfers between devices  12.9 us (7%)
  local copies, waits for them, and re-layouts  4.12 us (2%)
    all_to_all x4, blocking collectives, exchange(): return lax.all_to_all(blocks, axis, 0, 0, tiled=True)  77.2 us
    ppermute x7, starting transfers between devices, shift(): return lax.ppermute(block, axis, [(i, (i + by) % n) for i in range(n)])  31.9 us
    all_gather x1, blocking collectives, on_device(): own = lax.all_gather(own, 'zl')  16.4 us
    all_gather x1, blocking collectives, on_device(): other = lax.all_gather(other, 'zl')  15.3 us
    all_to_all x2, starting transfers between devices, exchange(): return lax.all_to_all(blocks, axis, 0, 0, tiled=True)  14.5 us
    ppermute x7, waiting for transfers between devices, shift(): return lax.ppermute(block, axis, [(i, (i + by) % n) for i in range(n)])  12.9 us
    unnamed x10, local copies, waits for them, and re-layouts  4.12 us
  transfers between devices with their start and end apart: 9, of which 4 were waited for; matrix products, arithmetic and copies ran while one was open for 0% of the time, Pallas kernels for 3%

profile of v11, /device:TPU:1, one launch (start us, length us, event | category | flops | bytes accessed | tf_op | source)
XLA Modules:
  0.0 187.4 jit_solution(4806033599843919577)
XLA Ops:
  0.6 0.1 pad_add_fusion.place_ref.refs_0_
  0.7 2.9 %pack.1 = (bf16[4,64,384]{2,1,0:T(8,128)(2,1)S(1)}, bf16[4,64,384]{2,1,0:T(8,128)(2,1)S(1)}, bf16[4,2,4,64,384]{4,3,2,1,0:T(8,128)(2,1)}) custom-call(s32[2]{0:T(128)S(1)} %pad_add_fusion.place_ref.refs_0_, bf16[4,64,384]{2,1,0:T(8,128)(2,1)} %q_hbm.1, bf16[4,64,384]{2,1,0:T(8,128)(2,1)} %k_hbm.1, bf16[4,64,384]{2,1,0:T(8,128)(2,1)} %v_hbm.1, ...), custom_call_target="tpu_custom_call" | custom-call | tf_op jit(solution)/shard_map/pack/pallas_call | solution.py:271
  3.7 10.4 %all-to-all-start = ((bf16[8,4,64,384]{3,2,1,0:T(8,128)(2,1)}), bf16[8,4,64,384]{3,2,1,0:T(8,128)(2,1)S(1)}, u32[]{:S(2)}, u32[]{:S(2)}) async-start(bf16[8,4,64,384]{3,2,1,0:T(8,128)(2,1)} %bitcast.12), calls=%async_computation | async-start | bytes 3145728 | tf_op jit(solution)/shard_map/all_to_all | solution.py:21
  14.0 2.0 %collective-permute-start = (bf16[4,64,384]{2,1,0:T(8,128)(2,1)S(1)}, bf16[4,64,384]{2,1,0:T(8,128)(2,1)S(1)}, u32[]{:S(2)}, u32[]{:S(2)}) collective-permute-start(bf16[4,64,384]{2,1,0:T(8,128)(2,1)S(1)} %get-tuple-element.25), channel_id=1, source_target_pairs={{0,16},{16,0},{1,17},{17,1},{2,18},{18,2},{3,19},{19,3},{4,20},{20... | collective-permute-start | bytes 589832 | tf_op jit(solution)/shard_map/ppermute | solution.py:26
  16.0 16.4 %all-gather = bf16[16,64,384]{2,1,0:T(8,128)(2,1)S(1)} all-gather(bf16[4,64,384]{2,1,0:T(8,128)(2,1)S(1)} %get-tuple-element.24), channel_id=2, replica_groups=mesh['zh'=4,'y'=4,'c'=2,'x'=4,'zl'=4] {'zl'}, dimensions={0}, use_global_device_ids=true | all-gather | bytes 983040 | tf_op jit(solution)/shard_map/all_gather | solution.py:283
  32.5 0.0 collective-permute-done
  32.5 15.3 %all-gather.1 = bf16[16,64,384]{2,1,0:T(8,128)(2,1)S(1)} all-gather(bf16[4,64,384]{2,1,0:T(8,128)(2,1)S(1)} %collective-permute-done), channel_id=3, replica_groups=mesh['zh'=4,'y'=4,'c'=2,'x'=4,'zl'=4] {'zl'}, dimensions={0}, use_global_device_ids=true | all-gather | bytes 983040 | tf_op jit(solution)/shard_map/all_gather | solution.py:284
  47.7 0.0 all-to-all-done
  47.7 1.6 products.1
  49.3 18.7 %all_to_all.30.part_ref = f32[4,6,64,256]{3,2,1,0:T(8,128)S(1)} all-to-all(f32[4,6,64,256]{3,2,1,0:T(8,128)S(1)} %products.1), channel_id=1, replica_groups=mesh['zh'=4,'y'=4,'c'=2,'x'=4,'zl'=4] {'y'}, dimensions={0} | all-to-all | bytes 3145728 | tf_op jit(solution)/shard_map/all_to_all | solution.py:21
  68.1 0.1 rows.1
  68.1 25.3 %all_to_all.31.refs_0_ = f32[16,24,256]{2,1,0:T(8,128)S(1)} all-to-all(f32[16,24,256]{2,1,0:T(8,128)S(1)} %rows.1), channel_id=1, replica_groups=mesh['zh'=4,'y'=4,'c'=2,'x'=4,'zl'=4] {'zh','zl'}, dimensions={0} | all-to-all | bytes 786432 | tf_op jit(solution)/shard_map/all_to_all | solution.py:21
  93.5 0.3 softmax.1
  93.8 22.4 %all_to_all.32.mats_ref = bf16[16,48,128]{2,1,0:T(8,128)(2,1)S(1)} all-to-all(bf16[16,48,128]{2,1,0:T(8,128)(2,1)S(1)} %softmax.1), channel_id=1, replica_groups=mesh['zh'=4,'y'=4,'c'=2,'x'=4,'zl'=4] {'zh','zl'}, dimensions={0} | all-to-all | bytes 393216 | tf_op jit(solution)/shard_map/all_to_all | solution.py:21
  116.1 0.1 unpack.1
  116.2 10.7 %all_to_all.33.refs_1_ = bf16[4,6,64,256]{3,2,1,0:T(8,128)(2,1)S(1)} all-to-all(bf16[4,6,64,256]{3,2,1,0:T(8,128)(2,1)S(1)} %unpack.1), channel_id=1, replica_groups=mesh['zh'=4,'y'=4,'c'=2,'x'=4,'zl'=4] {'y'}, dimensions={0} | all-to-all | bytes 1572864 | tf_op jit(solution)/shard_map/all_to_all | solution.py:21
  127.0 2.6 %row_products.1 = (bf16[4,2,4,64,384]{4,3,2,1,0:T(8,128)(2,1)}, bf16[4,6,64,256]{3,2,1,0:T(8,128)(2,1)}) custom-call(s32[2]{0:T(128)S(1)} %pad_add_fusion.place_ref.refs_0_, bf16[4,6,64,256]{3,2,1,0:T(8,128)(2,1)S(1)} %all_to_all.33.refs_1_, bf16[4,2,4,64,384]{4,3,2,1,0:T(8,128)(2,1)S(1)} %bitcast.7), custom_call_target="tpu_custom_call" | custom-call | tf_op jit(solution)/shard_map/row_products/pallas_call | solution.py:314
  129.6 4.1 %all-to-all-start.5 = ((bf16[4,2,4,64,384]{4,3,2,1,0:T(8,128)(2,1)}), bf16[4,2,4,64,384]{4,3,2,1,0:T(8,128)(2,1)S(1)}, u32[]{:S(2)}, u32[]{:S(2)}) async-start(bf16[4,2,4,64,384]{4,3,2,1,0:T(8,128)(2,1)} %get-tuple-element.27), calls=%async_computation.5 | async-start | bytes 3145728 | tf_op jit(solution)/shard_map/all_to_all | solution.py:21
  133.7 0.0 copy-start.1
  133.7 1.1 copy-done.1
  134.8 2.3 %col_products.1 = (bf16[2,4,64,384]{3,2,1,0:T(8,128)(2,1)}, bf16[2,4,64,384]{3,2,1,0:T(8,128)(2,1)}, bf16[4,64,384]{2,1,0:T(8,128)(2,1)}, bf16[4,64,384]{2,1,0:T(8,128)(2,1)}, bf16[2,4,64,384]{3,2,1,0:T(8,128)(2,1)}) custom-call(bf16[4,6,64,256]{3,2,1,0:T(8,128)(2,1)S(1)} %copy-done.1, bf16[4,4,64,384]{3,2,1,0:T(8,128)(2,1)S(1)} %bitcast.9, ...), custom_call_target="tpu_custom_call" | custom-call | tf_op jit(solution)/shard_map/col_products/pallas_call | solution.py:325
  137.2 9.8 %collective-permute-start.2 = (bf16[4,64,384]{2,1,0:T(8,128)(2,1)}, bf16[4,64,384]{2,1,0:T(8,128)(2,1)S(1)}, u32[]{:S(2)}, u32[]{:S(2)}) collective-permute-start(bf16[4,64,384]{2,1,0:T(8,128)(2,1)} %get-tuple-element.36), channel_id=1, source_target_pairs={{0,12},{4,0},{8,4},{12,8},{1,13},{5,1},{9,5},{13,9},{2,14},{6,2},{... | collective-permute-start | bytes 589832 | tf_op jit(solution)/shard_map/ppermute | solution.py:26
  147.0 1.9 %collective-permute-start.3 = (bf16[4,64,384]{2,1,0:T(8,128)(2,1)}, bf16[4,64,384]{2,1,0:T(8,128)(2,1)S(1)}, u32[]{:S(2)}, u32[]{:S(2)}) collective-permute-start(bf16[4,64,384]{2,1,0:T(8,128)(2,1)} %get-tuple-element.37), channel_id=1, source_target_pairs={{0,4},{4,8},{8,12},{12,0},{1,5},{5,9},{9,13},{13,1},{2,6},{6,10},{... | collective-permute-start | bytes 589832 | tf_op jit(solution)/shard_map/ppermute | solution.py:26
  148.9 1.0 collective-permute-done.2.down_got_ref
  149.9 5.2 %collective-permute-done.3.up_got_ref = bf16[4,64,384]{2,1,0:T(8,128)(2,1)S(1)} collective-permute-done((bf16[4,64,384]{2,1,0:T(8,128)(2,1)}, bf16[4,64,384]{2,1,0:T(8,128)(2,1)S(1)}, u32[]{:S(2)}, u32[]{:S(2)}) %collective-permute-start.3) | collective-permute-done | bytes 196640 | tf_op jit(solution)/shard_map/ppermute | solution.py:26
  155.1 0.0 copy-start.3
  155.2 1.0 copy-done.3
  156.1 0.0 copy-start.4
  156.1 1.0 copy-done.4
  157.1 0.9 relay.1
  158.1 1.9 %collective-permute-start.4 = (bf16[2,4,64,384]{3,2,1,0:T(8,128)(2,1)}, bf16[2,4,64,384]{3,2,1,0:T(8,128)(2,1)S(1)}, u32[]{:S(2)}, u32[]{:S(2)}) collective-permute-start(bf16[2,4,64,384]{3,2,1,0:T(8,128)(2,1)} %get-tuple-element.38), channel_id=1, source_target_pairs={{0,12},{4,0},{8,4},{12,8},{1,13},{5,1},{9,5},{13,9},{2,14},{6,2},{... | collective-permute-start | bytes 1179656 | tf_op jit(solution)/shard_map/ppermute | solution.py:26
  160.0 3.4 %collective-permute-start.5 = (bf16[2,4,64,384]{3,2,1,0:T(8,128)(2,1)}, bf16[2,4,64,384]{3,2,1,0:T(8,128)(2,1)S(1)}, u32[]{:S(2)}, u32[]{:S(2)}) collective-permute-start(bf16[2,4,64,384]{3,2,1,0:T(8,128)(2,1)} %get-tuple-element.39), channel_id=1, source_target_pairs={{0,4},{4,8},{8,12},{12,0},{1,5},{5,9},{9,13},{13,1},{2,6},{6,10},{... | collective-permute-start | bytes 1179656 | tf_op jit(solution)/shard_map/ppermute | solution.py:26
  163.4 3.7 %collective-permute-done.4.down_ref = bf16[2,4,64,384]{3,2,1,0:T(8,128)(2,1)S(1)} collective-permute-done((bf16[2,4,64,384]{3,2,1,0:T(8,128)(2,1)}, bf16[2,4,64,384]{3,2,1,0:T(8,128)(2,1)S(1)}, u32[]{:S(2)}, u32[]{:S(2)}) %collective-permute-start.4) | collective-permute-done | bytes 393248 | tf_op jit(solution)/shard_map/ppermute | solution.py:26
  167.1 3.0 %collective-permute-done.5.up_ref = bf16[2,4,64,384]{3,2,1,0:T(8,128)(2,1)S(1)} collective-permute-done((bf16[2,4,64,384]{3,2,1,0:T(8,128)(2,1)}, bf16[2,4,64,384]{3,2,1,0:T(8,128)(2,1)S(1)}, u32[]{:S(2)}, u32[]{:S(2)}) %collective-permute-start.5) | collective-permute-done | bytes 393248 | tf_op jit(solution)/shard_map/ppermute | solution.py:26
  170.1 0.0 copy-start.2
  170.1 1.0 copy-done.2
  171.1 0.0 copy-start
  171.1 0.1 total_columns.1
  171.2 10.9 %collective-permute-start.6 = (bf16[4,64,384]{2,1,0:T(8,128)(2,1)S(1)}, bf16[4,64,384]{2,1,0:T(8,128)(2,1)S(1)}, u32[]{:S(2)}, u32[]{:S(2)}) collective-permute-start(bf16[4,64,384]{2,1,0:T(8,128)(2,1)S(1)} %get-tuple-element.41), channel_id=1, source_target_pairs={{0,16},{16,0},{1,17},{17,1},{2,18},{18,2},{3,19},{19,3},{4,20},{20... | collective-permute-start | bytes 589832 | tf_op jit(solution)/shard_map/ppermute | solution.py:26
  182.1 0.0 all-to-all-done.5.part_ref
  182.1 0.2 total_rows.1
  182.3 1.9 %collective-permute-start.1 = (bf16[4,64,384]{2,1,0:T(8,128)(2,1)S(1)}, bf16[4,64,384]{2,1,0:T(8,128)(2,1)S(1)}, u32[]{:S(2)}, u32[]{:S(2)}) collective-permute-start(bf16[4,64,384]{2,1,0:T(8,128)(2,1)S(1)} %get-tuple-element.29), channel_id=1, source_target_pairs={{0,16},{16,0},{1,17},{17,1},{2,18},{18,2},{3,19},{19,3},{4,20},{20... | collective-permute-start | bytes 589832 | tf_op jit(solution)/shard_map/ppermute | solution.py:26
  184.3 0.0 collective-permute-done.6.got_ref
  184.3 1.4 finish_columns.1
  185.7 0.0 collective-permute-done.1.got_ref
  185.7 0.0 copy-done
  185.7 1.7 finish_rows.1
Async XLA Ops:
  3.7 44.1 %all-to-all-start = ((bf16[8,4,64,384]{3,2,1,0:T(8,128)(2,1)}), bf16[8,4,64,384]{3,2,1,0:T(8,128)(2,1)S(1)}, u32[]{:S(2)}, u32[]{:S(2)}) async-start(bf16[8,4,64,384]{3,2,1,0:T(8,128)(2,1)} %bitcast.12), calls=%async_computation | async-start | bytes 3145728 | tf_op jit(solution)/shard_map/all_to_all | solution.py:21
  14.0 18.5 %collective-permute-start = (bf16[4,64,384]{2,1,0:T(8,128)(2,1)S(1)}, bf16[4,64,384]{2,1,0:T(8,128)(2,1)S(1)}, u32[]{:S(2)}, u32[]{:S(2)}) collective-permute-start(bf16[4,64,384]{2,1,0:T(8,128)(2,1)S(1)} %get-tuple-element.25), channel_id=1, source_target_pairs={{0,16},{16,0},{1,17},{17,1},{2,18},{18,2},{3,19},{19,3},{4,20},{20... | collective-permute-start | bytes 589832 | tf_op jit(solution)/shard_map/ppermute | solution.py:26
  129.6 52.5 %all-to-all-start.5 = ((bf16[4,2,4,64,384]{4,3,2,1,0:T(8,128)(2,1)}), bf16[4,2,4,64,384]{4,3,2,1,0:T(8,128)(2,1)S(1)}, u32[]{:S(2)}, u32[]{:S(2)}) async-start(bf16[4,2,4,64,384]{4,3,2,1,0:T(8,128)(2,1)} %get-tuple-element.27), calls=%async_computation.5 | async-start | bytes 3145728 | tf_op jit(solution)/shard_map/all_to_all | solution.py:21
  133.7 1.1 copy-start.1
  137.2 12.8 %collective-permute-start.2 = (bf16[4,64,384]{2,1,0:T(8,128)(2,1)}, bf16[4,64,384]{2,1,0:T(8,128)(2,1)S(1)}, u32[]{:S(2)}, u32[]{:S(2)}) collective-permute-start(bf16[4,64,384]{2,1,0:T(8,128)(2,1)} %get-tuple-element.36), channel_id=1, source_target_pairs={{0,12},{4,0},{8,4},{12,8},{1,13},{5,1},{9,5},{13,9},{2,14},{6,2},{... | collective-permute-start | bytes 589832 | tf_op jit(solution)/shard_map/ppermute | solution.py:26
  147.0 8.1 %collective-permute-start.3 = (bf16[4,64,384]{2,1,0:T(8,128)(2,1)}, bf16[4,64,384]{2,1,0:T(8,128)(2,1)S(1)}, u32[]{:S(2)}, u32[]{:S(2)}) collective-permute-start(bf16[4,64,384]{2,1,0:T(8,128)(2,1)} %get-tuple-element.37), channel_id=1, source_target_pairs={{0,4},{4,8},{8,12},{12,0},{1,5},{5,9},{9,13},{13,1},{2,6},{6,10},{... | collective-permute-start | bytes 589832 | tf_op jit(solution)/shard_map/ppermute | solution.py:26
  155.1 1.0 copy-start.3
  156.1 1.0 copy-start.4
  158.1 9.0 %collective-permute-start.4 = (bf16[2,4,64,384]{3,2,1,0:T(8,128)(2,1)}, bf16[2,4,64,384]{3,2,1,0:T(8,128)(2,1)S(1)}, u32[]{:S(2)}, u32[]{:S(2)}) collective-permute-start(bf16[2,4,64,384]{3,2,1,0:T(8,128)(2,1)} %get-tuple-element.38), channel_id=1, source_target_pairs={{0,12},{4,0},{8,4},{12,8},{1,13},{5,1},{9,5},{13,9},{2,14},{6,2},{... | collective-permute-start | bytes 1179656 | tf_op jit(solution)/shard_map/ppermute | solution.py:26
  160.0 10.1 %collective-permute-start.5 = (bf16[2,4,64,384]{3,2,1,0:T(8,128)(2,1)}, bf16[2,4,64,384]{3,2,1,0:T(8,128)(2,1)S(1)}, u32[]{:S(2)}, u32[]{:S(2)}) collective-permute-start(bf16[2,4,64,384]{3,2,1,0:T(8,128)(2,1)} %get-tuple-element.39), channel_id=1, source_target_pairs={{0,4},{4,8},{8,12},{12,0},{1,5},{5,9},{9,13},{13,1},{2,6},{6,10},{... | collective-permute-start | bytes 1179656 | tf_op jit(solution)/shard_map/ppermute | solution.py:26
  170.1 1.0 copy-start.2
  171.1 14.6 %copy-start = (bf16[384,768]{1,0:T(8,128)(2,1)S(1)}, bf16[384,768]{1,0:T(8,128)(2,1)}, u32[]{:S(2)}) copy-start(bf16[384,768]{1,0:T(8,128)(2,1)} %w_ref.1) | copy-start | bytes 1769476
  171.2 13.0 %collective-permute-start.6 = (bf16[4,64,384]{2,1,0:T(8,128)(2,1)S(1)}, bf16[4,64,384]{2,1,0:T(8,128)(2,1)S(1)}, u32[]{:S(2)}, u32[]{:S(2)}) collective-permute-start(bf16[4,64,384]{2,1,0:T(8,128)(2,1)S(1)} %get-tuple-element.41), channel_id=1, source_target_pairs={{0,16},{16,0},{1,17},{17,1},{2,18},{18,2},{3,19},{19,3},{4,20},{20... | collective-permute-start | bytes 589832 | tf_op jit(solution)/shard_map/ppermute | solution.py:26
  182.3 3.4 %collective-permute-start.1 = (bf16[4,64,384]{2,1,0:T(8,128)(2,1)S(1)}, bf16[4,64,384]{2,1,0:T(8,128)(2,1)S(1)}, u32[]{:S(2)}, u32[]{:S(2)}) collective-permute-start(bf16[4,64,384]{2,1,0:T(8,128)(2,1)S(1)} %get-tuple-element.29), channel_id=1, source_target_pairs={{0,16},{16,0},{1,17},{17,1},{2,18},{18,2},{3,19},{19,3},{4,20},{20... | collective-permute-start | bytes 589832 | tf_op jit(solution)/shard_map/ppermute | solution.py:26

commit v12 on v10

--- a/solution.py
+++ b/solution.py
@@ -311,7 +311,6 @@
         compiler_params=params(),
         name="finish_columns",
     )(place, keep, shift(send, "c", 1))
-    row, grad_key, grad_value = lax.optimization_barrier((row, grad_key, grad_value))
     keep, send = pl.pallas_call(
         total_blocks_kernel, out_shape=(array(block), array(block)), compiler_params=params(), name="total_rows"
     )(row)

time: 182 us -> 182 us (level); the launches traced: 181 us -> 179 us
  waiting for transfers between devices: 12.8 us -> 10.7 us
    ppermute x6, waiting for transfers between devices: 12.8 us -> 10.7 us  [shift(): return lax.ppermute(block, axis, [(i, (i + by) % n) for i in range(n)])]
  transfers between devices with their start and end apart: 8 -> 8, of which waited for: 5 -> 3; matrix products, arithmetic and copies ran while one was open for 0% -> 0% of each run, Pallas kernels for 2% -> 2%
where the time goes in v12:
time: 182 us; the launch traced here: 179 us
  blocking collectives  109 us (60%)
  starting transfers between devices  43.1 us (24%)
  Pallas kernels  13.4 us (7%)
  waiting for transfers between devices  10.7 us (6%)
  local copies, waits for them, and re-layouts  2.13 us (1%)
    all_to_all x4, blocking collectives, exchange(): return lax.all_to_all(blocks, axis, 0, 0, tiled=True)  77.2 us
    ppermute x6, starting transfers between devices, shift(): return lax.ppermute(block, axis, [(i, (i + by) % n) for i in range(n)])  28.6 us
    all_gather x1, blocking collectives, on_device(): own = lax.all_gather(own, 'zl')  16.4 us
    all_gather x1, blocking collectives, on_device(): other = lax.all_gather(other, 'zl')  15.3 us
    all_to_all x2, starting transfers between devices, exchange(): return lax.all_to_all(blocks, axis, 0, 0, tiled=True)  14.5 us
    ppermute x6, waiting for transfers between devices, shift(): return lax.ppermute(block, axis, [(i, (i + by) % n) for i in range(n)])  10.7 us
  transfers between devices with their start and end apart: 8, of which 3 were waited for; matrix products, arithmetic and copies ran while one was open for 0% of the time, Pallas kernels for 2%

profile of v12, /device:TPU:1, one launch (start us, length us, event | category | flops | bytes accessed | tf_op | source)
XLA Modules:
  0.0 179.0 jit_solution(8664346142051851963)
XLA Ops:
  0.6 0.1 pad_add_fusion.place_ref.refs_0_
  0.7 3.0 %pack.1 = (bf16[4,64,384]{2,1,0:T(8,128)(2,1)S(1)}, bf16[4,64,384]{2,1,0:T(8,128)(2,1)S(1)}, bf16[4,2,4,64,384]{4,3,2,1,0:T(8,128)(2,1)}) custom-call(s32[2]{0:T(128)S(1)} %pad_add_fusion.place_ref.refs_0_, bf16[4,64,384]{2,1,0:T(8,128)(2,1)} %q_hbm.1, bf16[4,64,384]{2,1,0:T(8,128)(2,1)} %k_hbm.1, bf16[4,64,384]{2,1,0:T(8,128)(2,1)} %v_hbm.1, ...), custom_call_target="tpu_custom_call" | custom-call | tf_op jit(solution)/shard_map/pack/pallas_call | solution.py:241
  3.7 10.4 %all-to-all-start = ((bf16[8,4,64,384]{3,2,1,0:T(8,128)(2,1)}), bf16[8,4,64,384]{3,2,1,0:T(8,128)(2,1)S(1)}, u32[]{:S(2)}, u32[]{:S(2)}) async-start(bf16[8,4,64,384]{3,2,1,0:T(8,128)(2,1)} %bitcast.12), calls=%async_computation | async-start | bytes 3145728 | tf_op jit(solution)/shard_map/all_to_all | solution.py:21
  14.0 2.0 %collective-permute-start = (bf16[4,64,384]{2,1,0:T(8,128)(2,1)S(1)}, bf16[4,64,384]{2,1,0:T(8,128)(2,1)S(1)}, u32[]{:S(2)}, u32[]{:S(2)}) collective-permute-start(bf16[4,64,384]{2,1,0:T(8,128)(2,1)S(1)} %get-tuple-element.22), channel_id=1, source_target_pairs={{0,16},{16,0},{1,17},{17,1},{2,18},{18,2},{3,19},{19,3},{4,20},{20... | collective-permute-start | bytes 589832 | tf_op jit(solution)/shard_map/ppermute | solution.py:26
  16.1 16.4 %all-gather = bf16[16,64,384]{2,1,0:T(8,128)(2,1)S(1)} all-gather(bf16[4,64,384]{2,1,0:T(8,128)(2,1)S(1)} %get-tuple-element.21), channel_id=2, replica_groups=mesh['zh'=4,'y'=4,'c'=2,'x'=4,'zl'=4] {'zl'}, dimensions={0}, use_global_device_ids=true | all-gather | bytes 983040 | tf_op jit(solution)/shard_map/all_gather | solution.py:253
  32.5 0.0 collective-permute-done
  32.5 15.3 %all-gather.1 = bf16[16,64,384]{2,1,0:T(8,128)(2,1)S(1)} all-gather(bf16[4,64,384]{2,1,0:T(8,128)(2,1)S(1)} %collective-permute-done), channel_id=3, replica_groups=mesh['zh'=4,'y'=4,'c'=2,'x'=4,'zl'=4] {'zl'}, dimensions={0}, use_global_device_ids=true | all-gather | bytes 983040 | tf_op jit(solution)/shard_map/all_gather | solution.py:254
  47.8 0.0 all-to-all-done
  47.8 1.6 products.1
  49.3 18.7 %all_to_all.30.part_ref = f32[4,6,64,256]{3,2,1,0:T(8,128)S(1)} all-to-all(f32[4,6,64,256]{3,2,1,0:T(8,128)S(1)} %products.1), channel_id=1, replica_groups=mesh['zh'=4,'y'=4,'c'=2,'x'=4,'zl'=4] {'y'}, dimensions={0} | all-to-all | bytes 3145728 | tf_op jit(solution)/shard_map/all_to_all | solution.py:21
  68.1 0.1 rows.1
  68.2 25.3 %all_to_all.31.refs_0_ = f32[16,24,256]{2,1,0:T(8,128)S(1)} all-to-all(f32[16,24,256]{2,1,0:T(8,128)S(1)} %rows.1), channel_id=1, replica_groups=mesh['zh'=4,'y'=4,'c'=2,'x'=4,'zl'=4] {'zh','zl'}, dimensions={0} | all-to-all | bytes 786432 | tf_op jit(solution)/shard_map/all_to_all | solution.py:21
  93.5 0.3 softmax.1
  93.8 22.4 %all_to_all.32.mats_ref = bf16[16,48,128]{2,1,0:T(8,128)(2,1)S(1)} all-to-all(bf16[16,48,128]{2,1,0:T(8,128)(2,1)S(1)} %softmax.1), channel_id=1, replica_groups=mesh['zh'=4,'y'=4,'c'=2,'x'=4,'zl'=4] {'zh','zl'}, dimensions={0} | all-to-all | bytes 393216 | tf_op jit(solution)/shard_map/all_to_all | solution.py:21
  116.2 0.1 unpack.1
  116.3 10.7 %all_to_all.33.refs_1_ = bf16[4,6,64,256]{3,2,1,0:T(8,128)(2,1)S(1)} all-to-all(bf16[4,6,64,256]{3,2,1,0:T(8,128)(2,1)S(1)} %unpack.1), channel_id=1, replica_groups=mesh['zh'=4,'y'=4,'c'=2,'x'=4,'zl'=4] {'y'}, dimensions={0} | all-to-all | bytes 1572864 | tf_op jit(solution)/shard_map/all_to_all | solution.py:21
  127.0 2.6 %row_products.1 = (bf16[4,2,4,64,384]{4,3,2,1,0:T(8,128)(2,1)}, bf16[4,6,64,256]{3,2,1,0:T(8,128)(2,1)}) custom-call(s32[2]{0:T(128)S(1)} %pad_add_fusion.place_ref.refs_0_, bf16[4,6,64,256]{3,2,1,0:T(8,128)(2,1)S(1)} %all_to_all.33.refs_1_, bf16[4,2,4,64,384]{4,3,2,1,0:T(8,128)(2,1)S(1)} %bitcast.7), custom_call_target="tpu_custom_call" | custom-call | tf_op jit(solution)/shard_map/row_products/pallas_call | solution.py:284
  129.6 4.1 %all-to-all-start.5 = ((bf16[4,2,4,64,384]{4,3,2,1,0:T(8,128)(2,1)}), bf16[4,2,4,64,384]{4,3,2,1,0:T(8,128)(2,1)S(1)}, u32[]{:S(2)}, u32[]{:S(2)}) async-start(bf16[4,2,4,64,384]{4,3,2,1,0:T(8,128)(2,1)} %get-tuple-element.24), calls=%async_computation.5 | async-start | bytes 3145728 | tf_op jit(solution)/shard_map/all_to_all | solution.py:21
  133.7 0.0 copy-start.1
  133.7 1.1 copy-done.1
  134.9 2.3 %col_products.1 = (bf16[2,4,64,384]{3,2,1,0:T(8,128)(2,1)}, bf16[2,4,64,384]{3,2,1,0:T(8,128)(2,1)}, bf16[2,4,64,384]{3,2,1,0:T(8,128)(2,1)}, bf16[2,4,64,384]{3,2,1,0:T(8,128)(2,1)}) custom-call(bf16[4,6,64,256]{3,2,1,0:T(8,128)(2,1)S(1)} %copy-done.1, bf16[4,4,64,384]{3,2,1,0:T(8,128)(2,1)S(1)} %bitcast.9, bf16[4,4,64,384]{3,2,1,0:T(8,128)(2,1)S(1)} %bitcast.11), custom_call_target="tpu_custom_call" | custom-call | tf_op jit(solution)/shard_map/col_products/pallas_call | solution.py:293
  137.2 9.9 %collective-permute-start.2 = (bf16[2,4,64,384]{3,2,1,0:T(8,128)(2,1)}, bf16[2,4,64,384]{3,2,1,0:T(8,128)(2,1)S(1)}, u32[]{:S(2)}, u32[]{:S(2)}) collective-permute-start(bf16[2,4,64,384]{3,2,1,0:T(8,128)(2,1)} %get-tuple-element.31), channel_id=1, source_target_pairs={{0,12},{4,0},{8,4},{12,8},{1,13},{5,1},{9,5},{13,9},{2,14},{6,2},{... | collective-permute-start | bytes 1179656 | tf_op jit(solution)/shard_map/ppermute | solution.py:26
  147.0 2.5 %collective-permute-start.3 = (bf16[2,4,64,384]{3,2,1,0:T(8,128)(2,1)}, bf16[2,4,64,384]{3,2,1,0:T(8,128)(2,1)S(1)}, u32[]{:S(2)}, u32[]{:S(2)}) collective-permute-start(bf16[2,4,64,384]{3,2,1,0:T(8,128)(2,1)} %get-tuple-element.32), channel_id=1, source_target_pairs={{0,8},{4,12},{8,0},{12,4},{1,9},{5,13},{9,1},{13,5},{2,10},{6,14},... | collective-permute-start | bytes 1179656 | tf_op jit(solution)/shard_map/ppermute | solution.py:26
  149.5 2.5 %collective-permute-start.4 = (bf16[2,4,64,384]{3,2,1,0:T(8,128)(2,1)}, bf16[2,4,64,384]{3,2,1,0:T(8,128)(2,1)S(1)}, u32[]{:S(2)}, u32[]{:S(2)}) collective-permute-start(bf16[2,4,64,384]{3,2,1,0:T(8,128)(2,1)} %get-tuple-element.33), channel_id=1, source_target_pairs={{0,4},{4,8},{8,12},{12,0},{1,5},{5,9},{9,13},{13,1},{2,6},{6,10},{... | collective-permute-start | bytes 1179656 | tf_op jit(solution)/shard_map/ppermute | solution.py:26
  152.0 4.5 %collective-permute-done.2.one_ref = bf16[2,4,64,384]{3,2,1,0:T(8,128)(2,1)S(1)} collective-permute-done((bf16[2,4,64,384]{3,2,1,0:T(8,128)(2,1)}, bf16[2,4,64,384]{3,2,1,0:T(8,128)(2,1)S(1)}, u32[]{:S(2)}, u32[]{:S(2)}) %collective-permute-start.2) | collective-permute-done | bytes 393248 | tf_op jit(solution)/shard_map/ppermute | solution.py:26
  156.5 0.9 collective-permute-done.3.two_ref
  157.4 5.3 %collective-permute-done.4.three_ref = bf16[2,4,64,384]{3,2,1,0:T(8,128)(2,1)S(1)} collective-permute-done((bf16[2,4,64,384]{3,2,1,0:T(8,128)(2,1)}, bf16[2,4,64,384]{3,2,1,0:T(8,128)(2,1)S(1)}, u32[]{:S(2)}, u32[]{:S(2)}) %collective-permute-start.4) | collective-permute-done | bytes 393248 | tf_op jit(solution)/shard_map/ppermute | solution.py:26
  162.7 0.0 copy-start.2
  162.7 1.0 copy-done.2
  163.7 0.0 copy-start
  163.7 0.2 total_columns.1
  163.9 9.8 %collective-permute-start.5 = (bf16[4,64,384]{2,1,0:T(8,128)(2,1)S(1)}, bf16[4,64,384]{2,1,0:T(8,128)(2,1)S(1)}, u32[]{:S(2)}, u32[]{:S(2)}) collective-permute-start(bf16[4,64,384]{2,1,0:T(8,128)(2,1)S(1)} %get-tuple-element.35), channel_id=1, source_target_pairs={{0,16},{16,0},{1,17},{17,1},{2,18},{18,2},{3,19},{19,3},{4,20},{20... | collective-permute-start | bytes 589832 | tf_op jit(solution)/shard_map/ppermute | solution.py:26
  173.8 0.0 all-to-all-done.5.part_ref
  173.8 0.2 total_rows.1
  174.0 1.9 %collective-permute-start.1 = (bf16[4,64,384]{2,1,0:T(8,128)(2,1)S(1)}, bf16[4,64,384]{2,1,0:T(8,128)(2,1)S(1)}, u32[]{:S(2)}, u32[]{:S(2)}) collective-permute-start(bf16[4,64,384]{2,1,0:T(8,128)(2,1)S(1)} %get-tuple-element.26), channel_id=1, source_target_pairs={{0,16},{16,0},{1,17},{17,1},{2,18},{18,2},{3,19},{19,3},{4,20},{20... | collective-permute-start | bytes 589832 | tf_op jit(solution)/shard_map/ppermute | solution.py:26
  175.9 0.0 collective-permute-done.5.got_ref
  175.9 1.4 finish_columns.1
  177.3 0.0 collective-permute-done.1.got_ref
  177.3 0.0 copy-done
  177.3 1.7 finish_rows.1
Async XLA Ops:
  3.7 44.1 %all-to-all-start = ((bf16[8,4,64,384]{3,2,1,0:T(8,128)(2,1)}), bf16[8,4,64,384]{3,2,1,0:T(8,128)(2,1)S(1)}, u32[]{:S(2)}, u32[]{:S(2)}) async-start(bf16[8,4,64,384]{3,2,1,0:T(8,128)(2,1)} %bitcast.12), calls=%async_computation | async-start | bytes 3145728 | tf_op jit(solution)/shard_map/all_to_all | solution.py:21
  14.0 18.5 %collective-permute-start = (bf16[4,64,384]{2,1,0:T(8,128)(2,1)S(1)}, bf16[4,64,384]{2,1,0:T(8,128)(2,1)S(1)}, u32[]{:S(2)}, u32[]{:S(2)}) collective-permute-start(bf16[4,64,384]{2,1,0:T(8,128)(2,1)S(1)} %get-tuple-element.22), channel_id=1, source_target_pairs={{0,16},{16,0},{1,17},{17,1},{2,18},{18,2},{3,19},{19,3},{4,20},{20... | collective-permute-start | bytes 589832 | tf_op jit(solution)/shard_map/ppermute | solution.py:26
  129.6 44.2 %all-to-all-start.5 = ((bf16[4,2,4,64,384]{4,3,2,1,0:T(8,128)(2,1)}), bf16[4,2,4,64,384]{4,3,2,1,0:T(8,128)(2,1)S(1)}, u32[]{:S(2)}, u32[]{:S(2)}) async-start(bf16[4,2,4,64,384]{4,3,2,1,0:T(8,128)(2,1)} %get-tuple-element.24), calls=%async_computation.5 | async-start | bytes 3145728 | tf_op jit(solution)/shard_map/all_to_all | solution.py:21
  133.7 1.1 copy-start.1
  137.2 19.3 %collective-permute-start.2 = (bf16[2,4,64,384]{3,2,1,0:T(8,128)(2,1)}, bf16[2,4,64,384]{3,2,1,0:T(8,128)(2,1)S(1)}, u32[]{:S(2)}, u32[]{:S(2)}) collective-permute-start(bf16[2,4,64,384]{3,2,1,0:T(8,128)(2,1)} %get-tuple-element.31), channel_id=1, source_target_pairs={{0,12},{4,0},{8,4},{12,8},{1,13},{5,1},{9,5},{13,9},{2,14},{6,2},{... | collective-permute-start | bytes 1179656 | tf_op jit(solution)/shard_map/ppermute | solution.py:26
  147.0 10.3 %collective-permute-start.3 = (bf16[2,4,64,384]{3,2,1,0:T(8,128)(2,1)}, bf16[2,4,64,384]{3,2,1,0:T(8,128)(2,1)S(1)}, u32[]{:S(2)}, u32[]{:S(2)}) collective-permute-start(bf16[2,4,64,384]{3,2,1,0:T(8,128)(2,1)} %get-tuple-element.32), channel_id=1, source_target_pairs={{0,8},{4,12},{8,0},{12,4},{1,9},{5,13},{9,1},{13,5},{2,10},{6,14},... | collective-permute-start | bytes 1179656 | tf_op jit(solution)/shard_map/ppermute | solution.py:26
  149.5 13.2 %collective-permute-start.4 = (bf16[2,4,64,384]{3,2,1,0:T(8,128)(2,1)}, bf16[2,4,64,384]{3,2,1,0:T(8,128)(2,1)S(1)}, u32[]{:S(2)}, u32[]{:S(2)}) collective-permute-start(bf16[2,4,64,384]{3,2,1,0:T(8,128)(2,1)} %get-tuple-element.33), channel_id=1, source_target_pairs={{0,4},{4,8},{8,12},{12,0},{1,5},{5,9},{9,13},{13,1},{2,6},{6,10},{... | collective-permute-start | bytes 1179656 | tf_op jit(solution)/shard_map/ppermute | solution.py:26
  162.7 1.0 copy-start.2
  163.7 13.6 %copy-start = (bf16[384,768]{1,0:T(8,128)(2,1)S(1)}, bf16[384,768]{1,0:T(8,128)(2,1)}, u32[]{:S(2)}) copy-start(bf16[384,768]{1,0:T(8,128)(2,1)} %w_ref.1) | copy-start | bytes 1769476
  163.9 12.0 %collective-permute-start.5 = (bf16[4,64,384]{2,1,0:T(8,128)(2,1)S(1)}, bf16[4,64,384]{2,1,0:T(8,128)(2,1)S(1)}, u32[]{:S(2)}, u32[]{:S(2)}) collective-permute-start(bf16[4,64,384]{2,1,0:T(8,128)(2,1)S(1)} %get-tuple-element.35), channel_id=1, source_target_pairs={{0,16},{16,0},{1,17},{17,1},{2,18},{18,2},{3,19},{19,3},{4,20},{20... | collective-permute-start | bytes 589832 | tf_op jit(solution)/shard_map/ppermute | solution.py:26
  174.0 3.4 %collective-permute-start.1 = (bf16[4,64,384]{2,1,0:T(8,128)(2,1)S(1)}, bf16[4,64,384]{2,1,0:T(8,128)(2,1)S(1)}, u32[]{:S(2)}, u32[]{:S(2)}) collective-permute-start(bf16[4,64,384]{2,1,0:T(8,128)(2,1)S(1)} %get-tuple-element.26), channel_id=1, source_target_pairs={{0,16},{16,0},{1,17},{17,1},{2,18},{18,2},{3,19},{19,3},{4,20},{20... | collective-permute-start | bytes 589832 | tf_op jit(solution)/shard_map/ppermute | solution.py:26

commit v13 on v12

--- a/solution.py
+++ b/solution.py
@@ -92,6 +92,11 @@
     return (lax.broadcasted_iota(jnp.int32, shape, 1) // 64) % 2 == 1
 
 
+def two_terms(value):
+    high = value.astype(BF16)
+    return high, (value - high.astype(F32)).astype(BF16)
+
+
 def product_kernel(place_ref, own_ref, other_ref, right_ref, out_ref):
     for p in range(3):
         left = slab(lefts(own_ref, other_ref), p)
@@ -100,24 +105,37 @@
         zero = jnp.zeros_like(left)
         for parity, part in enumerate((jnp.where(odd, zero, left), jnp.where(odd, left, zero))):
             full = lax.dot_general(part, right, (((1,), (1,)), ((), ())), preferred_element_type=F32)
-            out_ref[:, 2 * p + parity] = full.reshape(out_ref.shape[0], out_ref.shape[2], out_ref.shape[3])
-
-
-def rows_kernel(part_ref, out_ref):
-    total = (part_ref[0] + part_ref[1]) + (part_ref[2] + part_ref[3])
+            chunk = 2 * p + parity
+            for at, term in zip((chunk, chunk + 3) if chunk < 3 else (chunk + 3,), two_terms(full)):
+                out_ref[:, at] = term.reshape(out_ref.shape[0], out_ref.shape[2], out_ref.shape[3])
+
+
+def rows_kernel(part_ref, out_ref, rows_ref):
+    def added(j):
+        p = [part_ref[n, j].astype(F32) for n in range(4)]
+        return (p[0] + p[1]) + (p[2] + p[3])
+
+    for t in range(3):
+        terms = [term.astype(F32) for term in two_terms(added(t) + added(t + 3))] + [added(t + 6)]
+        for kind, term in enumerate(terms):
+            for n in range(16):
+                at = (kind * 3 + t) * 4
+                rows_ref[n, at : at + 4] = term[n * 4 : n * 4 + 4, :128]
+                rows_ref[n, 36 + at : 40 + at] = term[n * 4 : n * 4 + 4, 128:]
     for n in range(16):
-        for j in range(6):
-            out_ref[n, j * 4 : j * 4 + 4] = total[j, n * 4 : n * 4 + 4]
+        out_ref[n] = rows_ref[n].astype(BF16)
 
 
 def softmax_kernel(scale, part_ref, out_ref):
-    tiles = []
+    logits, grads = [], []
     for col in range(4):
-        parts = [part_ref[n * 4 + col] for n in range(4)]
-        tiles.append((parts[0] + parts[1]) + (parts[2] + parts[3]))
-    total = jnp.concatenate(tiles, axis=1)
-    logits = total[:12] * scale
-    grads = total[12:]
+        parts = [part_ref[n * 4 + col].astype(F32) for n in range(4)]
+        total = (parts[0] + parts[1]) + (parts[2] + parts[3])
+        for at in (0, 36):
+            logits.append(total[at : at + 12] + total[at + 12 : at + 24])
+            grads.append(total[at + 24 : at + 36])
+    logits = jnp.concatenate(logits, axis=1) * scale
+    grads = jnp.concatenate(grads, axis=1)
     expo = jnp.exp(logits - jnp.max(logits, axis=-1, keepdims=True))
     weights = expo / jnp.sum(expo, axis=-1, keepdims=True)
     scores = weights * (grads - jnp.sum(weights * grads, axis=-1, keepdims=True))
@@ -256,13 +274,17 @@
     partial = pl.pallas_call(
         product_kernel,
         in_specs=[smem] + [vmem] * 3,
-        out_shape=array((4, 6, 64, 256), F32),
+        out_shape=array((4, 9, 64, 256)),
         compiler_params=params(),
         name="products",
     )(place, own, other, right)
     partial = exchange(partial, "y")
     partial = pl.pallas_call(
-        rows_kernel, out_shape=array((16, 24, 256), F32), compiler_params=params(), name="rows"
+        rows_kernel,
+        out_shape=array((16, 72, 128)),
+        scratch_shapes=[pltpu.VMEM((16, 72, 128), F32)],
+        compiler_params=params(),
+        name="rows",
     )(partial)
     partial = exchange(partial, ("zh", "zl"))
     mats = pl.pallas_call(

time: 182 us -> 174 us (0.956)
  blocking collectives: 109 us -> 99.4 us
    all_to_all x4, blocking collectives: 77.2 us -> 67.7 us  [exchange(): return lax.all_to_all(blocks, axis, 0, 0, tiled=True)]
where the time goes in v13:
time: 174 us; the launch traced here: 170 us
  blocking collectives  99.4 us (57%)
  starting transfers between devices  44.1 us (25%)
  Pallas kernels  13.5 us (8%)
  waiting for transfers between devices  10.4 us (6%)
  local copies, waits for them, and re-layouts  2.13 us (1%)
    all_to_all x4, blocking collectives, exchange(): return lax.all_to_all(blocks, axis, 0, 0, tiled=True)  67.7 us
    ppermute x6, starting transfers between devices, shift(): return lax.ppermute(block, axis, [(i, (i + by) % n) for i in range(n)])  29.8 us
    all_gather x1, blocking collectives, on_device(): own = lax.all_gather(own, 'zl')  16.4 us
    all_gather x1, blocking collectives, on_device(): other = lax.all_gather(other, 'zl')  15.3 us
    all_to_all x2, starting transfers between devices, exchange(): return lax.all_to_all(blocks, axis, 0, 0, tiled=True)  14.3 us
    ppermute x6, waiting for transfers between devices, shift(): return lax.ppermute(block, axis, [(i, (i + by) % n) for i in range(n)])  10.4 us
  transfers between devices with their start and end apart: 8, of which 3 were waited for; matrix products, arithmetic and copies ran while one was open for 0% of the time, Pallas kernels for 2%

profile of v13, /device:TPU:1, one launch (start us, length us, event | category | flops | bytes accessed | tf_op | source)
XLA Modules:
  0.0 170.4 jit_solution(8103060609927259257)
XLA Ops:
  0.6 0.1 pad_add_fusion.place_ref.refs_0_
  0.7 3.0 %pack.1 = (bf16[4,64,384]{2,1,0:T(8,128)(2,1)S(1)}, bf16[4,64,384]{2,1,0:T(8,128)(2,1)S(1)}, bf16[4,2,4,64,384]{4,3,2,1,0:T(8,128)(2,1)}) custom-call(s32[2]{0:T(128)S(1)} %pad_add_fusion.place_ref.refs_0_, bf16[4,64,384]{2,1,0:T(8,128)(2,1)} %q_hbm.1, bf16[4,64,384]{2,1,0:T(8,128)(2,1)} %k_hbm.1, bf16[4,64,384]{2,1,0:T(8,128)(2,1)} %v_hbm.1, ...), custom_call_target="tpu_custom_call" | custom-call | tf_op jit(solution)/shard_map/pack/pallas_call | solution.py:259
  3.7 10.4 %all-to-all-start = ((bf16[8,4,64,384]{3,2,1,0:T(8,128)(2,1)}), bf16[8,4,64,384]{3,2,1,0:T(8,128)(2,1)S(1)}, u32[]{:S(2)}, u32[]{:S(2)}) async-start(bf16[8,4,64,384]{3,2,1,0:T(8,128)(2,1)} %bitcast.12), calls=%async_computation | async-start | bytes 3145728 | tf_op jit(solution)/shard_map/all_to_all | solution.py:21
  14.0 2.0 %collective-permute-start = (bf16[4,64,384]{2,1,0:T(8,128)(2,1)S(1)}, bf16[4,64,384]{2,1,0:T(8,128)(2,1)S(1)}, u32[]{:S(2)}, u32[]{:S(2)}) collective-permute-start(bf16[4,64,384]{2,1,0:T(8,128)(2,1)S(1)} %get-tuple-element.22), channel_id=1, source_target_pairs={{0,16},{16,0},{1,17},{17,1},{2,18},{18,2},{3,19},{19,3},{4,20},{20... | collective-permute-start | bytes 589832 | tf_op jit(solution)/shard_map/ppermute | solution.py:26
  16.1 16.4 %all-gather = bf16[16,64,384]{2,1,0:T(8,128)(2,1)S(1)} all-gather(bf16[4,64,384]{2,1,0:T(8,128)(2,1)S(1)} %get-tuple-element.21), channel_id=2, replica_groups=mesh['zh'=4,'y'=4,'c'=2,'x'=4,'zl'=4] {'zl'}, dimensions={0}, use_global_device_ids=true | all-gather | bytes 983040 | tf_op jit(solution)/shard_map/all_gather | solution.py:271
  32.5 0.0 collective-permute-done
  32.5 15.3 %all-gather.1 = bf16[16,64,384]{2,1,0:T(8,128)(2,1)S(1)} all-gather(bf16[4,64,384]{2,1,0:T(8,128)(2,1)S(1)} %collective-permute-done), channel_id=3, replica_groups=mesh['zh'=4,'y'=4,'c'=2,'x'=4,'zl'=4] {'zl'}, dimensions={0}, use_global_device_ids=true | all-gather | bytes 983040 | tf_op jit(solution)/shard_map/all_gather | solution.py:272
  47.8 0.0 all-to-all-done
  47.8 1.6 products.1
  49.3 14.5 %all_to_all.30.part_ref = bf16[4,9,64,256]{3,2,1,0:T(8,128)(2,1)S(1)} all-to-all(bf16[4,9,64,256]{3,2,1,0:T(8,128)(2,1)S(1)} %products.1), channel_id=1, replica_groups=mesh['zh'=4,'y'=4,'c'=2,'x'=4,'zl'=4] {'y'}, dimensions={0} | all-to-all | bytes 2359296 | tf_op jit(solution)/shard_map/all_to_all | solution.py:21
  63.8 0.2 rows.1
  64.0 23.8 %all_to_all.31.refs_0_ = bf16[16,72,128]{2,1,0:T(8,128)(2,1)S(1)} all-to-all(bf16[16,72,128]{2,1,0:T(8,128)(2,1)S(1)} %rows.1), channel_id=1, replica_groups=mesh['zh'=4,'y'=4,'c'=2,'x'=4,'zl'=4] {'zh','zl'}, dimensions={0} | all-to-all | bytes 589824 | tf_op jit(solution)/shard_map/all_to_all | solution.py:21
  87.8 0.3 softmax.1
  88.1 18.7 %all_to_all.32.mats_ref = bf16[16,48,128]{2,1,0:T(8,128)(2,1)S(1)} all-to-all(bf16[16,48,128]{2,1,0:T(8,128)(2,1)S(1)} %softmax.1), channel_id=1, replica_groups=mesh['zh'=4,'y'=4,'c'=2,'x'=4,'zl'=4] {'zh','zl'}, dimensions={0} | all-to-all | bytes 393216 | tf_op jit(solution)/shard_map/all_to_all | solution.py:21
  106.8 0.1 unpack.1
  106.9 10.7 %all_to_all.33.refs_1_ = bf16[4,6,64,256]{3,2,1,0:T(8,128)(2,1)S(1)} all-to-all(bf16[4,6,64,256]{3,2,1,0:T(8,128)(2,1)S(1)} %unpack.1), channel_id=1, replica_groups=mesh['zh'=4,'y'=4,'c'=2,'x'=4,'zl'=4] {'y'}, dimensions={0} | all-to-all | bytes 1572864 | tf_op jit(solution)/shard_map/all_to_all | solution.py:21
  117.6 2.6 %row_products.1 = (bf16[4,2,4,64,384]{4,3,2,1,0:T(8,128)(2,1)}, bf16[4,6,64,256]{3,2,1,0:T(8,128)(2,1)}) custom-call(s32[2]{0:T(128)S(1)} %pad_add_fusion.place_ref.refs_0_, bf16[4,6,64,256]{3,2,1,0:T(8,128)(2,1)S(1)} %all_to_all.33.refs_1_, bf16[4,2,4,64,384]{4,3,2,1,0:T(8,128)(2,1)S(1)} %bitcast.7), custom_call_target="tpu_custom_call" | custom-call | tf_op jit(solution)/shard_map/row_products/pallas_call | solution.py:306
  120.2 4.0 %all-to-all-start.5 = ((bf16[4,2,4,64,384]{4,3,2,1,0:T(8,128)(2,1)}), bf16[4,2,4,64,384]{4,3,2,1,0:T(8,128)(2,1)S(1)}, u32[]{:S(2)}, u32[]{:S(2)}) async-start(bf16[4,2,4,64,384]{4,3,2,1,0:T(8,128)(2,1)} %get-tuple-element.24), calls=%async_computation.5 | async-start | bytes 3145728 | tf_op jit(solution)/shard_map/all_to_all | solution.py:21
  124.2 0.0 copy-start.1
  124.2 1.1 copy-done.1
  125.3 2.3 %col_products.1 = (bf16[2,4,64,384]{3,2,1,0:T(8,128)(2,1)}, bf16[2,4,64,384]{3,2,1,0:T(8,128)(2,1)}, bf16[2,4,64,384]{3,2,1,0:T(8,128)(2,1)}, bf16[2,4,64,384]{3,2,1,0:T(8,128)(2,1)}) custom-call(bf16[4,6,64,256]{3,2,1,0:T(8,128)(2,1)S(1)} %copy-done.1, bf16[4,4,64,384]{3,2,1,0:T(8,128)(2,1)S(1)} %bitcast.9, bf16[4,4,64,384]{3,2,1,0:T(8,128)(2,1)S(1)} %bitcast.11), custom_call_target="tpu_custom_call" | custom-call | tf_op jit(solution)/shard_map/col_products/pallas_call | solution.py:315
  127.7 10.7 %collective-permute-start.2 = (bf16[2,4,64,384]{3,2,1,0:T(8,128)(2,1)}, bf16[2,4,64,384]{3,2,1,0:T(8,128)(2,1)S(1)}, u32[]{:S(2)}, u32[]{:S(2)}) collective-permute-start(bf16[2,4,64,384]{3,2,1,0:T(8,128)(2,1)} %get-tuple-element.31), channel_id=1, source_target_pairs={{0,12},{4,0},{8,4},{12,8},{1,13},{5,1},{9,5},{13,9},{2,14},{6,2},{... | collective-permute-start | bytes 1179656 | tf_op jit(solution)/shard_map/ppermute | solution.py:26
  138.4 2.5 %collective-permute-start.3 = (bf16[2,4,64,384]{3,2,1,0:T(8,128)(2,1)}, bf16[2,4,64,384]{3,2,1,0:T(8,128)(2,1)S(1)}, u32[]{:S(2)}, u32[]{:S(2)}) collective-permute-start(bf16[2,4,64,384]{3,2,1,0:T(8,128)(2,1)} %get-tuple-element.32), channel_id=1, source_target_pairs={{0,8},{4,12},{8,0},{12,4},{1,9},{5,13},{9,1},{13,5},{2,10},{6,14},... | collective-permute-start | bytes 1179656 | tf_op jit(solution)/shard_map/ppermute | solution.py:26
  140.9 2.5 %collective-permute-start.4 = (bf16[2,4,64,384]{3,2,1,0:T(8,128)(2,1)}, bf16[2,4,64,384]{3,2,1,0:T(8,128)(2,1)S(1)}, u32[]{:S(2)}, u32[]{:S(2)}) collective-permute-start(bf16[2,4,64,384]{3,2,1,0:T(8,128)(2,1)} %get-tuple-element.33), channel_id=1, source_target_pairs={{0,4},{4,8},{8,12},{12,0},{1,5},{5,9},{9,13},{13,1},{2,6},{6,10},{... | collective-permute-start | bytes 1179656 | tf_op jit(solution)/shard_map/ppermute | solution.py:26
  143.4 4.6 %collective-permute-done.2.one_ref = bf16[2,4,64,384]{3,2,1,0:T(8,128)(2,1)S(1)} collective-permute-done((bf16[2,4,64,384]{3,2,1,0:T(8,128)(2,1)}, bf16[2,4,64,384]{3,2,1,0:T(8,128)(2,1)S(1)}, u32[]{:S(2)}, u32[]{:S(2)}) %collective-permute-start.2) | collective-permute-done | bytes 393248 | tf_op jit(solution)/shard_map/ppermute | solution.py:26
  148.0 0.8 collective-permute-done.3.two_ref
  148.7 5.1 %collective-permute-done.4.three_ref = bf16[2,4,64,384]{3,2,1,0:T(8,128)(2,1)S(1)} collective-permute-done((bf16[2,4,64,384]{3,2,1,0:T(8,128)(2,1)}, bf16[2,4,64,384]{3,2,1,0:T(8,128)(2,1)S(1)}, u32[]{:S(2)}, u32[]{:S(2)}) %collective-permute-start.4) | collective-permute-done | bytes 393248 | tf_op jit(solution)/shard_map/ppermute | solution.py:26
  153.8 0.0 copy-start.2
  153.8 1.0 copy-done.2
  154.8 0.0 copy-start
  154.8 0.2 total_columns.1
  155.0 10.1 %collective-permute-start.5 = (bf16[4,64,384]{2,1,0:T(8,128)(2,1)S(1)}, bf16[4,64,384]{2,1,0:T(8,128)(2,1)S(1)}, u32[]{:S(2)}, u32[]{:S(2)}) collective-permute-start(bf16[4,64,384]{2,1,0:T(8,128)(2,1)S(1)} %get-tuple-element.35), channel_id=1, source_target_pairs={{0,16},{16,0},{1,17},{17,1},{2,18},{18,2},{3,19},{19,3},{4,20},{20... | collective-permute-start | bytes 589832 | tf_op jit(solution)/shard_map/ppermute | solution.py:26
  165.1 0.0 all-to-all-done.5.part_ref
  165.1 0.2 total_rows.1
  165.3 1.9 %collective-permute-start.1 = (bf16[4,64,384]{2,1,0:T(8,128)(2,1)S(1)}, bf16[4,64,384]{2,1,0:T(8,128)(2,1)S(1)}, u32[]{:S(2)}, u32[]{:S(2)}) collective-permute-start(bf16[4,64,384]{2,1,0:T(8,128)(2,1)S(1)} %get-tuple-element.26), channel_id=1, source_target_pairs={{0,16},{16,0},{1,17},{17,1},{2,18},{18,2},{3,19},{19,3},{4,20},{20... | collective-permute-start | bytes 589832 | tf_op jit(solution)/shard_map/ppermute | solution.py:26
  167.3 0.0 collective-permute-done.5.got_ref
  167.3 1.4 finish_columns.1
  168.7 0.0 collective-permute-done.1.got_ref
  168.7 0.0 copy-done
  168.7 1.7 finish_rows.1
Async XLA Ops:
  3.7 44.1 %all-to-all-start = ((bf16[8,4,64,384]{3,2,1,0:T(8,128)(2,1)}), bf16[8,4,64,384]{3,2,1,0:T(8,128)(2,1)S(1)}, u32[]{:S(2)}, u32[]{:S(2)}) async-start(bf16[8,4,64,384]{3,2,1,0:T(8,128)(2,1)} %bitcast.12), calls=%async_computation | async-start | bytes 3145728 | tf_op jit(solution)/shard_map/all_to_all | solution.py:21
  14.0 18.5 %collective-permute-start = (bf16[4,64,384]{2,1,0:T(8,128)(2,1)S(1)}, bf16[4,64,384]{2,1,0:T(8,128)(2,1)S(1)}, u32[]{:S(2)}, u32[]{:S(2)}) collective-permute-start(bf16[4,64,384]{2,1,0:T(8,128)(2,1)S(1)} %get-tuple-element.22), channel_id=1, source_target_pairs={{0,16},{16,0},{1,17},{17,1},{2,18},{18,2},{3,19},{19,3},{4,20},{20... | collective-permute-start | bytes 589832 | tf_op jit(solution)/shard_map/ppermute | solution.py:26
  120.2 44.9 %all-to-all-start.5 = ((bf16[4,2,4,64,384]{4,3,2,1,0:T(8,128)(2,1)}), bf16[4,2,4,64,384]{4,3,2,1,0:T(8,128)(2,1)S(1)}, u32[]{:S(2)}, u32[]{:S(2)}) async-start(bf16[4,2,4,64,384]{4,3,2,1,0:T(8,128)(2,1)} %get-tuple-element.24), calls=%async_computation.5 | async-start | bytes 3145728 | tf_op jit(solution)/shard_map/all_to_all | solution.py:21
  124.2 1.1 copy-start.1
  127.7 20.3 %collective-permute-start.2 = (bf16[2,4,64,384]{3,2,1,0:T(8,128)(2,1)}, bf16[2,4,64,384]{3,2,1,0:T(8,128)(2,1)S(1)}, u32[]{:S(2)}, u32[]{:S(2)}) collective-permute-start(bf16[2,4,64,384]{3,2,1,0:T(8,128)(2,1)} %get-tuple-element.31), channel_id=1, source_target_pairs={{0,12},{4,0},{8,4},{12,8},{1,13},{5,1},{9,5},{13,9},{2,14},{6,2},{... | collective-permute-start | bytes 1179656 | tf_op jit(solution)/shard_map/ppermute | solution.py:26
  138.4 10.3 %collective-permute-start.3 = (bf16[2,4,64,384]{3,2,1,0:T(8,128)(2,1)}, bf16[2,4,64,384]{3,2,1,0:T(8,128)(2,1)S(1)}, u32[]{:S(2)}, u32[]{:S(2)}) collective-permute-start(bf16[2,4,64,384]{3,2,1,0:T(8,128)(2,1)} %get-tuple-element.32), channel_id=1, source_target_pairs={{0,8},{4,12},{8,0},{12,4},{1,9},{5,13},{9,1},{13,5},{2,10},{6,14},... | collective-permute-start | bytes 1179656 | tf_op jit(solution)/shard_map/ppermute | solution.py:26
  140.9 12.9 %collective-permute-start.4 = (bf16[2,4,64,384]{3,2,1,0:T(8,128)(2,1)}, bf16[2,4,64,384]{3,2,1,0:T(8,128)(2,1)S(1)}, u32[]{:S(2)}, u32[]{:S(2)}) collective-permute-start(bf16[2,4,64,384]{3,2,1,0:T(8,128)(2,1)} %get-tuple-element.33), channel_id=1, source_target_pairs={{0,4},{4,8},{8,12},{12,0},{1,5},{5,9},{9,13},{13,1},{2,6},{6,10},{... | collective-permute-start | bytes 1179656 | tf_op jit(solution)/shard_map/ppermute | solution.py:26
  153.8 1.0 copy-start.2
  154.8 13.9 %copy-start = (bf16[384,768]{1,0:T(8,128)(2,1)S(1)}, bf16[384,768]{1,0:T(8,128)(2,1)}, u32[]{:S(2)}) copy-start(bf16[384,768]{1,0:T(8,128)(2,1)} %w_ref.1) | copy-start | bytes 1769476
  155.0 12.3 %collective-permute-start.5 = (bf16[4,64,384]{2,1,0:T(8,128)(2,1)S(1)}, bf16[4,64,384]{2,1,0:T(8,128)(2,1)S(1)}, u32[]{:S(2)}, u32[]{:S(2)}) collective-permute-start(bf16[4,64,384]{2,1,0:T(8,128)(2,1)S(1)} %get-tuple-element.35), channel_id=1, source_target_pairs={{0,16},{16,0},{1,17},{17,1},{2,18},{18,2},{3,19},{19,3},{4,20},{20... | collective-permute-start | bytes 589832 | tf_op jit(solution)/shard_map/ppermute | solution.py:26
  165.3 3.4 %collective-permute-start.1 = (bf16[4,64,384]{2,1,0:T(8,128)(2,1)S(1)}, bf16[4,64,384]{2,1,0:T(8,128)(2,1)S(1)}, u32[]{:S(2)}, u32[]{:S(2)}) collective-permute-start(bf16[4,64,384]{2,1,0:T(8,128)(2,1)S(1)} %get-tuple-element.26), channel_id=1, source_target_pairs={{0,16},{16,0},{1,17},{17,1},{2,18},{18,2},{3,19},{19,3},{4,20},{20... | collective-permute-start | bytes 589832 | tf_op jit(solution)/shard_map/ppermute | solution.py:26

commit v14 on v13

--- a/solution.py
+++ b/solution.py
@@ -97,7 +97,22 @@
     return high, (value - high.astype(F32)).astype(BF16)
 
 
+def centred(value):
+    mean = jnp.sum(value, axis=1, keepdims=True) * (1.0 / value.shape[1])
+    terms = [term.astype(F32) for term in two_terms(mean)]
+    return terms, (value - (terms[0] + terms[1])).astype(BF16)
+
+
+def lanes_of(shape):
+    return lax.broadcasted_iota(jnp.int32, shape, 1)
+
+
 def product_kernel(place_ref, own_ref, other_ref, right_ref, out_ref):
+    means = jnp.zeros((256, 128), F32)
+
+    def put_slab(at, value):
+        out_ref[:, at] = value.reshape(out_ref.shape[0], out_ref.shape[2], out_ref.shape[3])
+
     for p in range(3):
         left = slab(lefts(own_ref, other_ref), p)
         right = slab(rights(place_ref, right_ref), p)
@@ -106,23 +121,43 @@
         for parity, part in enumerate((jnp.where(odd, zero, left), jnp.where(odd, left, zero))):
             full = lax.dot_general(part, right, (((1,), (1,)), ((), ())), preferred_element_type=F32)
             chunk = 2 * p + parity
-            for at, term in zip((chunk, chunk + 3) if chunk < 3 else (chunk + 3,), two_terms(full)):
-                out_ref[:, at] = term.reshape(out_ref.shape[0], out_ref.shape[2], out_ref.shape[3])
+            if chunk < 3:
+                terms = zip((chunk, chunk + 3), two_terms(full))
+            else:
+                mean, rest = centred(full)
+                terms = ((chunk + 3, rest),)
+                for n, term in enumerate(mean):
+                    means = jnp.where(lanes_of(means.shape) == 2 * (chunk - 3) + n, term, means)
+            for at, term in terms:
+                put_slab(2 * at, term[:, :128])
+                put_slab(2 * at + 1, term[:, 128:])
+    put_slab(18, means.astype(BF16))
 
 
 def rows_kernel(part_ref, out_ref, rows_ref):
-    def added(j):
-        p = [part_ref[n, j].astype(F32) for n in range(4)]
+    def added(at):
+        p = [part_ref[n, at].astype(F32) for n in range(4)]
         return (p[0] + p[1]) + (p[2] + p[3])
 
+    def both(j):
+        return jnp.concatenate([added(2 * j), added(2 * j + 1)], axis=1)
+
+    sums = added(18)
+    lanes = lanes_of(sums.shape)
+    inner = lax.broadcasted_iota(jnp.int32, sums.shape, 0) % 4
+    spread = [jnp.zeros_like(sums), jnp.zeros_like(sums)]
     for t in range(3):
-        terms = [term.astype(F32) for term in two_terms(added(t) + added(t + 3))] + [added(t + 6)]
+        mean, rest = centred(both(t + 6) + (sums[:, 2 * t : 2 * t + 1] + sums[:, 2 * t + 1 : 2 * t + 2]))
+        spread = [jnp.where(lanes == t * 4 + inner, term, rows) for term, rows in zip(mean, spread)]
+        terms = [term.astype(F32) for term in two_terms(both(t) + both(t + 3))] + [rest.astype(F32)]
         for kind, term in enumerate(terms):
             for n in range(16):
                 at = (kind * 3 + t) * 4
                 rows_ref[n, at : at + 4] = term[n * 4 : n * 4 + 4, :128]
                 rows_ref[n, 36 + at : 40 + at] = term[n * 4 : n * 4 + 4, 128:]
     for n in range(16):
+        for kind in range(2):
+            rows_ref[n, 72 + kind * 4 : 76 + kind * 4] = spread[kind][n * 4 : n * 4 + 4]
         out_ref[n] = rows_ref[n].astype(BF16)
 
 
@@ -131,9 +166,12 @@
     for col in range(4):
         parts = [part_ref[n * 4 + col].astype(F32) for n in range(4)]
         total = (parts[0] + parts[1]) + (parts[2] + parts[3])
+        means = jnp.broadcast_to(jnp.sum(total[72:80], axis=0, keepdims=True), (12, 128))
+        here = lanes_of(means.shape) == lax.broadcasted_iota(jnp.int32, means.shape, 0)
+        mean = jnp.sum(jnp.where(here, means, 0.0), axis=1, keepdims=True)
         for at in (0, 36):
             logits.append(total[at : at + 12] + total[at + 12 : at + 24])
-            grads.append(total[at + 24 : at + 36])
+            grads.append(total[at + 24 : at + 36] + mean)
     logits = jnp.concatenate(logits, axis=1) * scale
     grads = jnp.concatenate(grads, axis=1)
     expo = jnp.exp(logits - jnp.max(logits, axis=-1, keepdims=True))
@@ -274,15 +312,15 @@
     partial = pl.pallas_call(
         product_kernel,
         in_specs=[smem] + [vmem] * 3,
-        out_shape=array((4, 9, 64, 256)),
+        out_shape=array((4, 19, 64, 128)),
         compiler_params=params(),
         name="products",
     )(place, own, other, right)
     partial = exchange(partial, "y")
     partial = pl.pallas_call(
         rows_kernel,
-        out_shape=array((16, 72, 128)),
-        scratch_shapes=[pltpu.VMEM((16, 72, 128), F32)],
+        out_shape=array((16, 80, 128)),
+        scratch_shapes=[pltpu.VMEM((16, 80, 128), F32)],
         compiler_params=params(),
         name="rows",
     )(partial)

time: 174 us -> 177 us (1.017)
  waiting for transfers between devices: 10.4 us -> 14.8 us
  starting transfers between devices: 44.1 us -> 40.4 us
  blocking collectives: 99.4 us -> 102 us
    ppermute x6, waiting for transfers between devices: 10.4 us -> 14.8 us  [shift(): return lax.ppermute(block, axis, [(i, (i + by) % n) for i in range(n)])]
    ppermute x6, starting transfers between devices: 29.8 us -> 26.1 us  [shift(): return lax.ppermute(block, axis, [(i, (i + by) % n) for i in range(n)])]
    all_to_all x4, blocking collectives: 67.7 us -> 70.3 us  [exchange(): return lax.all_to_all(blocks, axis, 0, 0, tiled=True)]
where the time goes in v14:
time: 177 us; the launch traced here: 174 us
  blocking collectives  102 us (58%)
  starting transfers between devices  40.4 us (23%)
  waiting for transfers between devices  14.8 us (8%)
  Pallas kernels  13.8 us (8%)
  local copies, waits for them, and re-layouts  2.13 us (1%)
    all_to_all x4, blocking collectives, exchange(): return lax.all_to_all(blocks, axis, 0, 0, tiled=True)  70.3 us
    ppermute x6, starting transfers between devices, shift(): return lax.ppermute(block, axis, [(i, (i + by) % n) for i in range(n)])  26.1 us
    all_gather x1, blocking collectives, on_device(): own = lax.all_gather(own, 'zl')  16.4 us
    all_gather x1, blocking collectives, on_device(): other = lax.all_gather(other, 'zl')  15.3 us
    ppermute x6, waiting for transfers between devices, shift(): return lax.ppermute(block, axis, [(i, (i + by) % n) for i in range(n)])  14.8 us
    all_to_all x2, starting transfers between devices, exchange(): return lax.all_to_all(blocks, axis, 0, 0, tiled=True)  14.3 us
  transfers between devices with their start and end apart: 8, of which 3 were waited for; matrix products, arithmetic and copies ran while one was open for 0% of the time, Pallas kernels for 2%

profile of v14, /device:TPU:1, one launch (start us, length us, event | category | flops | bytes accessed | tf_op | source)
XLA Modules:
  0.0 174.0 jit_solution(11100971010593753657)
XLA Ops:
  0.6 0.1 pad_add_fusion.place_ref.refs_0_
  0.7 3.0 %pack.1 = (bf16[4,64,384]{2,1,0:T(8,128)(2,1)S(1)}, bf16[4,64,384]{2,1,0:T(8,128)(2,1)S(1)}, bf16[4,2,4,64,384]{4,3,2,1,0:T(8,128)(2,1)}) custom-call(s32[2]{0:T(128)S(1)} %pad_add_fusion.place_ref.refs_0_, bf16[4,64,384]{2,1,0:T(8,128)(2,1)} %q_hbm.1, bf16[4,64,384]{2,1,0:T(8,128)(2,1)} %k_hbm.1, bf16[4,64,384]{2,1,0:T(8,128)(2,1)} %v_hbm.1, ...), custom_call_target="tpu_custom_call" | custom-call | tf_op jit(solution)/shard_map/pack/pallas_call | solution.py:297
  3.7 10.4 %all-to-all-start = ((bf16[8,4,64,384]{3,2,1,0:T(8,128)(2,1)}), bf16[8,4,64,384]{3,2,1,0:T(8,128)(2,1)S(1)}, u32[]{:S(2)}, u32[]{:S(2)}) async-start(bf16[8,4,64,384]{3,2,1,0:T(8,128)(2,1)} %bitcast.12), calls=%async_computation | async-start | bytes 3145728 | tf_op jit(solution)/shard_map/all_to_all | solution.py:21
  14.0 2.0 %collective-permute-start = (bf16[4,64,384]{2,1,0:T(8,128)(2,1)S(1)}, bf16[4,64,384]{2,1,0:T(8,128)(2,1)S(1)}, u32[]{:S(2)}, u32[]{:S(2)}) collective-permute-start(bf16[4,64,384]{2,1,0:T(8,128)(2,1)S(1)} %get-tuple-element.22), channel_id=1, source_target_pairs={{0,16},{16,0},{1,17},{17,1},{2,18},{18,2},{3,19},{19,3},{4,20},{20... | collective-permute-start | bytes 589832 | tf_op jit(solution)/shard_map/ppermute | solution.py:26
  16.1 16.4 %all-gather = bf16[16,64,384]{2,1,0:T(8,128)(2,1)S(1)} all-gather(bf16[4,64,384]{2,1,0:T(8,128)(2,1)S(1)} %get-tuple-element.21), channel_id=2, replica_groups=mesh['zh'=4,'y'=4,'c'=2,'x'=4,'zl'=4] {'zl'}, dimensions={0}, use_global_device_ids=true | all-gather | bytes 983040 | tf_op jit(solution)/shard_map/all_gather | solution.py:309
  32.5 0.0 collective-permute-done
  32.5 15.3 %all-gather.1 = bf16[16,64,384]{2,1,0:T(8,128)(2,1)S(1)} all-gather(bf16[4,64,384]{2,1,0:T(8,128)(2,1)S(1)} %collective-permute-done), channel_id=3, replica_groups=mesh['zh'=4,'y'=4,'c'=2,'x'=4,'zl'=4] {'zl'}, dimensions={0}, use_global_device_ids=true | all-gather | bytes 983040 | tf_op jit(solution)/shard_map/all_gather | solution.py:310
  47.8 0.0 all-to-all-done
  47.8 1.7 products.1
  49.4 14.9 %all_to_all.30.part_ref = bf16[4,19,64,128]{3,2,1,0:T(8,128)(2,1)S(1)} all-to-all(bf16[4,19,64,128]{3,2,1,0:T(8,128)(2,1)S(1)} %products.1), channel_id=1, replica_groups=mesh['zh'=4,'y'=4,'c'=2,'x'=4,'zl'=4] {'y'}, dimensions={0} | all-to-all | bytes 2490368 | tf_op jit(solution)/shard_map/all_to_all | solution.py:21
  64.3 0.4 rows.1
  64.7 24.5 %all_to_all.31.refs_0_ = bf16[16,80,128]{2,1,0:T(8,128)(2,1)S(1)} all-to-all(bf16[16,80,128]{2,1,0:T(8,128)(2,1)S(1)} %rows.1), channel_id=1, replica_groups=mesh['zh'=4,'y'=4,'c'=2,'x'=4,'zl'=4] {'zh','zl'}, dimensions={0} | all-to-all | bytes 655360 | tf_op jit(solution)/shard_map/all_to_all | solution.py:21
  89.2 0.3 softmax.1
  89.5 20.2 %all_to_all.32.mats_ref = bf16[16,48,128]{2,1,0:T(8,128)(2,1)S(1)} all-to-all(bf16[16,48,128]{2,1,0:T(8,128)(2,1)S(1)} %softmax.1), channel_id=1, replica_groups=mesh['zh'=4,'y'=4,'c'=2,'x'=4,'zl'=4] {'zh','zl'}, dimensions={0} | all-to-all | bytes 393216 | tf_op jit(solution)/shard_map/all_to_all | solution.py:21
  109.7 0.1 unpack.1
  109.8 10.7 %all_to_all.33.refs_1_ = bf16[4,6,64,256]{3,2,1,0:T(8,128)(2,1)S(1)} all-to-all(bf16[4,6,64,256]{3,2,1,0:T(8,128)(2,1)S(1)} %unpack.1), channel_id=1, replica_groups=mesh['zh'=4,'y'=4,'c'=2,'x'=4,'zl'=4] {'y'}, dimensions={0} | all-to-all | bytes 1572864 | tf_op jit(solution)/shard_map/all_to_all | solution.py:21
  120.6 2.6 %row_products.1 = (bf16[4,2,4,64,384]{4,3,2,1,0:T(8,128)(2,1)}, bf16[4,6,64,256]{3,2,1,0:T(8,128)(2,1)}) custom-call(s32[2]{0:T(128)S(1)} %pad_add_fusion.place_ref.refs_0_, bf16[4,6,64,256]{3,2,1,0:T(8,128)(2,1)S(1)} %all_to_all.33.refs_1_, bf16[4,2,4,64,384]{4,3,2,1,0:T(8,128)(2,1)S(1)} %bitcast.7), custom_call_target="tpu_custom_call" | custom-call | tf_op jit(solution)/shard_map/row_products/pallas_call | solution.py:344
  123.2 3.9 %all-to-all-start.5 = ((bf16[4,2,4,64,384]{4,3,2,1,0:T(8,128)(2,1)}), bf16[4,2,4,64,384]{4,3,2,1,0:T(8,128)(2,1)S(1)}, u32[]{:S(2)}, u32[]{:S(2)}) async-start(bf16[4,2,4,64,384]{4,3,2,1,0:T(8,128)(2,1)} %get-tuple-element.24), calls=%async_computation.5 | async-start | bytes 3145728 | tf_op jit(solution)/shard_map/all_to_all | solution.py:21
  127.1 0.0 copy-start.1
  127.1 1.1 copy-done.1
  128.2 2.3 %col_products.1 = (bf16[2,4,64,384]{3,2,1,0:T(8,128)(2,1)}, bf16[2,4,64,384]{3,2,1,0:T(8,128)(2,1)}, bf16[2,4,64,384]{3,2,1,0:T(8,128)(2,1)}, bf16[2,4,64,384]{3,2,1,0:T(8,128)(2,1)}) custom-call(bf16[4,6,64,256]{3,2,1,0:T(8,128)(2,1)S(1)} %copy-done.1, bf16[4,4,64,384]{3,2,1,0:T(8,128)(2,1)S(1)} %bitcast.9, bf16[4,4,64,384]{3,2,1,0:T(8,128)(2,1)S(1)} %bitcast.11), custom_call_target="tpu_custom_call" | custom-call | tf_op jit(solution)/shard_map/col_products/pallas_call | solution.py:353
  130.6 11.5 %collective-permute-start.2 = (bf16[2,4,64,384]{3,2,1,0:T(8,128)(2,1)}, bf16[2,4,64,384]{3,2,1,0:T(8,128)(2,1)S(1)}, u32[]{:S(2)}, u32[]{:S(2)}) collective-permute-start(bf16[2,4,64,384]{3,2,1,0:T(8,128)(2,1)} %get-tuple-element.31), channel_id=1, source_target_pairs={{0,12},{4,0},{8,4},{12,8},{1,13},{5,1},{9,5},{13,9},{2,14},{6,2},{... | collective-permute-start | bytes 1179656 | tf_op jit(solution)/shard_map/ppermute | solution.py:26
  142.0 2.5 %collective-permute-start.3 = (bf16[2,4,64,384]{3,2,1,0:T(8,128)(2,1)}, bf16[2,4,64,384]{3,2,1,0:T(8,128)(2,1)S(1)}, u32[]{:S(2)}, u32[]{:S(2)}) collective-permute-start(bf16[2,4,64,384]{3,2,1,0:T(8,128)(2,1)} %get-tuple-element.32), channel_id=1, source_target_pairs={{0,8},{4,12},{8,0},{12,4},{1,9},{5,13},{9,1},{13,5},{2,10},{6,14},... | collective-permute-start | bytes 1179656 | tf_op jit(solution)/shard_map/ppermute | solution.py:26
  144.5 2.5 %collective-permute-start.4 = (bf16[2,4,64,384]{3,2,1,0:T(8,128)(2,1)}, bf16[2,4,64,384]{3,2,1,0:T(8,128)(2,1)S(1)}, u32[]{:S(2)}, u32[]{:S(2)}) collective-permute-start(bf16[2,4,64,384]{3,2,1,0:T(8,128)(2,1)} %get-tuple-element.33), channel_id=1, source_target_pairs={{0,4},{4,8},{8,12},{12,0},{1,5},{5,9},{9,13},{13,1},{2,6},{6,10},{... | collective-permute-start | bytes 1179656 | tf_op jit(solution)/shard_map/ppermute | solution.py:26
  147.0 3.3 %collective-permute-done.2.one_ref = bf16[2,4,64,384]{3,2,1,0:T(8,128)(2,1)S(1)} collective-permute-done((bf16[2,4,64,384]{3,2,1,0:T(8,128)(2,1)}, bf16[2,4,64,384]{3,2,1,0:T(8,128)(2,1)S(1)}, u32[]{:S(2)}, u32[]{:S(2)}) %collective-permute-start.2) | collective-permute-done | bytes 393248 | tf_op jit(solution)/shard_map/ppermute | solution.py:26
  150.4 2.0 %collective-permute-done.3.two_ref = bf16[2,4,64,384]{3,2,1,0:T(8,128)(2,1)S(1)} collective-permute-done((bf16[2,4,64,384]{3,2,1,0:T(8,128)(2,1)}, bf16[2,4,64,384]{3,2,1,0:T(8,128)(2,1)S(1)}, u32[]{:S(2)}, u32[]{:S(2)}) %collective-permute-start.3) | collective-permute-done | bytes 393248 | tf_op jit(solution)/shard_map/ppermute | solution.py:26
  152.4 9.4 %collective-permute-done.4.three_ref = bf16[2,4,64,384]{3,2,1,0:T(8,128)(2,1)S(1)} collective-permute-done((bf16[2,4,64,384]{3,2,1,0:T(8,128)(2,1)}, bf16[2,4,64,384]{3,2,1,0:T(8,128)(2,1)S(1)}, u32[]{:S(2)}, u32[]{:S(2)}) %collective-permute-start.4) | collective-permute-done | bytes 393248 | tf_op jit(solution)/shard_map/ppermute | solution.py:26
  161.8 0.0 copy-start.2
  161.8 1.0 copy-done.2
  162.8 0.0 copy-start
  162.8 0.2 total_columns.1
  163.0 5.7 %collective-permute-start.5 = (bf16[4,64,384]{2,1,0:T(8,128)(2,1)S(1)}, bf16[4,64,384]{2,1,0:T(8,128)(2,1)S(1)}, u32[]{:S(2)}, u32[]{:S(2)}) collective-permute-start(bf16[4,64,384]{2,1,0:T(8,128)(2,1)S(1)} %get-tuple-element.35), channel_id=1, source_target_pairs={{0,16},{16,0},{1,17},{17,1},{2,18},{18,2},{3,19},{19,3},{4,20},{20... | collective-permute-start | bytes 589832 | tf_op jit(solution)/shard_map/ppermute | solution.py:26
  168.7 0.0 all-to-all-done.5.part_ref
  168.7 0.2 total_rows.1
  168.9 1.9 %collective-permute-start.1 = (bf16[4,64,384]{2,1,0:T(8,128)(2,1)S(1)}, bf16[4,64,384]{2,1,0:T(8,128)(2,1)S(1)}, u32[]{:S(2)}, u32[]{:S(2)}) collective-permute-start(bf16[4,64,384]{2,1,0:T(8,128)(2,1)S(1)} %get-tuple-element.26), channel_id=1, source_target_pairs={{0,16},{16,0},{1,17},{17,1},{2,18},{18,2},{3,19},{19,3},{4,20},{20... | collective-permute-start | bytes 589832 | tf_op jit(solution)/shard_map/ppermute | solution.py:26
  170.9 0.0 collective-permute-done.5.got_ref
  170.9 1.4 finish_columns.1
  172.3 0.0 collective-permute-done.1.got_ref
  172.3 0.0 copy-done
  172.3 1.7 finish_rows.1
Async XLA Ops:
  3.7 44.1 %all-to-all-start = ((bf16[8,4,64,384]{3,2,1,0:T(8,128)(2,1)}), bf16[8,4,64,384]{3,2,1,0:T(8,128)(2,1)S(1)}, u32[]{:S(2)}, u32[]{:S(2)}) async-start(bf16[8,4,64,384]{3,2,1,0:T(8,128)(2,1)} %bitcast.12), calls=%async_computation | async-start | bytes 3145728 | tf_op jit(solution)/shard_map/all_to_all | solution.py:21
  14.0 18.5 %collective-permute-start = (bf16[4,64,384]{2,1,0:T(8,128)(2,1)S(1)}, bf16[4,64,384]{2,1,0:T(8,128)(2,1)S(1)}, u32[]{:S(2)}, u32[]{:S(2)}) collective-permute-start(bf16[4,64,384]{2,1,0:T(8,128)(2,1)S(1)} %get-tuple-element.22), channel_id=1, source_target_pairs={{0,16},{16,0},{1,17},{17,1},{2,18},{18,2},{3,19},{19,3},{4,20},{20... | collective-permute-start | bytes 589832 | tf_op jit(solution)/shard_map/ppermute | solution.py:26
  123.2 45.6 %all-to-all-start.5 = ((bf16[4,2,4,64,384]{4,3,2,1,0:T(8,128)(2,1)}), bf16[4,2,4,64,384]{4,3,2,1,0:T(8,128)(2,1)S(1)}, u32[]{:S(2)}, u32[]{:S(2)}) async-start(bf16[4,2,4,64,384]{4,3,2,1,0:T(8,128)(2,1)} %get-tuple-element.24), calls=%async_computation.5 | async-start | bytes 3145728 | tf_op jit(solution)/shard_map/all_to_all | solution.py:21
  127.1 1.1 copy-start.1
  130.6 19.8 %collective-permute-start.2 = (bf16[2,4,64,384]{3,2,1,0:T(8,128)(2,1)}, bf16[2,4,64,384]{3,2,1,0:T(8,128)(2,1)S(1)}, u32[]{:S(2)}, u32[]{:S(2)}) collective-permute-start(bf16[2,4,64,384]{3,2,1,0:T(8,128)(2,1)} %get-tuple-element.31), channel_id=1, source_target_pairs={{0,12},{4,0},{8,4},{12,8},{1,13},{5,1},{9,5},{13,9},{2,14},{6,2},{... | collective-permute-start | bytes 1179656 | tf_op jit(solution)/shard_map/ppermute | solution.py:26
  142.0 10.3 %collective-permute-start.3 = (bf16[2,4,64,384]{3,2,1,0:T(8,128)(2,1)}, bf16[2,4,64,384]{3,2,1,0:T(8,128)(2,1)S(1)}, u32[]{:S(2)}, u32[]{:S(2)}) collective-permute-start(bf16[2,4,64,384]{3,2,1,0:T(8,128)(2,1)} %get-tuple-element.32), channel_id=1, source_target_pairs={{0,8},{4,12},{8,0},{12,4},{1,9},{5,13},{9,1},{13,5},{2,10},{6,14},... | collective-permute-start | bytes 1179656 | tf_op jit(solution)/shard_map/ppermute | solution.py:26
  144.5 17.2 %collective-permute-start.4 = (bf16[2,4,64,384]{3,2,1,0:T(8,128)(2,1)}, bf16[2,4,64,384]{3,2,1,0:T(8,128)(2,1)S(1)}, u32[]{:S(2)}, u32[]{:S(2)}) collective-permute-start(bf16[2,4,64,384]{3,2,1,0:T(8,128)(2,1)} %get-tuple-element.33), channel_id=1, source_target_pairs={{0,4},{4,8},{8,12},{12,0},{1,5},{5,9},{9,13},{13,1},{2,6},{6,10},{... | collective-permute-start | bytes 1179656 | tf_op jit(solution)/shard_map/ppermute | solution.py:26
  161.8 1.0 copy-start.2
  162.8 9.5 %copy-start = (bf16[384,768]{1,0:T(8,128)(2,1)S(1)}, bf16[384,768]{1,0:T(8,128)(2,1)}, u32[]{:S(2)}) copy-start(bf16[384,768]{1,0:T(8,128)(2,1)} %w_ref.1) | copy-start | bytes 1769476
  163.0 7.9 %collective-permute-start.5 = (bf16[4,64,384]{2,1,0:T(8,128)(2,1)S(1)}, bf16[4,64,384]{2,1,0:T(8,128)(2,1)S(1)}, u32[]{:S(2)}, u32[]{:S(2)}) collective-permute-start(bf16[4,64,384]{2,1,0:T(8,128)(2,1)S(1)} %get-tuple-element.35), channel_id=1, source_target_pairs={{0,16},{16,0},{1,17},{17,1},{2,18},{18,2},{3,19},{19,3},{4,20},{20... | collective-permute-start | bytes 589832 | tf_op jit(solution)/shard_map/ppermute | solution.py:26
  168.9 3.4 %collective-permute-start.1 = (bf16[4,64,384]{2,1,0:T(8,128)(2,1)S(1)}, bf16[4,64,384]{2,1,0:T(8,128)(2,1)S(1)}, u32[]{:S(2)}, u32[]{:S(2)}) collective-permute-start(bf16[4,64,384]{2,1,0:T(8,128)(2,1)S(1)} %get-tuple-element.26), channel_id=1, source_target_pairs={{0,16},{16,0},{1,17},{17,1},{2,18},{18,2},{3,19},{19,3},{4,20},{20... | collective-permute-start | bytes 589832 | tf_op jit(solution)/shard_map/ppermute | solution.py:26

commit v15 on v13

--- a/solution.py
+++ b/solution.py
@@ -32,6 +32,11 @@
         jnp.concatenate([one[:, :half], two[:, :half]], axis=1),
         jnp.concatenate([one[:, half:], two[:, half:]], axis=1),
     )
+
+
+def swap(block, axis, bit):
+    n = lax.axis_size(axis)
+    return lax.ppermute(block, axis, [(i, i ^ bit) for i in range(n)])
 
 
 def pack_kernel(
@@ -179,19 +184,43 @@
             ref[s, :, p * 128 : p * 128 + 128] = value[n * res : (n + 1) * res, s * 128 : s * 128 + 128]
 
 
-def row_kernel(scale, place_ref, mats_ref, right_ref, row_hbm, mats_hbm, row_ref, sems):
-    handed = pltpu.make_async_copy(mats_ref, mats_hbm, sems.at[2])
+def row_kernel(scale, place_ref, mats_ref, right_ref, own_hbm, near_hbm, mine_hbm, cross_hbm, mats_hbm, row_ref, sems):
+    handed = pltpu.make_async_copy(mats_ref, mats_hbm, sems.at[0])
     handed.start()
-    copies = [pltpu.make_async_copy(row_ref.at[:, slot], row_hbm.at[:, slot], sems.at[slot]) for slot in range(2)]
+    here = place_ref[2]
+    near = here + 1 - 2 * lax.rem(here, 2)
     blocks = rights(place_ref, right_ref)
-    for slot in range(2):
+    copies = [handed]
+    for slot in (1, 0):
         for p in range(3):
             side = slab([(pair[slot],) for pair in blocks], p)
-            put([row_ref.at[n, slot] for n in range(4)], product(mats_ref, p, side, 1, scale), p)
-        copies[slot].start()
-    handed.wait()
+            put([row_ref.at[slot, n] for n in range(4)], product(mats_ref, p, side, 1, scale), p)
+        if slot == 1:
+            moves = (
+                (row_ref.at[1, near], near_hbm.at[0]),
+                (row_ref.at[1, lax.rem(near + 2, 4)], near_hbm.at[1]),
+                (row_ref.at[1, here], mine_hbm),
+                (row_ref.at[1, lax.rem(here + 2, 4)], cross_hbm),
+            )
+        else:
+            moves = ((row_ref.at[0], own_hbm),)
+        for src, dst in moves:
+            copy = pltpu.make_async_copy(src, dst, sems.at[len(copies)])
+            copy.start()
+            copies.append(copy)
     for copy in copies:
         copy.wait()
+
+
+def cross_kernel(cross_ref, got_ref, out_ref):
+    for s in range(out_ref.shape[0]):
+        out_ref[s] = (cross_ref[s].astype(F32) + got_ref[1, s].astype(F32)).astype(BF16)
+
+
+def other_rows_kernel(mine_ref, got_ref, crossed_ref, out_ref):
+    for s in range(out_ref.shape[0]):
+        total = mine_ref[s].astype(F32) + got_ref[0, s].astype(F32) + crossed_ref[s].astype(F32)
+        out_ref[s] = total.astype(BF16)
 
 
 def col_kernel(scale, mats_ref, own_ref, other_ref, *refs):
@@ -219,8 +248,9 @@
         send_ref[s] = four([ref.at[1] for ref in refs], s)
 
 
-def total_blocks_kernel(part_ref, keep_ref, send_ref):
-    total_kernel(*[part_ref.at[n] for n in range(4)], keep_ref, send_ref)
+def total_blocks_kernel(part_ref, out_ref):
+    for s in range(out_ref.shape[0]):
+        out_ref[s] = four([part_ref.at[n] for n in range(4)], s)
 
 
 def unpacked(first, keep, got):
@@ -246,7 +276,7 @@
     seqs, res, width = queries.shape
     model_dim = out_weight.shape[1]
     scale = 1.0 / math.sqrt(width // HEADS * seqs * 32)
-    place = jnp.stack([lax.axis_index("c"), lax.axis_index("x")]).astype(jnp.int32)
+    place = jnp.stack([lax.axis_index(axis) for axis in ("c", "x", "zl")]).astype(jnp.int32)
     block = (seqs, res, width)
     smem = pl.BlockSpec(memory_space=pltpu.SMEM)
     vmem = pl.BlockSpec(memory_space=pltpu.VMEM)
@@ -303,15 +333,17 @@
     )(mats)
     mats = exchange(mats, "y")
 
-    row, mats = pl.pallas_call(
+    pair, single = pltpu.HBM((2,) + block, BF16), pltpu.HBM(block, BF16)
+    row, near, mine, cross, mats = pl.pallas_call(
         lambda *refs: row_kernel(scale, *refs),
         in_specs=[smem] + [vmem] * 2,
-        out_specs=[hbm] * 2,
-        out_shape=(pltpu.HBM((4, 2) + block, BF16), pltpu.HBM(mats.shape, BF16)),
-        scratch_shapes=[pltpu.VMEM((4, 2) + block, BF16), pltpu.SemaphoreType.DMA((3,))],
+        out_specs=[hbm] * 5,
+        out_shape=(pltpu.HBM((4,) + block, BF16), pair, single, single, pltpu.HBM(mats.shape, BF16)),
+        scratch_shapes=[pltpu.VMEM((2, 4) + block, BF16), pltpu.SemaphoreType.DMA((6,))],
         compiler_params=params(),
         name="row_products",
     )(place, mats, right)
+    near = swap(near, "zl", 1)
     cols = pl.pallas_call(
         lambda *refs: col_kernel(scale, *refs),
         in_specs=[vmem] * 3,
@@ -333,8 +365,12 @@
         compiler_params=params(),
         name="finish_columns",
     )(place, keep, shift(send, "c", 1))
-    keep, send = pl.pallas_call(
-        total_blocks_kernel, out_shape=(array(block), array(block)), compiler_params=params(), name="total_rows"
+    cross = pl.pallas_call(cross_kernel, out_shape=array(block), compiler_params=params(), name="cross")(cross, near)
+    send = pl.pallas_call(
+        other_rows_kernel, out_shape=array(block), compiler_params=params(), name="other_rows"
+    )(mine, near, swap(cross, "zl", 2))
+    keep = pl.pallas_call(
+        total_blocks_kernel, out_shape=array(block), compiler_params=params(), name="total_rows"
     )(row)
     mixed, grad_query = pl.pallas_call(
         finish_rows_kernel,

time: 174 us -> 174 us (level); the launches traced: 170 us -> 173 us
  starting transfers between devices: 44.1 us -> 52.4 us
  waiting for transfers between devices: 10.4 us -> 5.91 us
    ppermute x0 -> x2, starting transfers between devices: none -> 7.48 us  [swap(): return lax.ppermute(block, axis, [(i, i ^ bit) for i in range(n)])]
    ppermute x6, waiting for transfers between devices: 10.4 us -> 5.9 us  [shift(): return lax.ppermute(block, axis, [(i, (i + by) % n) for i in range(n)])]
  transfers between devices with their start and end apart: 8 -> 10, of which waited for: 3 -> 3; matrix products, arithmetic and copies ran while one was open for 0% -> 0% of each run, Pallas kernels for 2% -> 2%
where the time goes in v15:
time: 174 us; the launch traced here: 173 us
  blocking collectives  99.4 us (57%)
  starting transfers between devices  52.4 us (30%)
  Pallas kernels  13.5 us (8%)
  waiting for transfers between devices  5.91 us (3%)
    all_to_all x4, blocking collectives, exchange(): return lax.all_to_all(blocks, axis, 0, 0, tiled=True)  67.7 us
    ppermute x6, starting transfers between devices, shift(): return lax.ppermute(block, axis, [(i, (i + by) % n) for i in range(n)])  30.5 us
    all_gather x1, blocking collectives, on_device(): own = lax.all_gather(own, 'zl')  16.4 us
    all_gather x1, blocking collectives, on_device(): other = lax.all_gather(other, 'zl')  15.3 us
    all_to_all x2, starting transfers between devices, exchange(): return lax.all_to_all(blocks, axis, 0, 0, tiled=True)  14.5 us
    ppermute x2, starting transfers between devices, swap(): return lax.ppermute(block, axis, [(i, i ^ bit) for i in range(n)])  7.48 us
    ppermute x6, waiting for transfers between devices, shift(): return lax.ppermute(block, axis, [(i, (i + by) % n) for i in range(n)])  5.9 us
  transfers between devices with their start and end apart: 10, of which 3 were waited for; matrix products, arithmetic and copies ran while one was open for 0% of the time, Pallas kernels for 2%

profile of v15, /device:TPU:1, one launch (start us, length us, event | category | flops | bytes accessed | tf_op | source)
XLA Modules:
  0.0 173.2 jit_solution(11069192759922451642)
XLA Ops:
  0.6 0.1 pad_add_fusion.place_ref.refs_0_
  0.7 2.9 %pack.1 = (bf16[4,64,384]{2,1,0:T(8,128)(2,1)S(1)}, bf16[4,64,384]{2,1,0:T(8,128)(2,1)S(1)}, bf16[4,2,4,64,384]{4,3,2,1,0:T(8,128)(2,1)}) custom-call(s32[3]{0:T(128)S(1)} %pad_add_fusion.place_ref.refs_0_, bf16[4,64,384]{2,1,0:T(8,128)(2,1)} %q_hbm.1, bf16[4,64,384]{2,1,0:T(8,128)(2,1)} %k_hbm.1, bf16[4,64,384]{2,1,0:T(8,128)(2,1)} %v_hbm.1, ...), custom_call_target="tpu_custom_call" | custom-call | tf_op jit(solution)/shard_map/pack/pallas_call | solution.py:289
  3.7 10.4 %all-to-all-start = ((bf16[8,4,64,384]{3,2,1,0:T(8,128)(2,1)}), bf16[8,4,64,384]{3,2,1,0:T(8,128)(2,1)S(1)}, u32[]{:S(2)}, u32[]{:S(2)}) async-start(bf16[8,4,64,384]{3,2,1,0:T(8,128)(2,1)} %bitcast.13), calls=%async_computation | async-start | bytes 3145728 | tf_op jit(solution)/shard_map/all_to_all | solution.py:21
  14.0 2.0 %collective-permute-start = (bf16[4,64,384]{2,1,0:T(8,128)(2,1)S(1)}, bf16[4,64,384]{2,1,0:T(8,128)(2,1)S(1)}, u32[]{:S(2)}, u32[]{:S(2)}) collective-permute-start(bf16[4,64,384]{2,1,0:T(8,128)(2,1)S(1)} %get-tuple-element.23), channel_id=1, source_target_pairs={{0,16},{16,0},{1,17},{17,1},{2,18},{18,2},{3,19},{19,3},{4,20},{20... | collective-permute-start | bytes 589832 | tf_op jit(solution)/shard_map/ppermute | solution.py:26
  16.1 16.4 %all-gather = bf16[16,64,384]{2,1,0:T(8,128)(2,1)S(1)} all-gather(bf16[4,64,384]{2,1,0:T(8,128)(2,1)S(1)} %get-tuple-element.22), channel_id=2, replica_groups=mesh['zh'=4,'y'=4,'c'=2,'x'=4,'zl'=4] {'zl'}, dimensions={0}, use_global_device_ids=true | all-gather | bytes 983040 | tf_op jit(solution)/shard_map/all_gather | solution.py:301
  32.5 0.0 collective-permute-done
  32.5 15.3 %all-gather.1 = bf16[16,64,384]{2,1,0:T(8,128)(2,1)S(1)} all-gather(bf16[4,64,384]{2,1,0:T(8,128)(2,1)S(1)} %collective-permute-done), channel_id=3, replica_groups=mesh['zh'=4,'y'=4,'c'=2,'x'=4,'zl'=4] {'zl'}, dimensions={0}, use_global_device_ids=true | all-gather | bytes 983040 | tf_op jit(solution)/shard_map/all_gather | solution.py:302
  47.7 0.0 all-to-all-done
  47.7 1.6 products.1
  49.3 14.5 %all_to_all.30.part_ref = bf16[4,9,64,256]{3,2,1,0:T(8,128)(2,1)S(1)} all-to-all(bf16[4,9,64,256]{3,2,1,0:T(8,128)(2,1)S(1)} %products.1), channel_id=1, replica_groups=mesh['zh'=4,'y'=4,'c'=2,'x'=4,'zl'=4] {'y'}, dimensions={0} | all-to-all | bytes 2359296 | tf_op jit(solution)/shard_map/all_to_all | solution.py:21
  63.8 0.2 rows.1
  64.0 23.8 %all_to_all.31.refs_0_ = bf16[16,72,128]{2,1,0:T(8,128)(2,1)S(1)} all-to-all(bf16[16,72,128]{2,1,0:T(8,128)(2,1)S(1)} %rows.1), channel_id=1, replica_groups=mesh['zh'=4,'y'=4,'c'=2,'x'=4,'zl'=4] {'zh','zl'}, dimensions={0} | all-to-all | bytes 589824 | tf_op jit(solution)/shard_map/all_to_all | solution.py:21
  87.8 0.3 softmax.1
  88.1 18.7 %all_to_all.32.mats_ref = bf16[16,48,128]{2,1,0:T(8,128)(2,1)S(1)} all-to-all(bf16[16,48,128]{2,1,0:T(8,128)(2,1)S(1)} %softmax.1), channel_id=1, replica_groups=mesh['zh'=4,'y'=4,'c'=2,'x'=4,'zl'=4] {'zh','zl'}, dimensions={0} | all-to-all | bytes 393216 | tf_op jit(solution)/shard_map/all_to_all | solution.py:21
  106.7 0.1 unpack.1
  106.9 10.7 %all_to_all.33.refs_1_ = bf16[4,6,64,256]{3,2,1,0:T(8,128)(2,1)S(1)} all-to-all(bf16[4,6,64,256]{3,2,1,0:T(8,128)(2,1)S(1)} %unpack.1), channel_id=1, replica_groups=mesh['zh'=4,'y'=4,'c'=2,'x'=4,'zl'=4] {'y'}, dimensions={0} | all-to-all | bytes 1572864 | tf_op jit(solution)/shard_map/all_to_all | solution.py:21
  117.6 2.6 %row_products.1 = (bf16[4,4,64,384]{3,2,1,0:T(8,128)(2,1)}, bf16[2,4,64,384]{3,2,1,0:T(8,128)(2,1)}, bf16[4,64,384]{2,1,0:T(8,128)(2,1)}, bf16[4,64,384]{2,1,0:T(8,128)(2,1)}, bf16[4,6,64,256]{3,2,1,0:T(8,128)(2,1)}) custom-call(s32[3]{0:T(128)S(1)} %pad_add_fusion.place_ref.refs_0_, bf16[4,6,64,256]{3,2,1,0:T(8,128)(2,1)S(1)} %all_to_all.33.refs_1_, ...), custom_call_target="tpu_custom_call" | custom-call | tf_op jit(solution)/shard_map/row_products/pallas_call | solution.py:337
  120.2 0.0 copy-start.5
  120.2 0.0 copy-start.1
  120.2 4.1 %all-to-all-start.5 = ((bf16[4,4,64,384]{3,2,1,0:T(8,128)(2,1)}), bf16[4,4,64,384]{3,2,1,0:T(8,128)(2,1)S(1)}, u32[]{:S(2)}, u32[]{:S(2)}) async-start(bf16[4,4,64,384]{3,2,1,0:T(8,128)(2,1)} %get-tuple-element.25), calls=%async_computation.5 | async-start | bytes 1572864 | tf_op jit(solution)/shard_map/all_to_all | solution.py:21
  124.3 0.0 copy-start.3
  124.3 0.0 copy-done.5
  124.3 3.5 %collective-permute-start.1 = (bf16[2,4,64,384]{3,2,1,0:T(8,128)(2,1)S(1)}, bf16[2,4,64,384]{3,2,1,0:T(8,128)(2,1)S(1)}, u32[]{:S(2)}, u32[]{:S(2)}) collective-permute-start(bf16[2,4,64,384]{3,2,1,0:T(8,128)(2,1)S(1)} %copy-done.5), channel_id=1, source_target_pairs={{0,1},{1,0},{2,3},{3,2},{4,5},{5,4},{6,7},{7,6},{8,9},{9,8},{10,11... | collective-permute-start | bytes 1179656 | tf_op jit(solution)/shard_map/ppermute | solution.py:39
  127.8 0.0 copy-done.1
  127.8 2.3 %col_products.1 = (bf16[2,4,64,384]{3,2,1,0:T(8,128)(2,1)}, bf16[2,4,64,384]{3,2,1,0:T(8,128)(2,1)}, bf16[2,4,64,384]{3,2,1,0:T(8,128)(2,1)}, bf16[2,4,64,384]{3,2,1,0:T(8,128)(2,1)}) custom-call(bf16[4,6,64,256]{3,2,1,0:T(8,128)(2,1)S(1)} %copy-done.1, bf16[4,4,64,384]{3,2,1,0:T(8,128)(2,1)S(1)} %bitcast.10, bf16[4,4,64,384]{3,2,1,0:T(8,128)(2,1)S(1)} %bitcast.12), custom_call_target="tpu_custom_call" | custom-call | tf_op jit(solution)/shard_map/col_products/pallas_call | solution.py:347
  130.1 0.0 copy-start.4
  130.1 10.9 %collective-permute-start.4 = (bf16[2,4,64,384]{3,2,1,0:T(8,128)(2,1)}, bf16[2,4,64,384]{3,2,1,0:T(8,128)(2,1)S(1)}, u32[]{:S(2)}, u32[]{:S(2)}) collective-permute-start(bf16[2,4,64,384]{3,2,1,0:T(8,128)(2,1)} %get-tuple-element.33), channel_id=1, source_target_pairs={{0,12},{4,0},{8,4},{12,8},{1,13},{5,1},{9,5},{13,9},{2,14},{6,2},{... | collective-permute-start | bytes 1179656 | tf_op jit(solution)/shard_map/ppermute | solution.py:26
  141.0 2.5 %collective-permute-start.5 = (bf16[2,4,64,384]{3,2,1,0:T(8,128)(2,1)}, bf16[2,4,64,384]{3,2,1,0:T(8,128)(2,1)S(1)}, u32[]{:S(2)}, u32[]{:S(2)}) collective-permute-start(bf16[2,4,64,384]{3,2,1,0:T(8,128)(2,1)} %get-tuple-element.34), channel_id=1, source_target_pairs={{0,8},{4,12},{8,0},{12,4},{1,9},{5,13},{9,1},{13,5},{2,10},{6,14},... | collective-permute-start | bytes 1179656 | tf_op jit(solution)/shard_map/ppermute | solution.py:26
  143.5 2.5 %collective-permute-start.6 = (bf16[2,4,64,384]{3,2,1,0:T(8,128)(2,1)}, bf16[2,4,64,384]{3,2,1,0:T(8,128)(2,1)S(1)}, u32[]{:S(2)}, u32[]{:S(2)}) collective-permute-start(bf16[2,4,64,384]{3,2,1,0:T(8,128)(2,1)} %get-tuple-element.35), channel_id=1, source_target_pairs={{0,4},{4,8},{8,12},{12,0},{1,5},{5,9},{9,13},{13,1},{2,6},{6,10},{... | collective-permute-start | bytes 1179656 | tf_op jit(solution)/shard_map/ppermute | solution.py:26
  146.0 0.0 collective-permute-done.1.got_ref
  146.0 0.0 copy-done.3
  146.0 0.1 cross.1
  146.1 4.0 %collective-permute-start.2 = (bf16[4,64,384]{2,1,0:T(8,128)(2,1)S(1)}, bf16[4,64,384]{2,1,0:T(8,128)(2,1)S(1)}, u32[]{:S(2)}, u32[]{:S(2)}) collective-permute-start(bf16[4,64,384]{2,1,0:T(8,128)(2,1)S(1)} %cross.1), channel_id=1, source_target_pairs={{0,2},{1,3},{2,0},{3,1},{4,6},{5,7},{6,4},{7,5},{8,10},{9,11},{10,... | collective-permute-start | bytes 589832 | tf_op jit(solution)/shard_map/ppermute | solution.py:39
  150.1 0.5 collective-permute-done.4.one_ref
  150.6 0.8 collective-permute-done.5.two_ref
  151.4 4.6 %collective-permute-done.6.three_ref = bf16[2,4,64,384]{3,2,1,0:T(8,128)(2,1)S(1)} collective-permute-done((bf16[2,4,64,384]{3,2,1,0:T(8,128)(2,1)}, bf16[2,4,64,384]{3,2,1,0:T(8,128)(2,1)S(1)}, u32[]{:S(2)}, u32[]{:S(2)}) %collective-permute-start.6) | collective-permute-done | bytes 393248 | tf_op jit(solution)/shard_map/ppermute | solution.py:26
  156.0 0.0 copy-start.2
  156.0 1.0 copy-done.2
  157.0 0.2 total_columns.1
  157.2 0.0 copy-start
  157.2 10.7 %collective-permute-start.7 = (bf16[4,64,384]{2,1,0:T(8,128)(2,1)S(1)}, bf16[4,64,384]{2,1,0:T(8,128)(2,1)S(1)}, u32[]{:S(2)}, u32[]{:S(2)}) collective-permute-start(bf16[4,64,384]{2,1,0:T(8,128)(2,1)S(1)} %get-tuple-element.37), channel_id=1, source_target_pairs={{0,16},{16,0},{1,17},{17,1},{2,18},{18,2},{3,19},{19,3},{4,20},{20... | collective-permute-start | bytes 589832 | tf_op jit(solution)/shard_map/ppermute | solution.py:26
  167.9 0.0 collective-permute-done.2.crossed_ref
  167.9 0.0 copy-done.4
  167.9 0.1 other_rows.1
  168.0 1.9 %collective-permute-start.3 = (bf16[4,64,384]{2,1,0:T(8,128)(2,1)S(1)}, bf16[4,64,384]{2,1,0:T(8,128)(2,1)S(1)}, u32[]{:S(2)}, u32[]{:S(2)}) collective-permute-start(bf16[4,64,384]{2,1,0:T(8,128)(2,1)S(1)} %other_rows.1), channel_id=1, source_target_pairs={{0,16},{16,0},{1,17},{17,1},{2,18},{18,2},{3,19},{19,3},{4,20},{20... | collective-permute-start | bytes 589832 | tf_op jit(solution)/shard_map/ppermute | solution.py:26
  169.9 0.0 collective-permute-done.7.got_ref
  169.9 1.4 finish_columns.1
  171.4 0.0 all-to-all-done.5.part_ref
  171.4 0.1 total_rows.1.keep_ref
  171.5 0.0 collective-permute-done.3.got_ref
  171.5 0.0 copy-done
  171.5 1.7 finish_rows.1
Async XLA Ops:
  3.7 44.1 %all-to-all-start = ((bf16[8,4,64,384]{3,2,1,0:T(8,128)(2,1)}), bf16[8,4,64,384]{3,2,1,0:T(8,128)(2,1)S(1)}, u32[]{:S(2)}, u32[]{:S(2)}) async-start(bf16[8,4,64,384]{3,2,1,0:T(8,128)(2,1)} %bitcast.13), calls=%async_computation | async-start | bytes 3145728 | tf_op jit(solution)/shard_map/all_to_all | solution.py:21
  14.0 18.5 %collective-permute-start = (bf16[4,64,384]{2,1,0:T(8,128)(2,1)S(1)}, bf16[4,64,384]{2,1,0:T(8,128)(2,1)S(1)}, u32[]{:S(2)}, u32[]{:S(2)}) collective-permute-start(bf16[4,64,384]{2,1,0:T(8,128)(2,1)S(1)} %get-tuple-element.23), channel_id=1, source_target_pairs={{0,16},{16,0},{1,17},{17,1},{2,18},{18,2},{3,19},{19,3},{4,20},{20... | collective-permute-start | bytes 589832 | tf_op jit(solution)/shard_map/ppermute | solution.py:26
  120.2 4.1 %copy-start.5 = (bf16[2,4,64,384]{3,2,1,0:T(8,128)(2,1)S(1)}, bf16[2,4,64,384]{3,2,1,0:T(8,128)(2,1)}, u32[]{:S(2)}) copy-start(bf16[2,4,64,384]{3,2,1,0:T(8,128)(2,1)} %get-tuple-element.27) | copy-start | bytes 1179652
  120.2 7.6 %copy-start.1 = (bf16[4,6,64,256]{3,2,1,0:T(8,128)(2,1)S(1)}, bf16[4,6,64,256]{3,2,1,0:T(8,128)(2,1)}, u32[]{:S(2)}) copy-start(bf16[4,6,64,256]{3,2,1,0:T(8,128)(2,1)} %get-tuple-element.31.refs_0_) | copy-start | bytes 2359300
  120.2 51.1 %all-to-all-start.5 = ((bf16[4,4,64,384]{3,2,1,0:T(8,128)(2,1)}), bf16[4,4,64,384]{3,2,1,0:T(8,128)(2,1)S(1)}, u32[]{:S(2)}, u32[]{:S(2)}) async-start(bf16[4,4,64,384]{3,2,1,0:T(8,128)(2,1)} %get-tuple-element.25), calls=%async_computation.5 | async-start | bytes 1572864 | tf_op jit(solution)/shard_map/all_to_all | solution.py:21
  124.3 21.7 %copy-start.3 = (bf16[4,64,384]{2,1,0:T(8,128)(2,1)S(1)}, bf16[4,64,384]{2,1,0:T(8,128)(2,1)}, u32[]{:S(2)}) copy-start(bf16[4,64,384]{2,1,0:T(8,128)(2,1)} %get-tuple-element.28.cross_ref) | copy-start | bytes 589828
  124.3 21.7 %collective-permute-start.1 = (bf16[2,4,64,384]{3,2,1,0:T(8,128)(2,1)S(1)}, bf16[2,4,64,384]{3,2,1,0:T(8,128)(2,1)S(1)}, u32[]{:S(2)}, u32[]{:S(2)}) collective-permute-start(bf16[2,4,64,384]{3,2,1,0:T(8,128)(2,1)S(1)} %copy-done.5), channel_id=1, source_target_pairs={{0,1},{1,0},{2,3},{3,2},{4,5},{5,4},{6,7},{7,6},{8,9},{9,8},{10,11... | collective-permute-start | bytes 1179656 | tf_op jit(solution)/shard_map/ppermute | solution.py:39
  130.1 37.8 %copy-start.4 = (bf16[4,64,384]{2,1,0:T(8,128)(2,1)S(1)}, bf16[4,64,384]{2,1,0:T(8,128)(2,1)}, u32[]{:S(2)}) copy-start(bf16[4,64,384]{2,1,0:T(8,128)(2,1)} %get-tuple-element.26.mine_ref) | copy-start | bytes 589828
  130.1 20.5 %collective-permute-start.4 = (bf16[2,4,64,384]{3,2,1,0:T(8,128)(2,1)}, bf16[2,4,64,384]{3,2,1,0:T(8,128)(2,1)S(1)}, u32[]{:S(2)}, u32[]{:S(2)}) collective-permute-start(bf16[2,4,64,384]{3,2,1,0:T(8,128)(2,1)} %get-tuple-element.33), channel_id=1, source_target_pairs={{0,12},{4,0},{8,4},{12,8},{1,13},{5,1},{9,5},{13,9},{2,14},{6,2},{... | collective-permute-start | bytes 1179656 | tf_op jit(solution)/shard_map/ppermute | solution.py:26
  141.0 10.3 %collective-permute-start.5 = (bf16[2,4,64,384]{3,2,1,0:T(8,128)(2,1)}, bf16[2,4,64,384]{3,2,1,0:T(8,128)(2,1)S(1)}, u32[]{:S(2)}, u32[]{:S(2)}) collective-permute-start(bf16[2,4,64,384]{3,2,1,0:T(8,128)(2,1)} %get-tuple-element.34), channel_id=1, source_target_pairs={{0,8},{4,12},{8,0},{12,4},{1,9},{5,13},{9,1},{13,5},{2,10},{6,14},... | collective-permute-start | bytes 1179656 | tf_op jit(solution)/shard_map/ppermute | solution.py:26
  143.5 12.5 %collective-permute-start.6 = (bf16[2,4,64,384]{3,2,1,0:T(8,128)(2,1)}, bf16[2,4,64,384]{3,2,1,0:T(8,128)(2,1)S(1)}, u32[]{:S(2)}, u32[]{:S(2)}) collective-permute-start(bf16[2,4,64,384]{3,2,1,0:T(8,128)(2,1)} %get-tuple-element.35), channel_id=1, source_target_pairs={{0,4},{4,8},{8,12},{12,0},{1,5},{5,9},{9,13},{13,1},{2,6},{6,10},{... | collective-permute-start | bytes 1179656 | tf_op jit(solution)/shard_map/ppermute | solution.py:26
  146.1 21.8 %collective-permute-start.2 = (bf16[4,64,384]{2,1,0:T(8,128)(2,1)S(1)}, bf16[4,64,384]{2,1,0:T(8,128)(2,1)S(1)}, u32[]{:S(2)}, u32[]{:S(2)}) collective-permute-start(bf16[4,64,384]{2,1,0:T(8,128)(2,1)S(1)} %cross.1), channel_id=1, source_target_pairs={{0,2},{1,3},{2,0},{3,1},{4,6},{5,7},{6,4},{7,5},{8,10},{9,11},{10,... | collective-permute-start | bytes 589832 | tf_op jit(solution)/shard_map/ppermute | solution.py:39
  156.0 1.0 copy-start.2
  157.2 14.3 %copy-start = (bf16[384,768]{1,0:T(8,128)(2,1)S(1)}, bf16[384,768]{1,0:T(8,128)(2,1)}, u32[]{:S(2)}) copy-start(bf16[384,768]{1,0:T(8,128)(2,1)} %w_ref.1) | copy-start | bytes 1769476
  157.2 12.7 %collective-permute-start.7 = (bf16[4,64,384]{2,1,0:T(8,128)(2,1)S(1)}, bf16[4,64,384]{2,1,0:T(8,128)(2,1)S(1)}, u32[]{:S(2)}, u32[]{:S(2)}) collective-permute-start(bf16[4,64,384]{2,1,0:T(8,128)(2,1)S(1)} %get-tuple-element.37), channel_id=1, source_target_pairs={{0,16},{16,0},{1,17},{17,1},{2,18},{18,2},{3,19},{19,3},{4,20},{20... | collective-permute-start | bytes 589832 | tf_op jit(solution)/shard_map/ppermute | solution.py:26
  168.0 3.5 %collective-permute-start.3 = (bf16[4,64,384]{2,1,0:T(8,128)(2,1)S(1)}, bf16[4,64,384]{2,1,0:T(8,128)(2,1)S(1)}, u32[]{:S(2)}, u32[]{:S(2)}) collective-permute-start(bf16[4,64,384]{2,1,0:T(8,128)(2,1)S(1)} %other_rows.1), channel_id=1, source_target_pairs={{0,16},{16,0},{1,17},{17,1},{2,18},{18,2},{3,19},{19,3},{4,20},{20... | collective-permute-start | bytes 589832 | tf_op jit(solution)/shard_map/ppermute | solution.py:26

commit v16 on v15

--- a/solution.py
+++ b/solution.py
@@ -355,21 +355,16 @@
     )(mats, own, other)
     row = exchange(row, "zl")
     cols = [cols[0]] + [shift(cols[by], "x", -by) for by in (1, 2, 3)]
+    cross = pl.pallas_call(cross_kernel, out_shape=array(block), compiler_params=params(), name="cross")(cross, near)
+    send_rows = pl.pallas_call(
+        other_rows_kernel, out_shape=array(block), compiler_params=params(), name="other_rows"
+    )(mine, near, swap(cross, "zl", 2))
+    got_rows, cols = lax.optimization_barrier((shift(send_rows, "c", 1), cols))
     keep, send = pl.pallas_call(
         total_kernel, out_shape=(array(block), array(block)), compiler_params=params(), name="total_columns"
     )(*cols)
-    grad_key, grad_value = pl.pallas_call(
-        finish_columns_kernel,
-        in_specs=[smem, vmem, vmem],
-        out_shape=(array(block), array(block)),
-        compiler_params=params(),
-        name="finish_columns",
-    )(place, keep, shift(send, "c", 1))
-    cross = pl.pallas_call(cross_kernel, out_shape=array(block), compiler_params=params(), name="cross")(cross, near)
-    send = pl.pallas_call(
-        other_rows_kernel, out_shape=array(block), compiler_params=params(), name="other_rows"
-    )(mine, near, swap(cross, "zl", 2))
-    keep = pl.pallas_call(
+    got_columns = shift(send, "c", 1)
+    keep_rows = pl.pallas_call(
         total_blocks_kernel, out_shape=array(block), compiler_params=params(), name="total_rows"
     )(row)
     mixed, grad_query = pl.pallas_call(
@@ -378,7 +373,15 @@
         out_shape=(array((seqs, res, model_dim)), array(block)),
         compiler_params=params(),
         name="finish_rows",
-    )(place, keep, shift(send, "c", 1), out_weight)
+    )(place, keep_rows, got_rows, out_weight)
+    got_columns, mixed, grad_query = lax.optimization_barrier((got_columns, mixed, grad_query))
+    grad_key, grad_value = pl.pallas_call(
+        finish_columns_kernel,
+        in_specs=[smem, vmem, vmem],
+        out_shape=(array(block), array(block)),
+        compiler_params=params(),
+        name="finish_columns",
+    )(place, keep, got_columns)
     return mixed, grad_query, grad_key, grad_value
 
 

time: 174 us -> 177 us (1.017)
  starting transfers between devices: 52.4 us -> 61.8 us
  waiting for transfers between devices: 5.91 us -> 1.04 us
    ppermute x6, starting transfers between devices: 30.5 us -> 39.9 us  [shift(): return lax.ppermute(block, axis, [(i, (i + by) % n) for i in range(n)])]
    ppermute x6, waiting for transfers between devices: 5.9 us -> 1.03 us  [shift(): return lax.ppermute(block, axis, [(i, (i + by) % n) for i in range(n)])]
  transfers between devices with their start and end apart: 10 -> 10, of which waited for: 3 -> 1; matrix products, arithmetic and copies ran while one was open for 0% -> 0% of each run, Pallas kernels for 2% -> 2%
where the time goes in v16:
time: 177 us
  blocking collectives  99.4 us (56%)
  starting transfers between devices  61.8 us (35%)
  Pallas kernels  13.5 us (8%)
    all_to_all x4, blocking collectives, exchange(): return lax.all_to_all(blocks, axis, 0, 0, tiled=True)  67.7 us
    ppermute x6, starting transfers between devices, shift(): return lax.ppermute(block, axis, [(i, (i + by) % n) for i in range(n)])  39.9 us
    all_gather x1, blocking collectives, on_device(): own = lax.all_gather(own, 'zl')  16.4 us
    all_gather x1, blocking collectives, on_device(): other = lax.all_gather(other, 'zl')  15.3 us
    all_to_all x2, starting transfers between devices, exchange(): return lax.all_to_all(blocks, axis, 0, 0, tiled=True)  14.5 us
    ppermute x2, starting transfers between devices, swap(): return lax.ppermute(block, axis, [(i, i ^ bit) for i in range(n)])  7.49 us
  transfers between devices with their start and end apart: 10, of which 1 were waited for; matrix products, arithmetic and copies ran while one was open for 0% of the time, Pallas kernels for 2%

profile of v16, /device:TPU:1, one launch (start us, length us, event | category | flops | bytes accessed | tf_op | source)
XLA Modules:
  0.0 176.7 jit_solution(2172212298680029288)
XLA Ops:
  0.6 0.1 pad_add_fusion.place_ref.refs_0_
  0.7 2.9 %pack.1 = (bf16[4,64,384]{2,1,0:T(8,128)(2,1)S(1)}, bf16[4,64,384]{2,1,0:T(8,128)(2,1)S(1)}, bf16[4,2,4,64,384]{4,3,2,1,0:T(8,128)(2,1)}) custom-call(s32[3]{0:T(128)S(1)} %pad_add_fusion.place_ref.refs_0_, bf16[4,64,384]{2,1,0:T(8,128)(2,1)} %q_hbm.1, bf16[4,64,384]{2,1,0:T(8,128)(2,1)} %k_hbm.1, bf16[4,64,384]{2,1,0:T(8,128)(2,1)} %v_hbm.1, ...), custom_call_target="tpu_custom_call" | custom-call | tf_op jit(solution)/shard_map/pack/pallas_call | solution.py:289
  3.7 10.4 %all-to-all-start = ((bf16[8,4,64,384]{3,2,1,0:T(8,128)(2,1)}), bf16[8,4,64,384]{3,2,1,0:T(8,128)(2,1)S(1)}, u32[]{:S(2)}, u32[]{:S(2)}) async-start(bf16[8,4,64,384]{3,2,1,0:T(8,128)(2,1)} %bitcast.13), calls=%async_computation | async-start | bytes 3145728 | tf_op jit(solution)/shard_map/all_to_all | solution.py:21
  14.0 2.0 %collective-permute-start = (bf16[4,64,384]{2,1,0:T(8,128)(2,1)S(1)}, bf16[4,64,384]{2,1,0:T(8,128)(2,1)S(1)}, u32[]{:S(2)}, u32[]{:S(2)}) collective-permute-start(bf16[4,64,384]{2,1,0:T(8,128)(2,1)S(1)} %get-tuple-element.31), channel_id=1, source_target_pairs={{0,16},{16,0},{1,17},{17,1},{2,18},{18,2},{3,19},{19,3},{4,20},{20... | collective-permute-start | bytes 589832 | tf_op jit(solution)/shard_map/ppermute | solution.py:26
  16.1 16.4 %all-gather = bf16[16,64,384]{2,1,0:T(8,128)(2,1)S(1)} all-gather(bf16[4,64,384]{2,1,0:T(8,128)(2,1)S(1)} %get-tuple-element.30), channel_id=2, replica_groups=mesh['zh'=4,'y'=4,'c'=2,'x'=4,'zl'=4] {'zl'}, dimensions={0}, use_global_device_ids=true | all-gather | bytes 983040 | tf_op jit(solution)/shard_map/all_gather | solution.py:301
  32.5 0.0 collective-permute-done
  32.5 15.3 %all-gather.1 = bf16[16,64,384]{2,1,0:T(8,128)(2,1)S(1)} all-gather(bf16[4,64,384]{2,1,0:T(8,128)(2,1)S(1)} %collective-permute-done), channel_id=3, replica_groups=mesh['zh'=4,'y'=4,'c'=2,'x'=4,'zl'=4] {'zl'}, dimensions={0}, use_global_device_ids=true | all-gather | bytes 983040 | tf_op jit(solution)/shard_map/all_gather | solution.py:302
  47.7 0.0 all-to-all-done
  47.7 1.6 products.1
  49.3 14.5 %all_to_all.30.part_ref = bf16[4,9,64,256]{3,2,1,0:T(8,128)(2,1)S(1)} all-to-all(bf16[4,9,64,256]{3,2,1,0:T(8,128)(2,1)S(1)} %products.1), channel_id=1, replica_groups=mesh['zh'=4,'y'=4,'c'=2,'x'=4,'zl'=4] {'y'}, dimensions={0} | all-to-all | bytes 2359296 | tf_op jit(solution)/shard_map/all_to_all | solution.py:21
  63.8 0.2 rows.1
  64.0 23.8 %all_to_all.31.refs_0_ = bf16[16,72,128]{2,1,0:T(8,128)(2,1)S(1)} all-to-all(bf16[16,72,128]{2,1,0:T(8,128)(2,1)S(1)} %rows.1), channel_id=1, replica_groups=mesh['zh'=4,'y'=4,'c'=2,'x'=4,'zl'=4] {'zh','zl'}, dimensions={0} | all-to-all | bytes 589824 | tf_op jit(solution)/shard_map/all_to_all | solution.py:21
  87.8 0.3 softmax.1
  88.1 18.7 %all_to_all.32.mats_ref = bf16[16,48,128]{2,1,0:T(8,128)(2,1)S(1)} all-to-all(bf16[16,48,128]{2,1,0:T(8,128)(2,1)S(1)} %softmax.1), channel_id=1, replica_groups=mesh['zh'=4,'y'=4,'c'=2,'x'=4,'zl'=4] {'zh','zl'}, dimensions={0} | all-to-all | bytes 393216 | tf_op jit(solution)/shard_map/all_to_all | solution.py:21
  106.7 0.1 unpack.1
  106.9 10.7 %all_to_all.33.refs_1_ = bf16[4,6,64,256]{3,2,1,0:T(8,128)(2,1)S(1)} all-to-all(bf16[4,6,64,256]{3,2,1,0:T(8,128)(2,1)S(1)} %unpack.1), channel_id=1, replica_groups=mesh['zh'=4,'y'=4,'c'=2,'x'=4,'zl'=4] {'y'}, dimensions={0} | all-to-all | bytes 1572864 | tf_op jit(solution)/shard_map/all_to_all | solution.py:21
  117.6 2.6 %row_products.1 = (bf16[4,4,64,384]{3,2,1,0:T(8,128)(2,1)}, bf16[2,4,64,384]{3,2,1,0:T(8,128)(2,1)}, bf16[4,64,384]{2,1,0:T(8,128)(2,1)}, bf16[4,64,384]{2,1,0:T(8,128)(2,1)}, bf16[4,6,64,256]{3,2,1,0:T(8,128)(2,1)}) custom-call(s32[3]{0:T(128)S(1)} %pad_add_fusion.place_ref.refs_0_, bf16[4,6,64,256]{3,2,1,0:T(8,128)(2,1)S(1)} %all_to_all.33.refs_1_, ...), custom_call_target="tpu_custom_call" | custom-call | tf_op jit(solution)/shard_map/row_products/pallas_call | solution.py:337
  120.2 0.0 copy-start.5
  120.2 0.0 copy-start.1
  120.2 4.1 %all-to-all-start.5 = ((bf16[4,4,64,384]{3,2,1,0:T(8,128)(2,1)}), bf16[4,4,64,384]{3,2,1,0:T(8,128)(2,1)S(1)}, u32[]{:S(2)}, u32[]{:S(2)}) async-start(bf16[4,4,64,384]{3,2,1,0:T(8,128)(2,1)} %get-tuple-element.46), calls=%async_computation.5 | async-start | bytes 1572864 | tf_op jit(solution)/shard_map/all_to_all | solution.py:21
  124.3 0.0 copy-start.3
  124.3 0.0 copy-done.5
  124.3 3.5 %collective-permute-start.1 = (bf16[2,4,64,384]{3,2,1,0:T(8,128)(2,1)S(1)}, bf16[2,4,64,384]{3,2,1,0:T(8,128)(2,1)S(1)}, u32[]{:S(2)}, u32[]{:S(2)}) collective-permute-start(bf16[2,4,64,384]{3,2,1,0:T(8,128)(2,1)S(1)} %copy-done.5), channel_id=1, source_target_pairs={{0,1},{1,0},{2,3},{3,2},{4,5},{5,4},{6,7},{7,6},{8,9},{9,8},{10,11... | collective-permute-start | bytes 1179656 | tf_op jit(solution)/shard_map/ppermute | solution.py:39
  127.8 0.0 copy-done.1
  127.8 0.0 copy-start.4
  127.8 2.3 %col_products.1 = (bf16[2,4,64,384]{3,2,1,0:T(8,128)(2,1)}, bf16[2,4,64,384]{3,2,1,0:T(8,128)(2,1)}, bf16[2,4,64,384]{3,2,1,0:T(8,128)(2,1)}, bf16[2,4,64,384]{3,2,1,0:T(8,128)(2,1)}) custom-call(bf16[4,6,64,256]{3,2,1,0:T(8,128)(2,1)S(1)} %copy-done.1, bf16[4,4,64,384]{3,2,1,0:T(8,128)(2,1)S(1)} %bitcast.10, bf16[4,4,64,384]{3,2,1,0:T(8,128)(2,1)S(1)} %bitcast.12), custom_call_target="tpu_custom_call" | custom-call | tf_op jit(solution)/shard_map/col_products/pallas_call | solution.py:347
  130.1 0.0 copy-start.2
  130.1 10.9 %collective-permute-start.4 = (bf16[2,4,64,384]{3,2,1,0:T(8,128)(2,1)}, bf16[2,4,64,384]{3,2,1,0:T(8,128)(2,1)S(1)}, u32[]{:S(2)}, u32[]{:S(2)}) collective-permute-start(bf16[2,4,64,384]{3,2,1,0:T(8,128)(2,1)} %get-tuple-element.38), channel_id=1, source_target_pairs={{0,12},{4,0},{8,4},{12,8},{1,13},{5,1},{9,5},{13,9},{2,14},{6,2},{... | collective-permute-start | bytes 1179656 | tf_op jit(solution)/shard_map/ppermute | solution.py:26
  141.0 2.5 %collective-permute-start.5 = (bf16[2,4,64,384]{3,2,1,0:T(8,128)(2,1)}, bf16[2,4,64,384]{3,2,1,0:T(8,128)(2,1)S(1)}, u32[]{:S(2)}, u32[]{:S(2)}) collective-permute-start(bf16[2,4,64,384]{3,2,1,0:T(8,128)(2,1)} %get-tuple-element.39), channel_id=1, source_target_pairs={{0,8},{4,12},{8,0},{12,4},{1,9},{5,13},{9,1},{13,5},{2,10},{6,14},... | collective-permute-start | bytes 1179656 | tf_op jit(solution)/shard_map/ppermute | solution.py:26
  143.5 0.0 collective-permute-done.1.got_ref
  143.5 0.0 copy-done.3
  143.5 0.1 cross.1
  143.6 4.0 %collective-permute-start.2 = (bf16[4,64,384]{2,1,0:T(8,128)(2,1)S(1)}, bf16[4,64,384]{2,1,0:T(8,128)(2,1)S(1)}, u32[]{:S(2)}, u32[]{:S(2)}) collective-permute-start(bf16[4,64,384]{2,1,0:T(8,128)(2,1)S(1)} %cross.1), channel_id=1, source_target_pairs={{0,2},{1,3},{2,0},{3,1},{4,6},{5,7},{6,4},{7,5},{8,10},{9,11},{10,... | collective-permute-start | bytes 589832 | tf_op jit(solution)/shard_map/ppermute | solution.py:39
  147.6 8.0 %collective-permute-start.6 = (bf16[2,4,64,384]{3,2,1,0:T(8,128)(2,1)}, bf16[2,4,64,384]{3,2,1,0:T(8,128)(2,1)S(1)}, u32[]{:S(2)}, u32[]{:S(2)}) collective-permute-start(bf16[2,4,64,384]{3,2,1,0:T(8,128)(2,1)} %get-tuple-element.40), channel_id=1, source_target_pairs={{0,4},{4,8},{8,12},{12,0},{1,5},{5,9},{9,13},{13,1},{2,6},{6,10},{... | collective-permute-start | bytes 1179656 | tf_op jit(solution)/shard_map/ppermute | solution.py:26
  155.6 0.0 collective-permute-done.2.crossed_ref
  155.6 0.0 copy-done.4
  155.6 0.0 copy-start
  155.6 0.1 other_rows.1
  155.7 10.6 %collective-permute-start.3 = (bf16[4,64,384]{2,1,0:T(8,128)(2,1)S(1)}, bf16[4,64,384]{2,1,0:T(8,128)(2,1)S(1)}, u32[]{:S(2)}, u32[]{:S(2)}) collective-permute-start(bf16[4,64,384]{2,1,0:T(8,128)(2,1)S(1)} %other_rows.1), channel_id=1, source_target_pairs={{0,16},{16,0},{1,17},{17,1},{2,18},{18,2},{3,19},{19,3},{4,20},{20... | collective-permute-start | bytes 589832 | tf_op jit(solution)/shard_map/ppermute | solution.py:26
  166.3 0.0 collective-permute-done.4.one_ref
  166.4 0.0 collective-permute-done.5.two_ref
  166.4 0.0 collective-permute-done.6.three_ref
  166.4 1.0 collective-permute-done.3.got_ref
  167.4 0.0 copy-done.2
  167.4 0.2 total_columns.1
  167.6 5.9 %collective-permute-start.7 = (bf16[4,64,384]{2,1,0:T(8,128)(2,1)S(1)}, bf16[4,64,384]{2,1,0:T(8,128)(2,1)S(1)}, u32[]{:S(2)}, u32[]{:S(2)}) collective-permute-start(bf16[4,64,384]{2,1,0:T(8,128)(2,1)S(1)} %get-tuple-element.45), channel_id=1, source_target_pairs={{0,16},{16,0},{1,17},{17,1},{2,18},{18,2},{3,19},{19,3},{4,20},{20... | collective-permute-start | bytes 589832 | tf_op jit(solution)/shard_map/ppermute | solution.py:26
  173.5 0.0 all-to-all-done.5.part_ref
  173.5 0.1 total_rows.1.keep_ref
  173.6 0.0 copy-done
  173.6 1.7 finish_rows.1
  175.3 0.0 collective-permute-done.7.got_ref
  175.3 1.4 finish_columns.1
Async XLA Ops:
  3.7 44.1 %all-to-all-start = ((bf16[8,4,64,384]{3,2,1,0:T(8,128)(2,1)}), bf16[8,4,64,384]{3,2,1,0:T(8,128)(2,1)S(1)}, u32[]{:S(2)}, u32[]{:S(2)}) async-start(bf16[8,4,64,384]{3,2,1,0:T(8,128)(2,1)} %bitcast.13), calls=%async_computation | async-start | bytes 3145728 | tf_op jit(solution)/shard_map/all_to_all | solution.py:21
  14.0 18.5 %collective-permute-start = (bf16[4,64,384]{2,1,0:T(8,128)(2,1)S(1)}, bf16[4,64,384]{2,1,0:T(8,128)(2,1)S(1)}, u32[]{:S(2)}, u32[]{:S(2)}) collective-permute-start(bf16[4,64,384]{2,1,0:T(8,128)(2,1)S(1)} %get-tuple-element.31), channel_id=1, source_target_pairs={{0,16},{16,0},{1,17},{17,1},{2,18},{18,2},{3,19},{19,3},{4,20},{20... | collective-permute-start | bytes 589832 | tf_op jit(solution)/shard_map/ppermute | solution.py:26
  120.2 4.1 %copy-start.5 = (bf16[2,4,64,384]{3,2,1,0:T(8,128)(2,1)S(1)}, bf16[2,4,64,384]{3,2,1,0:T(8,128)(2,1)}, u32[]{:S(2)}) copy-start(bf16[2,4,64,384]{3,2,1,0:T(8,128)(2,1)} %get-tuple-element.34) | copy-start | bytes 1179652
  120.2 7.6 %copy-start.1 = (bf16[4,6,64,256]{3,2,1,0:T(8,128)(2,1)S(1)}, bf16[4,6,64,256]{3,2,1,0:T(8,128)(2,1)}, u32[]{:S(2)}) copy-start(bf16[4,6,64,256]{3,2,1,0:T(8,128)(2,1)} %get-tuple-element.36.refs_0_) | copy-start | bytes 2359300
  120.2 53.3 %all-to-all-start.5 = ((bf16[4,4,64,384]{3,2,1,0:T(8,128)(2,1)}), bf16[4,4,64,384]{3,2,1,0:T(8,128)(2,1)S(1)}, u32[]{:S(2)}, u32[]{:S(2)}) async-start(bf16[4,4,64,384]{3,2,1,0:T(8,128)(2,1)} %get-tuple-element.46), calls=%async_computation.5 | async-start | bytes 1572864 | tf_op jit(solution)/shard_map/all_to_all | solution.py:21
  124.3 19.2 %copy-start.3 = (bf16[4,64,384]{2,1,0:T(8,128)(2,1)S(1)}, bf16[4,64,384]{2,1,0:T(8,128)(2,1)}, u32[]{:S(2)}) copy-start(bf16[4,64,384]{2,1,0:T(8,128)(2,1)} %get-tuple-element.35.cross_ref) | copy-start | bytes 589828
  124.3 19.2 %collective-permute-start.1 = (bf16[2,4,64,384]{3,2,1,0:T(8,128)(2,1)S(1)}, bf16[2,4,64,384]{3,2,1,0:T(8,128)(2,1)S(1)}, u32[]{:S(2)}, u32[]{:S(2)}) collective-permute-start(bf16[2,4,64,384]{3,2,1,0:T(8,128)(2,1)S(1)} %copy-done.5), channel_id=1, source_target_pairs={{0,1},{1,0},{2,3},{3,2},{4,5},{5,4},{6,7},{7,6},{8,9},{9,8},{10,11... | collective-permute-start | bytes 1179656 | tf_op jit(solution)/shard_map/ppermute | solution.py:39
  127.8 27.8 %copy-start.4 = (bf16[4,64,384]{2,1,0:T(8,128)(2,1)S(1)}, bf16[4,64,384]{2,1,0:T(8,128)(2,1)}, u32[]{:S(2)}) copy-start(bf16[4,64,384]{2,1,0:T(8,128)(2,1)} %get-tuple-element.33.mine_ref) | copy-start | bytes 589828
  130.1 37.3 %copy-start.2 = (bf16[2,4,64,384]{3,2,1,0:T(8,128)(2,1)S(1)}, bf16[2,4,64,384]{3,2,1,0:T(8,128)(2,1)}, u32[]{:S(2)}) copy-start(bf16[2,4,64,384]{3,2,1,0:T(8,128)(2,1)} %get-tuple-element.41.zero_ref) | copy-start | bytes 1179652
  130.1 36.2 %collective-permute-start.4 = (bf16[2,4,64,384]{3,2,1,0:T(8,128)(2,1)}, bf16[2,4,64,384]{3,2,1,0:T(8,128)(2,1)S(1)}, u32[]{:S(2)}, u32[]{:S(2)}) collective-permute-start(bf16[2,4,64,384]{3,2,1,0:T(8,128)(2,1)} %get-tuple-element.38), channel_id=1, source_target_pairs={{0,12},{4,0},{8,4},{12,8},{1,13},{5,1},{9,5},{13,9},{2,14},{6,2},{... | collective-permute-start | bytes 1179656 | tf_op jit(solution)/shard_map/ppermute | solution.py:26
  141.0 25.3 %collective-permute-start.5 = (bf16[2,4,64,384]{3,2,1,0:T(8,128)(2,1)}, bf16[2,4,64,384]{3,2,1,0:T(8,128)(2,1)S(1)}, u32[]{:S(2)}, u32[]{:S(2)}) collective-permute-start(bf16[2,4,64,384]{3,2,1,0:T(8,128)(2,1)} %get-tuple-element.39), channel_id=1, source_target_pairs={{0,8},{4,12},{8,0},{12,4},{1,9},{5,13},{9,1},{13,5},{2,10},{6,14},... | collective-permute-start | bytes 1179656 | tf_op jit(solution)/shard_map/ppermute | solution.py:26
  143.6 12.0 %collective-permute-start.2 = (bf16[4,64,384]{2,1,0:T(8,128)(2,1)S(1)}, bf16[4,64,384]{2,1,0:T(8,128)(2,1)S(1)}, u32[]{:S(2)}, u32[]{:S(2)}) collective-permute-start(bf16[4,64,384]{2,1,0:T(8,128)(2,1)S(1)} %cross.1), channel_id=1, source_target_pairs={{0,2},{1,3},{2,0},{3,1},{4,6},{5,7},{6,4},{7,5},{8,10},{9,11},{10,... | collective-permute-start | bytes 589832 | tf_op jit(solution)/shard_map/ppermute | solution.py:39
  147.6 18.8 %collective-permute-start.6 = (bf16[2,4,64,384]{3,2,1,0:T(8,128)(2,1)}, bf16[2,4,64,384]{3,2,1,0:T(8,128)(2,1)S(1)}, u32[]{:S(2)}, u32[]{:S(2)}) collective-permute-start(bf16[2,4,64,384]{3,2,1,0:T(8,128)(2,1)} %get-tuple-element.40), channel_id=1, source_target_pairs={{0,4},{4,8},{8,12},{12,0},{1,5},{5,9},{9,13},{13,1},{2,6},{6,10},{... | collective-permute-start | bytes 1179656 | tf_op jit(solution)/shard_map/ppermute | solution.py:26
  155.6 18.0 %copy-start = (bf16[384,768]{1,0:T(8,128)(2,1)S(1)}, bf16[384,768]{1,0:T(8,128)(2,1)}, u32[]{:S(2)}) copy-start(bf16[384,768]{1,0:T(8,128)(2,1)} %w_ref.1) | copy-start | bytes 1769476
  155.7 11.7 %collective-permute-start.3 = (bf16[4,64,384]{2,1,0:T(8,128)(2,1)S(1)}, bf16[4,64,384]{2,1,0:T(8,128)(2,1)S(1)}, u32[]{:S(2)}, u32[]{:S(2)}) collective-permute-start(bf16[4,64,384]{2,1,0:T(8,128)(2,1)S(1)} %other_rows.1), channel_id=1, source_target_pairs={{0,16},{16,0},{1,17},{17,1},{2,18},{18,2},{3,19},{19,3},{4,20},{20... | collective-permute-start | bytes 589832 | tf_op jit(solution)/shard_map/ppermute | solution.py:26
  167.6 7.7 %collective-permute-start.7 = (bf16[4,64,384]{2,1,0:T(8,128)(2,1)S(1)}, bf16[4,64,384]{2,1,0:T(8,128)(2,1)S(1)}, u32[]{:S(2)}, u32[]{:S(2)}) collective-permute-start(bf16[4,64,384]{2,1,0:T(8,128)(2,1)S(1)} %get-tuple-element.45), channel_id=1, source_target_pairs={{0,16},{16,0},{1,17},{17,1},{2,18},{18,2},{3,19},{19,3},{4,20},{20... | collective-permute-start | bytes 589832 | tf_op jit(solution)/shard_map/ppermute | solution.py:26

commit v17 on v15

--- a/solution.py
+++ b/solution.py
@@ -217,12 +217,6 @@
         out_ref[s] = (cross_ref[s].astype(F32) + got_ref[1, s].astype(F32)).astype(BF16)
 
 
-def other_rows_kernel(mine_ref, got_ref, crossed_ref, out_ref):
-    for s in range(out_ref.shape[0]):
-        total = mine_ref[s].astype(F32) + got_ref[0, s].astype(F32) + crossed_ref[s].astype(F32)
-        out_ref[s] = total.astype(BF16)
-
-
 def col_kernel(scale, mats_ref, own_ref, other_ref, *refs):
     col_hbms, col_ref, sems = refs[:4], refs[4], refs[5]
     for slot, ref in enumerate((own_ref, other_ref)):
@@ -241,34 +235,28 @@
     return ((p[0] + p[1]) + (p[2] + p[3])).astype(BF16)
 
 
-def total_kernel(zero_ref, one_ref, two_ref, three_ref, keep_ref, send_ref):
+def trade_kernel(zero_ref, one_ref, two_ref, three_ref, mine_ref, got_ref, crossed_ref, keep_ref, send_ref):
     refs = (zero_ref, one_ref, two_ref, three_ref)
     for s in range(keep_ref.shape[0]):
         keep_ref[s] = four([ref.at[0] for ref in refs], s)
-        send_ref[s] = four([ref.at[1] for ref in refs], s)
-
-
-def total_blocks_kernel(part_ref, out_ref):
-    for s in range(out_ref.shape[0]):
-        out_ref[s] = four([part_ref.at[n] for n in range(4)], s)
+        send_ref[0, s] = four([ref.at[1] for ref in refs], s)
+        total = mine_ref[s].astype(F32) + got_ref[0, s].astype(F32) + crossed_ref[s].astype(F32)
+        send_ref[1, s] = total.astype(BF16)
 
 
 def unpacked(first, keep, got):
     return halves(jnp.where(first, keep, got), jnp.where(first, got, keep))
 
 
-def finish_columns_kernel(place_ref, keep_ref, got_ref, gk_ref, gv_ref):
+def finish_kernel(place_ref, row_ref, keep_ref, got_ref, w_ref, mixed_ref, gq_ref, gk_ref, gv_ref):
     first = place_ref[0] == 0
+    attended = []
     for s in range(keep_ref.shape[0]):
-        gk_ref[s], gv_ref[s] = unpacked(first, keep_ref[s], got_ref[s])
-
-
-def finish_rows_kernel(place_ref, keep_ref, got_ref, w_ref, mixed_ref, gq_ref):
-    seqs, res, width = keep_ref.shape
-    keep, got = keep_ref[...].reshape(seqs * res, width), got_ref[...].reshape(seqs * res, width)
-    grad_query, attended = unpacked(place_ref[0] == 0, keep, got)
-    gq_ref[...] = grad_query.reshape(seqs, res, width)
-    mixed = jnp.dot(attended, w_ref[...], preferred_element_type=F32).astype(BF16)
+        gk_ref[s], gv_ref[s] = unpacked(first, keep_ref[s], got_ref[0, s])
+        rows = four([row_ref.at[n] for n in range(4)], s)
+        gq_ref[s], one = unpacked(first, rows, got_ref[1, s])
+        attended.append(one)
+    mixed = jnp.dot(jnp.concatenate(attended, axis=0), w_ref[...], preferred_element_type=F32).astype(BF16)
     mixed_ref[...] = mixed.reshape(mixed_ref.shape)
 
 
@@ -355,31 +343,17 @@
     )(mats, own, other)
     row = exchange(row, "zl")
     cols = [cols[0]] + [shift(cols[by], "x", -by) for by in (1, 2, 3)]
+    cross = pl.pallas_call(cross_kernel, out_shape=array(block), compiler_params=params(), name="cross")(cross, near)
     keep, send = pl.pallas_call(
-        total_kernel, out_shape=(array(block), array(block)), compiler_params=params(), name="total_columns"
-    )(*cols)
-    grad_key, grad_value = pl.pallas_call(
-        finish_columns_kernel,
-        in_specs=[smem, vmem, vmem],
-        out_shape=(array(block), array(block)),
-        compiler_params=params(),
-        name="finish_columns",
-    )(place, keep, shift(send, "c", 1))
-    cross = pl.pallas_call(cross_kernel, out_shape=array(block), compiler_params=params(), name="cross")(cross, near)
-    send = pl.pallas_call(
-        other_rows_kernel, out_shape=array(block), compiler_params=params(), name="other_rows"
-    )(mine, near, swap(cross, "zl", 2))
-    keep = pl.pallas_call(
-        total_blocks_kernel, out_shape=array(block), compiler_params=params(), name="total_rows"
-    )(row)
-    mixed, grad_query = pl.pallas_call(
-        finish_rows_kernel,
-        in_specs=[smem] + [vmem] * 3,
-        out_shape=(array((seqs, res, model_dim)), array(block)),
-        compiler_params=params(),
-        name="finish_rows",
-    )(place, keep, shift(send, "c", 1), out_weight)
-    return mixed, grad_query, grad_key, grad_value
+        trade_kernel, out_shape=(array(block), array((2,) + block)), compiler_params=params(), name="trade"
+    )(*cols, mine, near, swap(cross, "zl", 2))
+    return pl.pallas_call(
+        finish_kernel,
+        in_specs=[smem] + [vmem] * 4,
+        out_shape=(array((seqs, res, model_dim)), array(block), array(block), array(block)),
+        compiler_params=params(),
+        name="finish",
+    )(place, row, keep, shift(send, "c", 1), out_weight)
 
 
 def solution(mesh):

time: 174 us -> 172 us (0.989)
  starting transfers between devices: 52.4 us -> 50.4 us
    ppermute x6 -> x5, starting transfers between devices: 30.5 us -> 28.3 us  [shift(): return lax.ppermute(block, axis, [(i, (i + by) % n) for i in range(n)])]
    pallas_call x5 -> x2, Pallas kernels: 3.49 us -> 2.12 us  [the longest x1 1.85 us: on_device(): pl.pallas_call(finish_kernel, in_specs=[smem] + [vmem] * 4, out_shape=(ar...]
    ppermute x6 -> x5, waiting for transfers between devices: 5.9 us -> 7.08 us  [shift(): return lax.ppermute(block, axis, [(i, (i + by) % n) for i in range(n)])]
  transfers between devices with their start and end apart: 10 -> 9, of which waited for: 3 -> 4; matrix products, arithmetic and copies ran while one was open for 0% -> 0% of each run, Pallas kernels for 2% -> 2%
where the time goes in v17:
time: 172 us; the launch traced here: 171 us
  blocking collectives  99.4 us (58%)
  starting transfers between devices  50.4 us (29%)
  Pallas kernels  12.1 us (7%)
  waiting for transfers between devices  7.09 us (4%)
    all_to_all x4, blocking collectives, exchange(): return lax.all_to_all(blocks, axis, 0, 0, tiled=True)  67.7 us
    ppermute x5, starting transfers between devices, shift(): return lax.ppermute(block, axis, [(i, (i + by) % n) for i in range(n)])  28.3 us
    all_gather x1, blocking collectives, on_device(): own = lax.all_gather(own, 'zl')  16.4 us
    all_gather x1, blocking collectives, on_device(): other = lax.all_gather(other, 'zl')  15.3 us
    all_to_all x2, starting transfers between devices, exchange(): return lax.all_to_all(blocks, axis, 0, 0, tiled=True)  14.5 us
    ppermute x2, starting transfers between devices, swap(): return lax.ppermute(block, axis, [(i, i ^ bit) for i in range(n)])  7.61 us
    ppermute x5, waiting for transfers between devices, shift(): return lax.ppermute(block, axis, [(i, (i + by) % n) for i in range(n)])  7.08 us
  transfers between devices with their start and end apart: 9, of which 4 were waited for; matrix products, arithmetic and copies ran while one was open for 0% of the time, Pallas kernels for 2%

profile of v17, /device:TPU:1, one launch (start us, length us, event | category | flops | bytes accessed | tf_op | source)
XLA Modules:
  0.0 170.9 jit_solution(6717646051942915937)
XLA Ops:
  0.6 0.1 pad_add_fusion.place_ref.refs_0_
  0.7 2.9 %pack.1 = (bf16[4,64,384]{2,1,0:T(8,128)(2,1)S(1)}, bf16[4,64,384]{2,1,0:T(8,128)(2,1)S(1)}, bf16[4,2,4,64,384]{4,3,2,1,0:T(8,128)(2,1)}) custom-call(s32[3]{0:T(128)S(1)} %pad_add_fusion.place_ref.refs_0_, bf16[4,64,384]{2,1,0:T(8,128)(2,1)} %q_hbm.1, bf16[4,64,384]{2,1,0:T(8,128)(2,1)} %k_hbm.1, bf16[4,64,384]{2,1,0:T(8,128)(2,1)} %v_hbm.1, ...), custom_call_target="tpu_custom_call" | custom-call | tf_op jit(solution)/shard_map/pack/pallas_call | solution.py:277
  3.7 10.4 %all-to-all-start = ((bf16[8,4,64,384]{3,2,1,0:T(8,128)(2,1)}), bf16[8,4,64,384]{3,2,1,0:T(8,128)(2,1)S(1)}, u32[]{:S(2)}, u32[]{:S(2)}) async-start(bf16[8,4,64,384]{3,2,1,0:T(8,128)(2,1)} %bitcast.13), calls=%async_computation | async-start | bytes 3145728 | tf_op jit(solution)/shard_map/all_to_all | solution.py:21
  14.0 2.0 %collective-permute-start = (bf16[4,64,384]{2,1,0:T(8,128)(2,1)S(1)}, bf16[4,64,384]{2,1,0:T(8,128)(2,1)S(1)}, u32[]{:S(2)}, u32[]{:S(2)}) collective-permute-start(bf16[4,64,384]{2,1,0:T(8,128)(2,1)S(1)} %get-tuple-element.19), channel_id=1, source_target_pairs={{0,16},{16,0},{1,17},{17,1},{2,18},{18,2},{3,19},{19,3},{4,20},{20... | collective-permute-start | bytes 589832 | tf_op jit(solution)/shard_map/ppermute | solution.py:26
  16.1 16.4 %all-gather = bf16[16,64,384]{2,1,0:T(8,128)(2,1)S(1)} all-gather(bf16[4,64,384]{2,1,0:T(8,128)(2,1)S(1)} %get-tuple-element.18), channel_id=2, replica_groups=mesh['zh'=4,'y'=4,'c'=2,'x'=4,'zl'=4] {'zl'}, dimensions={0}, use_global_device_ids=true | all-gather | bytes 983040 | tf_op jit(solution)/shard_map/all_gather | solution.py:289
  32.5 0.0 collective-permute-done
  32.5 15.3 %all-gather.1 = bf16[16,64,384]{2,1,0:T(8,128)(2,1)S(1)} all-gather(bf16[4,64,384]{2,1,0:T(8,128)(2,1)S(1)} %collective-permute-done), channel_id=3, replica_groups=mesh['zh'=4,'y'=4,'c'=2,'x'=4,'zl'=4] {'zl'}, dimensions={0}, use_global_device_ids=true | all-gather | bytes 983040 | tf_op jit(solution)/shard_map/all_gather | solution.py:290
  47.8 0.0 all-to-all-done
  47.8 1.6 products.1
  49.3 14.5 %all_to_all.30.part_ref = bf16[4,9,64,256]{3,2,1,0:T(8,128)(2,1)S(1)} all-to-all(bf16[4,9,64,256]{3,2,1,0:T(8,128)(2,1)S(1)} %products.1), channel_id=1, replica_groups=mesh['zh'=4,'y'=4,'c'=2,'x'=4,'zl'=4] {'y'}, dimensions={0} | all-to-all | bytes 2359296 | tf_op jit(solution)/shard_map/all_to_all | solution.py:21
  63.8 0.2 rows.1
  64.0 23.8 %all_to_all.31.refs_0_ = bf16[16,72,128]{2,1,0:T(8,128)(2,1)S(1)} all-to-all(bf16[16,72,128]{2,1,0:T(8,128)(2,1)S(1)} %rows.1), channel_id=1, replica_groups=mesh['zh'=4,'y'=4,'c'=2,'x'=4,'zl'=4] {'zh','zl'}, dimensions={0} | all-to-all | bytes 589824 | tf_op jit(solution)/shard_map/all_to_all | solution.py:21
  87.8 0.3 softmax.1
  88.1 18.7 %all_to_all.32.mats_ref = bf16[16,48,128]{2,1,0:T(8,128)(2,1)S(1)} all-to-all(bf16[16,48,128]{2,1,0:T(8,128)(2,1)S(1)} %softmax.1), channel_id=1, replica_groups=mesh['zh'=4,'y'=4,'c'=2,'x'=4,'zl'=4] {'zh','zl'}, dimensions={0} | all-to-all | bytes 393216 | tf_op jit(solution)/shard_map/all_to_all | solution.py:21
  106.8 0.1 unpack.1
  106.9 10.7 %all_to_all.33.refs_1_ = bf16[4,6,64,256]{3,2,1,0:T(8,128)(2,1)S(1)} all-to-all(bf16[4,6,64,256]{3,2,1,0:T(8,128)(2,1)S(1)} %unpack.1), channel_id=1, replica_groups=mesh['zh'=4,'y'=4,'c'=2,'x'=4,'zl'=4] {'y'}, dimensions={0} | all-to-all | bytes 1572864 | tf_op jit(solution)/shard_map/all_to_all | solution.py:21
  117.6 2.6 %row_products.1 = (bf16[4,4,64,384]{3,2,1,0:T(8,128)(2,1)}, bf16[2,4,64,384]{3,2,1,0:T(8,128)(2,1)}, bf16[4,64,384]{2,1,0:T(8,128)(2,1)}, bf16[4,64,384]{2,1,0:T(8,128)(2,1)}, bf16[4,6,64,256]{3,2,1,0:T(8,128)(2,1)}) custom-call(s32[3]{0:T(128)S(1)} %pad_add_fusion.place_ref.refs_0_, bf16[4,6,64,256]{3,2,1,0:T(8,128)(2,1)S(1)} %all_to_all.33.refs_1_, ...), custom_call_target="tpu_custom_call" | custom-call | tf_op jit(solution)/shard_map/row_products/pallas_call | solution.py:325
  120.2 0.0 copy-start.5
  120.2 0.0 copy-start.1
  120.2 4.1 %all-to-all-start.5 = ((bf16[4,4,64,384]{3,2,1,0:T(8,128)(2,1)}), bf16[4,4,64,384]{3,2,1,0:T(8,128)(2,1)S(1)}, u32[]{:S(2)}, u32[]{:S(2)}) async-start(bf16[4,4,64,384]{3,2,1,0:T(8,128)(2,1)} %get-tuple-element.21), calls=%async_computation.5 | async-start | bytes 1572864 | tf_op jit(solution)/shard_map/all_to_all | solution.py:21
  124.3 0.0 copy-start.4
  124.3 0.0 copy-done.5
  124.3 3.5 %collective-permute-start.4 = (bf16[2,4,64,384]{3,2,1,0:T(8,128)(2,1)S(1)}, bf16[2,4,64,384]{3,2,1,0:T(8,128)(2,1)S(1)}, u32[]{:S(2)}, u32[]{:S(2)}) collective-permute-start(bf16[2,4,64,384]{3,2,1,0:T(8,128)(2,1)S(1)} %copy-done.5), channel_id=1, source_target_pairs={{0,1},{1,0},{2,3},{3,2},{4,5},{5,4},{6,7},{7,6},{8,9},{9,8},{10,11... | collective-permute-start | bytes 1179656 | tf_op jit(solution)/shard_map/ppermute | solution.py:39
  127.8 0.0 copy-done.1
  127.8 0.0 copy-start.3
  127.9 2.3 %col_products.1 = (bf16[2,4,64,384]{3,2,1,0:T(8,128)(2,1)}, bf16[2,4,64,384]{3,2,1,0:T(8,128)(2,1)}, bf16[2,4,64,384]{3,2,1,0:T(8,128)(2,1)}, bf16[2,4,64,384]{3,2,1,0:T(8,128)(2,1)}) custom-call(bf16[4,6,64,256]{3,2,1,0:T(8,128)(2,1)S(1)} %copy-done.1, bf16[4,4,64,384]{3,2,1,0:T(8,128)(2,1)S(1)} %bitcast.10, bf16[4,4,64,384]{3,2,1,0:T(8,128)(2,1)S(1)} %bitcast.12), custom_call_target="tpu_custom_call" | custom-call | tf_op jit(solution)/shard_map/col_products/pallas_call | solution.py:335
  130.1 10.8 %collective-permute-start.1 = (bf16[2,4,64,384]{3,2,1,0:T(8,128)(2,1)}, bf16[2,4,64,384]{3,2,1,0:T(8,128)(2,1)S(1)}, u32[]{:S(2)}, u32[]{:S(2)}) collective-permute-start(bf16[2,4,64,384]{3,2,1,0:T(8,128)(2,1)} %get-tuple-element.24), channel_id=1, source_target_pairs={{0,12},{4,0},{8,4},{12,8},{1,13},{5,1},{9,5},{13,9},{2,14},{6,2},{... | collective-permute-start | bytes 1179656 | tf_op jit(solution)/shard_map/ppermute | solution.py:26
  140.9 2.5 %collective-permute-start.2 = (bf16[2,4,64,384]{3,2,1,0:T(8,128)(2,1)}, bf16[2,4,64,384]{3,2,1,0:T(8,128)(2,1)S(1)}, u32[]{:S(2)}, u32[]{:S(2)}) collective-permute-start(bf16[2,4,64,384]{3,2,1,0:T(8,128)(2,1)} %get-tuple-element.25), channel_id=1, source_target_pairs={{0,8},{4,12},{8,0},{12,4},{1,9},{5,13},{9,1},{13,5},{2,10},{6,14},... | collective-permute-start | bytes 1179656 | tf_op jit(solution)/shard_map/ppermute | solution.py:26
  143.4 2.5 %collective-permute-start.3 = (bf16[2,4,64,384]{3,2,1,0:T(8,128)(2,1)}, bf16[2,4,64,384]{3,2,1,0:T(8,128)(2,1)S(1)}, u32[]{:S(2)}, u32[]{:S(2)}) collective-permute-start(bf16[2,4,64,384]{3,2,1,0:T(8,128)(2,1)} %get-tuple-element.26), channel_id=1, source_target_pairs={{0,4},{4,8},{8,12},{12,0},{1,5},{5,9},{9,13},{13,1},{2,6},{6,10},{... | collective-permute-start | bytes 1179656 | tf_op jit(solution)/shard_map/ppermute | solution.py:26
  145.9 0.0 collective-permute-done.4.got_ref
  145.9 0.0 copy-done.4
  145.9 0.0 copy-start
  145.9 0.1 cross.1
  146.0 4.1 %collective-permute-start.5 = (bf16[4,64,384]{2,1,0:T(8,128)(2,1)S(1)}, bf16[4,64,384]{2,1,0:T(8,128)(2,1)S(1)}, u32[]{:S(2)}, u32[]{:S(2)}) collective-permute-start(bf16[4,64,384]{2,1,0:T(8,128)(2,1)S(1)} %cross.1), channel_id=1, source_target_pairs={{0,2},{1,3},{2,0},{3,1},{4,6},{5,7},{6,4},{7,5},{8,10},{9,11},{10,... | collective-permute-start | bytes 589832 | tf_op jit(solution)/shard_map/ppermute | solution.py:39
  150.1 0.3 collective-permute-done.1.one_ref
  150.5 0.8 collective-permute-done.2.two_ref
  151.2 4.6 %collective-permute-done.3.three_ref = bf16[2,4,64,384]{3,2,1,0:T(8,128)(2,1)S(1)} collective-permute-done((bf16[2,4,64,384]{3,2,1,0:T(8,128)(2,1)}, bf16[2,4,64,384]{3,2,1,0:T(8,128)(2,1)S(1)}, u32[]{:S(2)}, u32[]{:S(2)}) %collective-permute-start.3) | collective-permute-done | bytes 393248 | tf_op jit(solution)/shard_map/ppermute | solution.py:26
  155.9 0.0 collective-permute-done.5.crossed_ref
  155.9 0.0 copy-done.3
  155.9 0.0 copy-start.2
  155.9 1.0 copy-done.2
  156.9 0.3 trade.1
  157.1 10.6 %collective-permute-start.6 = (bf16[2,4,64,384]{3,2,1,0:T(8,128)(2,1)S(1)}, bf16[2,4,64,384]{3,2,1,0:T(8,128)(2,1)S(1)}, u32[]{:S(2)}, u32[]{:S(2)}) collective-permute-start(bf16[2,4,64,384]{3,2,1,0:T(8,128)(2,1)S(1)} %get-tuple-element.31), channel_id=1, source_target_pairs={{0,16},{16,0},{1,17},{17,1},{2,18},{18,2},{3,19},{19,3},{4,20},{20... | collective-permute-start | bytes 1179656 | tf_op jit(solution)/shard_map/ppermute | solution.py:26
  167.7 1.3 collective-permute-done.6.got_ref
  169.0 0.0 all-to-all-done.5.row_ref
  169.0 0.0 copy-done
  169.0 1.8 %finish.1 = (bf16[4,64,768]{2,1,0:T(8,128)(2,1)}, bf16[4,64,384]{2,1,0:T(8,128)(2,1)}, bf16[4,64,384]{2,1,0:T(8,128)(2,1)}, bf16[4,64,384]{2,1,0:T(8,128)(2,1)}) custom-call(s32[3]{0:T(128)S(1)} %pad_add_fusion.place_ref.refs_0_, bf16[4,4,64,384]{3,2,1,0:T(8,128)(2,1)S(1)} %all-to-all-done.5.row_ref, bf16[4,64,384]{2,1,0:T(8,128)(2,1)S(1)} %get-tuple-element.30.keep_ref, ...), custom_call_target="tpu_custom_call" | custom-call | tf_op jit(solution)/shard_map/finish/pallas_call | solution.py:350
Async XLA Ops:
  3.7 44.1 %all-to-all-start = ((bf16[8,4,64,384]{3,2,1,0:T(8,128)(2,1)}), bf16[8,4,64,384]{3,2,1,0:T(8,128)(2,1)S(1)}, u32[]{:S(2)}, u32[]{:S(2)}) async-start(bf16[8,4,64,384]{3,2,1,0:T(8,128)(2,1)} %bitcast.13), calls=%async_computation | async-start | bytes 3145728 | tf_op jit(solution)/shard_map/all_to_all | solution.py:21
  14.0 18.5 %collective-permute-start = (bf16[4,64,384]{2,1,0:T(8,128)(2,1)S(1)}, bf16[4,64,384]{2,1,0:T(8,128)(2,1)S(1)}, u32[]{:S(2)}, u32[]{:S(2)}) collective-permute-start(bf16[4,64,384]{2,1,0:T(8,128)(2,1)S(1)} %get-tuple-element.19), channel_id=1, source_target_pairs={{0,16},{16,0},{1,17},{17,1},{2,18},{18,2},{3,19},{19,3},{4,20},{20... | collective-permute-start | bytes 589832 | tf_op jit(solution)/shard_map/ppermute | solution.py:26
  120.2 4.1 %copy-start.5 = (bf16[2,4,64,384]{3,2,1,0:T(8,128)(2,1)S(1)}, bf16[2,4,64,384]{3,2,1,0:T(8,128)(2,1)}, u32[]{:S(2)}) copy-start(bf16[2,4,64,384]{3,2,1,0:T(8,128)(2,1)} %get-tuple-element.28) | copy-start | bytes 1179652
  120.2 7.6 %copy-start.1 = (bf16[4,6,64,256]{3,2,1,0:T(8,128)(2,1)S(1)}, bf16[4,6,64,256]{3,2,1,0:T(8,128)(2,1)}, u32[]{:S(2)}) copy-start(bf16[4,6,64,256]{3,2,1,0:T(8,128)(2,1)} %get-tuple-element.22.refs_0_) | copy-start | bytes 2359300
  120.2 48.8 %all-to-all-start.5 = ((bf16[4,4,64,384]{3,2,1,0:T(8,128)(2,1)}), bf16[4,4,64,384]{3,2,1,0:T(8,128)(2,1)S(1)}, u32[]{:S(2)}, u32[]{:S(2)}) async-start(bf16[4,4,64,384]{3,2,1,0:T(8,128)(2,1)} %get-tuple-element.21), calls=%async_computation.5 | async-start | bytes 1572864 | tf_op jit(solution)/shard_map/all_to_all | solution.py:21
  124.3 21.6 %copy-start.4 = (bf16[4,64,384]{2,1,0:T(8,128)(2,1)S(1)}, bf16[4,64,384]{2,1,0:T(8,128)(2,1)}, u32[]{:S(2)}) copy-start(bf16[4,64,384]{2,1,0:T(8,128)(2,1)} %get-tuple-element.29.cross_ref) | copy-start | bytes 589828
  124.3 21.6 %collective-permute-start.4 = (bf16[2,4,64,384]{3,2,1,0:T(8,128)(2,1)S(1)}, bf16[2,4,64,384]{3,2,1,0:T(8,128)(2,1)S(1)}, u32[]{:S(2)}, u32[]{:S(2)}) collective-permute-start(bf16[2,4,64,384]{3,2,1,0:T(8,128)(2,1)S(1)} %copy-done.5), channel_id=1, source_target_pairs={{0,1},{1,0},{2,3},{3,2},{4,5},{5,4},{6,7},{7,6},{8,9},{9,8},{10,11... | collective-permute-start | bytes 1179656 | tf_op jit(solution)/shard_map/ppermute | solution.py:39
  127.8 28.0 %copy-start.3 = (bf16[4,64,384]{2,1,0:T(8,128)(2,1)S(1)}, bf16[4,64,384]{2,1,0:T(8,128)(2,1)}, u32[]{:S(2)}) copy-start(bf16[4,64,384]{2,1,0:T(8,128)(2,1)} %get-tuple-element.27.mine_ref) | copy-start | bytes 589828
  130.1 20.3 %collective-permute-start.1 = (bf16[2,4,64,384]{3,2,1,0:T(8,128)(2,1)}, bf16[2,4,64,384]{3,2,1,0:T(8,128)(2,1)S(1)}, u32[]{:S(2)}, u32[]{:S(2)}) collective-permute-start(bf16[2,4,64,384]{3,2,1,0:T(8,128)(2,1)} %get-tuple-element.24), channel_id=1, source_target_pairs={{0,12},{4,0},{8,4},{12,8},{1,13},{5,1},{9,5},{13,9},{2,14},{6,2},{... | collective-permute-start | bytes 1179656 | tf_op jit(solution)/shard_map/ppermute | solution.py:26
  140.9 10.3 %collective-permute-start.2 = (bf16[2,4,64,384]{3,2,1,0:T(8,128)(2,1)}, bf16[2,4,64,384]{3,2,1,0:T(8,128)(2,1)S(1)}, u32[]{:S(2)}, u32[]{:S(2)}) collective-permute-start(bf16[2,4,64,384]{3,2,1,0:T(8,128)(2,1)} %get-tuple-element.25), channel_id=1, source_target_pairs={{0,8},{4,12},{8,0},{12,4},{1,9},{5,13},{9,1},{13,5},{2,10},{6,14},... | collective-permute-start | bytes 1179656 | tf_op jit(solution)/shard_map/ppermute | solution.py:26
  143.4 12.5 %collective-permute-start.3 = (bf16[2,4,64,384]{3,2,1,0:T(8,128)(2,1)}, bf16[2,4,64,384]{3,2,1,0:T(8,128)(2,1)S(1)}, u32[]{:S(2)}, u32[]{:S(2)}) collective-permute-start(bf16[2,4,64,384]{3,2,1,0:T(8,128)(2,1)} %get-tuple-element.26), channel_id=1, source_target_pairs={{0,4},{4,8},{8,12},{12,0},{1,5},{5,9},{9,13},{13,1},{2,6},{6,10},{... | collective-permute-start | bytes 1179656 | tf_op jit(solution)/shard_map/ppermute | solution.py:26
  145.9 23.1 %copy-start = (bf16[384,768]{1,0:T(8,128)(2,1)S(1)}, bf16[384,768]{1,0:T(8,128)(2,1)}, u32[]{:S(2)}) copy-start(bf16[384,768]{1,0:T(8,128)(2,1)} %w_ref.1) | copy-start | bytes 1769476
  146.0 9.9 %collective-permute-start.5 = (bf16[4,64,384]{2,1,0:T(8,128)(2,1)S(1)}, bf16[4,64,384]{2,1,0:T(8,128)(2,1)S(1)}, u32[]{:S(2)}, u32[]{:S(2)}) collective-permute-start(bf16[4,64,384]{2,1,0:T(8,128)(2,1)S(1)} %cross.1), channel_id=1, source_target_pairs={{0,2},{1,3},{2,0},{3,1},{4,6},{5,7},{6,4},{7,5},{8,10},{9,11},{10,... | collective-permute-start | bytes 589832 | tf_op jit(solution)/shard_map/ppermute | solution.py:39
  155.9 1.0 copy-start.2
  157.1 11.9 %collective-permute-start.6 = (bf16[2,4,64,384]{3,2,1,0:T(8,128)(2,1)S(1)}, bf16[2,4,64,384]{3,2,1,0:T(8,128)(2,1)S(1)}, u32[]{:S(2)}, u32[]{:S(2)}) collective-permute-start(bf16[2,4,64,384]{3,2,1,0:T(8,128)(2,1)S(1)} %get-tuple-element.31), channel_id=1, source_target_pairs={{0,16},{16,0},{1,17},{17,1},{2,18},{18,2},{3,19},{19,3},{4,20},{20... | collective-permute-start | bytes 1179656 | tf_op jit(solution)/shard_map/ppermute | solution.py:26
